TPU v7x, 32 devices: a whole 2x2x4 slice. The times are simulated.
32 devices in a mesh: rows: 16 (over z, y, x), cols: 2 (over core).
Axes of the slice: x: 2, y: 2, z: 4, core: 2. Of those that a mesh axis runs over, the one named last changes fastest.
Arguments:
- lower_pivot: bfloat16 [4, 2048, 4, 2048], P(None, 'rows', None, 'cols'), may hold values from -0.0625 to 0.0625
- lower_rest: bfloat16 [24576, 4, 2048], P('rows', None, 'cols'), may hold values from -0.0625 to 0.0625
- diag_inverse: bfloat16 [4, 2048, 2048], P(None, 'cols', 'rows'), may hold values from -0.125 to 0.125
- rhs_pivot: bfloat16 [4, 2048, 512], P(None, 'rows', 'cols'), may hold values from -6 to 6
- rhs_rest: bfloat16 [512, 24576], P('cols', 'rows'), may hold values from -6 to 6
Outputs:
- solution: bfloat16 [4, 2048, 512], P(None, 'cols')
- remainder: bfloat16 [512, 24576], P('cols', 'rows')
All inputs are finite; a program needn't handle non-finite values.
Results may differ from a plain program's by a relative error of at most 0.017.
Values may be sent and summed in bfloat16 or wider, within the bound.
No kernel may reach another device: no remote copies, remote signals or barrier semaphores. Data moves between devices by JAX's collectives and lax.ppermute only.
A program may use at most 64 MiB of HBM per device.

v0:
```python
import jax
import jax.numpy as jnp
from jax import lax
from jax.sharding import PartitionSpec as P


def per_device(lower_pivot, lower_rest, diag_inverse, rhs_pivot, rhs_rest):
    block_count = lower_pivot.shape[0]
    pivot_rows = lower_pivot.shape[1]
    share_width = lower_pivot.shape[3]
    sides_share = rhs_pivot.shape[2]
    sides_total = sides_share * lax.axis_size("cols")
    rest_rows = lower_rest.shape[0]
    col_offset = lax.axis_index("cols") * sides_share
    solved = []
    for step_index in range(block_count):
        partials = jnp.zeros((pivot_rows, sides_total), jnp.float32)
        partials = lax.dynamic_update_slice(
            partials, rhs_pivot[step_index].astype(jnp.float32), (jnp.int32(0), col_offset)
        )
        if step_index > 0:
            factor_part = lower_pivot[step_index, :, :step_index, :].reshape(
                pivot_rows, step_index * share_width
            )
            known_part = jnp.concatenate(solved, axis=0)
            partials = partials - jnp.dot(
                factor_part, known_part, preferred_element_type=jnp.float32
            )
        residual = lax.psum(partials.astype(jnp.bfloat16), "cols")
        product = jnp.dot(diag_inverse[step_index], residual, preferred_element_type=jnp.float32)
        solved_block = lax.psum(product, "rows").astype(jnp.bfloat16)
        solved.append(solved_block)
    solution = jnp.stack(solved)
    flat_solution = solution.reshape(block_count * share_width, sides_total)
    flat_lower = lower_rest.reshape(rest_rows, block_count * share_width)
    total_sum = lax.psum_scatter(
        lax.dot_general(
            flat_solution, flat_lower, (((0,), (1,)), ((), ())), preferred_element_type=jnp.float32
        ).astype(jnp.bfloat16),
        "cols",
        scatter_dimension=0,
        tiled=True,
    ).astype(jnp.float32)
    remainder = (rhs_rest.astype(jnp.float32) - total_sum).astype(jnp.bfloat16)
    return (solution, remainder)


def solution(mesh):
    placed = (
        P(None, "rows", None, "cols"),
        P("rows", None, "cols"),
        P(None, "cols", "rows"),
        P(None, "rows", "cols"),
        P("cols", "rows"),
    )
    return jax.shard_map(
        per_device,
        mesh=mesh,
        in_specs=placed,
        out_specs=(P(None, "cols", None), P("cols", "rows")),
        check_vma=False,
    )
```

profile of v0, /device:TPU:0, one launch (start us, length us, event | category | flops | bytes accessed | tf_op | source)
XLA Modules:
  0.0 530.6 jit_solution(9156253284171110728)
XLA Ops:
  7.2 0.0 all-reduce.9.cloned.1.call-start
  7.2 0.9 convert_dynamic-update-slice_fusion.3
  8.1 0.7 convert_element_type.62
  8.8 0.0 all-reduce.9.cloned.1.call-update
  8.8 0.0 all-reduce.11.cloned.1.call-start
  8.8 2.4 slice.36
  11.2 1.6 slice.39
  12.8 1.6 slice.42
  14.4 1.2 copy.15
  15.6 1.5 copy.16
  17.1 0.9 convert_dynamic-update-slice_fusion.2
  18.0 13.0 %all-reduce.9.cloned.1.call-done = bf16[128,512]{1,0:T(8,128)(2,1)} async-done(((bf16[128,512]{1,0:T(8,128)(2,1)}), bf16[128,512]{1,0:T(8,128)(2,1)}) %all-reduce.9.cloned.1.call-update) | async-done | bytes 131088 | tf_op jit(solution)/shard_map/psum | solution.py:29
  30.9 1.5 convolution_bitcast_fusion.3
  32.4 100.3 %all-reduce.16 = bf16[1024,512]{0,1:T(8,128)(2,1)S(1)} all-reduce(f32[1024,512]{0,1:T(8,128)S(1)} %convolution_bitcast_fusion.3), channel_id=1, replica_groups=mesh['rows'=16,'cols'=2] {'rows'}, use_global_device_ids=true, to_apply=%region_1.0 | all-reduce | flops 524288 | bytes 3145728 | tf_op jit(solution)/shard_map/psum | solution.py:31
  132.7 2.2 fusion.37
  134.9 0.0 all-reduce.11.cloned.1.call-update
  134.9 0.0 all-reduce.13.cloned.1.call-start
  135.0 0.9 convert_dynamic-update-slice_fusion.1
  135.9 15.2 %all-reduce.11.cloned.1.call-done = bf16[128,512]{1,0:T(8,128)(2,1)} async-done(((bf16[128,512]{1,0:T(8,128)(2,1)}), bf16[128,512]{1,0:T(8,128)(2,1)}) %all-reduce.11.cloned.1.call-update) | async-done | bytes 131088 | tf_op jit(solution)/shard_map/psum | solution.py:29
  151.1 1.5 convolution_bitcast_fusion.2
  152.5 100.8 %all-reduce.17 = bf16[1024,512]{0,1:T(8,128)(2,1)} all-reduce(f32[1024,512]{0,1:T(8,128)S(1)} %convolution_bitcast_fusion.2), channel_id=1, replica_groups=mesh['rows'=16,'cols'=2] {'rows'}, use_global_device_ids=true, to_apply=%region_3.0 | all-reduce | flops 524288 | bytes 3145728 | tf_op jit(solution)/shard_map/psum | solution.py:31
  253.3 2.8 fusion.34
  256.2 0.0 all-reduce.13.cloned.1.call-update
  256.2 0.0 all-reduce.15.cloned.1.call-start
  256.3 0.9 convert_dynamic-update-slice_fusion
  257.1 15.2 %all-reduce.13.cloned.1.call-done = bf16[128,512]{1,0:T(8,128)(2,1)} async-done(((bf16[128,512]{1,0:T(8,128)(2,1)}), bf16[128,512]{1,0:T(8,128)(2,1)}) %all-reduce.13.cloned.1.call-update) | async-done | bytes 131088 | tf_op jit(solution)/shard_map/psum | solution.py:29
  272.3 1.5 convolution_bitcast_fusion.1
  273.8 100.8 %all-reduce.18 = bf16[1024,512]{0,1:T(8,128)(2,1)} all-reduce(f32[1024,512]{0,1:T(8,128)S(1)} %convolution_bitcast_fusion.1), channel_id=1, replica_groups=mesh['rows'=16,'cols'=2] {'rows'}, use_global_device_ids=true, to_apply=%region_5.0 | all-reduce | flops 524288 | bytes 3145728 | tf_op jit(solution)/shard_map/psum | solution.py:31
  374.6 3.6 fusion.31
  378.1 0.0 all-reduce.15.cloned.1.call-update
  378.2 0.0 reduce-scatter.2.cloned.1.call-start
  378.2 16.1 %all-reduce.15.cloned.1.call-done = bf16[128,512]{1,0:T(8,128)(2,1)} async-done(((bf16[128,512]{1,0:T(8,128)(2,1)}), bf16[128,512]{1,0:T(8,128)(2,1)}) %all-reduce.15.cloned.1.call-update) | async-done | bytes 131088 | tf_op jit(solution)/shard_map/psum | solution.py:29
  394.3 1.5 convolution_bitcast_fusion
  395.8 100.9 %all-reduce.19 = bf16[1024,512]{0,1:T(8,128)(2,1)} all-reduce(f32[1024,512]{0,1:T(8,128)S(1)} %convolution_bitcast_fusion), channel_id=1, replica_groups=mesh['rows'=16,'cols'=2] {'rows'}, use_global_device_ids=true, to_apply=%region_7.0 | all-reduce | flops 524288 | bytes 3145728 | tf_op jit(solution)/shard_map/psum | solution.py:31
  496.7 0.0 copy-start
  496.7 0.0 copy-start.1
  496.7 15.3 %fusion.11 = bf16[512,1536]{1,0:T(8,128)(2,1)} fusion(bf16[1536,4,1024]{2,1,0:T(4,128)(2,1)} %param.6, bf16[1,1024,512]{1,2,0:T(8,128)(2,1)} %bitcast.78, bf16[1,1024,512]{1,2,0:T(8,128)(2,1)} %bitcast.76, bf16[1,1024,512]{1,2,0:T(8,128)(2,1)} %bitcast.74, bf16[1,1024,512]{1,2,0:T(8,128)(2,1)S(1)} %bitcast.72), kind=kOutput, calls=%fused_computation.10 | convolution fusion | flops 6449528832 | bytes 18350080 | tf_op jit(solution)/shard_map/dot_general | solution.py:37
  512.0 0.0 reduce-scatter.2.cloned.1.call-update
  512.0 0.0 copy-done
  512.1 0.0 copy-done.1
  512.1 3.3 pad_maximum_fusion
  515.3 0.0 copy-start.2
  515.3 6.6 %copy.13 = bf16[4,1024,512]{2,1,0:T(8,128)(2,1)} copy(bf16[4,1024,512]{1,2,0:T(8,128)(2,1)} %pad_maximum_fusion) | data formatting | bytes 8388608
  521.9 0.0 reduce-scatter.2.cloned.1.call-done
  521.9 0.0 copy-done.2
  521.9 2.2 subtract_convert_fusion
  (4 shorter events, 0.1 us)
Async XLA Ops:
  7.2 23.8 %all-reduce.9.cloned.1.call-start = ((), (), s32[]{:S(2)}) async-start(), calls=%async_computation.1 | async-start | bytes 262144 | tf_op jit(solution)/shard_map/psum | solution.py:29
  8.8 142.3 %all-reduce.11.cloned.1.call-start = ((), (), s32[]{:S(2)}) async-start(), calls=%async_computation.2 | async-start | bytes 262144 | tf_op jit(solution)/shard_map/psum | solution.py:29
  134.9 137.4 %all-reduce.13.cloned.1.call-start = ((), (), s32[]{:S(2)}) async-start(), calls=%async_computation.3 | async-start | bytes 262144 | tf_op jit(solution)/shard_map/psum | solution.py:29
  256.2 138.1 %all-reduce.15.cloned.1.call-start = ((), (), s32[]{:S(2)}) async-start(), calls=%async_computation.4 | async-start | bytes 262144 | tf_op jit(solution)/shard_map/psum | solution.py:29
  378.2 143.7 %reduce-scatter.2.cloned.1.call-start = ((), (), s32[]{:S(2)}) async-start(), calls=%async_computation.5 | async-start | bytes 2359296 | tf_op jit(solution)/shard_map/reduce_scatter | solution.py:36
  496.7 15.3 %copy-start = (bf16[1024,512]{0,1:T(8,128)(2,1)S(1)}, bf16[1024,512]{0,1:T(8,128)(2,1)}, u32[]{:S(2)}) copy-start(bf16[1024,512]{0,1:T(8,128)(2,1)} %all-reduce.17) | copy-start | bytes 3145732
  496.7 15.3 %copy-start.1 = (bf16[1024,512]{0,1:T(8,128)(2,1)S(1)}, bf16[1024,512]{0,1:T(8,128)(2,1)}, u32[]{:S(2)}) copy-start(bf16[1024,512]{0,1:T(8,128)(2,1)} %all-reduce.18) | copy-start | bytes 3145732
  515.3 6.6 %copy-start.2 = (bf16[256,1536]{1,0:T(8,128)(2,1)S(1)}, bf16[256,1536]{1,0:T(8,128)(2,1)}, u32[]{:S(2)}) copy-start(bf16[256,1536]{1,0:T(8,128)(2,1)} %param.9) | copy-start | bytes 2359300
Sparse Core Ops, SparseCore 0:
  10.3 20.5 all-reduce.8
  135.1 15.9 all-reduce.10
  256.3 15.9 all-reduce.12
  378.3 15.9 all-reduce.14
  512.2 7.1 reduce-scatter.1
where the time goes:
time: 532 us; the launch traced here: 531 us
  blocking collectives  403 us (76%)
  waiting for transfers between devices  59.5 us (11%)
  matrix products  29.8 us (6%)
  local copies, waits for them, and re-layouts  14.9 us (3%)
  between operations  13.9 us (3%)
  other arithmetic  9.55 us (2%)
    psum x4, blocking collectives, per_device(): solved_block = lax.psum(product, 'rows').astype(jnp.bfloat16)  403 us
    psum x4, waiting for transfers between devices, per_device(): residual = lax.psum(partials.astype(jnp.bfloat16), 'cols')  59.5 us
    dot_general x1, matrix products, per_device(): lax.dot_general(flat_solution, flat_lower, (((0,), (1,)), ((), ())), pref...  15.3 us
  transfers between devices with their start and end apart: 5, of which 4 were waited for; matrix products, arithmetic and copies ran while one was open for 4% of the time, Pallas kernels for 0%

commit v1 on v0

v1 whole, which is shorter than its diff:
```python
import functools

import jax
import jax.numpy as jnp
from jax import lax
from jax.sharding import PartitionSpec as P
from jax.experimental import pallas as pl
from jax.experimental.pallas import tpu as pltpu

F32 = jnp.float32
BF16 = jnp.bfloat16


def split_of(count):
    best = 1
    for d in range(1, count + 1):
        if count % d == 0 and d * d <= count:
            best = d
    return best


def nt_dot(a, b):
    return lax.dot_general(a, b, (((1,), (1,)), ((), ())), preferred_element_type=F32)


def cut(n_rows, share):
    plane = split_of(n_rows)
    power = plane & (plane - 1) == 0
    code = [g ^ (g >> 1) if power else g for g in range(plane)]
    return plane, n_rows // plane, share // plane, code


def places(plane, code):
    row = lax.axis_index("rows")
    spot = row % plane
    g = sum(jnp.where(spot == code[i], i, 0) for i in range(plane))
    return g, row // plane, lax.axis_index("cols")


def movers(plane, depth, code, n_cols):
    def along_plane(x, k):
        pairs = [(b * plane + code[i], b * plane + code[(i + k) % plane]) for b in range(depth) for i in range(plane)]
        return lax.ppermute(x, "rows", pairs)

    def along_depth(x, k):
        pairs = [(b * plane + i, ((b + k) % depth) * plane + i) for b in range(depth) for i in range(plane)]
        return lax.ppermute(x, "rows", pairs)

    def along_cols(x, k):
        return lax.ppermute(x, "cols", [(i, (i + k) % n_cols) for i in range(n_cols)])

    return along_plane, along_depth, along_cols


def plain_path(lower_pivot, lower_rest, diag_inverse, rhs_pivot, rhs_rest):
    steps = lower_pivot.shape[0]
    eqs = lower_pivot.shape[1]
    share = lower_pivot.shape[3]
    sides = rhs_pivot.shape[2]
    rest = lower_rest.shape[0]
    n_rows = lax.axis_size("rows")
    n_cols = lax.axis_size("cols")
    plane, depth, width, code = cut(n_rows, share)
    g, z, core = places(plane, code)
    part = sides // depth
    along_plane, along_depth, along_cols = movers(plane, depth, code, n_cols)

    def gather(move, count, x, axis):
        return jnp.concatenate([x] + [move(x, k) for k in range(1, count)], axis=axis)

    def my_diag(s):
        block = diag_inverse[s].reshape(plane, width, eqs)
        parts = [lax.dynamic_index_in_dim(block, (g + k) % plane, 0, False) for k in range(plane)]
        held = jnp.concatenate([parts[0]] + [along_plane(parts[k], k) for k in range(1, plane)], axis=1)
        return gather(along_cols, n_cols, held, 0)

    def my_lower(s):
        parts = [
            lax.dynamic_slice_in_dim(lower_pivot[s, :, :s, :], ((g + k) % plane) * width, width, 2)
            for k in range(plane)
        ]
        held = jnp.concatenate([parts[0]] + [along_plane(parts[k], k) for k in range(1, plane)], axis=0)
        return gather(along_cols, n_cols, held, 2)

    def rolled(x, shift, axis):
        return jnp.roll(x, shift, axis)

    rhs_t = jnp.swapaxes(rhs_pivot, 1, 2)
    blocks = rhs_t.reshape(steps, depth, part, eqs)[:, ::-1]
    blocks = rolled(blocks, z + 1, 1).reshape(steps, sides, eqs)

    solved = []
    totals = jnp.zeros((sides, rest), F32)
    outs = []
    for s in range(steps):
        diag = my_diag(s)
        if s == 0:
            own = blocks[0]
        else:
            lower = my_lower(s)
            partial = jnp.zeros((sides, plane * eqs), F32)
            for t in range(s):
                partial = partial + nt_dot(solved[t], lower[:, t, :])
            total = blocks[s].astype(F32) - partial[:, :eqs]
            sent = partial.astype(BF16)
            for k in range(1, plane):
                total = total - along_plane(sent[:, k * eqs : (k + 1) * eqs], -k).astype(F32)
            own = total.astype(BF16)
        residual = gather(along_plane, plane, own, 1)
        product = nt_dot(residual, diag)
        sent = product.astype(BF16)
        total = product[:part]
        for k in range(1, depth):
            total = total + along_depth(sent[k * part : (k + 1) * part], -k).astype(F32)
        mine = total.astype(BF16)
        here = gather(along_depth, depth, mine, 0)
        solved.append(here)
        pieces = [here] + [along_plane(here, k) for k in range(1, plane)]
        pieces = [pieces[(-k) % plane] for k in range(plane)]
        full = jnp.stack([p.reshape(depth, part, n_cols, width) for p in pieces], axis=3)
        full = full[jnp.array([(-k) % depth for k in range(depth)])]
        full = rolled(full, z, 0)
        full = rolled(full, g, 3).reshape(sides, n_cols, share)
        rest_parts = [lower_rest[:, s, :]] + [along_cols(lower_rest[:, s, :], k) for k in range(1, n_cols)]
        for k in range(n_cols):
            totals = totals + nt_dot(full[:, k, :], rest_parts[k])
        theirs = [full[:, 0]] + [along_cols(full[:, k], -k) for k in range(1, n_cols)]
        theirs = rolled(jnp.stack(theirs, 0), core, 0).reshape(n_cols * sides, share)
        outs.append(theirs.T)
    remainder = (rhs_rest.astype(F32) - totals).astype(BF16)
    return jnp.stack(outs), remainder


VMEM_LIMIT = 40 * 1024 * 1024
SMALL = pl.BlockSpec(memory_space=pltpu.SMEM)
WHOLE = pl.BlockSpec(memory_space=pltpu.VMEM)


def call(body, outs, ins, specs, flops=0, scratch=(), **more):
    size = sum(x.size * x.dtype.itemsize for x in ins) + sum(o.size * o.dtype.itemsize for o in outs)
    return pl.pallas_call(
        body,
        out_shape=tuple(outs),
        in_specs=list(specs),
        scratch_shapes=list(scratch),
        compiler_params=pltpu.CompilerParams(vmem_limit_bytes=VMEM_LIMIT),
        cost_estimate=pl.CostEstimate(flops=flops, bytes_accessed=size, transcendentals=0),
        **more,
    )(*ins)


def shaped(dims, kind):
    return jax.ShapeDtypeStruct(dims, kind)


def prep_body(s, plane, width, eqs, meta, *refs):
    if s:
        diag, lower, *outs, flat = refs
        flat[...] = jnp.swapaxes(lower[0], 0, 1)
    else:
        diag, *outs = refs
    for k in range(plane):
        at = lax.rem(meta[0] + k, plane) * width
        for h in range(width // eqs):
            outs[k][0, :, h * eqs : (h + 1) * eqs] = diag[0, pl.ds(pl.multiple_of(at + h * eqs, eqs), eqs), :]
        for t in range(s):
            outs[k][1 + t] = flat[t, :, pl.ds(pl.multiple_of(at, width), width)]


def prep(s, plane, width, eqs, meta, diag_inverse, lower_pivot):
    share = plane * width
    steps = lower_pivot.shape[0]
    ins = [meta, diag_inverse]
    specs = [SMALL, pl.BlockSpec((1, share, eqs), lambda i: (s, 0, 0))]
    scratch = []
    if s:
        ins.append(lower_pivot)
        specs.append(pl.BlockSpec((1, eqs, steps, share), lambda i: (s, 0, 0, 0)))
        scratch.append(pltpu.VMEM((steps, eqs, share), BF16))
    out = shaped((s + 1, eqs, width), BF16)
    return call(
        functools.partial(prep_body, s, plane, width, eqs),
        [out] * plane,
        ins,
        specs,
        scratch=scratch,
        grid=(1,),
        out_specs=tuple(pl.BlockSpec((s + 1, eqs, width), lambda i: (0, 0, 0)) for _ in range(plane)),
    )


def diag_body(n_cols, plane, depth, width, eqs, meta, *refs):
    held = refs[: n_cols * plane]
    parts = refs[n_cols * plane : n_cols * plane + plane]
    outs, product = refs[n_cols * plane + plane : -1], refs[-1]
    sub = width // depth
    residual = jnp.concatenate([p[...] for p in parts], axis=0)
    for c in range(n_cols):
        for h in range(width // eqs):
            rows = jnp.concatenate(
                [held[c * plane + k][0, :, h * eqs : (h + 1) * eqs] for k in range(plane)], axis=1
            )
            product[c, h * eqs : (h + 1) * eqs] = jnp.dot(rows, residual, preferred_element_type=F32)
    for k in range(depth):
        at = pl.multiple_of(lax.rem(meta[1] + depth - k, depth) * sub, sub)
        for c in range(n_cols):
            outs[k][c * sub : (c + 1) * sub] = product[c, pl.ds(at, sub)].astype(outs[k].dtype)


def diag_product(n_cols, plane, depth, width, eqs, meta, held, parts):
    sides = parts[0].shape[1]
    dims = (n_cols * (width // depth), sides)
    first = pl.BlockSpec((1, eqs, width), lambda i: (0, 0, 0))
    full = pl.BlockSpec((eqs, sides), lambda i: (0, 0))
    return call(
        functools.partial(diag_body, n_cols, plane, depth, width, eqs),
        [shaped(dims, F32)] + [shaped(dims, BF16)] * (depth - 1),
        [meta, *held, *parts],
        [SMALL] + [first] * len(held) + [full] * plane,
        flops=2 * n_cols * width * plane * eqs * sides,
        scratch=[pltpu.VMEM((n_cols, width, sides), F32)],
        grid=(1,),
        out_specs=tuple(pl.BlockSpec(dims, lambda i: (0, 0)) for _ in range(depth)),
    )


def put_pieces(n_cols, depth, sub, meta, pieces, outs):
    for k in range(depth):
        at = pl.multiple_of(lax.rem(meta[1] + depth - k, depth) * sub, sub)
        for c in range(n_cols):
            outs[c][pl.ds(at, sub)] = pieces[k][c * sub : (c + 1) * sub]


def lower_body(s, n_cols, plane, depth, width, eqs, meta, *refs):
    refs = list(refs)
    held = [refs.pop(0) for _ in range(n_cols * plane)]
    known = [[refs.pop(0) for _ in range(n_cols)] for _ in range(s - 1)]
    pieces = [refs.pop(0) for _ in range(depth)]
    outs, newest = refs[:plane], refs[plane:]
    put_pieces(n_cols, depth, width // depth, meta, pieces, newest)
    total = None
    for t, blocks in enumerate(known + [newest]):
        for c in range(n_cols):
            rows = jnp.concatenate([held[c * plane + k][1 + t] for k in range(plane)], axis=0)
            term = jnp.dot(rows, blocks[c][...], preferred_element_type=F32)
            total = term if total is None else total + term
    for k in range(plane):
        outs[k][...] = total[k * eqs : (k + 1) * eqs].astype(outs[k].dtype)


def lower_product(s, n_cols, plane, depth, width, eqs, meta, held, known, pieces):
    sides = pieces[0].shape[1]
    flat = [x for blocks in known for x in blocks]
    ins = [meta, *held, *flat, *pieces]
    return call(
        functools.partial(lower_body, s, n_cols, plane, depth, width, eqs),
        [shaped((eqs, sides), F32)] + [shaped((eqs, sides), BF16)] * (plane - 1) + [shaped((width, sides), BF16)] * n_cols,
        ins,
        [SMALL] + [WHOLE] * (len(ins) - 1),
        flops=2 * s * n_cols * width * plane * eqs * sides,
    )


def place_body(n_cols, depth, sub, meta, *refs):
    put_pieces(n_cols, depth, sub, meta, refs[:depth], refs[depth:])


def place(n_cols, depth, width, meta, pieces):
    sides = pieces[0].shape[1]
    return call(
        functools.partial(place_body, n_cols, depth, width // depth),
        [shaped((width, sides), BF16)] * n_cols,
        [meta, *pieces],
        [SMALL] + [WHOLE] * depth,
    )


def join_body(n_cols, sides, meta, *refs):
    for k in range(n_cols):
        at = pl.multiple_of(lax.rem(meta[2] + k, n_cols) * sides, sides)
        refs[-1][:, pl.ds(at, sides)] = refs[k][...]


def join(n_cols, meta, parts):
    width, sides = parts[0].shape
    return call(
        functools.partial(join_body, n_cols, sides),
        [shaped((width, n_cols * sides), BF16)],
        [meta, *parts],
        [SMALL] + [WHOLE] * n_cols,
    )[0]


def flat_body(x, out):
    out[...] = jnp.swapaxes(x[...], 0, 1)


def flat_rest(lower_rest, start, count, block):
    _, steps, share = lower_rest.shape
    return call(
        flat_body,
        [shaped((steps, count, share), BF16)],
        [lower_rest],
        [pl.BlockSpec((block, steps, share), lambda i: (start // block + i, 0, 0))],
        grid=(count // block,),
        out_specs=(pl.BlockSpec((steps, block, share), lambda i: (0, i, 0)),),
    )[0]


def write_body(plane, width, has_buffer, meta, *refs):
    parts = refs[:plane]
    out, turned = refs[-2:]
    for k in range(plane):
        at = pl.multiple_of(lax.rem(meta[0] + plane - k, plane) * width, width)
        block = parts[k][...]
        out[0, pl.ds(at, width), :] = block
        turned[:, pl.ds(at, width)] = block.T


def write(s, steps, plane, meta, parts, buffer):
    width, total = parts[0].shape
    share = plane * width
    ins = [meta, *parts]
    specs = [SMALL] + [pl.BlockSpec((width, total), lambda i: (0, 0))] * plane
    alias = {}
    if buffer is not None:
        alias = {len(ins): 0}
        ins.append(buffer)
        specs.append(pl.BlockSpec(memory_space=pl.ANY))
    return call(
        functools.partial(write_body, plane, width, buffer is not None),
        [shaped((steps, share, total), BF16), shaped((total, share), BF16)],
        ins,
        specs,
        grid=(1,),
        out_specs=(
            pl.BlockSpec((1, share, total), lambda i: (s, 0, 0)),
            pl.BlockSpec((total, share), lambda i: (0, 0)),
        ),
        input_output_aliases=alias,
    )


def rest_body(ts, n_cols, sides, order, meta, *refs):
    turned = refs[: len(ts)]
    lower, out = refs[len(ts) :]
    at = pl.multiple_of(lax.rem(meta[2] + order, n_cols) * sides, sides)
    total = None
    for i, t in enumerate(ts):
        term = nt_dot(turned[i][pl.ds(at, sides), :], lower[i])
        total = term if total is None else total + term
    out[...] = total.astype(out.dtype)


def rest_product(ts, n_cols, sides, order, kind, meta, turned, lower):
    _, count, share = lower.shape
    return call(
        functools.partial(rest_body, ts, n_cols, sides, order),
        [shaped((sides, count), kind)],
        [meta, *turned, lower],
        [SMALL]
        + [pl.BlockSpec(x.shape, lambda i: (0, 0)) for x in turned]
        + [pl.BlockSpec((len(ts), count, share), lambda i: (ts[0] // len(ts), 0, 0))],
        flops=2 * len(ts) * share * sides * count,
        grid=(1,),
        out_specs=(pl.BlockSpec((sides, count), lambda i: (0, 0)),),
    )[0]


def kernel_path(lower_pivot, lower_rest, diag_inverse, rhs_pivot, rhs_rest):
    steps, eqs, _, share = lower_pivot.shape
    sides = rhs_pivot.shape[2]
    rest = lower_rest.shape[0]
    n_rows, n_cols = lax.axis_size("rows"), lax.axis_size("cols")
    plane, depth, width, code = cut(n_rows, share)
    g, z, core = places(plane, code)
    meta = jnp.stack([g, z, core]).astype(jnp.int32)
    along_plane, along_depth, along_cols = movers(plane, depth, code, n_cols)

    def held_of(s):
        packed = prep(s, plane, width, eqs, meta, diag_inverse, lower_pivot)
        mine = [packed[0]] + [along_plane(packed[k], k) for k in range(1, plane)]
        return mine + [along_cols(x, c) for c in range(1, n_cols) for x in mine]

    chunks = 4
    while rest % (chunks * 128):
        chunks -= 1
    count = rest // chunks
    rest_flat = [flat_rest(lower_rest, i * count, count, 128) for i in range(chunks)]

    known, pieces, buffer, turned = [], None, None, []

    def finish(s, blocks, buffer):
        parts = [blocks[0]] + [along_cols(blocks[k], -k) for k in range(1, n_cols)]
        whole = join(n_cols, meta, parts)
        gathered = [whole] + [along_plane(whole, k) for k in range(1, plane)]
        return write(s, steps, plane, meta, gathered, buffer)

    for s in range(steps):
        held = held_of(s)
        if s == 0:
            own = rhs_pivot[0]
        else:
            outs = lower_product(s, n_cols, plane, depth, width, eqs, meta, held, known, pieces)
            sums, blocks = outs[:plane], outs[plane:]
            known.append(blocks)
            total = rhs_pivot[s].astype(F32) - sums[0]
            for k in range(1, plane):
                total = total - along_plane(sums[k], -k).astype(F32)
            own = total.astype(BF16)
            buffer, last = finish(s - 1, blocks, buffer)
            turned.append(last)
        residual = [own] + [along_plane(own, k) for k in range(1, plane)]
        sums = diag_product(n_cols, plane, depth, width, eqs, meta, held, residual)
        total = sums[0]
        for k in range(1, depth):
            total = total + along_depth(sums[k], -k).astype(F32)
        mine = total.astype(BF16)
        pieces = [mine] + [along_depth(mine, k) for k in range(1, depth)]
    early = [
        [
            [rest_product([t], n_cols, sides, c, F32 if c == 0 else BF16, meta, [turned[t]], x) for x in rest_flat]
            for t in range(steps - 1)
        ]
        for c in range(n_cols)
    ]
    base = rhs_rest.astype(F32)
    for c in range(n_cols):
        lane = []
        for i in range(chunks):
            x = early[c][0][i].astype(F32)
            for t in range(1, steps - 1):
                x = x + early[c][t][i].astype(F32)
            lane.append(x)
        lane = jnp.concatenate(lane, axis=1)
        base = base - (lane if c == 0 else along_cols(lane.astype(BF16), c).astype(F32))
    buffer, last = finish(steps - 1, place(n_cols, depth, width, meta, pieces), buffer)
    late = [
        [rest_product([steps - 1], n_cols, sides, c, F32 if c == 0 else BF16, meta, [last], x) for x in rest_flat]
        for c in range(n_cols)
    ]
    total = base - jnp.concatenate(late[0], axis=1)
    for c in range(1, n_cols):
        total = total - along_cols(jnp.concatenate(late[c], axis=1), c).astype(F32)
    return buffer, total.astype(BF16)


def per_device(lower_pivot, lower_rest, diag_inverse, rhs_pivot, rhs_rest):
    eqs, share = lower_pivot.shape[1], lower_pivot.shape[3]
    plane, depth, width, _ = cut(lax.axis_size("rows"), share)
    fits = eqs % 128 == 0 and width % eqs == 0 and (width // depth) % 16 == 0 and rhs_pivot.shape[2] % 128 == 0
    fits = fits and lower_rest.shape[0] % 128 == 0
    path = kernel_path if fits else plain_path
    return path(lower_pivot, lower_rest, diag_inverse, rhs_pivot, rhs_rest)


def solution(mesh):
    placed = (
        P(None, "rows", None, "cols"),
        P("rows", None, "cols"),
        P(None, "cols", "rows"),
        P(None, "rows", "cols"),
        P("cols", "rows"),
    )
    return jax.shard_map(
        per_device,
        mesh=mesh,
        in_specs=placed,
        out_specs=(P(None, "cols", None), P("cols", "rows")),
        check_vma=False,
    )
```

time: 532 us -> 231 us (0.43)
  blocking collectives: 403 us -> 0 us
  starting transfers between devices: 0.21 us -> 102 us
  Pallas kernels: 0 us -> 64.2 us
  matrix products: 29.8 us -> 0 us
  between operations: 13.9 us -> 1.25 us
  local copies, waits for them, and re-layouts: 14.9 us -> 4.38 us
  other arithmetic: 9.55 us -> 2.36 us
    psum x4 -> x0, blocking collectives: 403 us -> none  [per_device(): solved_block = lax.psum(product, 'rows').astype(jnp.bfloat16)]
    ppermute x0 -> x91, starting transfers between devices: none -> 102 us  [the longest x45 61 us: along_plane(): return lax.ppermute(x, 'rows', pairs)]
    pallas_call x0 -> x56, Pallas kernels: none -> 64.2 us  [call(): pl.pallas_call(body, out_shape=tuple(outs), in_specs=list(specs), scratch...]
    psum x4 -> x0, waiting for transfers between devices: 59.5 us -> none  [per_device(): residual = lax.psum(partials.astype(jnp.bfloat16), 'cols')]
    ppermute x0 -> x91, waiting for transfers between devices: none -> 56.7 us  [the longest x45 34.1 us: along_plane(): return lax.ppermute(x, 'rows', pairs)]
    dot_general x8 -> x0, matrix products: 29.8 us -> none  [the longest x1 15.3 us: per_device(): lax.dot_general(flat_solution, flat_lower, (((0,), (1,)), ((), ())), pref...]
    unnamed x9 -> x12, local copies, waits for them, and re-layouts: 9.25 us -> 3.54 us
    slice x3 -> x0, local copies, waits for them, and re-layouts: 5.56 us -> none  [per_device(): lower_pivot[step_index, :, :step_index, :]]
  transfers between devices with their start and end apart: 5 -> 91, of which waited for: 4 -> 28; matrix products, arithmetic and copies ran while one was open for 4% -> 1% of each run, Pallas kernels for 0% -> 27%
where the time goes in v1:
time: 231 us
  starting transfers between devices  102 us (44%)
  Pallas kernels  64.2 us (28%)
  waiting for transfers between devices  56.7 us (25%)
  local copies, waits for them, and re-layouts  4.38 us (2%)
  other arithmetic  2.36 us (1%)
    pallas_call x56, Pallas kernels, call(): pl.pallas_call(body, out_shape=tuple(outs), in_specs=list(specs), scratch...  64.2 us
    ppermute x45, starting transfers between devices, along_plane(): return lax.ppermute(x, 'rows', pairs)  61 us
    ppermute x24, starting transfers between devices, along_depth(): return lax.ppermute(x, 'rows', pairs)  38.4 us
    ppermute x45, waiting for transfers between devices, along_plane(): return lax.ppermute(x, 'rows', pairs)  34.1 us
    ppermute x24, waiting for transfers between devices, along_depth(): return lax.ppermute(x, 'rows', pairs)  22.6 us
  transfers between devices with their start and end apart: 91, of which 28 were waited for; matrix products, arithmetic and copies ran while one was open for 1% of the time, Pallas kernels for 27%

profile of v1, /device:TPU:0, one launch (start us, length us, event | category | flops | bytes accessed | tf_op | source)
XLA Modules:
  0.0 230.7 jit_solution(10773960607683499747)
XLA Ops:
  2.6 3.0 %collective-permute-start.14 = (bf16[1,128,256]{2,1,0:T(8,128)(2,1)S(1)}, bf16[1,128,256]{2,1,0:T(8,128)(2,1)S(1)}, u32[]{:S(2)}, u32[]{:S(2)}) collective-permute-start(bf16[1,128,256]{2,1,0:T(8,128)(2,1)S(1)} %get-tuple-element.71), channel_id=1, source_target_pairs={{0,2},{2,6},{6,4},{4,0},{8,10},{10,14},{14,12},{12,8},{16,18},{18,... | collective-permute-start | bytes 196616 | tf_op jit(solution)/shard_map/ppermute | solution.py:43
  11.9 2.2 copy-done
  15.1 1.6 collective-permute-start.7
  21.0 1.6 collective-permute-start.26
  22.6 2.6 %collective-permute-start.25 = (bf16[128,256]{1,0:T(8,128)(2,1)S(1)}, bf16[128,256]{1,0:T(8,128)(2,1)S(1)}, u32[]{:S(2)}, u32[]{:S(2)}) collective-permute-start(bf16[128,256]{1,0:T(8,128)(2,1)S(1)} %get-tuple-element.76), channel_id=1, source_target_pairs={{0,16},{2,18},{4,20},{6,22},{8,24},{10,26},{12,28},{14,30},{16,0},... | collective-permute-start | bytes 196616 | tf_op jit(solution)/shard_map/ppermute | solution.py:47
  27.8 2.3 collective-permute-done.25
  31.5 2.0 collective-permute-start.28
  34.1 2.9 %collective-permute-done.27.refs_9_ = bf16[128,256]{1,0:T(8,128)(2,1)S(1)} collective-permute-done((bf16[128,256]{1,0:T(8,128)(2,1)S(1)}, bf16[128,256]{1,0:T(8,128)(2,1)S(1)}, u32[]{:S(2)}, u32[]{:S(2)}) %collective-permute-start.27) | collective-permute-done | bytes 65568 | tf_op jit(solution)/shard_map/ppermute | solution.py:47
  37.0 2.5 %collective-permute-done.28.refs_10_ = bf16[128,256]{1,0:T(8,128)(2,1)S(1)} collective-permute-done((bf16[128,256]{1,0:T(8,128)(2,1)S(1)}, bf16[128,256]{1,0:T(8,128)(2,1)S(1)}, u32[]{:S(2)}, u32[]{:S(2)}) %collective-permute-start.28) | collective-permute-done | bytes 65568 | tf_op jit(solution)/shard_map/ppermute | solution.py:47
  43.7 1.8 collective-permute-start.30
  54.7 2.4 %collective-permute-done.41.refs_10_ = bf16[128,256]{1,0:T(8,128)(2,1)S(1)} collective-permute-done((bf16[128,256]{1,0:T(8,128)(2,1)S(1)}, bf16[128,256]{1,0:T(8,128)(2,1)S(1)}, u32[]{:S(2)}, u32[]{:S(2)}) %collective-permute-start.41) | collective-permute-done | bytes 65568 | tf_op jit(solution)/shard_map/ppermute | solution.py:43
  57.1 2.3 %collective-permute-done.42.refs_11_ = bf16[128,256]{1,0:T(8,128)(2,1)S(1)} collective-permute-done((bf16[128,256]{1,0:T(8,128)(2,1)S(1)}, bf16[128,256]{1,0:T(8,128)(2,1)S(1)}, u32[]{:S(2)}, u32[]{:S(2)}) %collective-permute-start.42) | collective-permute-done | bytes 65568 | tf_op jit(solution)/shard_map/ppermute | solution.py:43
  60.3 2.2 collective-permute-start.45
  62.5 2.0 collective-permute-start.44
  69.2 2.7 %collective-permute-start.47 = (bf16[128,256]{1,0:T(8,128)(2,1)S(1)}, bf16[128,256]{1,0:T(8,128)(2,1)S(1)}, u32[]{:S(2)}, u32[]{:S(2)}) collective-permute-start(bf16[128,256]{1,0:T(8,128)(2,1)S(1)} %add_convert_fusion.6.refs_10_), channel_id=1, source_target_pairs={{0,16},{2,18},{4,20},{6,22},{8,24},{10,26},{12,28},{14,30},{16,0},... | collective-permute-start | bytes 196616 | tf_op jit(solution)/shard_map/ppermute | solution.py:47
  72.8 2.9 %collective-permute-done.46.refs_11_ = bf16[128,256]{1,0:T(8,128)(2,1)S(1)} collective-permute-done((bf16[128,256]{1,0:T(8,128)(2,1)S(1)}, bf16[128,256]{1,0:T(8,128)(2,1)S(1)}, u32[]{:S(2)}, u32[]{:S(2)}) %collective-permute-start.46) | collective-permute-done | bytes 65568 | tf_op jit(solution)/shard_map/ppermute | solution.py:47
  78.0 2.3 collective-permute-start.51
  82.8 1.6 collective-permute-start
  84.4 1.9 collective-permute-start.1
  86.9 3.2 %collective-permute-start.52 = (bf16[128,256]{1,0:T(8,128)(2,1)S(1)}, bf16[128,256]{1,0:T(8,128)(2,1)S(1)}, u32[]{:S(2)}, u32[]{:S(2)}) collective-permute-start(bf16[128,256]{1,0:T(8,128)(2,1)S(1)} %fusion.7.refs_8_), channel_id=1, source_target_pairs={{0,2},{2,6},{6,4},{4,0},{8,10},{10,14},{14,12},{12,8},{16,18},{18,... | collective-permute-start | bytes 196616 | tf_op jit(solution)/shard_map/ppermute | solution.py:43
  91.0 5.1 %collective-permute-done.52.refs_9_ = bf16[128,256]{1,0:T(8,128)(2,1)S(1)} collective-permute-done((bf16[128,256]{1,0:T(8,128)(2,1)S(1)}, bf16[128,256]{1,0:T(8,128)(2,1)S(1)}, u32[]{:S(2)}, u32[]{:S(2)}) %collective-permute-start.52) | collective-permute-done | bytes 65568 | tf_op jit(solution)/shard_map/ppermute | solution.py:43
  96.1 2.4 %collective-permute-start.54 = (bf16[128,256]{1,0:T(8,128)(2,1)S(1)}, bf16[128,256]{1,0:T(8,128)(2,1)S(1)}, u32[]{:S(2)}, u32[]{:S(2)}) collective-permute-start(bf16[128,256]{1,0:T(8,128)(2,1)S(1)} %fusion.7.refs_8_), channel_id=1, source_target_pairs={{0,4},{2,0},{6,2},{4,6},{8,12},{10,8},{14,10},{12,14},{16,20},{18,... | collective-permute-start | bytes 196616 | tf_op jit(solution)/shard_map/ppermute | solution.py:43
  98.6 2.2 collective-permute-done.54.refs_11_
  101.7 3.3 %collective-permute-start.57 = (bf16[128,256]{1,0:T(8,128)(2,1)S(1)}, bf16[128,256]{1,0:T(8,128)(2,1)S(1)}, u32[]{:S(2)}, u32[]{:S(2)}) collective-permute-start(bf16[128,256]{1,0:T(8,128)(2,1)S(1)} %get-tuple-element.101), channel_id=1, source_target_pairs={{0,8},{2,10},{4,12},{6,14},{8,16},{10,18},{12,20},{14,22},{16,24},... | collective-permute-start | bytes 196616 | tf_op jit(solution)/shard_map/ppermute | solution.py:47
  105.0 2.4 %collective-permute-start.55 = (bf16[128,256]{1,0:T(8,128)(2,1)S(1)}, bf16[128,256]{1,0:T(8,128)(2,1)S(1)}, u32[]{:S(2)}, u32[]{:S(2)}) collective-permute-start(bf16[128,256]{1,0:T(8,128)(2,1)S(1)} %get-tuple-element.99), channel_id=1, source_target_pairs={{0,24},{2,26},{4,28},{6,30},{8,0},{10,2},{12,4},{14,6},{16,8},{18,... | collective-permute-start | bytes 196616 | tf_op jit(solution)/shard_map/ppermute | solution.py:47
  108.0 2.3 %collective-permute-done.56 = bf16[128,256]{1,0:T(8,128)(2,1)S(1)} collective-permute-done((bf16[128,256]{1,0:T(8,128)(2,1)S(1)}, bf16[128,256]{1,0:T(8,128)(2,1)S(1)}, u32[]{:S(2)}, u32[]{:S(2)}) %collective-permute-start.56) | collective-permute-done | bytes 65568 | tf_op jit(solution)/shard_map/ppermute | solution.py:47
  111.7 2.4 %collective-permute-start.59 = (bf16[128,256]{1,0:T(8,128)(2,1)S(1)}, bf16[128,256]{1,0:T(8,128)(2,1)S(1)}, u32[]{:S(2)}, u32[]{:S(2)}) collective-permute-start(bf16[128,256]{1,0:T(8,128)(2,1)S(1)} %add_convert_fusion.5.refs_12_), channel_id=1, source_target_pairs={{0,16},{2,18},{4,20},{6,22},{8,24},{10,26},{12,28},{14,30},{16,0},... | collective-permute-start | bytes 196616 | tf_op jit(solution)/shard_map/ppermute | solution.py:47
  115.2 2.0 collective-permute-done.58.refs_13_
  117.3 2.3 collective-permute-done.59.refs_14_
  125.9 1.6 collective-permute-start.87
  131.4 6.3 %collective-permute-done.64.refs_9_ = bf16[128,256]{1,0:T(8,128)(2,1)S(1)} collective-permute-done((bf16[128,256]{1,0:T(8,128)(2,1)S(1)}, bf16[128,256]{1,0:T(8,128)(2,1)S(1)}, u32[]{:S(2)}, u32[]{:S(2)}) %collective-permute-start.64) | collective-permute-done | bytes 65568 | tf_op jit(solution)/shard_map/ppermute | solution.py:43
  137.7 2.8 %collective-permute-start.66 = (bf16[128,256]{1,0:T(8,128)(2,1)S(1)}, bf16[128,256]{1,0:T(8,128)(2,1)S(1)}, u32[]{:S(2)}, u32[]{:S(2)}) collective-permute-start(bf16[128,256]{1,0:T(8,128)(2,1)S(1)} %fusion.15.refs_8_), channel_id=1, source_target_pairs={{0,4},{2,0},{6,2},{4,6},{8,12},{10,8},{14,10},{12,14},{16,20},{18,... | collective-permute-start | bytes 196616 | tf_op jit(solution)/shard_map/ppermute | solution.py:43
  140.6 1.8 collective-permute-done.66.refs_11_
  143.3 3.3 %collective-permute-start.69 = (bf16[128,256]{1,0:T(8,128)(2,1)S(1)}, bf16[128,256]{1,0:T(8,128)(2,1)S(1)}, u32[]{:S(2)}, u32[]{:S(2)}) collective-permute-start(bf16[128,256]{1,0:T(8,128)(2,1)S(1)} %get-tuple-element.109), channel_id=1, source_target_pairs={{0,8},{2,10},{4,12},{6,14},{8,16},{10,18},{12,20},{14,22},{16,24},... | collective-permute-start | bytes 196616 | tf_op jit(solution)/shard_map/ppermute | solution.py:47
  146.6 1.6 collective-permute-start.68
  154.1 4.0 %collective-permute-done.88.refs_3_ = bf16[256,512]{1,0:T(8,128)(2,1)S(1)} collective-permute-done((bf16[256,512]{1,0:T(8,128)(2,1)S(1)}, bf16[256,512]{1,0:T(8,128)(2,1)S(1)}, u32[]{:S(2)}, u32[]{:S(2)}) %collective-permute-start.88) | collective-permute-done | bytes 262176 | tf_op jit(solution)/shard_map/ppermute | solution.py:43
  160.3 1.8 collective-permute-start.72
  162.1 3.1 %shard_map.100.refs_1_ = bf16[4,384,1024]{2,1,0:T(8,128)(2,1)S(1)} custom-call(bf16[1536,4,1024]{2,1,0:T(4,128)(2,1)} %x.7), custom_call_target="tpu_custom_call" | custom-call | bytes 15728640 | tf_op jit(solution)/shard_map/pallas_call | solution.py:141
  165.3 3.1 %shard_map.96.refs_1_ = bf16[4,384,1024]{2,1,0:T(8,128)(2,1)S(1)} custom-call(bf16[1536,4,1024]{2,1,0:T(4,128)(2,1)} %x.7), custom_call_target="tpu_custom_call" | custom-call | bytes 15728640 | tf_op jit(solution)/shard_map/pallas_call | solution.py:141
  168.4 3.1 %shard_map.92.refs_1_ = bf16[4,384,1024]{2,1,0:T(8,128)(2,1)S(1)} custom-call(bf16[1536,4,1024]{2,1,0:T(4,128)(2,1)} %x.7), custom_call_target="tpu_custom_call" | custom-call | bytes 15728640 | tf_op jit(solution)/shard_map/pallas_call | solution.py:141
  171.6 3.1 %shard_map.88.refs_1_ = bf16[4,384,1024]{2,1,0:T(8,128)(2,1)S(1)} custom-call(bf16[1536,4,1024]{2,1,0:T(4,128)(2,1)} %x.7), custom_call_target="tpu_custom_call" | custom-call | bytes 15728640 | tf_op jit(solution)/shard_map/pallas_call | solution.py:141
  174.7 1.7 shard_map.84
  178.4 1.6 collective-permute-start.79
  189.1 1.7 shard_map.85
  197.4 1.7 collective-permute-start.74
  201.2 1.7 shard_map.86
  207.4 5.3 %collective-permute-done.75.refs_2_ = bf16[256,512]{1,0:T(8,128)(2,1)S(1)} collective-permute-done((bf16[256,512]{1,0:T(8,128)(2,1)S(1)}, bf16[256,512]{1,0:T(8,128)(2,1)S(1)}, u32[]{:S(2)}, u32[]{:S(2)}) %collective-permute-start.75) | collective-permute-done | bytes 262176 | tf_op jit(solution)/shard_map/ppermute | solution.py:43
  213.1 1.7 shard_map.87
  (218 shorter events, 107.7 us)
Async XLA Ops:
  2.6 7.4 %collective-permute-start.14 = (bf16[1,128,256]{2,1,0:T(8,128)(2,1)S(1)}, bf16[1,128,256]{2,1,0:T(8,128)(2,1)S(1)}, u32[]{:S(2)}, u32[]{:S(2)}) collective-permute-start(bf16[1,128,256]{2,1,0:T(8,128)(2,1)S(1)} %get-tuple-element.71), channel_id=1, source_target_pairs={{0,2},{2,6},{6,4},{4,0},{8,10},{10,14},{14,12},{12,8},{16,18},{18,... | collective-permute-start | bytes 196616 | tf_op jit(solution)/shard_map/ppermute | solution.py:43
  9.4 7.3 %collective-permute-start.21 = (bf16[128,256]{1,0:T(8,128)(2,1)S(1)}, bf16[128,256]{1,0:T(8,128)(2,1)S(1)}, u32[]{:S(2)}, u32[]{:S(2)}) collective-permute-start(bf16[128,256]{1,0:T(8,128)(2,1)S(1)} %slice_bitcast_fusion.refs_8_), channel_id=1, source_target_pairs={{0,2},{2,6},{6,4},{4,0},{8,10},{10,14},{14,12},{12,8},{16,18},{18,... | collective-permute-start | bytes 196616 | tf_op jit(solution)/shard_map/ppermute | solution.py:43
  9.9 7.0 %collective-permute-start.22 = (bf16[128,256]{1,0:T(8,128)(2,1)S(1)}, bf16[128,256]{1,0:T(8,128)(2,1)S(1)}, u32[]{:S(2)}, u32[]{:S(2)}) collective-permute-start(bf16[128,256]{1,0:T(8,128)(2,1)S(1)} %slice_bitcast_fusion.refs_8_), channel_id=1, source_target_pairs={{0,6},{2,4},{6,0},{4,2},{8,14},{10,12},{14,8},{12,10},{16,22},{18,... | collective-permute-start | bytes 196616 | tf_op jit(solution)/shard_map/ppermute | solution.py:43
  15.1 10.2 %collective-permute-start.7 = (bf16[2,128,256]{2,1,0:T(8,128)(2,1)S(1)}, bf16[2,128,256]{2,1,0:T(8,128)(2,1)S(1)}, u32[]{:S(2)}, u32[]{:S(2)}) collective-permute-start(bf16[2,128,256]{2,1,0:T(8,128)(2,1)S(1)} %get-tuple-element.67), channel_id=1, source_target_pairs={{0,2},{2,6},{6,4},{4,0},{8,10},{10,14},{14,12},{12,8},{16,18},{18,... | collective-permute-start | bytes 393224 | tf_op jit(solution)/shard_map/ppermute | solution.py:43
  17.2 9.4 %collective-permute-start.8 = (bf16[2,128,256]{2,1,0:T(8,128)(2,1)S(1)}, bf16[2,128,256]{2,1,0:T(8,128)(2,1)S(1)}, u32[]{:S(2)}, u32[]{:S(2)}) collective-permute-start(bf16[2,128,256]{2,1,0:T(8,128)(2,1)S(1)} %get-tuple-element.68), channel_id=1, source_target_pairs={{0,6},{2,4},{6,0},{4,2},{8,14},{10,12},{14,8},{12,10},{16,22},{18,... | collective-permute-start | bytes 393224 | tf_op jit(solution)/shard_map/ppermute | solution.py:43
  18.6 8.0 %collective-permute-start.9 = (bf16[2,128,256]{2,1,0:T(8,128)(2,1)S(1)}, bf16[2,128,256]{2,1,0:T(8,128)(2,1)S(1)}, u32[]{:S(2)}, u32[]{:S(2)}) collective-permute-start(bf16[2,128,256]{2,1,0:T(8,128)(2,1)S(1)} %get-tuple-element.69), channel_id=1, source_target_pairs={{0,4},{2,0},{6,2},{4,6},{8,12},{10,8},{14,10},{12,14},{16,20},{18,... | collective-permute-start | bytes 393224 | tf_op jit(solution)/shard_map/ppermute | solution.py:43
  22.6 7.5 %collective-permute-start.25 = (bf16[128,256]{1,0:T(8,128)(2,1)S(1)}, bf16[128,256]{1,0:T(8,128)(2,1)S(1)}, u32[]{:S(2)}, u32[]{:S(2)}) collective-permute-start(bf16[128,256]{1,0:T(8,128)(2,1)S(1)} %get-tuple-element.76), channel_id=1, source_target_pairs={{0,16},{2,18},{4,20},{6,22},{8,24},{10,26},{12,28},{14,30},{16,0},... | collective-permute-start | bytes 196616 | tf_op jit(solution)/shard_map/ppermute | solution.py:47
  26.6 6.9 %collective-permute-start.11 = (bf16[2,128,256]{2,1,0:T(8,128)(2,1)S(1)}, bf16[2,128,256]{2,1,0:T(8,128)(2,1)S(1)}, u32[]{:S(2)}, u32[]{:S(2)}) collective-permute-start(bf16[2,128,256]{2,1,0:T(8,128)(2,1)S(1)} %collective-permute-done.7.refs_1_), channel_id=1, source_target_pairs={{0,1},{1,0},{2,3},{3,2},{4,5},{5,4},{6,7},{7,6},{8,9},{9,8},{10,11... | collective-permute-start | bytes 393224 | tf_op jit(solution)/shard_map/ppermute | solution.py:50
  30.1 6.8 %collective-permute-start.27 = (bf16[128,256]{1,0:T(8,128)(2,1)S(1)}, bf16[128,256]{1,0:T(8,128)(2,1)S(1)}, u32[]{:S(2)}, u32[]{:S(2)}) collective-permute-start(bf16[128,256]{1,0:T(8,128)(2,1)S(1)} %add_convert_fusion.7.refs_8_), channel_id=1, source_target_pairs={{0,8},{2,10},{4,12},{6,14},{8,16},{10,18},{12,20},{14,22},{16,24},... | collective-permute-start | bytes 196616 | tf_op jit(solution)/shard_map/ppermute | solution.py:47
  31.5 8.0 %collective-permute-start.28 = (bf16[128,256]{1,0:T(8,128)(2,1)S(1)}, bf16[128,256]{1,0:T(8,128)(2,1)S(1)}, u32[]{:S(2)}, u32[]{:S(2)}) collective-permute-start(bf16[128,256]{1,0:T(8,128)(2,1)S(1)} %add_convert_fusion.7.refs_8_), channel_id=1, source_target_pairs={{0,16},{2,18},{4,20},{6,22},{8,24},{10,26},{12,28},{14,30},{16,0},... | collective-permute-start | bytes 196616 | tf_op jit(solution)/shard_map/ppermute | solution.py:47
  43.7 20.9 %collective-permute-start.30 = (bf16[3,128,256]{2,1,0:T(8,128)(2,1)S(1)}, bf16[3,128,256]{2,1,0:T(8,128)(2,1)S(1)}, u32[]{:S(2)}, u32[]{:S(2)}) collective-permute-start(bf16[3,128,256]{2,1,0:T(8,128)(2,1)S(1)} %get-tuple-element.81), channel_id=1, source_target_pairs={{0,2},{2,6},{6,4},{4,0},{8,10},{10,14},{14,12},{12,8},{16,18},{18,... | collective-permute-start | bytes 589832 | tf_op jit(solution)/shard_map/ppermute | solution.py:43
  48.2 16.7 %collective-permute-start.31 = (bf16[3,128,256]{2,1,0:T(8,128)(2,1)S(1)}, bf16[3,128,256]{2,1,0:T(8,128)(2,1)S(1)}, u32[]{:S(2)}, u32[]{:S(2)}) collective-permute-start(bf16[3,128,256]{2,1,0:T(8,128)(2,1)S(1)} %get-tuple-element.82), channel_id=1, source_target_pairs={{0,6},{2,4},{6,0},{4,2},{8,14},{10,12},{14,8},{12,10},{16,22},{18,... | collective-permute-start | bytes 589832 | tf_op jit(solution)/shard_map/ppermute | solution.py:43
  49.2 15.7 %collective-permute-start.32 = (bf16[3,128,256]{2,1,0:T(8,128)(2,1)S(1)}, bf16[3,128,256]{2,1,0:T(8,128)(2,1)S(1)}, u32[]{:S(2)}, u32[]{:S(2)}) collective-permute-start(bf16[3,128,256]{2,1,0:T(8,128)(2,1)S(1)} %get-tuple-element.83), channel_id=1, source_target_pairs={{0,4},{2,0},{6,2},{4,6},{8,12},{10,8},{14,10},{12,14},{16,20},{18,... | collective-permute-start | bytes 589832 | tf_op jit(solution)/shard_map/ppermute | solution.py:43
  65.0 7.0 %collective-permute-start.34 = (bf16[3,128,256]{2,1,0:T(8,128)(2,1)S(1)}, bf16[3,128,256]{2,1,0:T(8,128)(2,1)S(1)}, u32[]{:S(2)}, u32[]{:S(2)}) collective-permute-start(bf16[3,128,256]{2,1,0:T(8,128)(2,1)S(1)} %collective-permute-done.30.refs_1_), channel_id=1, source_target_pairs={{0,1},{1,0},{2,3},{3,2},{4,5},{5,4},{6,7},{7,6},{8,9},{9,8},{10,11... | collective-permute-start | bytes 589832 | tf_op jit(solution)/shard_map/ppermute | solution.py:50
  68.8 6.9 %collective-permute-start.46 = (bf16[128,256]{1,0:T(8,128)(2,1)S(1)}, bf16[128,256]{1,0:T(8,128)(2,1)S(1)}, u32[]{:S(2)}, u32[]{:S(2)}) collective-permute-start(bf16[128,256]{1,0:T(8,128)(2,1)S(1)} %add_convert_fusion.6.refs_10_), channel_id=1, source_target_pairs={{0,8},{2,10},{4,12},{6,14},{8,16},{10,18},{12,20},{14,22},{16,24},... | collective-permute-start | bytes 196616 | tf_op jit(solution)/shard_map/ppermute | solution.py:47
  69.2 7.8 %collective-permute-start.47 = (bf16[128,256]{1,0:T(8,128)(2,1)S(1)}, bf16[128,256]{1,0:T(8,128)(2,1)S(1)}, u32[]{:S(2)}, u32[]{:S(2)}) collective-permute-start(bf16[128,256]{1,0:T(8,128)(2,1)S(1)} %add_convert_fusion.6.refs_10_), channel_id=1, source_target_pairs={{0,16},{2,18},{4,20},{6,22},{8,24},{10,26},{12,28},{14,30},{16,0},... | collective-permute-start | bytes 196616 | tf_op jit(solution)/shard_map/ppermute | solution.py:47
  78.0 8.3 %collective-permute-start.51 = (bf16[128,256]{1,0:T(8,128)(2,1)S(1)}, bf16[128,256]{1,0:T(8,128)(2,1)S(1)}, u32[]{:S(2)}, u32[]{:S(2)}) collective-permute-start(bf16[128,256]{1,0:T(8,128)(2,1)S(1)} %get-tuple-element.97), channel_id=1, source_target_pairs={{0,2},{2,6},{6,4},{4,0},{8,10},{10,14},{14,12},{12,8},{16,18},{18,... | collective-permute-start | bytes 196616 | tf_op jit(solution)/shard_map/ppermute | solution.py:43
  82.8 22.2 %collective-permute-start = (bf16[4,128,256]{2,1,0:T(8,128)(2,1)S(1)}, bf16[4,128,256]{2,1,0:T(8,128)(2,1)S(1)}, u32[]{:S(2)}, u32[]{:S(2)}) collective-permute-start(bf16[4,128,256]{2,1,0:T(8,128)(2,1)S(1)} %get-tuple-element.63), channel_id=1, source_target_pairs={{0,2},{2,6},{6,4},{4,0},{8,10},{10,14},{14,12},{12,8},{16,18},{18,... | collective-permute-start | bytes 786440 | tf_op jit(solution)/shard_map/ppermute | solution.py:43
  84.4 23.0 %collective-permute-start.1 = (bf16[4,128,256]{2,1,0:T(8,128)(2,1)S(1)}, bf16[4,128,256]{2,1,0:T(8,128)(2,1)S(1)}, u32[]{:S(2)}, u32[]{:S(2)}) collective-permute-start(bf16[4,128,256]{2,1,0:T(8,128)(2,1)S(1)} %get-tuple-element.64), channel_id=1, source_target_pairs={{0,6},{2,4},{6,0},{4,2},{8,14},{10,12},{14,8},{12,10},{16,22},{18,... | collective-permute-start | bytes 786440 | tf_op jit(solution)/shard_map/ppermute | solution.py:43
  86.3 21.1 %collective-permute-start.2 = (bf16[4,128,256]{2,1,0:T(8,128)(2,1)S(1)}, bf16[4,128,256]{2,1,0:T(8,128)(2,1)S(1)}, u32[]{:S(2)}, u32[]{:S(2)}) collective-permute-start(bf16[4,128,256]{2,1,0:T(8,128)(2,1)S(1)} %get-tuple-element.65), channel_id=1, source_target_pairs={{0,4},{2,0},{6,2},{4,6},{8,12},{10,8},{14,10},{12,14},{16,20},{18,... | collective-permute-start | bytes 786440 | tf_op jit(solution)/shard_map/ppermute | solution.py:43
  86.9 9.2 %collective-permute-start.52 = (bf16[128,256]{1,0:T(8,128)(2,1)S(1)}, bf16[128,256]{1,0:T(8,128)(2,1)S(1)}, u32[]{:S(2)}, u32[]{:S(2)}) collective-permute-start(bf16[128,256]{1,0:T(8,128)(2,1)S(1)} %fusion.7.refs_8_), channel_id=1, source_target_pairs={{0,2},{2,6},{6,4},{4,0},{8,10},{10,14},{14,12},{12,8},{16,18},{18,... | collective-permute-start | bytes 196616 | tf_op jit(solution)/shard_map/ppermute | solution.py:43
  90.1 8.5 %collective-permute-start.53 = (bf16[128,256]{1,0:T(8,128)(2,1)S(1)}, bf16[128,256]{1,0:T(8,128)(2,1)S(1)}, u32[]{:S(2)}, u32[]{:S(2)}) collective-permute-start(bf16[128,256]{1,0:T(8,128)(2,1)S(1)} %fusion.7.refs_8_), channel_id=1, source_target_pairs={{0,6},{2,4},{6,0},{4,2},{8,14},{10,12},{14,8},{12,10},{16,22},{18,... | collective-permute-start | bytes 196616 | tf_op jit(solution)/shard_map/ppermute | solution.py:43
  108.0 7.3 %collective-permute-start.5 = (bf16[4,128,256]{2,1,0:T(8,128)(2,1)S(1)}, bf16[4,128,256]{2,1,0:T(8,128)(2,1)S(1)}, u32[]{:S(2)}, u32[]{:S(2)}) collective-permute-start(bf16[4,128,256]{2,1,0:T(8,128)(2,1)S(1)} %collective-permute-done.1.refs_2_), channel_id=1, source_target_pairs={{0,1},{1,0},{2,3},{3,2},{4,5},{5,4},{6,7},{7,6},{8,9},{9,8},{10,11... | collective-permute-start | bytes 786440 | tf_op jit(solution)/shard_map/ppermute | solution.py:50
  110.4 6.8 %collective-permute-start.58 = (bf16[128,256]{1,0:T(8,128)(2,1)S(1)}, bf16[128,256]{1,0:T(8,128)(2,1)S(1)}, u32[]{:S(2)}, u32[]{:S(2)}) collective-permute-start(bf16[128,256]{1,0:T(8,128)(2,1)S(1)} %add_convert_fusion.5.refs_12_), channel_id=1, source_target_pairs={{0,8},{2,10},{4,12},{6,14},{8,16},{10,18},{12,20},{14,22},{16,24},... | collective-permute-start | bytes 196616 | tf_op jit(solution)/shard_map/ppermute | solution.py:47
  111.7 7.8 %collective-permute-start.59 = (bf16[128,256]{1,0:T(8,128)(2,1)S(1)}, bf16[128,256]{1,0:T(8,128)(2,1)S(1)}, u32[]{:S(2)}, u32[]{:S(2)}) collective-permute-start(bf16[128,256]{1,0:T(8,128)(2,1)S(1)} %add_convert_fusion.5.refs_12_), channel_id=1, source_target_pairs={{0,16},{2,18},{4,20},{6,22},{8,24},{10,26},{12,28},{14,30},{16,0},... | collective-permute-start | bytes 196616 | tf_op jit(solution)/shard_map/ppermute | solution.py:47
  115.2 8.9 %collective-permute-start.85 = (bf16[256,256]{1,0:T(8,128)(2,1)S(1)}, bf16[256,256]{1,0:T(8,128)(2,1)S(1)}, u32[]{:S(2)}, u32[]{:S(2)}) collective-permute-start(bf16[256,256]{1,0:T(8,128)(2,1)S(1)} %get-tuple-element.79.refs_9_), channel_id=1, source_target_pairs={{0,1},{1,0},{2,3},{3,2},{4,5},{5,4},{6,7},{7,6},{8,9},{9,8},{10,11... | collective-permute-start | bytes 393224 | tf_op jit(solution)/shard_map/ppermute | solution.py:50
  124.7 24.4 %collective-permute-start.86 = (bf16[256,512]{1,0:T(8,128)(2,1)S(1)}, bf16[256,512]{1,0:T(8,128)(2,1)S(1)}, u32[]{:S(2)}, u32[]{:S(2)}) collective-permute-start(bf16[256,512]{1,0:T(8,128)(2,1)S(1)} %shard_map.83.refs_0_), channel_id=1, source_target_pairs={{0,2},{2,6},{6,4},{4,0},{8,10},{10,14},{14,12},{12,8},{16,18},{18,... | collective-permute-start | bytes 786440 | tf_op jit(solution)/shard_map/ppermute | solution.py:43
  125.9 24.8 %collective-permute-start.87 = (bf16[256,512]{1,0:T(8,128)(2,1)S(1)}, bf16[256,512]{1,0:T(8,128)(2,1)S(1)}, u32[]{:S(2)}, u32[]{:S(2)}) collective-permute-start(bf16[256,512]{1,0:T(8,128)(2,1)S(1)} %shard_map.83.refs_0_), channel_id=1, source_target_pairs={{0,6},{2,4},{6,0},{4,2},{8,14},{10,12},{14,8},{12,10},{16,22},{18,... | collective-permute-start | bytes 786440 | tf_op jit(solution)/shard_map/ppermute | solution.py:43
  128.4 9.3 %collective-permute-start.64 = (bf16[128,256]{1,0:T(8,128)(2,1)S(1)}, bf16[128,256]{1,0:T(8,128)(2,1)S(1)}, u32[]{:S(2)}, u32[]{:S(2)}) collective-permute-start(bf16[128,256]{1,0:T(8,128)(2,1)S(1)} %fusion.15.refs_8_), channel_id=1, source_target_pairs={{0,2},{2,6},{6,4},{4,0},{8,10},{10,14},{14,12},{12,8},{16,18},{18,... | collective-permute-start | bytes 196616 | tf_op jit(solution)/shard_map/ppermute | solution.py:43
  129.9 18.4 %collective-permute-start.81 = (bf16[256,256]{1,0:T(8,128)(2,1)S(1)}, bf16[256,256]{1,0:T(8,128)(2,1)S(1)}, u32[]{:S(2)}, u32[]{:S(2)}) collective-permute-start(bf16[256,256]{1,0:T(8,128)(2,1)S(1)} %get-tuple-element.93.refs_11_), channel_id=1, source_target_pairs={{0,1},{1,0},{2,3},{3,2},{4,5},{5,4},{6,7},{7,6},{8,9},{9,8},{10,11... | collective-permute-start | bytes 393224 | tf_op jit(solution)/shard_map/ppermute | solution.py:50
  129.9 10.7 %collective-permute-start.65 = (bf16[128,256]{1,0:T(8,128)(2,1)S(1)}, bf16[128,256]{1,0:T(8,128)(2,1)S(1)}, u32[]{:S(2)}, u32[]{:S(2)}) collective-permute-start(bf16[128,256]{1,0:T(8,128)(2,1)S(1)} %fusion.15.refs_8_), channel_id=1, source_target_pairs={{0,6},{2,4},{6,0},{4,2},{8,14},{10,12},{14,8},{12,10},{16,22},{18,... | collective-permute-start | bytes 196616 | tf_op jit(solution)/shard_map/ppermute | solution.py:43
  143.3 8.4 %collective-permute-start.69 = (bf16[128,256]{1,0:T(8,128)(2,1)S(1)}, bf16[128,256]{1,0:T(8,128)(2,1)S(1)}, u32[]{:S(2)}, u32[]{:S(2)}) collective-permute-start(bf16[128,256]{1,0:T(8,128)(2,1)S(1)} %get-tuple-element.109), channel_id=1, source_target_pairs={{0,8},{2,10},{4,12},{6,14},{8,16},{10,18},{12,20},{14,22},{16,24},... | collective-permute-start | bytes 196616 | tf_op jit(solution)/shard_map/ppermute | solution.py:47
  149.1 9.0 %collective-permute-start.88 = (bf16[256,512]{1,0:T(8,128)(2,1)S(1)}, bf16[256,512]{1,0:T(8,128)(2,1)S(1)}, u32[]{:S(2)}, u32[]{:S(2)}) collective-permute-start(bf16[256,512]{1,0:T(8,128)(2,1)S(1)} %shard_map.83.refs_0_), channel_id=1, source_target_pairs={{0,4},{2,0},{6,2},{4,6},{8,12},{10,8},{14,10},{12,14},{16,20},{18,... | collective-permute-start | bytes 786440 | tf_op jit(solution)/shard_map/ppermute | solution.py:43
  150.7 9.6 %collective-permute-start.82 = (bf16[256,512]{1,0:T(8,128)(2,1)S(1)}, bf16[256,512]{1,0:T(8,128)(2,1)S(1)}, u32[]{:S(2)}, u32[]{:S(2)}) collective-permute-start(bf16[256,512]{1,0:T(8,128)(2,1)S(1)} %shard_map.82.refs_0_), channel_id=1, source_target_pairs={{0,2},{2,6},{6,4},{4,0},{8,10},{10,14},{14,12},{12,8},{16,18},{18,... | collective-permute-start | bytes 786440 | tf_op jit(solution)/shard_map/ppermute | solution.py:43
  151.7 36.3 %collective-permute-start.83 = (bf16[256,512]{1,0:T(8,128)(2,1)S(1)}, bf16[256,512]{1,0:T(8,128)(2,1)S(1)}, u32[]{:S(2)}, u32[]{:S(2)}) collective-permute-start(bf16[256,512]{1,0:T(8,128)(2,1)S(1)} %shard_map.82.refs_0_), channel_id=1, source_target_pairs={{0,6},{2,4},{6,0},{4,2},{8,14},{10,12},{14,8},{12,10},{16,22},{18,... | collective-permute-start | bytes 786440 | tf_op jit(solution)/shard_map/ppermute | solution.py:43
  153.2 35.9 %collective-permute-start.84 = (bf16[256,512]{1,0:T(8,128)(2,1)S(1)}, bf16[256,512]{1,0:T(8,128)(2,1)S(1)}, u32[]{:S(2)}, u32[]{:S(2)}) collective-permute-start(bf16[256,512]{1,0:T(8,128)(2,1)S(1)} %shard_map.82.refs_0_), channel_id=1, source_target_pairs={{0,4},{2,0},{6,2},{4,6},{8,12},{10,8},{14,10},{12,14},{16,20},{18,... | collective-permute-start | bytes 786440 | tf_op jit(solution)/shard_map/ppermute | solution.py:43
  158.1 19.0 %collective-permute-start.70 = (bf16[128,256]{1,0:T(8,128)(2,1)S(1)}, bf16[128,256]{1,0:T(8,128)(2,1)S(1)}, u32[]{:S(2)}, u32[]{:S(2)}) collective-permute-start(bf16[128,256]{1,0:T(8,128)(2,1)S(1)} %add_convert_fusion.4.refs_0_), channel_id=1, source_target_pairs={{0,8},{2,10},{4,12},{6,14},{8,16},{10,18},{12,20},{14,22},{16,24},... | collective-permute-start | bytes 196616 | tf_op jit(solution)/shard_map/ppermute | solution.py:47
  159.1 19.3 %collective-permute-start.71 = (bf16[128,256]{1,0:T(8,128)(2,1)S(1)}, bf16[128,256]{1,0:T(8,128)(2,1)S(1)}, u32[]{:S(2)}, u32[]{:S(2)}) collective-permute-start(bf16[128,256]{1,0:T(8,128)(2,1)S(1)} %add_convert_fusion.4.refs_0_), channel_id=1, source_target_pairs={{0,16},{2,18},{4,20},{6,22},{8,24},{10,26},{12,28},{14,30},{16,0},... | collective-permute-start | bytes 196616 | tf_op jit(solution)/shard_map/ppermute | solution.py:47
  160.3 19.7 %collective-permute-start.72 = (bf16[128,256]{1,0:T(8,128)(2,1)S(1)}, bf16[128,256]{1,0:T(8,128)(2,1)S(1)}, u32[]{:S(2)}, u32[]{:S(2)}) collective-permute-start(bf16[128,256]{1,0:T(8,128)(2,1)S(1)} %add_convert_fusion.4.refs_0_), channel_id=1, source_target_pairs={{0,24},{2,26},{4,28},{6,30},{8,0},{10,2},{12,4},{14,6},{16,8},{18,... | collective-permute-start | bytes 196616 | tf_op jit(solution)/shard_map/ppermute | solution.py:47
  177.1 23.3 %collective-permute-start.78 = (bf16[256,512]{1,0:T(8,128)(2,1)S(1)}, bf16[256,512]{1,0:T(8,128)(2,1)S(1)}, u32[]{:S(2)}, u32[]{:S(2)}) collective-permute-start(bf16[256,512]{1,0:T(8,128)(2,1)S(1)} %shard_map.81.refs_0_), channel_id=1, source_target_pairs={{0,2},{2,6},{6,4},{4,0},{8,10},{10,14},{14,12},{12,8},{16,18},{18,... | collective-permute-start | bytes 786440 | tf_op jit(solution)/shard_map/ppermute | solution.py:43
  178.4 22.8 %collective-permute-start.79 = (bf16[256,512]{1,0:T(8,128)(2,1)S(1)}, bf16[256,512]{1,0:T(8,128)(2,1)S(1)}, u32[]{:S(2)}, u32[]{:S(2)}) collective-permute-start(bf16[256,512]{1,0:T(8,128)(2,1)S(1)} %shard_map.81.refs_0_), channel_id=1, source_target_pairs={{0,6},{2,4},{6,0},{4,2},{8,14},{10,12},{14,8},{12,10},{16,22},{18,... | collective-permute-start | bytes 786440 | tf_op jit(solution)/shard_map/ppermute | solution.py:43
  180.0 21.2 %collective-permute-start.80 = (bf16[256,512]{1,0:T(8,128)(2,1)S(1)}, bf16[256,512]{1,0:T(8,128)(2,1)S(1)}, u32[]{:S(2)}, u32[]{:S(2)}) collective-permute-start(bf16[256,512]{1,0:T(8,128)(2,1)S(1)} %shard_map.81.refs_0_), channel_id=1, source_target_pairs={{0,4},{2,0},{6,2},{4,6},{8,12},{10,8},{14,10},{12,14},{16,20},{18,... | collective-permute-start | bytes 786440 | tf_op jit(solution)/shard_map/ppermute | solution.py:43
  188.0 8.8 %collective-permute-start.73 = (bf16[256,256]{1,0:T(8,128)(2,1)S(1)}, bf16[256,256]{1,0:T(8,128)(2,1)S(1)}, u32[]{:S(2)}, u32[]{:S(2)}) collective-permute-start(bf16[256,256]{1,0:T(8,128)(2,1)S(1)} %get-tuple-element.111), channel_id=1, source_target_pairs={{0,1},{1,0},{2,3},{3,2},{4,5},{5,4},{6,7},{7,6},{8,9},{9,8},{10,11... | collective-permute-start | bytes 393224 | tf_op jit(solution)/shard_map/ppermute | solution.py:50
  197.4 9.9 %collective-permute-start.74 = (bf16[256,512]{1,0:T(8,128)(2,1)S(1)}, bf16[256,512]{1,0:T(8,128)(2,1)S(1)}, u32[]{:S(2)}, u32[]{:S(2)}) collective-permute-start(bf16[256,512]{1,0:T(8,128)(2,1)S(1)} %shard_map.80.refs_0_), channel_id=1, source_target_pairs={{0,2},{2,6},{6,4},{4,0},{8,10},{10,14},{14,12},{12,8},{16,18},{18,... | collective-permute-start | bytes 786440 | tf_op jit(solution)/shard_map/ppermute | solution.py:43
  199.1 13.6 %collective-permute-start.75 = (bf16[256,512]{1,0:T(8,128)(2,1)S(1)}, bf16[256,512]{1,0:T(8,128)(2,1)S(1)}, u32[]{:S(2)}, u32[]{:S(2)}) collective-permute-start(bf16[256,512]{1,0:T(8,128)(2,1)S(1)} %shard_map.80.refs_0_), channel_id=1, source_target_pairs={{0,6},{2,4},{6,0},{4,2},{8,14},{10,12},{14,8},{12,10},{16,22},{18,... | collective-permute-start | bytes 786440 | tf_op jit(solution)/shard_map/ppermute | solution.py:43
  200.4 12.7 %collective-permute-start.76 = (bf16[256,512]{1,0:T(8,128)(2,1)S(1)}, bf16[256,512]{1,0:T(8,128)(2,1)S(1)}, u32[]{:S(2)}, u32[]{:S(2)}) collective-permute-start(bf16[256,512]{1,0:T(8,128)(2,1)S(1)} %shard_map.80.refs_0_), channel_id=1, source_target_pairs={{0,4},{2,0},{6,2},{4,6},{8,12},{10,8},{14,10},{12,14},{16,20},{18,... | collective-permute-start | bytes 786440 | tf_op jit(solution)/shard_map/ppermute | solution.py:43
  207.3 21.9 %collective-permute-start.89 = (bf16[256,1536]{1,0:T(8,128)(2,1)S(1)}, bf16[256,1536]{1,0:T(8,128)(2,1)S(1)}, u32[]{:S(2)}, u32[]{:S(2)}) collective-permute-start(bf16[256,1536]{1,0:T(8,128)(2,1)S(1)} %pad_maximum_fusion), channel_id=1, source_target_pairs={{0,1},{1,0},{2,3},{3,2},{4,5},{5,4},{6,7},{7,6},{8,9},{9,8},{10,11... | collective-permute-start | bytes 2359304 | tf_op jit(solution)/shard_map/ppermute | solution.py:50
  218.9 10.3 %collective-permute-start.90 = (bf16[256,1536]{1,0:T(8,128)(2,1)S(1)}, bf16[256,1536]{1,0:T(8,128)(2,1)S(1)}, u32[]{:S(2)}, u32[]{:S(2)}) collective-permute-start(bf16[256,1536]{1,0:T(8,128)(2,1)S(1)} %pad_maximum_fusion.1), channel_id=1, source_target_pairs={{0,1},{1,0},{2,3},{3,2},{4,5},{5,4},{6,7},{7,6},{8,9},{9,8},{10,11... | collective-permute-start | bytes 2359304 | tf_op jit(solution)/shard_map/ppermute | solution.py:50
  (49 other events, 299.8 us)

commit v2 on v1

v2 whole, which is shorter than its diff:
```python
import dataclasses
import functools
import math

import jax
import jax.numpy as jnp
from jax import lax
from jax.sharding import PartitionSpec as P
from jax.experimental import pallas as pl
from jax.experimental.pallas import tpu as pltpu

F32 = jnp.float32
BF16 = jnp.bfloat16


def split_of(count):
    best = 1
    for d in range(1, count + 1):
        if count % d == 0 and d * d <= count:
            best = d
    return best


def nt_dot(a, b):
    return lax.dot_general(a, b, (((1,), (1,)), ((), ())), preferred_element_type=F32)


def cut(n_rows, share):
    plane = split_of(n_rows)
    power = plane & (plane - 1) == 0
    code = [g ^ (g >> 1) if power else g for g in range(plane)]
    return plane, n_rows // plane, share // plane, code


def places(plane, code):
    row = lax.axis_index("rows")
    spot = row % plane
    g = sum(jnp.where(spot == code[i], i, 0) for i in range(plane))
    return g, row // plane, lax.axis_index("cols")


def movers(plane, depth, code, n_cols):
    def along_plane(x, k):
        pairs = [(b * plane + code[i], b * plane + code[(i + k) % plane]) for b in range(depth) for i in range(plane)]
        return lax.ppermute(x, "rows", pairs)

    def along_depth(x, k):
        pairs = [(b * plane + i, ((b + k) % depth) * plane + i) for b in range(depth) for i in range(plane)]
        return lax.ppermute(x, "rows", pairs)

    def along_cols(x, k):
        return lax.ppermute(x, "cols", [(i, (i + k) % n_cols) for i in range(n_cols)])

    return along_plane, along_depth, along_cols


def plain_path(lower_pivot, lower_rest, diag_inverse, rhs_pivot, rhs_rest):
    steps = lower_pivot.shape[0]
    eqs = lower_pivot.shape[1]
    share = lower_pivot.shape[3]
    sides = rhs_pivot.shape[2]
    rest = lower_rest.shape[0]
    n_rows = lax.axis_size("rows")
    n_cols = lax.axis_size("cols")
    plane, depth, width, code = cut(n_rows, share)
    g, z, core = places(plane, code)
    part = sides // depth
    along_plane, along_depth, along_cols = movers(plane, depth, code, n_cols)

    def gather(move, count, x, axis):
        return jnp.concatenate([x] + [move(x, k) for k in range(1, count)], axis=axis)

    def my_diag(s):
        block = diag_inverse[s].reshape(plane, width, eqs)
        parts = [lax.dynamic_index_in_dim(block, (g + k) % plane, 0, False) for k in range(plane)]
        held = jnp.concatenate([parts[0]] + [along_plane(parts[k], k) for k in range(1, plane)], axis=1)
        return gather(along_cols, n_cols, held, 0)

    def my_lower(s):
        parts = [
            lax.dynamic_slice_in_dim(lower_pivot[s, :, :s, :], ((g + k) % plane) * width, width, 2)
            for k in range(plane)
        ]
        held = jnp.concatenate([parts[0]] + [along_plane(parts[k], k) for k in range(1, plane)], axis=0)
        return gather(along_cols, n_cols, held, 2)

    def rolled(x, shift, axis):
        return jnp.roll(x, shift, axis)

    rhs_t = jnp.swapaxes(rhs_pivot, 1, 2)
    blocks = rhs_t.reshape(steps, depth, part, eqs)[:, ::-1]
    blocks = rolled(blocks, z + 1, 1).reshape(steps, sides, eqs)

    solved = []
    totals = jnp.zeros((sides, rest), F32)
    outs = []
    for s in range(steps):
        diag = my_diag(s)
        if s == 0:
            own = blocks[0]
        else:
            lower = my_lower(s)
            partial = jnp.zeros((sides, plane * eqs), F32)
            for t in range(s):
                partial = partial + nt_dot(solved[t], lower[:, t, :])
            total = blocks[s].astype(F32) - partial[:, :eqs]
            sent = partial.astype(BF16)
            for k in range(1, plane):
                total = total - along_plane(sent[:, k * eqs : (k + 1) * eqs], -k).astype(F32)
            own = total.astype(BF16)
        residual = gather(along_plane, plane, own, 1)
        product = nt_dot(residual, diag)
        sent = product.astype(BF16)
        total = product[:part]
        for k in range(1, depth):
            total = total + along_depth(sent[k * part : (k + 1) * part], -k).astype(F32)
        mine = total.astype(BF16)
        here = gather(along_depth, depth, mine, 0)
        solved.append(here)
        pieces = [here] + [along_plane(here, k) for k in range(1, plane)]
        pieces = [pieces[(-k) % plane] for k in range(plane)]
        full = jnp.stack([p.reshape(depth, part, n_cols, width) for p in pieces], axis=3)
        full = full[jnp.array([(-k) % depth for k in range(depth)])]
        full = rolled(full, z, 0)
        full = rolled(full, g, 3).reshape(sides, n_cols, share)
        rest_parts = [lower_rest[:, s, :]] + [along_cols(lower_rest[:, s, :], k) for k in range(1, n_cols)]
        for k in range(n_cols):
            totals = totals + nt_dot(full[:, k, :], rest_parts[k])
        theirs = [full[:, 0]] + [along_cols(full[:, k], -k) for k in range(1, n_cols)]
        theirs = rolled(jnp.stack(theirs, 0), core, 0).reshape(n_cols * sides, share)
        outs.append(theirs.T)
    remainder = (rhs_rest.astype(F32) - totals).astype(BF16)
    return jnp.stack(outs), remainder


VMEM_LIMIT = 40 * 1024 * 1024
WEIGHT = 8
SMALL = pl.BlockSpec(memory_space=pltpu.SMEM)
WHOLE = pl.BlockSpec(memory_space=pltpu.VMEM)


def call(body, outs, ins, specs, flops=0, scratch=(), after=(), weight=1, **more):
    size = sum(math.prod(x.shape) * x.dtype.itemsize for x in [*ins, *outs])
    first, last = len(ins), len(ins) + len(after)

    def run(*refs):
        body(*refs[:first], *refs[last:])

    return pl.pallas_call(
        run,
        out_shape=tuple(outs),
        in_specs=list(specs) + [pl.BlockSpec(memory_space=pl.ANY)] * len(after),
        scratch_shapes=list(scratch),
        compiler_params=pltpu.CompilerParams(vmem_limit_bytes=VMEM_LIMIT),
        cost_estimate=pl.CostEstimate(flops=flops, bytes_accessed=size * weight, transcendentals=0),
        **more,
    )(*ins, *after)


def shaped(dims, kind):
    return jax.ShapeDtypeStruct(dims, kind)


def prep_body(ss, form, meta, *refs):
    py, width, eqs = form.py, form.width, form.eqs
    refs = list(refs)
    diag, rhs = refs.pop(0), refs.pop(0)
    lower = refs.pop(0) if ss[-1] else None
    flat = refs.pop() if ss[-1] else None
    for i, s in enumerate(ss):
        outs = refs[i * py : (i + 1) * py]
        if s:
            flat[...] = jnp.swapaxes(lower[i], 0, 1)
        for dy in range(py):
            at = lax.rem(meta[0] + dy, py) * width
            for h in range(width // eqs):
                outs[dy][:, h * eqs : (h + 1) * eqs] = diag[i, pl.ds(pl.multiple_of(at + h * eqs, eqs), eqs), :]
            for t in range(s):
                outs[dy][:, (1 + t) * width : (2 + t) * width] = flat[t, :, pl.ds(pl.multiple_of(at, width), width)]
            outs[dy][:, (1 + s) * width :] = rhs[i]


def prep(ss, form, meta, diag_inverse, rhs_pivot, lower_pivot, after=()):
    width, eqs, share, sides = form.width, form.eqs, form.py * form.width, form.px * form.sides
    steps, count = lower_pivot.shape[0], len(ss)
    ins = [meta, diag_inverse, rhs_pivot]
    specs = [
        SMALL,
        pl.BlockSpec((pl.Element(count), pl.Element(share), pl.Element(eqs)), lambda i: (ss[0], 0, 0)),
        pl.BlockSpec((pl.Element(count), pl.Element(eqs), pl.Element(sides)), lambda i: (ss[0], 0, 0)),
    ]
    scratch = []
    if ss[-1]:
        ins.append(lower_pivot)
        specs.append(
            pl.BlockSpec(
                (pl.Element(count), pl.Element(eqs), pl.Element(steps), pl.Element(share)), lambda i: (ss[0], 0, 0, 0)
            )
        )
        scratch.append(pltpu.VMEM((steps, eqs, share), BF16))
    dims = [(eqs, (s + 1) * width + sides) for s in ss for _ in range(form.py)]
    outs = call(
        functools.partial(prep_body, ss, form),
        [shaped(d, BF16) for d in dims],
        ins,
        specs,
        scratch=scratch,
        after=after,
        weight=WEIGHT,
        grid=(1,),
        out_specs=tuple(pl.BlockSpec(d, lambda i: (0, 0)) for d in dims),
    )
    return {s: outs[i * form.py : (i + 1) * form.py] for i, s in enumerate(ss)}


def pack_body(chips, *refs):
    for k in range(chips):
        refs[-1][k] = refs[k][...]


def pack(parts, after=()):
    return call(
        functools.partial(pack_body, len(parts)),
        [shaped((len(parts), *parts[0].shape), BF16)],
        parts,
        [WHOLE] * len(parts),
        after=after,
        weight=WEIGHT,
    )[0]


def take_held(form, refs):
    held = []
    while len(held) < form.n_cols * form.chips:
        ref = refs.pop(0)
        held += [ref] if len(ref.shape) == 2 else [ref.at[k] for k in range(form.chips)]
    return held


def diag_body(form, terms, meta, *refs):
    chips, n_cols, depth, eqs, width, sides = form.chips, form.n_cols, form.depth, form.eqs, form.width, form.sides
    refs = list(refs)
    held = take_held(form, refs)
    sums = [refs.pop(0) for _ in range(terms)]
    outs, product = refs[:-1], refs[-1]
    sub = width // depth
    right = held[0].shape[-1] - form.px * sides
    right = pl.ds(pl.multiple_of(right + meta[1] * sides, sides), sides)
    residual = jnp.concatenate([held[k][:, right] for k in range(chips)], axis=0)
    if terms:
        total = residual.astype(F32)
        for x in sums:
            total = total - x[...].astype(F32)
        residual = total.astype(BF16)
    for c in range(n_cols):
        for h in range(width // eqs):
            rows = jnp.concatenate(
                [held[c * chips + k][:, h * eqs : (h + 1) * eqs] for k in range(chips)], axis=1
            )
            product[c, h * eqs : (h + 1) * eqs] = jnp.dot(rows, residual, preferred_element_type=F32)
    for k in range(depth):
        at = pl.multiple_of(lax.rem(meta[2] + depth - k, depth) * sub, sub)
        for c in range(n_cols):
            outs[k][c * sub : (c + 1) * sub] = product[c, pl.ds(at, sub)].astype(outs[k].dtype)


def diag_product(form, meta, held, sums, after=()):
    width, eqs, sides, depth, n_cols, chips = form.width, form.eqs, form.sides, form.depth, form.n_cols, form.chips
    dims = (n_cols * (width // depth), sides)
    return call(
        functools.partial(diag_body, form, len(sums)),
        [shaped(dims, F32)] + [shaped(dims, BF16)] * (depth - 1),
        [meta, *held, *sums],
        [SMALL] + [WHOLE] * (len(held) + len(sums)),
        flops=2 * n_cols * width * chips * eqs * sides,
        scratch=[pltpu.VMEM((n_cols, width, sides), F32)],
        after=after,
    )


def put_pieces(form, meta, pieces, outs):
    depth, sub = form.depth, form.width // form.depth
    for k in range(depth):
        at = pl.multiple_of(lax.rem(meta[2] + depth - k, depth) * sub, sub)
        for c in range(form.n_cols):
            outs[c][pl.ds(at, sub)] = pieces[k][c * sub : (c + 1) * sub]


def lower_body(s, form, meta, *refs):
    chips, n_cols, eqs = form.chips, form.n_cols, form.eqs
    refs = list(refs)
    held = take_held(form, refs)
    width = form.width
    known = [[refs.pop(0) for _ in range(n_cols)] for _ in range(s - 1)]
    pieces = [refs.pop(0) for _ in range(form.depth)]
    outs, newest = refs[: form.py], refs[form.py :]
    put_pieces(form, meta, pieces, newest)
    total = None
    for t, blocks in enumerate(known + [newest]):
        for c in range(n_cols):
            lanes = slice((1 + t) * width, (2 + t) * width)
            rows = jnp.concatenate([held[c * chips + k][:, lanes] for k in range(chips)], axis=0)
            term = jnp.dot(rows, blocks[c][...], preferred_element_type=F32)
            total = term if total is None else total + term
    for e in range(form.py):
        for k, (dy, dx) in enumerate(form.shifts):
            mine = form.shifts.index(((dy - e) % form.py, dx))
            outs[e][k * eqs : (k + 1) * eqs] = total[mine * eqs : (mine + 1) * eqs].astype(outs[e].dtype)


def lower_product(s, form, meta, held, known, pieces, after=()):
    rows, sides = form.chips * form.eqs, form.sides
    flat = [x for blocks in known for x in blocks]
    ins = [meta, *held, *flat, *pieces]
    return call(
        functools.partial(lower_body, s, form),
        [shaped((rows, sides), F32)]
        + [shaped((rows, sides), BF16)] * (form.py - 1)
        + [shaped((form.width, sides), BF16)] * form.n_cols,
        ins,
        [SMALL] + [WHOLE] * (len(ins) - 1),
        flops=2 * s * form.n_cols * form.width * rows * sides,
        after=after,
    )


def place_body(form, meta, *refs):
    put_pieces(form, meta, refs[: form.depth], refs[form.depth :])


def place(form, meta, pieces, after=()):
    return call(
        functools.partial(place_body, form),
        [shaped((form.width, form.sides), BF16)] * form.n_cols,
        [meta, *pieces],
        [SMALL] + [WHOLE] * form.depth,
        after=after,
    )


def gate_body(*refs):
    pass


def gate(x, after):
    return call(
        gate_body,
        [shaped(x.shape, x.dtype)],
        [x],
        [pl.BlockSpec(memory_space=pl.ANY)],
        after=after,
        out_specs=(pl.BlockSpec(memory_space=pl.ANY),),
        input_output_aliases={0: 0},
    )[0]


def join_body(form, count, meta, *refs):
    width, sides = form.width, form.sides
    for i in range(count):
        for k in range(form.n_cols):
            at = pl.multiple_of(lax.rem(meta[3] + k, form.n_cols) * sides, sides)
            refs[-1][i * width : (i + 1) * width, pl.ds(at, sides)] = refs[i * form.n_cols + k][...]


def join(form, meta, parts, after=()):
    count = len(parts) // form.n_cols
    return call(
        functools.partial(join_body, form, count),
        [shaped((count * form.width, form.n_cols * form.sides), BF16)],
        [meta, *parts],
        [SMALL] + [WHOLE] * len(parts),
        after=after,
    )[0]


def flat_body(x, *refs):
    refs[-2][...] = jnp.swapaxes(x[...], 0, 1)
    refs[-1][...] = jnp.zeros_like(refs[-1])


def flat_rest(lower_rest, buffer, turn, turns, block, after=()):
    rest, steps, share = lower_rest.shape
    first = turn * (rest // turns // block)
    ins, alias = [lower_rest], {}
    specs = [pl.BlockSpec((block, steps, share), lambda i: (first + i, 0, 0))]
    if buffer is not None:
        alias = {1: 0}
        ins.append(buffer)
        specs.append(pl.BlockSpec(memory_space=pltpu.HBM))
    return call(
        flat_body,
        [pltpu.HBM((steps, rest, share), BF16), shaped((8, 128), F32)],
        ins,
        specs,
        after=after,
        grid=(rest // turns // block,),
        out_specs=(
            pl.BlockSpec((steps, block, share), lambda i: (0, first + i, 0)),
            pl.BlockSpec((8, 128), lambda i: (0, 0)),
        ),
        input_output_aliases=alias,
    )


def write_body(form, count, meta, *refs):
    parts = refs[: form.chips]
    out, turned = refs[-2:]
    width, sides = form.width, form.sides
    for i in range(count):
        for k, (dy, dx) in enumerate(form.shifts):
            y, x = lax.rem(meta[0] + form.py - dy, form.py), lax.rem(meta[1] + form.px - dx, form.px)
            block = parts[k][i * width : (i + 1) * width]
            row = pl.ds(pl.multiple_of(y * width, width), width)
            for c in range(form.n_cols):
                lane = pl.ds(pl.multiple_of((c * form.px + x) * sides, sides), sides)
                piece = block[:, c * sides : (c + 1) * sides]
                out[i, row, lane] = piece
                turned[i, lane, row] = piece.T


def write(s, steps, form, meta, parts, buffer, after=()):
    share, total = form.py * form.width, form.px * form.n_cols * form.sides
    count = parts[0].shape[0] // form.width
    ins = [meta, *parts]
    specs = [SMALL] + [pl.BlockSpec(x.shape, lambda i: (0, 0)) for x in parts]
    alias = {}
    if buffer is not None:
        alias = {len(ins): 0}
        ins.append(buffer)
        specs.append(pl.BlockSpec(memory_space=pltpu.HBM))
    return call(
        functools.partial(write_body, form, count),
        [pltpu.HBM((steps, share, total), BF16), shaped((count, total, share), BF16)],
        ins,
        specs,
        after=after,
        grid=(1,),
        out_specs=(
            pl.BlockSpec((count, share, total), lambda i: (s // count, 0, 0)),
            pl.BlockSpec((count, total, share), lambda i: (0, 0, 0)),
        ),
        input_output_aliases=alias,
    )


def rest_body(form, orders, counts, meta, *refs):
    turned, lower, outs = refs[: len(counts)], refs[len(counts)], refs[len(counts) + 1 :]
    sides = form.px * form.sides
    for order, out in zip(orders, outs):
        at = pl.multiple_of(lax.rem(meta[3] + order, form.n_cols) * sides, sides)
        total, t = None, 0
        for x, count in zip(turned, counts):
            for i in range(count):
                term = nt_dot(x[i, pl.ds(at, sides), :], lower[t])
                total = term if total is None else total + term
                t += 1
        out[...] = total.astype(out.dtype)


def rest_product(first, form, orders, meta, turned, lower, after=()):
    _, rest, share = lower.shape
    counts = [x.shape[0] for x in turned]
    count = sum(counts)
    sides = form.px * form.sides
    block = max(n for n in (512, 384, 256, 128) if rest % n == 0)
    return call(
        functools.partial(rest_body, form, orders, counts),
        [shaped((sides, rest), F32 if order == 0 else BF16) for order in orders],
        [meta, *turned, pltpu.with_memory_space_constraint(lower, pltpu.HBM)],
        [SMALL]
        + [pl.BlockSpec(x.shape, lambda i: (0, 0, 0)) for x in turned]
        + [pl.BlockSpec((count, block, share), lambda i: (first // count, i, 0))],
        flops=2 * count * share * sides * rest * len(orders),
        after=after,
        grid=(rest // block,),
        out_specs=tuple(pl.BlockSpec((sides, block), lambda i: (0, i)) for _ in orders),
    )


@dataclasses.dataclass
class Form:
    py: int
    px: int
    depth: int
    n_cols: int
    eqs: int
    width: int
    sides: int

    def __post_init__(self):
        self.shifts = [(dy, dx) for dy in range(self.py) for dx in range(self.px)]
        self.chips = len(self.shifts)


def form_of(lower_pivot, rhs_pivot):
    n_rows = lax.axis_size("rows")
    plane = split_of(n_rows)
    px = split_of(plane)
    py = plane // px
    return Form(
        py, px, n_rows // plane, lax.axis_size("cols"), lower_pivot.shape[1], lower_pivot.shape[3] // py,
        rhs_pivot.shape[2] // px,
    )


def kernel_path(form, lower_pivot, lower_rest, diag_inverse, rhs_pivot, rhs_rest):
    lower_pivot, lower_rest, diag_inverse, rhs_pivot = (
        pltpu.with_memory_space_constraint(x, pltpu.HBM) for x in (lower_pivot, lower_rest, diag_inverse, rhs_pivot)
    )
    steps = lower_pivot.shape[0]
    rest = lower_rest.shape[0]
    py, px, depth, n_cols, chips = form.py, form.px, form.depth, form.n_cols, form.chips
    row = lax.axis_index("rows")
    meta = jnp.stack([row // px % py, row % px, row // chips, lax.axis_index("cols")]).astype(jnp.int32)

    def along_plane(x, dy, dx):
        pairs = [
            ((b * py + y) * px + i, (b * py + (y + dy) % py) * px + (i + dx) % px)
            for b in range(depth)
            for y in range(py)
            for i in range(px)
        ]
        return lax.ppermute(x, "rows", pairs)

    def along_depth(x, k):
        pairs = [(b * chips + i, (b + k) % depth * chips + i) for b in range(depth) for i in range(chips)]
        return lax.ppermute(x, "rows", pairs)

    def along_cols(x, k):
        return lax.ppermute(x, "cols", [(i, (i + k) % n_cols) for i in range(n_cols)])

    def out(blocks):
        first = [blocks[0]] + [along_plane(blocks[dy], dy, 0) for dy in range(1, py)]
        return first, [along_plane(blocks[0], 0, dx) for dx in range(1, px)]

    def onward(state, after=()):
        first, got = state
        got = [first[0], *got]
        for x in first[1:]:
            x = gate(x, after) if after else x
            got += [x] + [along_plane(x, 0, dx) for dx in range(1, px)]
        return got

    def held_of(parts, after):
        if not after:
            return parts + [along_cols(x, c) for c in range(1, n_cols) for x in parts]
        mine = pack(parts, after)
        return [mine] + [along_cols(mine, c) for c in range(1, n_cols)]

    def joined(ts, after=()):
        parts = []
        for t in ts:
            parts += [known[t][0]] + [along_cols(known[t][k], -k) for k in range(1, n_cols)]
        return join(form, meta, parts, after)

    turns = 3
    block = 128
    while rest % (turns * block):
        turns -= 1
    last = steps - 1
    inputs = (diag_inverse, rhs_pivot, lower_pivot)
    first = out(prep((0,), form, meta, *inputs)[0])
    packed = prep(tuple(range(1, steps)), form, meta, *inputs)
    held = held_of(onward(first), ())
    moving, moved, leaving = {}, {}, {}
    known, sums, turned, flat, buffer = [], [], [], None, None
    by_lower, by_diag, by_sum = ({s: [] for s in range(steps + 1)} for _ in range(3))
    if last:
        moving[1] = out(packed[1])
        by_diag[0] += [packed[last][0], *moving[1][0][1:], *moving[1][1]]
    for s in range(steps):
        if s > 0:
            outs = lower_product(s, form, meta, held, known, pieces, by_lower[s])
            known.append(outs[py:])
            sums = [outs[0]] + [along_plane(outs[e], e, 0) for e in range(1, py)]
            if s < last:
                moved[s + 1] = onward(moving[s + 1], [outs[0]])
                by_sum[s] += moved[s + 1]
            else:
                ready = onward(leaving[0], [outs[0]])
                by_sum[s] += ready
            if s == last - 1:
                whole = joined(range(s), [outs[0]])
                by_diag[s].append(whole)
            if s == last:
                newest = joined([s - 1], [outs[0]])
                by_diag[s].append(newest)
        products = diag_product(form, meta, held, sums, by_diag[s])
        if s == 0 and last:
            moved[1] = onward(moving[1], [products[0]])
            by_sum[0] += moved[1]
        if s < last - 1:
            first = [gate(x, [products[0]]) for x in packed[s + 2]]
        elif s == last - 1:
            first = [gate(whole, [products[0]])] * py
        else:
            first = [gate(newest, [products[0]])] * py
        first = [first[0]] + [along_plane(first[dy], dy, 0) for dy in range(1, py)]
        by_sum[s] += first[1:]
        arrivals = [along_depth(products[k], -k) for k in range(1, depth)]
        arrivals[-1] = gate(arrivals[-1], by_sum[s])
        total = products[0]
        for x in arrivals:
            total = total + x.astype(F32)
        mine = total.astype(BF16)
        if s < last:
            held = held_of(moved[s + 1], [mine])
        send = gate(first[0], [mine])
        direct = [along_plane(send, 0, dx) for dx in range(1, px)]
        (by_diag if 0 < s < last else by_lower)[s + 1] += direct
        if s < last - 1:
            moving[s + 2] = ([send, *first[1:]], direct)
        else:
            leaving[s - last + 1] = ([send, *first[1:]], direct)
        pieces = [mine] + [along_depth(mine, k) for k in range(1, depth)]
        if s < turns:
            flat, mark = flat_rest(lower_rest, flat, s, turns, block, [mine])
            by_lower[s + 1].append(mark)
        if s == last:
            buffer, new = write(0, steps, form, meta, ready, buffer, [mine])
            turned.append(new)
            by_lower[s + 1].append(new)
    newest = onward(leaving[1], [mine])
    known.append(place(form, meta, pieces, by_lower[steps]))
    final, direct = out([joined([last])] * py)
    gathered = onward((final, direct))
    buffer, new = write(last - 1, steps, form, meta, newest, buffer, [mine])
    turned.append(new)
    early = rest_product(0, form, range(n_cols), meta, turned, flat, direct)
    base = rhs_rest.astype(F32) - early[0]
    for c in range(1, n_cols):
        base = base - along_cols(early[c], c).astype(F32)
    buffer, new = write(last, steps, form, meta, gathered, buffer)
    late = rest_product(last, form, range(n_cols), meta, [new], flat)
    total = base - late[0]
    for c in range(1, n_cols):
        total = total - along_cols(late[c], c).astype(F32)
    return buffer, total.astype(BF16)


def per_device(lower_pivot, lower_rest, diag_inverse, rhs_pivot, rhs_rest):
    form = form_of(lower_pivot, rhs_pivot)
    fits = form.eqs % 128 == 0 and form.width % form.eqs == 0 and form.sides % 128 == 0
    fits = fits and (form.width // form.depth) % 16 == 0 and lower_rest.shape[0] % 128 == 0
    if fits:
        return kernel_path(form, lower_pivot, lower_rest, diag_inverse, rhs_pivot, rhs_rest)
    return plain_path(lower_pivot, lower_rest, diag_inverse, rhs_pivot, rhs_rest)


def solution(mesh):
    placed = (
        P(None, "rows", None, "cols"),
        P("rows", None, "cols"),
        P(None, "cols", "rows"),
        P(None, "rows", "cols"),
        P("cols", "rows"),
    )
    return jax.shard_map(
        per_device,
        mesh=mesh,
        in_specs=placed,
        out_specs=(P(None, "cols", None), P("cols", "rows")),
        check_vma=False,
    )
```

time: 231 us -> 177 us (0.77)
  starting transfers between devices: 102 us -> 61 us
  Pallas kernels: 64.2 us -> 48.8 us
  waiting for transfers between devices: 56.7 us -> 63.7 us
  local copies, waits for them, and re-layouts: 4.38 us -> 0.01 us
    ppermute x45 -> x24, starting transfers between devices: 61 us -> 30.8 us  [along_plane(): return lax.ppermute(x, 'rows', pairs)]
    pallas_call x56 -> x43, Pallas kernels: 64.2 us -> 48.8 us  [call(): pl.pallas_call(run, out_shape=tuple(outs), in_specs=list(specs) + [pl.Blo...]
    ppermute x24, starting transfers between devices: 38.4 us -> 28.7 us  [along_depth(): return lax.ppermute(x, 'rows', pairs)]
    ppermute x45 -> x24, waiting for transfers between devices: 34.1 us -> 43.6 us  [along_plane(): return lax.ppermute(x, 'rows', pairs)]
    ppermute x24, waiting for transfers between devices: 22.6 us -> 18.2 us  [along_depth(): return lax.ppermute(x, 'rows', pairs)]
    unnamed x12 -> x2, local copies, waits for them, and re-layouts: 3.54 us -> 0.01 us
  transfers between devices with their start and end apart: 91 -> 61, of which waited for: 28 -> 27; matrix products, arithmetic and copies ran while one was open for 1% -> 0% of each run, Pallas kernels for 27% -> 25%
where the time goes in v2:
time: 177 us; the launch traced here: 176 us
  waiting for transfers between devices  63.7 us (36%)
  starting transfers between devices  61 us (34%)
  Pallas kernels  48.8 us (28%)
    pallas_call x43, Pallas kernels, call(): pl.pallas_call(run, out_shape=tuple(outs), in_specs=list(specs) + [pl.Blo...  48.8 us
    ppermute x24, waiting for transfers between devices, along_plane(): return lax.ppermute(x, 'rows', pairs)  43.6 us
    ppermute x24, starting transfers between devices, along_plane(): return lax.ppermute(x, 'rows', pairs)  30.8 us
    ppermute x24, starting transfers between devices, along_depth(): return lax.ppermute(x, 'rows', pairs)  28.7 us
    ppermute x24, waiting for transfers between devices, along_depth(): return lax.ppermute(x, 'rows', pairs)  18.2 us
  transfers between devices with their start and end apart: 61, of which 27 were waited for; matrix products, arithmetic and copies ran while one was open for 0% of the time, Pallas kernels for 25%

profile of v2, /device:TPU:0, one launch (start us, length us, event | category | flops | bytes accessed | tf_op | source)
XLA Modules:
  0.0 176.2 jit_solution(337710686126187572)
XLA Ops:
  1.8 3.0 %collective-permute-start.3 = (bf16[128,768]{1,0:T(8,128)(2,1)S(1)}, bf16[128,768]{1,0:T(8,128)(2,1)S(1)}, u32[]{:S(2)}, u32[]{:S(2)}) collective-permute-start(bf16[128,768]{1,0:T(8,128)(2,1)S(1)} %get-tuple-element.60), channel_id=1, source_target_pairs={{0,4},{2,6},{4,0},{6,2},{8,12},{10,14},{12,8},{14,10},{16,20},{18,... | collective-permute-start | bytes 589832 | tf_op jit(solution)/shard_map/ppermute | solution.py:523
  4.8 1.5 collective-permute-start.2
  6.3 3.4 %collective-permute-done.3.refs_3_ = bf16[128,768]{1,0:T(8,128)(2,1)S(1)} collective-permute-done((bf16[128,768]{1,0:T(8,128)(2,1)S(1)}, bf16[128,768]{1,0:T(8,128)(2,1)S(1)}, u32[]{:S(2)}, u32[]{:S(2)}) %collective-permute-start.3) | collective-permute-done | bytes 196640 | tf_op jit(solution)/shard_map/ppermute | solution.py:523
  9.7 1.7 collective-permute-start.4
  11.4 3.5 %shard_map.68 = (bf16[128,1280]{1,0:T(8,128)(2,1)S(1)}, bf16[128,1280]{1,0:T(8,128)(2,1)S(1)}, bf16[128,1792]{1,0:T(8,128)(2,1)S(1)}, bf16[128,1792]{1,0:T(8,128...) custom-call(s32[4]{0:T(128)S(1)} %pad_add_fusion.refs_0_, bf16[4,1024,128]{2,1,0:T(8,128)(2,1)} %refs_1_.3, ...), custom_call_target="tpu_custom_call" | custom-call | bytes 66060416 | tf_op jit(solution)/shard_map/pallas_call | solution.py:149
  14.9 1.6 collective-permute-start.1
  17.6 5.7 %collective-permute-done.1.refs_10_.refs_0_ = bf16[128,1280]{1,0:T(8,128)(2,1)S(1)} collective-permute-done((bf16[128,1280]{1,0:T(8,128)(2,1)S(1)}, bf16[128,1280]{1,0:T(8,128)(2,1)S(1)}, u32[]{:S(2)}, u32[]{:S(2)}) %collective-permute-start.1) | collective-permute-done | bytes 327712 | tf_op jit(solution)/shard_map/ppermute | solution.py:523
  26.8 1.6 collective-permute-start.12
  28.4 2.2 %collective-permute-start.10 = (bf16[256,128]{1,0:T(8,128)(2,1)S(1)}, bf16[256,128]{1,0:T(8,128)(2,1)S(1)}, u32[]{:S(2)}, u32[]{:S(2)}) collective-permute-start(bf16[256,128]{1,0:T(8,128)(2,1)S(1)} %get-tuple-element.62), channel_id=1, source_target_pairs={{0,24},{2,26},{4,28},{6,30},{8,0},{10,2},{12,4},{14,6},{16,8},{18,... | collective-permute-start | bytes 196616 | tf_op jit(solution)/shard_map/ppermute | solution.py:527
  31.5 1.6 collective-permute-done.12.refs_0_
  33.2 2.3 %collective-permute-done.13.refs_5_.refs_0_ = bf16[128,1792]{1,0:T(8,128)(2,1)S(1)} collective-permute-done((bf16[128,1792]{1,0:T(8,128)(2,1)S(1)}, bf16[128,1792]{1,0:T(8,128)(2,1)S(1)}, u32[]{:S(2)}, u32[]{:S(2)}) %collective-permute-start.13) | collective-permute-done | bytes 458784 | tf_op jit(solution)/shard_map/ppermute | solution.py:523
  37.7 2.2 %collective-permute-start.17 = (bf16[256,128]{1,0:T(8,128)(2,1)S(1)}, bf16[256,128]{1,0:T(8,128)(2,1)S(1)}, u32[]{:S(2)}, u32[]{:S(2)}) collective-permute-start(bf16[256,128]{1,0:T(8,128)(2,1)S(1)} %add_convert_fusion.3.refs_4_.refs_1_.refs_3_), channel_id=1, source_target_pairs={{0,24},{2,26},{4,28},{6,30},{8,0},{10,2},{12,4},{14,6},{16,8},{18,... | collective-permute-start | bytes 196616 | tf_op jit(solution)/shard_map/ppermute | solution.py:527
  41.0 5.1 %shard_map.77 = (bf16[4,1536,1024]{2,1,0:T(8,128)(2,1)}, f32[8,128]{1,0:T(8,128)S(1)}) custom-call(bf16[1536,4,1024]{2,1,0:T(4,128)(2,1)} %refs_0_.5, bf16[256,128]{1,0:T(8,128)(2,1)S(1)} %add_convert_fusion.3.refs_4_.refs_1_.refs_3_), custom_call_target="tpu_custom_call" | custom-call | bytes 25169920 | tf_op jit(solution)/shard_map/pallas_call | solution.py:149
  46.8 2.4 %collective-permute-done.18.refs_7_.refs_2_.refs_1_ = bf16[128,1792]{1,0:T(8,128)(2,1)S(1)} collective-permute-done((bf16[128,1792]{1,0:T(8,128)(2,1)S(1)}, bf16[128,1792]{1,0:T(8,128)(2,1)S(1)}, u32[]{:S(2)}, u32[]{:S(2)}) %collective-permute-start.18) | collective-permute-done | bytes 458784 | tf_op jit(solution)/shard_map/ppermute | solution.py:523
  51.7 3.7 %collective-permute-done.19.refs_4_ = bf16[512,128]{1,0:T(8,128)(2,1)S(1)} collective-permute-done((bf16[512,128]{1,0:T(8,128)(2,1)S(1)}, bf16[512,128]{1,0:T(8,128)(2,1)S(1)}, u32[]{:S(2)}, u32[]{:S(2)}) %collective-permute-start.19) | collective-permute-done | bytes 131104 | tf_op jit(solution)/shard_map/ppermute | solution.py:523
  57.8 1.5 collective-permute-start.23
  59.3 3.8 %collective-permute-start.20 = (bf16[256,128]{1,0:T(8,128)(2,1)S(1)}, bf16[256,128]{1,0:T(8,128)(2,1)S(1)}, u32[]{:S(2)}, u32[]{:S(2)}) collective-permute-start(bf16[256,128]{1,0:T(8,128)(2,1)S(1)} %get-tuple-element.71), channel_id=1, source_target_pairs={{0,24},{2,26},{4,28},{6,30},{8,0},{10,2},{12,4},{14,6},{16,8},{18,... | collective-permute-start | bytes 196616 | tf_op jit(solution)/shard_map/ppermute | solution.py:527
  63.1 2.3 %collective-permute-done.22.refs_0_ = bf16[256,128]{1,0:T(8,128)(2,1)S(1)} collective-permute-done((bf16[256,128]{1,0:T(8,128)(2,1)S(1)}, bf16[256,128]{1,0:T(8,128)(2,1)S(1)}, u32[]{:S(2)}, u32[]{:S(2)}) %collective-permute-start.22) | collective-permute-done | bytes 65568 | tf_op jit(solution)/shard_map/ppermute | solution.py:527
  65.5 3.2 %collective-permute-done.23.refs_4_.refs_3_ = bf16[128,1792]{1,0:T(8,128)(2,1)S(1)} collective-permute-done((bf16[128,1792]{1,0:T(8,128)(2,1)S(1)}, bf16[128,1792]{1,0:T(8,128)(2,1)S(1)}, u32[]{:S(2)}, u32[]{:S(2)}) %collective-permute-start.23) | collective-permute-done | bytes 458784 | tf_op jit(solution)/shard_map/ppermute | solution.py:523
  68.7 1.8 %collective-permute-done.24.refs_5_.refs_0_ = bf16[128,2304]{1,0:T(8,128)(2,1)S(1)} collective-permute-done((bf16[128,2304]{1,0:T(8,128)(2,1)S(1)}, bf16[128,2304]{1,0:T(8,128)(2,1)S(1)}, u32[]{:S(2)}, u32[]{:S(2)}) %collective-permute-start.24) | collective-permute-done | bytes 589856 | tf_op jit(solution)/shard_map/ppermute | solution.py:523
  72.1 2.2 %collective-permute-start.29 = (bf16[256,128]{1,0:T(8,128)(2,1)S(1)}, bf16[256,128]{1,0:T(8,128)(2,1)S(1)}, u32[]{:S(2)}, u32[]{:S(2)}) collective-permute-start(bf16[256,128]{1,0:T(8,128)(2,1)S(1)} %add_convert_fusion.2.refs_1_.refs_4_.refs_2_.refs_5_), channel_id=1, source_target_pairs={{0,24},{2,26},{4,28},{6,30},{8,0},{10,2},{12,4},{14,6},{16,8},{18,... | collective-permute-start | bytes 196616 | tf_op jit(solution)/shard_map/ppermute | solution.py:527
  75.4 5.1 %shard_map.86 = (bf16[4,1536,1024]{2,1,0:T(8,128)(2,1)}, f32[8,128]{1,0:T(8,128)S(1)}) custom-call(bf16[1536,4,1024]{2,1,0:T(4,128)(2,1)} %refs_0_.5, bf16[4,1536,1024]{2,1,0:T(8,128)(2,1)} %get-tuple-element.77.refs_1_, bf16[256,128]{1,0:T(8,128)(2,1)S(1)} %add_convert_fusion.2.refs_1_.refs_4_.refs_2_.refs_5_), custom_call_target="tpu_custom_call", output_to_operand_aliasing={{0}: (1, {})} | custom-call | bytes 37752832 | tf_op jit(solution)/shard_map/pallas_call | solution.py:149
  82.6 1.5 collective-permute-start.31
  86.5 2.0 %collective-permute-done.31.refs_4_ = bf16[512,128]{1,0:T(8,128)(2,1)S(1)} collective-permute-done((bf16[512,128]{1,0:T(8,128)(2,1)S(1)}, bf16[512,128]{1,0:T(8,128)(2,1)S(1)}, u32[]{:S(2)}, u32[]{:S(2)}) %collective-permute-start.31) | collective-permute-done | bytes 131104 | tf_op jit(solution)/shard_map/ppermute | solution.py:523
  89.6 1.5 collective-permute-start.37
  91.0 1.8 %collective-permute-start.36 = (bf16[256,128]{1,0:T(8,128)(2,1)S(1)}, bf16[256,128]{1,0:T(8,128)(2,1)S(1)}, u32[]{:S(2)}, u32[]{:S(2)}) collective-permute-start(bf16[256,128]{1,0:T(8,128)(2,1)S(1)} %get-tuple-element.86), channel_id=1, source_target_pairs={{0,8},{2,10},{4,12},{6,14},{8,16},{10,18},{12,20},{14,22},{16,24},... | collective-permute-start | bytes 196616 | tf_op jit(solution)/shard_map/ppermute | solution.py:527
  92.8 2.1 %collective-permute-start.34 = (bf16[256,128]{1,0:T(8,128)(2,1)S(1)}, bf16[256,128]{1,0:T(8,128)(2,1)S(1)}, u32[]{:S(2)}, u32[]{:S(2)}) collective-permute-start(bf16[256,128]{1,0:T(8,128)(2,1)S(1)} %get-tuple-element.84), channel_id=1, source_target_pairs={{0,24},{2,26},{4,28},{6,30},{8,0},{10,2},{12,4},{14,6},{16,8},{18,... | collective-permute-start | bytes 196616 | tf_op jit(solution)/shard_map/ppermute | solution.py:527
  94.9 2.9 %collective-permute-done.36.refs_0_ = bf16[256,128]{1,0:T(8,128)(2,1)S(1)} collective-permute-done((bf16[256,128]{1,0:T(8,128)(2,1)S(1)}, bf16[256,128]{1,0:T(8,128)(2,1)S(1)}, u32[]{:S(2)}, u32[]{:S(2)}) %collective-permute-start.36) | collective-permute-done | bytes 65568 | tf_op jit(solution)/shard_map/ppermute | solution.py:527
  97.8 1.7 collective-permute-done.30.refs_4_.refs_3_
  99.5 3.6 %collective-permute-done.37.refs_5_.refs_0_ = bf16[1024,256]{1,0:T(8,128)(2,1)S(1)} collective-permute-done((bf16[1024,256]{1,0:T(8,128)(2,1)S(1)}, bf16[1024,256]{1,0:T(8,128)(2,1)S(1)}, u32[]{:S(2)}, u32[]{:S(2)}) %collective-permute-start.37) | collective-permute-done | bytes 524320 | tf_op jit(solution)/shard_map/ppermute | solution.py:523
  104.9 1.8 %collective-permute-start.41 = (bf16[256,128]{1,0:T(8,128)(2,1)S(1)}, bf16[256,128]{1,0:T(8,128)(2,1)S(1)}, u32[]{:S(2)}, u32[]{:S(2)}) collective-permute-start(bf16[256,128]{1,0:T(8,128)(2,1)S(1)} %add_convert_fusion.1.refs_4_.refs_2_.refs_7_.refs_1_), channel_id=1, source_target_pairs={{0,24},{2,26},{4,28},{6,30},{8,0},{10,2},{12,4},{14,6},{16,8},{18,... | collective-permute-start | bytes 196616 | tf_op jit(solution)/shard_map/ppermute | solution.py:527
  108.7 5.1 %shard_map.94 = (bf16[4,1536,1024]{2,1,0:T(8,128)(2,1)}, f32[8,128]{1,0:T(8,128)S(1)}) custom-call(bf16[1536,4,1024]{2,1,0:T(4,128)(2,1)} %refs_0_.5, bf16[4,1536,1024]{2,1,0:T(8,128)(2,1)} %get-tuple-element.87.refs_1_, bf16[256,128]{1,0:T(8,128)(2,1)S(1)} %add_convert_fusion.1.refs_4_.refs_2_.refs_7_.refs_1_), custom_call_target="tpu_custom_call", output_to_operand_aliasing={{0}: (1, {})} | custom-call | bytes 37752832 | tf_op jit(solution)/shard_map/pallas_call | solution.py:149
  114.3 1.5 shard_map.95
  118.4 3.9 %collective-permute-done.42.refs_4_ = bf16[512,128]{1,0:T(8,128)(2,1)S(1)} collective-permute-done((bf16[512,128]{1,0:T(8,128)(2,1)S(1)}, bf16[512,128]{1,0:T(8,128)(2,1)S(1)}, u32[]{:S(2)}, u32[]{:S(2)}) %collective-permute-start.42) | collective-permute-done | bytes 131104 | tf_op jit(solution)/shard_map/ppermute | solution.py:523
  123.4 1.4 collective-permute-start.49
  125.9 2.8 %collective-permute-start.45 = (bf16[256,128]{1,0:T(8,128)(2,1)S(1)}, bf16[256,128]{1,0:T(8,128)(2,1)S(1)}, u32[]{:S(2)}, u32[]{:S(2)}) collective-permute-start(bf16[256,128]{1,0:T(8,128)(2,1)S(1)} %get-tuple-element.94), channel_id=1, source_target_pairs={{0,24},{2,26},{4,28},{6,30},{8,0},{10,2},{12,4},{14,6},{16,8},{18,... | collective-permute-start | bytes 196616 | tf_op jit(solution)/shard_map/ppermute | solution.py:527
  128.7 2.9 %collective-permute-done.47.refs_0_ = bf16[256,128]{1,0:T(8,128)(2,1)S(1)} collective-permute-done((bf16[256,128]{1,0:T(8,128)(2,1)S(1)}, bf16[256,128]{1,0:T(8,128)(2,1)S(1)}, u32[]{:S(2)}, u32[]{:S(2)}) %collective-permute-start.47) | collective-permute-done | bytes 65568 | tf_op jit(solution)/shard_map/ppermute | solution.py:527
  131.6 2.7 %collective-permute-done.46 = bf16[256,128]{1,0:T(8,128)(2,1)S(1)} collective-permute-done((bf16[256,128]{1,0:T(8,128)(2,1)S(1)}, bf16[256,128]{1,0:T(8,128)(2,1)S(1)}, u32[]{:S(2)}, u32[]{:S(2)}) %collective-permute-start.46) | collective-permute-done | bytes 65568 | tf_op jit(solution)/shard_map/ppermute | solution.py:527
  135.1 1.7 collective-permute-start.52
  137.4 2.6 %shard_map.103 = (bf16[4,1024,512]{2,1,0:T(8,128)(2,1)}, bf16[2,512,1024]{2,1,0:T(8,128)(2,1)S(1)}) custom-call(s32[4]{0:T(128)S(1)} %pad_add_fusion.refs_0_, bf16[1024,256]{1,0:T(8,128)(2,1)S(1)} %shard_map.96.refs_1_, bf16[1024,256]{1,0:T(8,128)(2,1)S(1)} %collective-permute-done.43.refs_5_.refs_2_, bf16[1024,256]{1,0:T(8,128)(2,1)S(1)} %shard_map.99.refs_3_, ...), custom_call_target="tpu_custom_call" | custom-call | bytes 8388624 | tf_op jit(solution)/shard_map/pallas_call | solution.py:149
  140.0 3.1 %collective-permute-done.51.refs_3_ = bf16[256,128]{1,0:T(8,128)(2,1)S(1)} collective-permute-done((bf16[256,128]{1,0:T(8,128)(2,1)S(1)}, bf16[256,128]{1,0:T(8,128)(2,1)S(1)}, u32[]{:S(2)}, u32[]{:S(2)}) %collective-permute-start.51) | collective-permute-done | bytes 65568 | tf_op jit(solution)/shard_map/ppermute | solution.py:527
  148.0 4.9 %collective-permute-done.58.refs_4_ = bf16[512,256]{1,0:T(8,128)(2,1)S(1)} collective-permute-done((bf16[512,256]{1,0:T(8,128)(2,1)S(1)}, bf16[512,256]{1,0:T(8,128)(2,1)S(1)}, u32[]{:S(2)}, u32[]{:S(2)}) %collective-permute-start.58) | collective-permute-done | bytes 262176 | tf_op jit(solution)/shard_map/ppermute | solution.py:523
  153.0 1.9 %shard_map.107 = (bf16[4,1024,512]{2,1,0:T(8,128)(2,1)}, bf16[1,512,1024]{2,1,0:T(8,128)(2,1)S(1)}) custom-call(s32[4]{0:T(128)S(1)} %pad_add_fusion.refs_0_, bf16[512,256]{1,0:T(8,128)(2,1)S(1)} %shard_map.102.refs_1_, bf16[512,256]{1,0:T(8,128)(2,1)S(1)} %collective-permute-done.53.refs_5_.refs_2_, ...), custom_call_target="tpu_custom_call", output_to_operand_aliasing={{0}: (5, {})} | custom-call | bytes 10485776 | tf_op jit(solution)/shard_map/pallas_call | solution.py:149
  156.2 2.4 %collective-permute-done.55.refs_2_.refs_4_ = bf16[512,256]{1,0:T(8,128)(2,1)S(1)} collective-permute-done((bf16[512,256]{1,0:T(8,128)(2,1)S(1)}, bf16[512,256]{1,0:T(8,128)(2,1)S(1)}, u32[]{:S(2)}, u32[]{:S(2)}) %collective-permute-start.55) | collective-permute-done | bytes 262176 | tf_op jit(solution)/shard_map/ppermute | solution.py:523
  158.6 7.6 %shard_map.109 = (f32[256,1536]{1,0:T(8,128)S(1)}, bf16[256,1536]{1,0:T(8,128)(2,1)S(1)}) custom-call(s32[4]{0:T(128)S(1)} %pad_add_fusion.refs_0_, bf16[2,512,1024]{2,1,0:T(8,128)(2,1)S(1)} %get-tuple-element.97.refs_6_.refs_1_, bf16[1,512,1024]{2,1,0:T(8,128)(2,1)S(1)} %get-tuple-element.103.refs_2_, ...), custom_call_target="tpu_custom_call" | custom-call | flops 4831838208 | bytes 18087952 | tf_op jit(solution)/shard_map/pallas_call | solution.py:149
  166.2 1.9 %shard_map.108 = (bf16[4,1024,512]{2,1,0:T(8,128)(2,1)}, bf16[1,512,1024]{2,1,0:T(8,128)(2,1)S(1)}) custom-call(s32[4]{0:T(128)S(1)} %pad_add_fusion.refs_0_, bf16[512,256]{1,0:T(8,128)(2,1)S(1)} %shard_map.105.refs_1_, bf16[512,256]{1,0:T(8,128)(2,1)S(1)} %collective-permute-done.55.refs_2_.refs_4_, ...), custom_call_target="tpu_custom_call", output_to_operand_aliasing={{0}: (5, {})} | custom-call | bytes 10485776 | tf_op jit(solution)/shard_map/pallas_call | solution.py:149
  168.1 4.1 %shard_map.110 = (f32[256,1536]{1,0:T(8,128)S(1)}, bf16[256,1536]{1,0:T(8,128)(2,1)S(1)}) custom-call(s32[4]{0:T(128)S(1)} %pad_add_fusion.refs_0_, bf16[1,512,1024]{2,1,0:T(8,128)(2,1)S(1)} %get-tuple-element.107.refs_1_, bf16[4,1536,1024]{2,1,0:T(8,128)(2,1)} %get-tuple-element.104.refs_3_.refs_2_), custom_call_target="tpu_custom_call" | custom-call | flops 1610612736 | bytes 15990800 | tf_op jit(solution)/shard_map/pallas_call | solution.py:149
  172.8 1.9 %collective-permute-done.60 = bf16[256,1536]{1,0:T(8,128)(2,1)S(1)} collective-permute-done((bf16[256,1536]{1,0:T(8,128)(2,1)S(1)}, bf16[256,1536]{1,0:T(8,128)(2,1)S(1)}, u32[]{:S(2)}, u32[]{:S(2)}) %collective-permute-start.60) | collective-permute-done | bytes 786464 | tf_op jit(solution)/shard_map/ppermute | solution.py:530
  (125 shorter events, 42.2 us)
Async XLA Ops:
  1.8 7.9 %collective-permute-start.3 = (bf16[128,768]{1,0:T(8,128)(2,1)S(1)}, bf16[128,768]{1,0:T(8,128)(2,1)S(1)}, u32[]{:S(2)}, u32[]{:S(2)}) collective-permute-start(bf16[128,768]{1,0:T(8,128)(2,1)S(1)} %get-tuple-element.60), channel_id=1, source_target_pairs={{0,4},{2,6},{4,0},{6,2},{8,12},{10,14},{12,8},{14,10},{16,20},{18,... | collective-permute-start | bytes 589832 | tf_op jit(solution)/shard_map/ppermute | solution.py:523
  4.8 12.2 %collective-permute-start.5 = (bf16[128,768]{1,0:T(8,128)(2,1)S(1)}, bf16[128,768]{1,0:T(8,128)(2,1)S(1)}, u32[]{:S(2)}, u32[]{:S(2)}) collective-permute-start(bf16[128,768]{1,0:T(8,128)(2,1)S(1)} %get-tuple-element.59.refs_1_), channel_id=1, source_target_pairs={{0,1},{1,0},{2,3},{3,2},{4,5},{5,4},{6,7},{7,6},{8,9},{9,8},{10,11... | collective-permute-start | bytes 589832 | tf_op jit(solution)/shard_map/ppermute | solution.py:530
  4.8 12.2 %collective-permute-start.2 = (bf16[128,768]{1,0:T(8,128)(2,1)S(1)}, bf16[128,768]{1,0:T(8,128)(2,1)S(1)}, u32[]{:S(2)}, u32[]{:S(2)}) collective-permute-start(bf16[128,768]{1,0:T(8,128)(2,1)S(1)} %get-tuple-element.59.refs_1_), channel_id=1, source_target_pairs={{0,2},{2,0},{4,6},{6,4},{8,10},{10,8},{12,14},{14,12},{16,18},{18,... | collective-permute-start | bytes 589832 | tf_op jit(solution)/shard_map/ppermute | solution.py:523
  9.7 7.8 %collective-permute-start.4 = (bf16[128,768]{1,0:T(8,128)(2,1)S(1)}, bf16[128,768]{1,0:T(8,128)(2,1)S(1)}, u32[]{:S(2)}, u32[]{:S(2)}) collective-permute-start(bf16[128,768]{1,0:T(8,128)(2,1)S(1)} %collective-permute-done.3.refs_3_), channel_id=1, source_target_pairs={{0,2},{2,0},{4,6},{6,4},{8,10},{10,8},{12,14},{14,12},{16,18},{18,... | collective-permute-start | bytes 589832 | tf_op jit(solution)/shard_map/ppermute | solution.py:523
  14.9 8.4 %collective-permute-start.1 = (bf16[128,1280]{1,0:T(8,128)(2,1)S(1)}, bf16[128,1280]{1,0:T(8,128)(2,1)S(1)}, u32[]{:S(2)}, u32[]{:S(2)}) collective-permute-start(bf16[128,1280]{1,0:T(8,128)(2,1)S(1)} %get-tuple-element.58), channel_id=1, source_target_pairs={{0,4},{2,6},{4,0},{6,2},{8,12},{10,14},{12,8},{14,10},{16,20},{18,... | collective-permute-start | bytes 983048 | tf_op jit(solution)/shard_map/ppermute | solution.py:523
  16.5 8.0 %collective-permute-start = (bf16[128,1280]{1,0:T(8,128)(2,1)S(1)}, bf16[128,1280]{1,0:T(8,128)(2,1)S(1)}, u32[]{:S(2)}, u32[]{:S(2)}) collective-permute-start(bf16[128,1280]{1,0:T(8,128)(2,1)S(1)} %get-tuple-element.57.refs_1_.refs_0_), channel_id=1, source_target_pairs={{0,2},{2,0},{4,6},{6,4},{8,10},{10,8},{12,14},{14,12},{16,18},{18,... | collective-permute-start | bytes 983048 | tf_op jit(solution)/shard_map/ppermute | solution.py:523
  17.0 7.5 %collective-permute-start.7 = (bf16[128,768]{1,0:T(8,128)(2,1)S(1)}, bf16[128,768]{1,0:T(8,128)(2,1)S(1)}, u32[]{:S(2)}, u32[]{:S(2)}) collective-permute-start(bf16[128,768]{1,0:T(8,128)(2,1)S(1)} %collective-permute-done.3.refs_3_), channel_id=1, source_target_pairs={{0,1},{1,0},{2,3},{3,2},{4,5},{5,4},{6,7},{7,6},{8,9},{9,8},{10,11... | collective-permute-start | bytes 589832 | tf_op jit(solution)/shard_map/ppermute | solution.py:530
  17.0 7.5 %collective-permute-start.6 = (bf16[128,768]{1,0:T(8,128)(2,1)S(1)}, bf16[128,768]{1,0:T(8,128)(2,1)S(1)}, u32[]{:S(2)}, u32[]{:S(2)}) collective-permute-start(bf16[128,768]{1,0:T(8,128)(2,1)S(1)} %collective-permute-done.2.refs_2_), channel_id=1, source_target_pairs={{0,1},{1,0},{2,3},{3,2},{4,5},{5,4},{6,7},{7,6},{8,9},{9,8},{10,11... | collective-permute-start | bytes 589832 | tf_op jit(solution)/shard_map/ppermute | solution.py:530
  17.5 7.0 %collective-permute-start.8 = (bf16[128,768]{1,0:T(8,128)(2,1)S(1)}, bf16[128,768]{1,0:T(8,128)(2,1)S(1)}, u32[]{:S(2)}, u32[]{:S(2)}) collective-permute-start(bf16[128,768]{1,0:T(8,128)(2,1)S(1)} %collective-permute-done.4.refs_4_), channel_id=1, source_target_pairs={{0,1},{1,0},{2,3},{3,2},{4,5},{5,4},{6,7},{7,6},{8,9},{9,8},{10,11... | collective-permute-start | bytes 589832 | tf_op jit(solution)/shard_map/ppermute | solution.py:530
  25.5 10.0 %collective-permute-start.13 = (bf16[128,1792]{1,0:T(8,128)(2,1)S(1)}, bf16[128,1792]{1,0:T(8,128)(2,1)S(1)}, u32[]{:S(2)}, u32[]{:S(2)}) collective-permute-start(bf16[128,1792]{1,0:T(8,128)(2,1)S(1)} %shard_map.72), channel_id=1, source_target_pairs={{0,4},{2,6},{4,0},{6,2},{8,12},{10,14},{12,8},{14,10},{16,20},{18,... | collective-permute-start | bytes 1376264 | tf_op jit(solution)/shard_map/ppermute | solution.py:523
  26.1 7.1 %collective-permute-start.9 = (bf16[128,1280]{1,0:T(8,128)(2,1)S(1)}, bf16[128,1280]{1,0:T(8,128)(2,1)S(1)}, u32[]{:S(2)}, u32[]{:S(2)}) collective-permute-start(bf16[128,1280]{1,0:T(8,128)(2,1)S(1)} %shard_map.71.refs_3_.refs_2_), channel_id=1, source_target_pairs={{0,2},{2,0},{4,6},{6,4},{8,10},{10,8},{12,14},{14,12},{16,18},{18,... | collective-permute-start | bytes 983048 | tf_op jit(solution)/shard_map/ppermute | solution.py:523
  26.8 6.2 %collective-permute-start.12 = (bf16[256,128]{1,0:T(8,128)(2,1)S(1)}, bf16[256,128]{1,0:T(8,128)(2,1)S(1)}, u32[]{:S(2)}, u32[]{:S(2)}) collective-permute-start(bf16[256,128]{1,0:T(8,128)(2,1)S(1)} %get-tuple-element.64), channel_id=1, source_target_pairs={{0,8},{2,10},{4,12},{6,14},{8,16},{10,18},{12,20},{14,22},{16,24},... | collective-permute-start | bytes 196616 | tf_op jit(solution)/shard_map/ppermute | solution.py:527
  28.4 7.1 %collective-permute-start.10 = (bf16[256,128]{1,0:T(8,128)(2,1)S(1)}, bf16[256,128]{1,0:T(8,128)(2,1)S(1)}, u32[]{:S(2)}, u32[]{:S(2)}) collective-permute-start(bf16[256,128]{1,0:T(8,128)(2,1)S(1)} %get-tuple-element.62), channel_id=1, source_target_pairs={{0,24},{2,26},{4,28},{6,30},{8,0},{10,2},{12,4},{14,6},{16,8},{18,... | collective-permute-start | bytes 196616 | tf_op jit(solution)/shard_map/ppermute | solution.py:527
  36.2 13.0 %collective-permute-start.14 = (bf16[4,128,1280]{2,1,0:T(8,128)(2,1)S(1)}, bf16[4,128,1280]{2,1,0:T(8,128)(2,1)S(1)}, u32[]{:S(2)}, u32[]{:S(2)}) collective-permute-start(bf16[4,128,1280]{2,1,0:T(8,128)(2,1)S(1)} %shard_map.74.refs_1_), channel_id=1, source_target_pairs={{0,1},{1,0},{2,3},{3,2},{4,5},{5,4},{6,7},{7,6},{8,9},{9,8},{10,11... | collective-permute-start | bytes 3932168 | tf_op jit(solution)/shard_map/ppermute | solution.py:530
  36.3 12.9 %collective-permute-start.18 = (bf16[128,1792]{1,0:T(8,128)(2,1)S(1)}, bf16[128,1792]{1,0:T(8,128)(2,1)S(1)}, u32[]{:S(2)}, u32[]{:S(2)}) collective-permute-start(bf16[128,1792]{1,0:T(8,128)(2,1)S(1)} %shard_map.76.refs_1_.refs_0_), channel_id=1, source_target_pairs={{0,2},{2,0},{4,6},{6,4},{8,10},{10,8},{12,14},{14,12},{16,18},{18,... | collective-permute-start | bytes 1376264 | tf_op jit(solution)/shard_map/ppermute | solution.py:523
  37.7 8.4 %collective-permute-start.17 = (bf16[256,128]{1,0:T(8,128)(2,1)S(1)}, bf16[256,128]{1,0:T(8,128)(2,1)S(1)}, u32[]{:S(2)}, u32[]{:S(2)}) collective-permute-start(bf16[256,128]{1,0:T(8,128)(2,1)S(1)} %add_convert_fusion.3.refs_4_.refs_1_.refs_3_), channel_id=1, source_target_pairs={{0,24},{2,26},{4,28},{6,30},{8,0},{10,2},{12,4},{14,6},{16,8},{18,... | collective-permute-start | bytes 196616 | tf_op jit(solution)/shard_map/ppermute | solution.py:527
  39.9 6.9 %collective-permute-start.16 = (bf16[256,128]{1,0:T(8,128)(2,1)S(1)}, bf16[256,128]{1,0:T(8,128)(2,1)S(1)}, u32[]{:S(2)}, u32[]{:S(2)}) collective-permute-start(bf16[256,128]{1,0:T(8,128)(2,1)S(1)} %add_convert_fusion.3.refs_4_.refs_1_.refs_3_), channel_id=1, source_target_pairs={{0,16},{2,18},{4,20},{6,22},{8,24},{10,26},{12,28},{14,30},{16,0},... | collective-permute-start | bytes 196616 | tf_op jit(solution)/shard_map/ppermute | solution.py:527
  39.9 6.9 %collective-permute-start.15 = (bf16[256,128]{1,0:T(8,128)(2,1)S(1)}, bf16[256,128]{1,0:T(8,128)(2,1)S(1)}, u32[]{:S(2)}, u32[]{:S(2)}) collective-permute-start(bf16[256,128]{1,0:T(8,128)(2,1)S(1)} %add_convert_fusion.3.refs_4_.refs_1_.refs_3_), channel_id=1, source_target_pairs={{0,8},{2,10},{4,12},{6,14},{8,16},{10,18},{12,20},{14,22},{16,24},... | collective-permute-start | bytes 196616 | tf_op jit(solution)/shard_map/ppermute | solution.py:527
  56.4 14.0 %collective-permute-start.24 = (bf16[128,2304]{1,0:T(8,128)(2,1)S(1)}, bf16[128,2304]{1,0:T(8,128)(2,1)S(1)}, u32[]{:S(2)}, u32[]{:S(2)}) collective-permute-start(bf16[128,2304]{1,0:T(8,128)(2,1)S(1)} %shard_map.82), channel_id=1, source_target_pairs={{0,4},{2,6},{4,0},{6,2},{8,12},{10,14},{12,8},{14,10},{16,20},{18,... | collective-permute-start | bytes 1769480 | tf_op jit(solution)/shard_map/ppermute | solution.py:523
  57.8 10.9 %collective-permute-start.23 = (bf16[128,1792]{1,0:T(8,128)(2,1)S(1)}, bf16[128,1792]{1,0:T(8,128)(2,1)S(1)}, u32[]{:S(2)}, u32[]{:S(2)}) collective-permute-start(bf16[128,1792]{1,0:T(8,128)(2,1)S(1)} %shard_map.81.refs_3_.refs_2_), channel_id=1, source_target_pairs={{0,2},{2,0},{4,6},{6,4},{8,10},{10,8},{12,14},{14,12},{16,18},{18,... | collective-permute-start | bytes 1376264 | tf_op jit(solution)/shard_map/ppermute | solution.py:523
  59.3 11.2 %collective-permute-start.20 = (bf16[256,128]{1,0:T(8,128)(2,1)S(1)}, bf16[256,128]{1,0:T(8,128)(2,1)S(1)}, u32[]{:S(2)}, u32[]{:S(2)}) collective-permute-start(bf16[256,128]{1,0:T(8,128)(2,1)S(1)} %get-tuple-element.71), channel_id=1, source_target_pairs={{0,24},{2,26},{4,28},{6,30},{8,0},{10,2},{12,4},{14,6},{16,8},{18,... | collective-permute-start | bytes 196616 | tf_op jit(solution)/shard_map/ppermute | solution.py:527
  63.1 7.3 %collective-permute-start.21 = (bf16[256,128]{1,0:T(8,128)(2,1)S(1)}, bf16[256,128]{1,0:T(8,128)(2,1)S(1)}, u32[]{:S(2)}, u32[]{:S(2)}) collective-permute-start(bf16[256,128]{1,0:T(8,128)(2,1)S(1)} %get-tuple-element.72), channel_id=1, source_target_pairs={{0,16},{2,18},{4,20},{6,22},{8,24},{10,26},{12,28},{14,30},{16,0},... | collective-permute-start | bytes 196616 | tf_op jit(solution)/shard_map/ppermute | solution.py:527
  70.6 10.6 %collective-permute-start.26 = (bf16[4,128,1792]{2,1,0:T(8,128)(2,1)S(1)}, bf16[4,128,1792]{2,1,0:T(8,128)(2,1)S(1)}, u32[]{:S(2)}, u32[]{:S(2)}) collective-permute-start(bf16[4,128,1792]{2,1,0:T(8,128)(2,1)S(1)} %shard_map.85.refs_1_), channel_id=1, source_target_pairs={{0,1},{1,0},{2,3},{3,2},{4,5},{5,4},{6,7},{7,6},{8,9},{9,8},{10,11... | collective-permute-start | bytes 5505032 | tf_op jit(solution)/shard_map/ppermute | solution.py:530
  70.7 15.7 %collective-permute-start.25 = (bf16[128,2304]{1,0:T(8,128)(2,1)S(1)}, bf16[128,2304]{1,0:T(8,128)(2,1)S(1)}, u32[]{:S(2)}, u32[]{:S(2)}) collective-permute-start(bf16[128,2304]{1,0:T(8,128)(2,1)S(1)} %shard_map.84.refs_1_.refs_0_), channel_id=1, source_target_pairs={{0,2},{2,0},{4,6},{6,4},{8,10},{10,8},{12,14},{14,12},{16,18},{18,... | collective-permute-start | bytes 1769480 | tf_op jit(solution)/shard_map/ppermute | solution.py:523
  72.1 8.4 %collective-permute-start.29 = (bf16[256,128]{1,0:T(8,128)(2,1)S(1)}, bf16[256,128]{1,0:T(8,128)(2,1)S(1)}, u32[]{:S(2)}, u32[]{:S(2)}) collective-permute-start(bf16[256,128]{1,0:T(8,128)(2,1)S(1)} %add_convert_fusion.2.refs_1_.refs_4_.refs_2_.refs_5_), channel_id=1, source_target_pairs={{0,24},{2,26},{4,28},{6,30},{8,0},{10,2},{12,4},{14,6},{16,8},{18,... | collective-permute-start | bytes 196616 | tf_op jit(solution)/shard_map/ppermute | solution.py:527
  74.3 6.9 %collective-permute-start.28 = (bf16[256,128]{1,0:T(8,128)(2,1)S(1)}, bf16[256,128]{1,0:T(8,128)(2,1)S(1)}, u32[]{:S(2)}, u32[]{:S(2)}) collective-permute-start(bf16[256,128]{1,0:T(8,128)(2,1)S(1)} %add_convert_fusion.2.refs_1_.refs_4_.refs_2_.refs_5_), channel_id=1, source_target_pairs={{0,16},{2,18},{4,20},{6,22},{8,24},{10,26},{12,28},{14,30},{16,0},... | collective-permute-start | bytes 196616 | tf_op jit(solution)/shard_map/ppermute | solution.py:527
  74.4 6.9 %collective-permute-start.27 = (bf16[256,128]{1,0:T(8,128)(2,1)S(1)}, bf16[256,128]{1,0:T(8,128)(2,1)S(1)}, u32[]{:S(2)}, u32[]{:S(2)}) collective-permute-start(bf16[256,128]{1,0:T(8,128)(2,1)S(1)} %add_convert_fusion.2.refs_1_.refs_4_.refs_2_.refs_5_), channel_id=1, source_target_pairs={{0,8},{2,10},{4,12},{6,14},{8,16},{10,18},{12,20},{14,22},{16,24},... | collective-permute-start | bytes 196616 | tf_op jit(solution)/shard_map/ppermute | solution.py:527
  84.1 15.4 %collective-permute-start.30 = (bf16[128,2304]{1,0:T(8,128)(2,1)S(1)}, bf16[128,2304]{1,0:T(8,128)(2,1)S(1)}, u32[]{:S(2)}, u32[]{:S(2)}) collective-permute-start(bf16[128,2304]{1,0:T(8,128)(2,1)S(1)} %shard_map.88.refs_3_.refs_2_), channel_id=1, source_target_pairs={{0,2},{2,0},{4,6},{6,4},{8,10},{10,8},{12,14},{14,12},{16,18},{18,... | collective-permute-start | bytes 1769480 | tf_op jit(solution)/shard_map/ppermute | solution.py:523
  89.6 13.6 %collective-permute-start.37 = (bf16[1024,256]{1,0:T(8,128)(2,1)S(1)}, bf16[1024,256]{1,0:T(8,128)(2,1)S(1)}, u32[]{:S(2)}, u32[]{:S(2)}) collective-permute-start(bf16[1024,256]{1,0:T(8,128)(2,1)S(1)} %shard_map.91.refs_0_), channel_id=1, source_target_pairs={{0,4},{2,6},{4,0},{6,2},{8,12},{10,14},{12,8},{14,10},{16,20},{18,... | collective-permute-start | bytes 1572872 | tf_op jit(solution)/shard_map/ppermute | solution.py:523
  91.0 6.7 %collective-permute-start.36 = (bf16[256,128]{1,0:T(8,128)(2,1)S(1)}, bf16[256,128]{1,0:T(8,128)(2,1)S(1)}, u32[]{:S(2)}, u32[]{:S(2)}) collective-permute-start(bf16[256,128]{1,0:T(8,128)(2,1)S(1)} %get-tuple-element.86), channel_id=1, source_target_pairs={{0,8},{2,10},{4,12},{6,14},{8,16},{10,18},{12,20},{14,22},{16,24},... | collective-permute-start | bytes 196616 | tf_op jit(solution)/shard_map/ppermute | solution.py:527
  92.8 10.3 %collective-permute-start.34 = (bf16[256,128]{1,0:T(8,128)(2,1)S(1)}, bf16[256,128]{1,0:T(8,128)(2,1)S(1)}, u32[]{:S(2)}, u32[]{:S(2)}) collective-permute-start(bf16[256,128]{1,0:T(8,128)(2,1)S(1)} %get-tuple-element.84), channel_id=1, source_target_pairs={{0,24},{2,26},{4,28},{6,30},{8,0},{10,2},{12,4},{14,6},{16,8},{18,... | collective-permute-start | bytes 196616 | tf_op jit(solution)/shard_map/ppermute | solution.py:527
  94.9 8.3 %collective-permute-start.35 = (bf16[256,128]{1,0:T(8,128)(2,1)S(1)}, bf16[256,128]{1,0:T(8,128)(2,1)S(1)}, u32[]{:S(2)}, u32[]{:S(2)}) collective-permute-start(bf16[256,128]{1,0:T(8,128)(2,1)S(1)} %get-tuple-element.85), channel_id=1, source_target_pairs={{0,16},{2,18},{4,20},{6,22},{8,24},{10,26},{12,28},{14,30},{16,0},... | collective-permute-start | bytes 196616 | tf_op jit(solution)/shard_map/ppermute | solution.py:527
  103.3 10.9 %collective-permute-start.38 = (bf16[4,128,2304]{2,1,0:T(8,128)(2,1)S(1)}, bf16[4,128,2304]{2,1,0:T(8,128)(2,1)S(1)}, u32[]{:S(2)}, u32[]{:S(2)}) collective-permute-start(bf16[4,128,2304]{2,1,0:T(8,128)(2,1)S(1)} %shard_map.93.refs_1_), channel_id=1, source_target_pairs={{0,1},{1,0},{2,3},{3,2},{4,5},{5,4},{6,7},{7,6},{8,9},{9,8},{10,11... | collective-permute-start | bytes 7077896 | tf_op jit(solution)/shard_map/ppermute | solution.py:530
  103.4 15.0 %collective-permute-start.43 = (bf16[1024,256]{1,0:T(8,128)(2,1)S(1)}, bf16[1024,256]{1,0:T(8,128)(2,1)S(1)}, u32[]{:S(2)}, u32[]{:S(2)}) collective-permute-start(bf16[1024,256]{1,0:T(8,128)(2,1)S(1)} %shard_map.96.refs_1_), channel_id=1, source_target_pairs={{0,2},{2,0},{4,6},{6,4},{8,10},{10,8},{12,14},{14,12},{16,18},{18,... | collective-permute-start | bytes 1572872 | tf_op jit(solution)/shard_map/ppermute | solution.py:523
  104.9 8.9 %collective-permute-start.41 = (bf16[256,128]{1,0:T(8,128)(2,1)S(1)}, bf16[256,128]{1,0:T(8,128)(2,1)S(1)}, u32[]{:S(2)}, u32[]{:S(2)}) collective-permute-start(bf16[256,128]{1,0:T(8,128)(2,1)S(1)} %add_convert_fusion.1.refs_4_.refs_2_.refs_7_.refs_1_), channel_id=1, source_target_pairs={{0,24},{2,26},{4,28},{6,30},{8,0},{10,2},{12,4},{14,6},{16,8},{18,... | collective-permute-start | bytes 196616 | tf_op jit(solution)/shard_map/ppermute | solution.py:527
  106.7 7.6 %collective-permute-start.40 = (bf16[256,128]{1,0:T(8,128)(2,1)S(1)}, bf16[256,128]{1,0:T(8,128)(2,1)S(1)}, u32[]{:S(2)}, u32[]{:S(2)}) collective-permute-start(bf16[256,128]{1,0:T(8,128)(2,1)S(1)} %add_convert_fusion.1.refs_4_.refs_2_.refs_7_.refs_1_), channel_id=1, source_target_pairs={{0,16},{2,18},{4,20},{6,22},{8,24},{10,26},{12,28},{14,30},{16,0},... | collective-permute-start | bytes 196616 | tf_op jit(solution)/shard_map/ppermute | solution.py:527
  107.8 6.5 %collective-permute-start.39 = (bf16[256,128]{1,0:T(8,128)(2,1)S(1)}, bf16[256,128]{1,0:T(8,128)(2,1)S(1)}, u32[]{:S(2)}, u32[]{:S(2)}) collective-permute-start(bf16[256,128]{1,0:T(8,128)(2,1)S(1)} %add_convert_fusion.1.refs_4_.refs_2_.refs_7_.refs_1_), channel_id=1, source_target_pairs={{0,8},{2,10},{4,12},{6,14},{8,16},{10,18},{12,20},{14,22},{16,24},... | collective-permute-start | bytes 196616 | tf_op jit(solution)/shard_map/ppermute | solution.py:527
  115.8 15.8 %collective-permute-start.48 = (bf16[1024,256]{1,0:T(8,128)(2,1)S(1)}, bf16[1024,256]{1,0:T(8,128)(2,1)S(1)}, u32[]{:S(2)}, u32[]{:S(2)}) collective-permute-start(bf16[1024,256]{1,0:T(8,128)(2,1)S(1)} %shard_map.99.refs_3_), channel_id=1, source_target_pairs={{0,2},{2,0},{4,6},{6,4},{8,10},{10,8},{12,14},{14,12},{16,18},{18,... | collective-permute-start | bytes 1572872 | tf_op jit(solution)/shard_map/ppermute | solution.py:523
  123.4 8.2 %collective-permute-start.49 = (bf16[512,256]{1,0:T(8,128)(2,1)S(1)}, bf16[512,256]{1,0:T(8,128)(2,1)S(1)}, u32[]{:S(2)}, u32[]{:S(2)}) collective-permute-start(bf16[512,256]{1,0:T(8,128)(2,1)S(1)} %shard_map.100.refs_0_), channel_id=1, source_target_pairs={{0,4},{2,6},{4,0},{6,2},{8,12},{10,14},{12,8},{14,10},{16,20},{18,... | collective-permute-start | bytes 786440 | tf_op jit(solution)/shard_map/ppermute | solution.py:523
  124.8 6.7 %collective-permute-start.47 = (bf16[256,128]{1,0:T(8,128)(2,1)S(1)}, bf16[256,128]{1,0:T(8,128)(2,1)S(1)}, u32[]{:S(2)}, u32[]{:S(2)}) collective-permute-start(bf16[256,128]{1,0:T(8,128)(2,1)S(1)} %get-tuple-element.96), channel_id=1, source_target_pairs={{0,8},{2,10},{4,12},{6,14},{8,16},{10,18},{12,20},{14,22},{16,24},... | collective-permute-start | bytes 196616 | tf_op jit(solution)/shard_map/ppermute | solution.py:527
  134.3 8.8 %collective-permute-start.53 = (bf16[512,256]{1,0:T(8,128)(2,1)S(1)}, bf16[512,256]{1,0:T(8,128)(2,1)S(1)}, u32[]{:S(2)}, u32[]{:S(2)}) collective-permute-start(bf16[512,256]{1,0:T(8,128)(2,1)S(1)} %shard_map.102.refs_1_), channel_id=1, source_target_pairs={{0,2},{2,0},{4,6},{6,4},{8,10},{10,8},{12,14},{14,12},{16,18},{18,... | collective-permute-start | bytes 786440 | tf_op jit(solution)/shard_map/ppermute | solution.py:523
  136.8 6.3 %collective-permute-start.51 = (bf16[256,128]{1,0:T(8,128)(2,1)S(1)}, bf16[256,128]{1,0:T(8,128)(2,1)S(1)}, u32[]{:S(2)}, u32[]{:S(2)}) collective-permute-start(bf16[256,128]{1,0:T(8,128)(2,1)S(1)} %add_convert_fusion.refs_1_.refs_5_.refs_6_), channel_id=1, source_target_pairs={{0,16},{2,18},{4,20},{6,22},{8,24},{10,26},{12,28},{14,30},{16,0},... | collective-permute-start | bytes 196616 | tf_op jit(solution)/shard_map/ppermute | solution.py:527
  136.8 6.3 %collective-permute-start.50 = (bf16[256,128]{1,0:T(8,128)(2,1)S(1)}, bf16[256,128]{1,0:T(8,128)(2,1)S(1)}, u32[]{:S(2)}, u32[]{:S(2)}) collective-permute-start(bf16[256,128]{1,0:T(8,128)(2,1)S(1)} %add_convert_fusion.refs_1_.refs_5_.refs_6_), channel_id=1, source_target_pairs={{0,8},{2,10},{4,12},{6,14},{8,16},{10,18},{12,20},{14,22},{16,24},... | collective-permute-start | bytes 196616 | tf_op jit(solution)/shard_map/ppermute | solution.py:527
  143.8 9.2 %collective-permute-start.58 = (bf16[512,256]{1,0:T(8,128)(2,1)S(1)}, bf16[512,256]{1,0:T(8,128)(2,1)S(1)}, u32[]{:S(2)}, u32[]{:S(2)}) collective-permute-start(bf16[512,256]{1,0:T(8,128)(2,1)S(1)} %shard_map.106.refs_3_), channel_id=1, source_target_pairs={{0,2},{2,0},{4,6},{6,4},{8,10},{10,8},{12,14},{14,12},{16,18},{18,... | collective-permute-start | bytes 786440 | tf_op jit(solution)/shard_map/ppermute | solution.py:523
  145.8 9.0 %collective-permute-start.56 = (bf16[512,256]{1,0:T(8,128)(2,1)S(1)}, bf16[512,256]{1,0:T(8,128)(2,1)S(1)}, u32[]{:S(2)}, u32[]{:S(2)}) collective-permute-start(bf16[512,256]{1,0:T(8,128)(2,1)S(1)} %shard_map.105.refs_1_), channel_id=1, source_target_pairs={{0,4},{2,6},{4,0},{6,2},{8,12},{10,14},{12,8},{14,10},{16,20},{18,... | collective-permute-start | bytes 786440 | tf_op jit(solution)/shard_map/ppermute | solution.py:523
  147.3 11.3 %collective-permute-start.55 = (bf16[512,256]{1,0:T(8,128)(2,1)S(1)}, bf16[512,256]{1,0:T(8,128)(2,1)S(1)}, u32[]{:S(2)}, u32[]{:S(2)}) collective-permute-start(bf16[512,256]{1,0:T(8,128)(2,1)S(1)} %shard_map.105.refs_1_), channel_id=1, source_target_pairs={{0,2},{2,0},{4,6},{6,4},{8,10},{10,8},{12,14},{14,12},{16,18},{18,... | collective-permute-start | bytes 786440 | tf_op jit(solution)/shard_map/ppermute | solution.py:523
  154.9 11.4 %collective-permute-start.57 = (bf16[512,256]{1,0:T(8,128)(2,1)S(1)}, bf16[512,256]{1,0:T(8,128)(2,1)S(1)}, u32[]{:S(2)}, u32[]{:S(2)}) collective-permute-start(bf16[512,256]{1,0:T(8,128)(2,1)S(1)} %collective-permute-done.56.refs_3_), channel_id=1, source_target_pairs={{0,2},{2,0},{4,6},{6,4},{8,10},{10,8},{12,14},{14,12},{16,18},{18,... | collective-permute-start | bytes 786440 | tf_op jit(solution)/shard_map/ppermute | solution.py:523
  166.2 6.7 %collective-permute-start.59 = (bf16[256,1536]{1,0:T(8,128)(2,1)S(1)}, bf16[256,1536]{1,0:T(8,128)(2,1)S(1)}, u32[]{:S(2)}, u32[]{:S(2)}) collective-permute-start(bf16[256,1536]{1,0:T(8,128)(2,1)S(1)} %get-tuple-element.106), channel_id=1, source_target_pairs={{0,1},{1,0},{2,3},{3,2},{4,5},{5,4},{6,7},{7,6},{8,9},{9,8},{10,11... | collective-permute-start | bytes 2359304 | tf_op jit(solution)/shard_map/ppermute | solution.py:530
  (14 other events, 63.2 us)

commit v3 on v2

--- a/solution.py
+++ b/solution.py
@@ -161,50 +161,83 @@
     return jax.ShapeDtypeStruct(dims, kind)
 
 
-def prep_body(ss, form, meta, *refs):
-    py, width, eqs = form.py, form.width, form.eqs
-    refs = list(refs)
-    diag, rhs = refs.pop(0), refs.pop(0)
-    lower = refs.pop(0) if ss[-1] else None
-    flat = refs.pop() if ss[-1] else None
+def put_diag(form, meta, dy, block, out):
+    at = lax.rem(meta[0] + dy, form.py) * form.width
+    for h in range(form.width // form.eqs):
+        lanes = slice(h * form.eqs, (h + 1) * form.eqs)
+        out[:, lanes] = block[pl.ds(pl.multiple_of(at + h * form.eqs, form.eqs), form.eqs), :]
+
+
+def start_body(form, meta, diag, rhs, *refs):
+    py, px, width, sides = form.py, form.px, form.width, form.sides
+    own, outs, far = refs[-1], refs[:py], refs[py:-1]
+
+    def part(s, dx):
+        return rhs[s, :, pl.ds(pl.multiple_of(lax.rem(meta[1] + dx, px) * sides, sides), sides)]
+
+    for dy in range(py):
+        put_diag(form, meta, dy, diag.at[0], outs[dy])
+        outs[dy][:, width:] = rhs[0]
+    for dx in range(1, px):
+        out = far[dx - 1]
+        put_diag(form, meta, 0, diag.at[0], out)
+        out[:, width : width + px * sides] = rhs[0]
+        for s in range(1, rhs.shape[0]):
+            out[:, width + (px + s - 1) * sides : width + (px + s) * sides] = part(s, dx)
+    for s in range(rhs.shape[0]):
+        own[s] = part(s, 0)
+
+
+def start(form, meta, diag_inverse, rhs_pivot):
+    width, eqs, sides, share = form.width, form.eqs, form.sides, form.py * form.width
+    steps = rhs_pivot.shape[0]
+    dims = [(eqs, width + form.px * sides)] * form.py
+    dims += [(eqs, width + (form.px + steps - 1) * sides)] * (form.px - 1) + [(steps, eqs, sides)]
+    outs = call(
+        functools.partial(start_body, form),
+        [shaped(d, BF16) for d in dims],
+        [meta, diag_inverse, rhs_pivot],
+        [
+            SMALL,
+            pl.BlockSpec((1, share, eqs), lambda i: (0, 0, 0)),
+            pl.BlockSpec(rhs_pivot.shape, lambda i: (0, 0, 0)),
+        ],
+        weight=WEIGHT,
+        grid=(1,),
+        out_specs=tuple(pl.BlockSpec(d, lambda i, n=len(d): (0,) * n) for d in dims),
+    )
+    return outs[: form.py], outs[form.py : -1], outs[-1]
+
+
+def prep_body(ss, form, meta, diag, lower, *refs):
+    py, width = form.py, form.width
+    flat = refs[-1]
     for i, s in enumerate(ss):
         outs = refs[i * py : (i + 1) * py]
-        if s:
-            flat[...] = jnp.swapaxes(lower[i], 0, 1)
+        flat[...] = jnp.swapaxes(lower[i], 0, 1)
         for dy in range(py):
+            put_diag(form, meta, dy, diag.at[i], outs[dy])
             at = lax.rem(meta[0] + dy, py) * width
-            for h in range(width // eqs):
-                outs[dy][:, h * eqs : (h + 1) * eqs] = diag[i, pl.ds(pl.multiple_of(at + h * eqs, eqs), eqs), :]
             for t in range(s):
                 outs[dy][:, (1 + t) * width : (2 + t) * width] = flat[t, :, pl.ds(pl.multiple_of(at, width), width)]
-            outs[dy][:, (1 + s) * width :] = rhs[i]
-
-
-def prep(ss, form, meta, diag_inverse, rhs_pivot, lower_pivot, after=()):
-    width, eqs, share, sides = form.width, form.eqs, form.py * form.width, form.px * form.sides
+
+
+def prep(ss, form, meta, diag_inverse, lower_pivot, after=()):
+    width, eqs, share = form.width, form.eqs, form.py * form.width
     steps, count = lower_pivot.shape[0], len(ss)
-    ins = [meta, diag_inverse, rhs_pivot]
-    specs = [
-        SMALL,
-        pl.BlockSpec((pl.Element(count), pl.Element(share), pl.Element(eqs)), lambda i: (ss[0], 0, 0)),
-        pl.BlockSpec((pl.Element(count), pl.Element(eqs), pl.Element(sides)), lambda i: (ss[0], 0, 0)),
-    ]
-    scratch = []
-    if ss[-1]:
-        ins.append(lower_pivot)
-        specs.append(
-            pl.BlockSpec(
-                (pl.Element(count), pl.Element(eqs), pl.Element(steps), pl.Element(share)), lambda i: (ss[0], 0, 0, 0)
-            )
-        )
-        scratch.append(pltpu.VMEM((steps, eqs, share), BF16))
-    dims = [(eqs, (s + 1) * width + sides) for s in ss for _ in range(form.py)]
+    dims = [(eqs, (s + 1) * width) for s in ss for _ in range(form.py)]
     outs = call(
         functools.partial(prep_body, ss, form),
         [shaped(d, BF16) for d in dims],
-        ins,
-        specs,
-        scratch=scratch,
+        [meta, diag_inverse, lower_pivot],
+        [
+            SMALL,
+            pl.BlockSpec((pl.Element(count), pl.Element(share), pl.Element(eqs)), lambda i: (ss[0], 0, 0)),
+            pl.BlockSpec(
+                (pl.Element(count), pl.Element(eqs), pl.Element(steps), pl.Element(share)), lambda i: (ss[0], 0, 0, 0)
+            ),
+        ],
+        scratch=[pltpu.VMEM((steps, eqs, share), BF16)],
         after=after,
         weight=WEIGHT,
         grid=(1,),
@@ -213,15 +246,16 @@
     return {s: outs[i * form.py : (i + 1) * form.py] for i, s in enumerate(ss)}
 
 
-def pack_body(chips, *refs):
-    for k in range(chips):
-        refs[-1][k] = refs[k][...]
+def pack_body(count, *refs):
+    for k, part in enumerate(take(list(refs), count)):
+        refs[-1][k] = part[...]
 
 
 def pack(parts, after=()):
-    return call(
-        functools.partial(pack_body, len(parts)),
-        [shaped((len(parts), *parts[0].shape), BF16)],
+    count = sum(1 if x.ndim == 2 else x.shape[0] for x in parts)
+    return call(
+        functools.partial(pack_body, count),
+        [shaped((count, *parts[0].shape[-2:]), BF16)],
         parts,
         [WHOLE] * len(parts),
         after=after,
@@ -229,29 +263,29 @@
     )[0]
 
 
-def take_held(form, refs):
-    held = []
-    while len(held) < form.n_cols * form.chips:
+def take(refs, count):
+    got = []
+    while len(got) < count:
         ref = refs.pop(0)
-        held += [ref] if len(ref.shape) == 2 else [ref.at[k] for k in range(form.chips)]
-    return held
+        got += [ref] if len(ref.shape) == 2 else [ref.at[k] for k in range(ref.shape[0])]
+    return got
 
 
 def diag_body(form, terms, meta, *refs):
     chips, n_cols, depth, eqs, width, sides = form.chips, form.n_cols, form.depth, form.eqs, form.width, form.sides
     refs = list(refs)
-    held = take_held(form, refs)
+    held = take(refs, n_cols * chips)
     sums = [refs.pop(0) for _ in range(terms)]
     outs, product = refs[:-1], refs[-1]
     sub = width // depth
-    right = held[0].shape[-1] - form.px * sides
-    right = pl.ds(pl.multiple_of(right + meta[1] * sides, sides), sides)
-    residual = jnp.concatenate([held[k][:, right] for k in range(chips)], axis=0)
     if terms:
-        total = residual.astype(F32)
-        for x in sums:
-            total = total - x[...].astype(F32)
-        residual = total.astype(BF16)
+        total = sums[0][...]
+        for x in sums[1:]:
+            total = total + x[...].astype(F32)
+        residual = (-total).astype(BF16)
+    else:
+        right = pl.ds(pl.multiple_of(width + meta[1] * sides, sides), sides)
+        residual = jnp.concatenate([held[k][:, right] for k in range(chips)], axis=0)
     for c in range(n_cols):
         for h in range(width // eqs):
             rows = jnp.concatenate(
@@ -289,10 +323,12 @@
 def lower_body(s, form, meta, *refs):
     chips, n_cols, eqs = form.chips, form.n_cols, form.eqs
     refs = list(refs)
-    held = take_held(form, refs)
+    held = take(refs, n_cols * chips)
     width = form.width
     known = [[refs.pop(0) for _ in range(n_cols)] for _ in range(s - 1)]
     pieces = [refs.pop(0) for _ in range(form.depth)]
+    own = refs.pop(0)
+    far = [refs.pop(0) for _ in range(form.px - 1)]
     outs, newest = refs[: form.py], refs[form.py :]
     put_pieces(form, meta, pieces, newest)
     total = None
@@ -302,16 +338,22 @@
             rows = jnp.concatenate([held[c * chips + k][:, lanes] for k in range(chips)], axis=0)
             term = jnp.dot(rows, blocks[c][...], preferred_element_type=F32)
             total = term if total is None else total + term
+    parts = [total[k * eqs : (k + 1) * eqs] for k in range(chips)]
+    lane = width + (form.px + s - 1) * form.sides
+    for k, (dy, dx) in enumerate(form.shifts):
+        if dy == 0:
+            right = far[dx - 1][:, lane : lane + form.sides] if dx else own[s]
+            parts[k] = parts[k] - right.astype(F32)
     for e in range(form.py):
         for k, (dy, dx) in enumerate(form.shifts):
             mine = form.shifts.index(((dy - e) % form.py, dx))
-            outs[e][k * eqs : (k + 1) * eqs] = total[mine * eqs : (mine + 1) * eqs].astype(outs[e].dtype)
-
-
-def lower_product(s, form, meta, held, known, pieces, after=()):
+            outs[e][k * eqs : (k + 1) * eqs] = parts[mine].astype(outs[e].dtype)
+
+
+def lower_product(s, form, meta, held, known, pieces, own, far, after=()):
     rows, sides = form.chips * form.eqs, form.sides
     flat = [x for blocks in known for x in blocks]
-    ins = [meta, *held, *flat, *pieces]
+    ins = [meta, *held, *flat, *pieces, own, *far]
     return call(
         functools.partial(lower_body, s, form),
         [shaped((rows, sides), F32)]
@@ -403,8 +445,11 @@
 
 
 def write_body(form, count, meta, *refs):
-    parts = refs[: form.chips]
-    out, turned = refs[-2:]
+    parts = take(list(refs), form.chips)
+    put_solved(form, count, meta, parts, *refs[-2:])
+
+
+def put_solved(form, count, meta, parts, out, turned):
     width, sides = form.width, form.sides
     for i in range(count):
         for k, (dy, dx) in enumerate(form.shifts):
@@ -420,9 +465,9 @@
 
 def write(s, steps, form, meta, parts, buffer, after=()):
     share, total = form.py * form.width, form.px * form.n_cols * form.sides
-    count = parts[0].shape[0] // form.width
+    count = parts[0].shape[-2] // form.width
     ins = [meta, *parts]
-    specs = [SMALL] + [pl.BlockSpec(x.shape, lambda i: (0, 0)) for x in parts]
+    specs = [SMALL] + [pl.BlockSpec(x.shape, lambda i, n=x.ndim: (0,) * n) for x in parts]
     alias = {}
     if buffer is not None:
         alias = {len(ins): 0}
@@ -443,8 +488,9 @@
     )
 
 
-def rest_body(form, orders, counts, meta, *refs):
-    turned, lower, outs = refs[: len(counts)], refs[len(counts)], refs[len(counts) + 1 :]
+def rest_body(form, orders, counts, running, meta, *refs):
+    turned, lower, refs = refs[: len(counts)], refs[len(counts)], refs[len(counts) + 1 :]
+    before, outs = refs[:running], refs[running:]
     sides = form.px * form.sides
     for order, out in zip(orders, outs):
         at = pl.multiple_of(lax.rem(meta[3] + order, form.n_cols) * sides, sides)
@@ -454,26 +500,69 @@
                 term = nt_dot(x[i, pl.ds(at, sides), :], lower[t])
                 total = term if total is None else total + term
                 t += 1
+        if running:
+            total = total + before[order][...].astype(F32)
         out[...] = total.astype(out.dtype)
 
 
-def rest_product(first, form, orders, meta, turned, lower, after=()):
+def rest_product(first, form, meta, turned, lower, before=(), after=()):
+    orders = range(form.n_cols)
     _, rest, share = lower.shape
     counts = [x.shape[0] for x in turned]
     count = sum(counts)
     sides = form.px * form.sides
     block = max(n for n in (512, 384, 256, 128) if rest % n == 0)
-    return call(
-        functools.partial(rest_body, form, orders, counts),
+    side_block = pl.BlockSpec((sides, block), lambda i: (0, i))
+    return call(
+        functools.partial(rest_body, form, orders, counts, len(before)),
         [shaped((sides, rest), F32 if order == 0 else BF16) for order in orders],
-        [meta, *turned, pltpu.with_memory_space_constraint(lower, pltpu.HBM)],
+        [meta, *turned, pltpu.with_memory_space_constraint(lower, pltpu.HBM), *before],
         [SMALL]
         + [pl.BlockSpec(x.shape, lambda i: (0, 0, 0)) for x in turned]
-        + [pl.BlockSpec((count, block, share), lambda i: (first // count, i, 0))],
+        + [pl.BlockSpec((count, block, share), lambda i: (first // count, i, 0))]
+        + [side_block] * len(before),
         flops=2 * count * share * sides * rest * len(orders),
         after=after,
         grid=(rest // block,),
-        out_specs=tuple(pl.BlockSpec((sides, block), lambda i: (0, i)) for _ in orders),
+        out_specs=(side_block,) * len(orders),
+    )
+
+
+def last_body(form, meta, *refs):
+    refs = list(refs)
+    parts = take(refs, form.chips)
+    lower, _, out, *sums, turned = refs
+
+    @pl.when(pl.program_id(0) == 0)
+    def _():
+        put_solved(form, 1, meta, parts, out, turned)
+
+    sides = form.px * form.sides
+    for order, to in enumerate(sums):
+        at = pl.multiple_of(lax.rem(meta[3] + order, form.n_cols) * sides, sides)
+        to[...] = nt_dot(turned[0, pl.ds(at, sides), :], lower[0]).astype(to.dtype)
+
+
+def last_step(form, meta, parts, lower, buffer):
+    steps, rest, share = lower.shape
+    total, sides = form.px * form.n_cols * form.sides, form.px * form.sides
+    block = max(n for n in (512, 384, 256, 128) if rest % n == 0)
+    lower = pltpu.with_memory_space_constraint(lower, pltpu.HBM)
+    side_block = pl.BlockSpec((sides, block), lambda i: (0, i))
+    return call(
+        functools.partial(last_body, form),
+        [pltpu.HBM((steps, share, total), BF16)]
+        + [shaped((sides, rest), F32 if order == 0 else BF16) for order in range(form.n_cols)],
+        [meta, *parts, lower, buffer],
+        [SMALL]
+        + [pl.BlockSpec(x.shape, lambda i, n=x.ndim: (0,) * n) for x in parts]
+        + [pl.BlockSpec((1, block, share), lambda i: (steps - 1, i, 0))]
+        + [pl.BlockSpec(memory_space=pltpu.HBM)],
+        flops=2 * share * total * rest,
+        scratch=[pltpu.VMEM((1, total, share), BF16)],
+        grid=(rest // block,),
+        out_specs=(pl.BlockSpec((1, share, total), lambda i: (steps - 1, 0, 0)), *[side_block] * form.n_cols),
+        input_output_aliases={len(parts) + 2: 0},
     )
 
 
@@ -488,7 +577,7 @@
     sides: int
 
     def __post_init__(self):
-        self.shifts = [(dy, dx) for dy in range(self.py) for dx in range(self.px)]
+        self.shifts = [(dy, dx) for dx in range(self.px) for dy in range(self.py)]
         self.chips = len(self.shifts)
 
 
@@ -529,23 +618,23 @@
     def along_cols(x, k):
         return lax.ppermute(x, "cols", [(i, (i + k) % n_cols) for i in range(n_cols)])
 
-    def out(blocks):
-        first = [blocks[0]] + [along_plane(blocks[dy], dy, 0) for dy in range(1, py)]
-        return first, [along_plane(blocks[0], 0, dx) for dx in range(1, px)]
-
-    def onward(state, after=()):
-        first, got = state
-        got = [first[0], *got]
-        for x in first[1:]:
-            x = gate(x, after) if after else x
-            got += [x] + [along_plane(x, 0, dx) for dx in range(1, px)]
+    def up(blocks):
+        return [blocks[0]] + [along_plane(blocks[dy], dy, 0) for dy in range(1, py)]
+
+    def across(x):
+        return [along_plane(x, 0, dx) for dx in range(1, px)]
+
+    def onward(first, direct, after=()):
+        rest = [gate(x, after) if after else x for x in first[1:]]
+        far = [across(x) for x in rest]
+        got = [first[0], *rest]
+        for dx in range(px - 1):
+            got += [direct[dx]] + [x[dx] for x in far]
         return got
 
     def held_of(parts, after):
-        if not after:
-            return parts + [along_cols(x, c) for c in range(1, n_cols) for x in parts]
-        mine = pack(parts, after)
-        return [mine] + [along_cols(mine, c) for c in range(1, n_cols)]
+        mine = [pack(parts, after)] if after else parts
+        return mine + [along_cols(x, c) for c in range(1, n_cols) for x in mine]
 
     def joined(ts, after=()):
         parts = []
@@ -558,45 +647,33 @@
     while rest % (turns * block):
         turns -= 1
     last = steps - 1
-    inputs = (diag_inverse, rhs_pivot, lower_pivot)
-    first = out(prep((0,), form, meta, *inputs)[0])
-    packed = prep(tuple(range(1, steps)), form, meta, *inputs)
-    held = held_of(onward(first), ())
-    moving, moved, leaving = {}, {}, {}
+    near, far, own = start(form, meta, diag_inverse, rhs_pivot)
+    got = up(near)
+    here = [along_plane(x, 0, dx + 1) for dx, x in enumerate(far)]
+    held = held_of(onward(got, here), ())
+    packed = prep(tuple(range(1, steps)), form, meta, diag_inverse, lower_pivot)
+    first = up([gate(x, here + got[1:]) for x in packed[1]])
+    moved = pack(first)
+    moved = [moved, *across(moved)]
     known, sums, turned, flat, buffer = [], [], [], None, None
     by_lower, by_diag, by_sum = ({s: [] for s in range(steps + 1)} for _ in range(3))
-    if last:
-        moving[1] = out(packed[1])
-        by_diag[0] += [packed[last][0], *moving[1][0][1:], *moving[1][1]]
+    by_diag[0] += [packed[last][0], *first[1:]]
     for s in range(steps):
         if s > 0:
-            outs = lower_product(s, form, meta, held, known, pieces, by_lower[s])
+            outs = lower_product(s, form, meta, held, known, pieces, own, here, by_lower[s])
             known.append(outs[py:])
             sums = [outs[0]] + [along_plane(outs[e], e, 0) for e in range(1, py)]
-            if s < last:
-                moved[s + 1] = onward(moving[s + 1], [outs[0]])
-                by_sum[s] += moved[s + 1]
-            else:
-                ready = onward(leaving[0], [outs[0]])
-                by_sum[s] += ready
-            if s == last - 1:
-                whole = joined(range(s), [outs[0]])
+            if s > 0:
+                moved = onward(first, direct, [outs[0]])
+            if s >= last - 1:
+                whole = joined(range(s) if s < last else [s - 1], [outs[0]])
                 by_diag[s].append(whole)
-            if s == last:
-                newest = joined([s - 1], [outs[0]])
-                by_diag[s].append(newest)
         products = diag_product(form, meta, held, sums, by_diag[s])
-        if s == 0 and last:
-            moved[1] = onward(moving[1], [products[0]])
-            by_sum[0] += moved[1]
         if s < last - 1:
-            first = [gate(x, [products[0]]) for x in packed[s + 2]]
-        elif s == last - 1:
-            first = [gate(whole, [products[0]])] * py
+            first = up([gate(x, [products[0]]) for x in packed[s + 2]])
         else:
-            first = [gate(newest, [products[0]])] * py
-        first = [first[0]] + [along_plane(first[dy], dy, 0) for dy in range(1, py)]
-        by_sum[s] += first[1:]
+            first = up([gate(whole, [products[0]])] * py)
+        by_sum[s] += moved + first[1:]
         arrivals = [along_depth(products[k], -k) for k in range(1, depth)]
         arrivals[-1] = gate(arrivals[-1], by_sum[s])
         total = products[0]
@@ -604,37 +681,33 @@
             total = total + x.astype(F32)
         mine = total.astype(BF16)
         if s < last:
-            held = held_of(moved[s + 1], [mine])
-        send = gate(first[0], [mine])
-        direct = [along_plane(send, 0, dx) for dx in range(1, px)]
-        (by_diag if 0 < s < last else by_lower)[s + 1] += direct
-        if s < last - 1:
-            moving[s + 2] = ([send, *first[1:]], direct)
+            held = held_of(moved, [mine])
+            first = [gate(first[0], [mine]), *first[1:]]
+            direct = across(first[0])
+            by_diag[s + 1] += direct
         else:
-            leaving[s - last + 1] = ([send, *first[1:]], direct)
+            newest = pack(first, [mine])
+            newest = [newest, *across(newest)]
         pieces = [mine] + [along_depth(mine, k) for k in range(1, depth)]
         if s < turns:
             flat, mark = flat_rest(lower_rest, flat, s, turns, block, [mine])
             by_lower[s + 1].append(mark)
         if s == last:
-            buffer, new = write(0, steps, form, meta, ready, buffer, [mine])
+            buffer, new = write(0, steps, form, meta, moved, buffer, [mine])
             turned.append(new)
             by_lower[s + 1].append(new)
-    newest = onward(leaving[1], [mine])
     known.append(place(form, meta, pieces, by_lower[steps]))
-    final, direct = out([joined([last])] * py)
-    gathered = onward((final, direct))
-    buffer, new = write(last - 1, steps, form, meta, newest, buffer, [mine])
-    turned.append(new)
-    early = rest_product(0, form, range(n_cols), meta, turned, flat, direct)
-    base = rhs_rest.astype(F32) - early[0]
+    whole = joined([last])
+    got = up([whole] * py)
+    direct = across(got[0])
+    early = rest_product(0, form, meta, turned, flat, (), [whole, *newest])
+    got = onward(got, direct, [early[0]])
+    buffer, new = write(last - 1, steps, form, meta, newest, buffer, [early[0]])
+    early = rest_product(last - 1, form, meta, [new], flat, early)
+    buffer, *late = last_step(form, meta, got, flat, buffer)
+    total = rhs_rest.astype(F32) - early[0] - late[0]
     for c in range(1, n_cols):
-        base = base - along_cols(early[c], c).astype(F32)
-    buffer, new = write(last, steps, form, meta, gathered, buffer)
-    late = rest_product(last, form, range(n_cols), meta, [new], flat)
-    total = base - late[0]
-    for c in range(1, n_cols):
-        total = total - along_cols(late[c], c).astype(F32)
+        total = total - along_cols(early[c], c).astype(F32) - along_cols(late[c], c).astype(F32)
     return buffer, total.astype(BF16)
 
 

time: 177 us -> 167 us (0.944)
  waiting for transfers between devices: 63.7 us -> 55.8 us
  starting transfers between devices: 61 us -> 57.1 us
  Pallas kernels: 48.8 us -> 50.6 us
    ppermute x24 -> x22, waiting for transfers between devices: 43.6 us -> 32.8 us  [along_plane(): return lax.ppermute(x, 'rows', pairs)]
    ppermute x24 -> x22, starting transfers between devices: 30.8 us -> 27.1 us  [along_plane(): return lax.ppermute(x, 'rows', pairs)]
    ppermute x13, waiting for transfers between devices: 1.94 us -> 3.91 us  [along_cols(): lax.ppermute(x, 'cols', [(i, (i + k) % n_cols) for i in range(n_cols)])]
    pallas_call x43 -> x45, Pallas kernels: 48.8 us -> 50.6 us  [call(): pl.pallas_call(run, out_shape=tuple(outs), in_specs=list(specs) + [pl.Blo...]
  transfers between devices with their start and end apart: 61 -> 59, of which waited for: 27 -> 26; matrix products, arithmetic and copies ran while one was open for 0% -> 0% of each run, Pallas kernels for 25% -> 29%
where the time goes in v3:
time: 167 us; the launch traced here: 166 us
  starting transfers between devices  57.1 us (34%)
  waiting for transfers between devices  55.8 us (33%)
  Pallas kernels  50.6 us (30%)
    pallas_call x45, Pallas kernels, call(): pl.pallas_call(run, out_shape=tuple(outs), in_specs=list(specs) + [pl.Blo...  50.6 us
    ppermute x22, waiting for transfers between devices, along_plane(): return lax.ppermute(x, 'rows', pairs)  32.8 us
    ppermute x24, starting transfers between devices, along_depth(): return lax.ppermute(x, 'rows', pairs)  28.1 us
    ppermute x22, starting transfers between devices, along_plane(): return lax.ppermute(x, 'rows', pairs)  27.1 us
    ppermute x24, waiting for transfers between devices, along_depth(): return lax.ppermute(x, 'rows', pairs)  19.1 us
    ppermute x13, waiting for transfers between devices, along_cols(): lax.ppermute(x, 'cols', [(i, (i + k) % n_cols) for i in range(n_cols)])  3.91 us
  transfers between devices with their start and end apart: 59, of which 26 were waited for; matrix products, arithmetic and copies ran while one was open for 0% of the time, Pallas kernels for 29%

profile of v3, /device:TPU:0, one launch (start us, length us, event | category | flops | bytes accessed | tf_op | source)
XLA Modules:
  0.0 166.1 jit_solution(7227251195781456498)
XLA Ops:
  1.9 3.0 %collective-permute-start = (bf16[128,1152]{1,0:T(8,128)(2,1)S(1)}, bf16[128,1152]{1,0:T(8,128)(2,1)S(1)}, u32[]{:S(2)}, u32[]{:S(2)}) collective-permute-start(bf16[128,1152]{1,0:T(8,128)(2,1)S(1)} %get-tuple-element.61), channel_id=1, source_target_pairs={{0,2},{2,0},{4,6},{6,4},{8,10},{10,8},{12,14},{14,12},{16,18},{18,... | collective-permute-start | bytes 884744 | tf_op jit(solution)/shard_map/ppermute | solution.py:612
  4.9 1.5 collective-permute-start.1
  6.4 4.8 %collective-permute-done.1.refs_2_ = bf16[128,768]{1,0:T(8,128)(2,1)S(1)} collective-permute-done((bf16[128,768]{1,0:T(8,128)(2,1)S(1)}, bf16[128,768]{1,0:T(8,128)(2,1)S(1)}, u32[]{:S(2)}, u32[]{:S(2)}) %collective-permute-start.1) | collective-permute-done | bytes 196640 | tf_op jit(solution)/shard_map/ppermute | solution.py:612
  11.6 3.4 %shard_map.68 = (bf16[128,1024]{1,0:T(8,128)(2,1)S(1)}, bf16[128,1024]{1,0:T(8,128)(2,1)S(1)}, bf16[128,1536]{1,0:T(8,128)(2,1)S(1)}, bf16[128,1536]{1,0:T(8,128...) custom-call(s32[4]{0:T(128)S(1)} %pad_add_fusion.refs_0_, bf16[4,1024,128]{2,1,0:T(8,128)(2,1)} %refs_1_.3, ...), custom_call_target="tpu_custom_call" | custom-call | bytes 60817536 | tf_op jit(solution)/shard_map/pallas_call | solution.py:149
  15.0 1.8 %collective-permute-start.2 = (bf16[128,1024]{1,0:T(8,128)(2,1)S(1)}, bf16[128,1024]{1,0:T(8,128)(2,1)S(1)}, u32[]{:S(2)}, u32[]{:S(2)}) collective-permute-start(bf16[128,1024]{1,0:T(8,128)(2,1)S(1)} %shard_map.71), channel_id=1, source_target_pairs={{0,4},{2,6},{4,0},{6,2},{8,12},{10,14},{12,8},{14,10},{16,20},{18,... | collective-permute-start | bytes 786440 | tf_op jit(solution)/shard_map/ppermute | solution.py:612
  17.8 4.2 %collective-permute-done.2.refs_1_.refs_10_ = bf16[128,1024]{1,0:T(8,128)(2,1)S(1)} collective-permute-done((bf16[128,1024]{1,0:T(8,128)(2,1)S(1)}, bf16[128,1024]{1,0:T(8,128)(2,1)S(1)}, u32[]{:S(2)}, u32[]{:S(2)}) %collective-permute-start.2) | collective-permute-done | bytes 262176 | tf_op jit(solution)/shard_map/ppermute | solution.py:612
  22.0 1.4 collective-permute-start.3
  24.5 1.6 collective-permute-start.12
  26.1 1.6 collective-permute-start.11
  27.7 2.2 %collective-permute-start.9 = (bf16[256,128]{1,0:T(8,128)(2,1)S(1)}, bf16[256,128]{1,0:T(8,128)(2,1)S(1)}, u32[]{:S(2)}, u32[]{:S(2)}) collective-permute-start(bf16[256,128]{1,0:T(8,128)(2,1)S(1)} %get-tuple-element.66), channel_id=1, source_target_pairs={{0,24},{2,26},{4,28},{6,30},{8,0},{10,2},{12,4},{14,6},{16,8},{18,... | collective-permute-start | bytes 196616 | tf_op jit(solution)/shard_map/ppermute | solution.py:616
  30.7 1.6 collective-permute-done.11.refs_0_
  33.7 1.7 collective-permute-done.10
  36.2 2.4 %collective-permute-start.16 = (bf16[256,128]{1,0:T(8,128)(2,1)S(1)}, bf16[256,128]{1,0:T(8,128)(2,1)S(1)}, u32[]{:S(2)}, u32[]{:S(2)}) collective-permute-start(bf16[256,128]{1,0:T(8,128)(2,1)S(1)} %add_convert_fusion.3.refs_2_.refs_1_.refs_3_), channel_id=1, source_target_pairs={{0,24},{2,26},{4,28},{6,30},{8,0},{10,2},{12,4},{14,6},{16,8},{18,... | collective-permute-start | bytes 196616 | tf_op jit(solution)/shard_map/ppermute | solution.py:616
  39.6 5.1 %shard_map.77 = (bf16[4,1536,1024]{2,1,0:T(8,128)(2,1)}, f32[8,128]{1,0:T(8,128)S(1)}) custom-call(bf16[1536,4,1024]{2,1,0:T(4,128)(2,1)} %refs_0_.5, bf16[256,128]{1,0:T(8,128)(2,1)S(1)} %add_convert_fusion.3.refs_2_.refs_1_.refs_3_), custom_call_target="tpu_custom_call" | custom-call | bytes 25169920 | tf_op jit(solution)/shard_map/pallas_call | solution.py:149
  46.6 1.5 collective-permute-start.17
  48.0 3.9 %collective-permute-done.17.refs_4_ = bf16[512,128]{1,0:T(8,128)(2,1)S(1)} collective-permute-done((bf16[512,128]{1,0:T(8,128)(2,1)S(1)}, bf16[512,128]{1,0:T(8,128)(2,1)S(1)}, u32[]{:S(2)}, u32[]{:S(2)}) %collective-permute-start.17) | collective-permute-done | bytes 131104 | tf_op jit(solution)/shard_map/ppermute | solution.py:612
  56.5 2.5 %collective-permute-start.19 = (bf16[256,128]{1,0:T(8,128)(2,1)S(1)}, bf16[256,128]{1,0:T(8,128)(2,1)S(1)}, u32[]{:S(2)}, u32[]{:S(2)}) collective-permute-start(bf16[256,128]{1,0:T(8,128)(2,1)S(1)} %get-tuple-element.76), channel_id=1, source_target_pairs={{0,24},{2,26},{4,28},{6,30},{8,0},{10,2},{12,4},{14,6},{16,8},{18,... | collective-permute-start | bytes 196616 | tf_op jit(solution)/shard_map/ppermute | solution.py:616
  59.0 2.3 %collective-permute-done.21.refs_0_ = bf16[256,128]{1,0:T(8,128)(2,1)S(1)} collective-permute-done((bf16[256,128]{1,0:T(8,128)(2,1)S(1)}, bf16[256,128]{1,0:T(8,128)(2,1)S(1)}, u32[]{:S(2)}, u32[]{:S(2)}) %collective-permute-start.21) | collective-permute-done | bytes 65568 | tf_op jit(solution)/shard_map/ppermute | solution.py:616
  61.3 2.8 %collective-permute-done.22.refs_4_.refs_3_ = bf16[128,1536]{1,0:T(8,128)(2,1)S(1)} collective-permute-done((bf16[128,1536]{1,0:T(8,128)(2,1)S(1)}, bf16[128,1536]{1,0:T(8,128)(2,1)S(1)}, u32[]{:S(2)}, u32[]{:S(2)}) %collective-permute-start.22) | collective-permute-done | bytes 393248 | tf_op jit(solution)/shard_map/ppermute | solution.py:612
  64.1 1.9 %collective-permute-done.23.refs_5_.refs_0_ = bf16[128,2048]{1,0:T(8,128)(2,1)S(1)} collective-permute-done((bf16[128,2048]{1,0:T(8,128)(2,1)S(1)}, bf16[128,2048]{1,0:T(8,128)(2,1)S(1)}, u32[]{:S(2)}, u32[]{:S(2)}) %collective-permute-start.23) | collective-permute-done | bytes 524320 | tf_op jit(solution)/shard_map/ppermute | solution.py:612
  67.0 1.5 collective-permute-start.27
  70.0 5.2 %shard_map.88 = (bf16[4,1536,1024]{2,1,0:T(8,128)(2,1)}, f32[8,128]{1,0:T(8,128)S(1)}) custom-call(bf16[1536,4,1024]{2,1,0:T(4,128)(2,1)} %refs_0_.5, bf16[4,1536,1024]{2,1,0:T(8,128)(2,1)} %get-tuple-element.82.refs_1_, bf16[256,128]{1,0:T(8,128)(2,1)S(1)} %add_convert_fusion.2.refs_1_.refs_4_.refs_2_.refs_5_), custom_call_target="tpu_custom_call", output_to_operand_aliasing={{0}: (1, {})} | custom-call | bytes 37752832 | tf_op jit(solution)/shard_map/pallas_call | solution.py:149
  78.4 1.5 collective-permute-start.29
  80.6 2.7 %collective-permute-done.30.refs_4_ = bf16[512,128]{1,0:T(8,128)(2,1)S(1)} collective-permute-done((bf16[512,128]{1,0:T(8,128)(2,1)S(1)}, bf16[512,128]{1,0:T(8,128)(2,1)S(1)}, u32[]{:S(2)}, u32[]{:S(2)}) %collective-permute-start.30) | collective-permute-done | bytes 131104 | tf_op jit(solution)/shard_map/ppermute | solution.py:612
  86.5 2.7 %collective-permute-start.33 = (bf16[256,128]{1,0:T(8,128)(2,1)S(1)}, bf16[256,128]{1,0:T(8,128)(2,1)S(1)}, u32[]{:S(2)}, u32[]{:S(2)}) collective-permute-start(bf16[256,128]{1,0:T(8,128)(2,1)S(1)} %get-tuple-element.89), channel_id=1, source_target_pairs={{0,24},{2,26},{4,28},{6,30},{8,0},{10,2},{12,4},{14,6},{16,8},{18,... | collective-permute-start | bytes 196616 | tf_op jit(solution)/shard_map/ppermute | solution.py:616
  89.2 2.9 %collective-permute-done.35.refs_0_ = bf16[256,128]{1,0:T(8,128)(2,1)S(1)} collective-permute-done((bf16[256,128]{1,0:T(8,128)(2,1)S(1)}, bf16[256,128]{1,0:T(8,128)(2,1)S(1)}, u32[]{:S(2)}, u32[]{:S(2)}) %collective-permute-start.35) | collective-permute-done | bytes 65568 | tf_op jit(solution)/shard_map/ppermute | solution.py:616
  92.4 5.5 %collective-permute-done.36.refs_5_.refs_0_ = bf16[1024,256]{1,0:T(8,128)(2,1)S(1)} collective-permute-done((bf16[1024,256]{1,0:T(8,128)(2,1)S(1)}, bf16[1024,256]{1,0:T(8,128)(2,1)S(1)}, u32[]{:S(2)}, u32[]{:S(2)}) %collective-permute-start.36) | collective-permute-done | bytes 524320 | tf_op jit(solution)/shard_map/ppermute | solution.py:612
  99.2 1.9 %collective-permute-start.40 = (bf16[256,128]{1,0:T(8,128)(2,1)S(1)}, bf16[256,128]{1,0:T(8,128)(2,1)S(1)}, u32[]{:S(2)}, u32[]{:S(2)}) collective-permute-start(bf16[256,128]{1,0:T(8,128)(2,1)S(1)} %add_convert_fusion.1.refs_4_.refs_2_.refs_7_.refs_1_), channel_id=1, source_target_pairs={{0,24},{2,26},{4,28},{6,30},{8,0},{10,2},{12,4},{14,6},{16,8},{18,... | collective-permute-start | bytes 196616 | tf_op jit(solution)/shard_map/ppermute | solution.py:616
  102.3 5.1 %shard_map.96 = (bf16[4,1536,1024]{2,1,0:T(8,128)(2,1)}, f32[8,128]{1,0:T(8,128)S(1)}) custom-call(bf16[1536,4,1024]{2,1,0:T(4,128)(2,1)} %refs_0_.5, bf16[4,1536,1024]{2,1,0:T(8,128)(2,1)} %get-tuple-element.92.refs_1_, bf16[256,128]{1,0:T(8,128)(2,1)S(1)} %add_convert_fusion.1.refs_4_.refs_2_.refs_7_.refs_1_), custom_call_target="tpu_custom_call", output_to_operand_aliasing={{0}: (1, {})} | custom-call | bytes 37752832 | tf_op jit(solution)/shard_map/pallas_call | solution.py:149
  108.2 1.5 shard_map.97
  109.8 1.4 collective-permute-start.47
  113.2 3.9 %collective-permute-done.41.refs_4_ = bf16[512,128]{1,0:T(8,128)(2,1)S(1)} collective-permute-done((bf16[512,128]{1,0:T(8,128)(2,1)S(1)}, bf16[512,128]{1,0:T(8,128)(2,1)S(1)}, u32[]{:S(2)}, u32[]{:S(2)}) %collective-permute-start.41) | collective-permute-done | bytes 131104 | tf_op jit(solution)/shard_map/ppermute | solution.py:612
  118.9 1.5 collective-permute-start.46
  120.4 2.3 %collective-permute-start.44 = (bf16[256,128]{1,0:T(8,128)(2,1)S(1)}, bf16[256,128]{1,0:T(8,128)(2,1)S(1)}, u32[]{:S(2)}, u32[]{:S(2)}) collective-permute-start(bf16[256,128]{1,0:T(8,128)(2,1)S(1)} %get-tuple-element.99), channel_id=1, source_target_pairs={{0,24},{2,26},{4,28},{6,30},{8,0},{10,2},{12,4},{14,6},{16,8},{18,... | collective-permute-start | bytes 196616 | tf_op jit(solution)/shard_map/ppermute | solution.py:616
  122.7 3.0 %collective-permute-done.46.refs_0_ = bf16[256,128]{1,0:T(8,128)(2,1)S(1)} collective-permute-done((bf16[256,128]{1,0:T(8,128)(2,1)S(1)}, bf16[256,128]{1,0:T(8,128)(2,1)S(1)}, u32[]{:S(2)}, u32[]{:S(2)}) %collective-permute-start.46) | collective-permute-done | bytes 65568 | tf_op jit(solution)/shard_map/ppermute | solution.py:616
  126.1 2.2 %collective-permute-done.45 = bf16[256,128]{1,0:T(8,128)(2,1)S(1)} collective-permute-done((bf16[256,128]{1,0:T(8,128)(2,1)S(1)}, bf16[256,128]{1,0:T(8,128)(2,1)S(1)}, u32[]{:S(2)}, u32[]{:S(2)}) %collective-permute-start.45) | collective-permute-done | bytes 65568 | tf_op jit(solution)/shard_map/ppermute | solution.py:616
  128.4 1.7 %collective-permute-start.54 = (bf16[2,512,256]{2,1,0:T(8,128)(2,1)S(1)}, bf16[2,512,256]{2,1,0:T(8,128)(2,1)S(1)}, u32[]{:S(2)}, u32[]{:S(2)}) collective-permute-start(bf16[2,512,256]{2,1,0:T(8,128)(2,1)S(1)} %shard_map.107.refs_4_.refs_1_), channel_id=1, source_target_pairs={{0,2},{2,0},{4,6},{6,4},{8,10},{10,8},{12,14},{14,12},{16,18},{18,... | collective-permute-start | bytes 1572872 | tf_op jit(solution)/shard_map/ppermute | solution.py:612
  130.1 1.6 collective-permute-start.51
  132.4 2.6 %shard_map.104 = (bf16[4,1024,512]{2,1,0:T(8,128)(2,1)}, bf16[2,512,1024]{2,1,0:T(8,128)(2,1)S(1)}) custom-call(s32[4]{0:T(128)S(1)} %pad_add_fusion.refs_0_, bf16[1024,256]{1,0:T(8,128)(2,1)S(1)} %shard_map.98.refs_1_, bf16[1024,256]{1,0:T(8,128)(2,1)S(1)} %shard_map.101.refs_2_, bf16[1024,256]{1,0:T(8,128)(2,1)S(1)} %collective-permute-done.42.refs_5_.refs_3_, ...), custom_call_target="tpu_custom_call" | custom-call | bytes 8388624 | tf_op jit(solution)/shard_map/pallas_call | solution.py:149
  135.0 3.1 %collective-permute-done.50.refs_3_ = bf16[256,128]{1,0:T(8,128)(2,1)S(1)} collective-permute-done((bf16[256,128]{1,0:T(8,128)(2,1)S(1)}, bf16[256,128]{1,0:T(8,128)(2,1)S(1)}, u32[]{:S(2)}, u32[]{:S(2)}) %collective-permute-start.50) | collective-permute-done | bytes 65568 | tf_op jit(solution)/shard_map/ppermute | solution.py:616
  141.2 1.4 collective-permute-start.53
  142.6 5.9 %shard_map.108 = (f32[256,1536]{1,0:T(8,128)S(1)}, bf16[256,1536]{1,0:T(8,128)(2,1)S(1)}) custom-call(s32[4]{0:T(128)S(1)} %pad_add_fusion.refs_0_, bf16[2,512,1024]{2,1,0:T(8,128)(2,1)S(1)} %get-tuple-element.102.refs_5_.refs_1_, bf16[4,1536,1024]{2,1,0:T(8,128)(2,1)} %get-tuple-element.105.refs_2_.refs_5_, ...), custom_call_target="tpu_custom_call" | custom-call | flops 3221225472 | bytes 17039376 | tf_op jit(solution)/shard_map/pallas_call | solution.py:149
  149.3 1.6 collective-permute-start.56
  150.9 1.9 %shard_map.110 = (bf16[4,1024,512]{2,1,0:T(8,128)(2,1)}, bf16[1,512,1024]{2,1,0:T(8,128)(2,1)S(1)}) custom-call(s32[4]{0:T(128)S(1)} %pad_add_fusion.refs_0_, bf16[2,512,256]{2,1,0:T(8,128)(2,1)S(1)} %shard_map.107.refs_4_.refs_1_, bf16[2,512,256]{2,1,0:T(8,128)(2,1)S(1)} %collective-permute-done.54.refs_5_.refs_2_, ...), custom_call_target="tpu_custom_call", output_to_operand_aliasing={{0}: (3, {})} | custom-call | bytes 10485776 | tf_op jit(solution)/shard_map/pallas_call | solution.py:149
  152.8 4.1 %shard_map.112 = (f32[256,1536]{1,0:T(8,128)S(1)}, bf16[256,1536]{1,0:T(8,128)(2,1)S(1)}) custom-call(s32[4]{0:T(128)S(1)} %pad_add_fusion.refs_0_, bf16[1,512,1024]{2,1,0:T(8,128)(2,1)S(1)} %get-tuple-element.110.refs_1_, bf16[4,1536,1024]{2,1,0:T(8,128)(2,1)} %get-tuple-element.105.refs_2_.refs_5_, ...), custom_call_target="tpu_custom_call" | custom-call | flops 1610612736 | bytes 18350096 | tf_op jit(solution)/shard_map/pallas_call | solution.py:149
  157.1 5.3 %shard_map.111 = (bf16[4,1024,512]{2,1,0:T(8,128)(2,1)}, f32[256,1536]{1,0:T(8,128)S(1)}, bf16[256,1536]{1,0:T(8,128)(2,1)S(1)}) custom-call(s32[4]{0:T(128)S(1)} %pad_add_fusion.refs_0_, bf16[512,256]{1,0:T(8,128)(2,1)S(1)} %shard_map.106.refs_3_.refs_1_, bf16[512,256]{1,0:T(8,128)(2,1)S(1)} %shard_map.109.refs_2_, ...), custom_call_target="tpu_custom_call", output_to_operand_aliasing={{0}: (6, {})} | custom-call | flops 1610612736 | bytes 24379408 | tf_op jit(solution)/shard_map/pallas_call | solution.py:149
  162.8 1.9 %collective-permute-done.58 = bf16[256,1536]{1,0:T(8,128)(2,1)S(1)} collective-permute-done((bf16[256,1536]{1,0:T(8,128)(2,1)S(1)}, bf16[256,1536]{1,0:T(8,128)(2,1)S(1)}, u32[]{:S(2)}, u32[]{:S(2)}) %collective-permute-start.58) | collective-permute-done | bytes 786464 | tf_op jit(solution)/shard_map/ppermute | solution.py:619
  164.8 1.4 subtract_convert_fusion
  (123 shorter events, 36.6 us)
Async XLA Ops:
  1.9 13.1 %collective-permute-start = (bf16[128,1152]{1,0:T(8,128)(2,1)S(1)}, bf16[128,1152]{1,0:T(8,128)(2,1)S(1)}, u32[]{:S(2)}, u32[]{:S(2)}) collective-permute-start(bf16[128,1152]{1,0:T(8,128)(2,1)S(1)} %get-tuple-element.61), channel_id=1, source_target_pairs={{0,2},{2,0},{4,6},{6,4},{8,10},{10,8},{12,14},{14,12},{16,18},{18,... | collective-permute-start | bytes 884744 | tf_op jit(solution)/shard_map/ppermute | solution.py:612
  4.9 6.4 %collective-permute-start.1 = (bf16[128,768]{1,0:T(8,128)(2,1)S(1)}, bf16[128,768]{1,0:T(8,128)(2,1)S(1)}, u32[]{:S(2)}, u32[]{:S(2)}) collective-permute-start(bf16[128,768]{1,0:T(8,128)(2,1)S(1)} %get-tuple-element.62), channel_id=1, source_target_pairs={{0,4},{2,6},{4,0},{6,2},{8,12},{10,14},{12,8},{14,10},{16,20},{18,... | collective-permute-start | bytes 589832 | tf_op jit(solution)/shard_map/ppermute | solution.py:612
  11.3 6.0 %collective-permute-start.4 = (bf16[128,768]{1,0:T(8,128)(2,1)S(1)}, bf16[128,768]{1,0:T(8,128)(2,1)S(1)}, u32[]{:S(2)}, u32[]{:S(2)}) collective-permute-start(bf16[128,768]{1,0:T(8,128)(2,1)S(1)} %collective-permute-done.1.refs_2_), channel_id=1, source_target_pairs={{0,2},{2,0},{4,6},{6,4},{8,10},{10,8},{12,14},{14,12},{16,18},{18,... | collective-permute-start | bytes 589832 | tf_op jit(solution)/shard_map/ppermute | solution.py:612
  15.0 7.0 %collective-permute-start.2 = (bf16[128,1024]{1,0:T(8,128)(2,1)S(1)}, bf16[128,1024]{1,0:T(8,128)(2,1)S(1)}, u32[]{:S(2)}, u32[]{:S(2)}) collective-permute-start(bf16[128,1024]{1,0:T(8,128)(2,1)S(1)} %shard_map.71), channel_id=1, source_target_pairs={{0,4},{2,6},{4,0},{6,2},{8,12},{10,14},{12,8},{14,10},{16,20},{18,... | collective-permute-start | bytes 786440 | tf_op jit(solution)/shard_map/ppermute | solution.py:612
  16.8 6.7 %collective-permute-start.7 = (bf16[128,1152]{1,0:T(8,128)(2,1)S(1)}, bf16[128,1152]{1,0:T(8,128)(2,1)S(1)}, u32[]{:S(2)}, u32[]{:S(2)}) collective-permute-start(bf16[128,1152]{1,0:T(8,128)(2,1)S(1)} %collective-permute-done.refs_1_.refs_3_.refs_8_.refs_10_.refs_12_), channel_id=1, source_target_pairs={{0,1},{1,0},{2,3},{3,2},{4,5},{5,4},{6,7},{7,6},{8,9},{9,8},{10,11... | collective-permute-start | bytes 884744 | tf_op jit(solution)/shard_map/ppermute | solution.py:619
  16.8 6.7 %collective-permute-start.5 = (bf16[128,768]{1,0:T(8,128)(2,1)S(1)}, bf16[128,768]{1,0:T(8,128)(2,1)S(1)}, u32[]{:S(2)}, u32[]{:S(2)}) collective-permute-start(bf16[128,768]{1,0:T(8,128)(2,1)S(1)} %get-tuple-element.64.refs_1_), channel_id=1, source_target_pairs={{0,1},{1,0},{2,3},{3,2},{4,5},{5,4},{6,7},{7,6},{8,9},{9,8},{10,11... | collective-permute-start | bytes 589832 | tf_op jit(solution)/shard_map/ppermute | solution.py:619
  17.3 6.2 %collective-permute-start.6 = (bf16[128,768]{1,0:T(8,128)(2,1)S(1)}, bf16[128,768]{1,0:T(8,128)(2,1)S(1)}, u32[]{:S(2)}, u32[]{:S(2)}) collective-permute-start(bf16[128,768]{1,0:T(8,128)(2,1)S(1)} %collective-permute-done.1.refs_2_), channel_id=1, source_target_pairs={{0,1},{1,0},{2,3},{3,2},{4,5},{5,4},{6,7},{7,6},{8,9},{9,8},{10,11... | collective-permute-start | bytes 589832 | tf_op jit(solution)/shard_map/ppermute | solution.py:619
  17.3 6.2 %collective-permute-start.8 = (bf16[128,768]{1,0:T(8,128)(2,1)S(1)}, bf16[128,768]{1,0:T(8,128)(2,1)S(1)}, u32[]{:S(2)}, u32[]{:S(2)}) collective-permute-start(bf16[128,768]{1,0:T(8,128)(2,1)S(1)} %collective-permute-done.4.refs_4_), channel_id=1, source_target_pairs={{0,1},{1,0},{2,3},{3,2},{4,5},{5,4},{6,7},{7,6},{8,9},{9,8},{10,11... | collective-permute-start | bytes 589832 | tf_op jit(solution)/shard_map/ppermute | solution.py:619
  22.0 11.7 %collective-permute-start.3 = (bf16[2,128,1024]{2,1,0:T(8,128)(2,1)S(1)}, bf16[2,128,1024]{2,1,0:T(8,128)(2,1)S(1)}, u32[]{:S(2)}, u32[]{:S(2)}) collective-permute-start(bf16[2,128,1024]{2,1,0:T(8,128)(2,1)S(1)} %shard_map.72.refs_1_.refs_0_), channel_id=1, source_target_pairs={{0,2},{2,0},{4,6},{6,4},{8,10},{10,8},{12,14},{14,12},{16,18},{18,... | collective-permute-start | bytes 1572872 | tf_op jit(solution)/shard_map/ppermute | solution.py:612
  24.5 8.2 %collective-permute-start.12 = (bf16[128,1536]{1,0:T(8,128)(2,1)S(1)}, bf16[128,1536]{1,0:T(8,128)(2,1)S(1)}, u32[]{:S(2)}, u32[]{:S(2)}) collective-permute-start(bf16[128,1536]{1,0:T(8,128)(2,1)S(1)} %shard_map.74), channel_id=1, source_target_pairs={{0,4},{2,6},{4,0},{6,2},{8,12},{10,14},{12,8},{14,10},{16,20},{18,... | collective-permute-start | bytes 1179656 | tf_op jit(solution)/shard_map/ppermute | solution.py:612
  26.1 6.2 %collective-permute-start.11 = (bf16[256,128]{1,0:T(8,128)(2,1)S(1)}, bf16[256,128]{1,0:T(8,128)(2,1)S(1)}, u32[]{:S(2)}, u32[]{:S(2)}) collective-permute-start(bf16[256,128]{1,0:T(8,128)(2,1)S(1)} %get-tuple-element.68), channel_id=1, source_target_pairs={{0,8},{2,10},{4,12},{6,14},{8,16},{10,18},{12,20},{14,22},{16,24},... | collective-permute-start | bytes 196616 | tf_op jit(solution)/shard_map/ppermute | solution.py:616
  27.7 6.0 %collective-permute-start.9 = (bf16[256,128]{1,0:T(8,128)(2,1)S(1)}, bf16[256,128]{1,0:T(8,128)(2,1)S(1)}, u32[]{:S(2)}, u32[]{:S(2)}) collective-permute-start(bf16[256,128]{1,0:T(8,128)(2,1)S(1)} %get-tuple-element.66), channel_id=1, source_target_pairs={{0,24},{2,26},{4,28},{6,30},{8,0},{10,2},{12,4},{14,6},{16,8},{18,... | collective-permute-start | bytes 196616 | tf_op jit(solution)/shard_map/ppermute | solution.py:616
  35.5 10.1 %collective-permute-start.13 = (bf16[4,128,1024]{2,1,0:T(8,128)(2,1)S(1)}, bf16[4,128,1024]{2,1,0:T(8,128)(2,1)S(1)}, u32[]{:S(2)}, u32[]{:S(2)}) collective-permute-start(bf16[4,128,1024]{2,1,0:T(8,128)(2,1)S(1)} %shard_map.76.refs_1_), channel_id=1, source_target_pairs={{0,1},{1,0},{2,3},{3,2},{4,5},{5,4},{6,7},{7,6},{8,9},{9,8},{10,11... | collective-permute-start | bytes 3145736 | tf_op jit(solution)/shard_map/ppermute | solution.py:619
  35.6 12.4 %collective-permute-start.18 = (bf16[128,1536]{1,0:T(8,128)(2,1)S(1)}, bf16[128,1536]{1,0:T(8,128)(2,1)S(1)}, u32[]{:S(2)}, u32[]{:S(2)}) collective-permute-start(bf16[128,1536]{1,0:T(8,128)(2,1)S(1)} %shard_map.80.refs_1_.refs_0_), channel_id=1, source_target_pairs={{0,2},{2,0},{4,6},{6,4},{8,10},{10,8},{12,14},{14,12},{16,18},{18,... | collective-permute-start | bytes 1179656 | tf_op jit(solution)/shard_map/ppermute | solution.py:612
  36.2 8.6 %collective-permute-start.16 = (bf16[256,128]{1,0:T(8,128)(2,1)S(1)}, bf16[256,128]{1,0:T(8,128)(2,1)S(1)}, u32[]{:S(2)}, u32[]{:S(2)}) collective-permute-start(bf16[256,128]{1,0:T(8,128)(2,1)S(1)} %add_convert_fusion.3.refs_2_.refs_1_.refs_3_), channel_id=1, source_target_pairs={{0,24},{2,26},{4,28},{6,30},{8,0},{10,2},{12,4},{14,6},{16,8},{18,... | collective-permute-start | bytes 196616 | tf_op jit(solution)/shard_map/ppermute | solution.py:616
  38.6 6.9 %collective-permute-start.15 = (bf16[256,128]{1,0:T(8,128)(2,1)S(1)}, bf16[256,128]{1,0:T(8,128)(2,1)S(1)}, u32[]{:S(2)}, u32[]{:S(2)}) collective-permute-start(bf16[256,128]{1,0:T(8,128)(2,1)S(1)} %add_convert_fusion.3.refs_2_.refs_1_.refs_3_), channel_id=1, source_target_pairs={{0,16},{2,18},{4,20},{6,22},{8,24},{10,26},{12,28},{14,30},{16,0},... | collective-permute-start | bytes 196616 | tf_op jit(solution)/shard_map/ppermute | solution.py:616
  38.6 6.9 %collective-permute-start.14 = (bf16[256,128]{1,0:T(8,128)(2,1)S(1)}, bf16[256,128]{1,0:T(8,128)(2,1)S(1)}, u32[]{:S(2)}, u32[]{:S(2)}) collective-permute-start(bf16[256,128]{1,0:T(8,128)(2,1)S(1)} %add_convert_fusion.3.refs_2_.refs_1_.refs_3_), channel_id=1, source_target_pairs={{0,8},{2,10},{4,12},{6,14},{8,16},{10,18},{12,20},{14,22},{16,24},... | collective-permute-start | bytes 196616 | tf_op jit(solution)/shard_map/ppermute | solution.py:616
  53.0 13.0 %collective-permute-start.23 = (bf16[128,2048]{1,0:T(8,128)(2,1)S(1)}, bf16[128,2048]{1,0:T(8,128)(2,1)S(1)}, u32[]{:S(2)}, u32[]{:S(2)}) collective-permute-start(bf16[128,2048]{1,0:T(8,128)(2,1)S(1)} %shard_map.84), channel_id=1, source_target_pairs={{0,4},{2,6},{4,0},{6,2},{8,12},{10,14},{12,8},{14,10},{16,20},{18,... | collective-permute-start | bytes 1572872 | tf_op jit(solution)/shard_map/ppermute | solution.py:612
  54.4 9.7 %collective-permute-start.22 = (bf16[128,1536]{1,0:T(8,128)(2,1)S(1)}, bf16[128,1536]{1,0:T(8,128)(2,1)S(1)}, u32[]{:S(2)}, u32[]{:S(2)}) collective-permute-start(bf16[128,1536]{1,0:T(8,128)(2,1)S(1)} %shard_map.83.refs_2_.refs_1_), channel_id=1, source_target_pairs={{0,2},{2,0},{4,6},{6,4},{8,10},{10,8},{12,14},{14,12},{16,18},{18,... | collective-permute-start | bytes 1179656 | tf_op jit(solution)/shard_map/ppermute | solution.py:612
  55.1 6.2 %collective-permute-start.21 = (bf16[256,128]{1,0:T(8,128)(2,1)S(1)}, bf16[256,128]{1,0:T(8,128)(2,1)S(1)}, u32[]{:S(2)}, u32[]{:S(2)}) collective-permute-start(bf16[256,128]{1,0:T(8,128)(2,1)S(1)} %get-tuple-element.78), channel_id=1, source_target_pairs={{0,8},{2,10},{4,12},{6,14},{8,16},{10,18},{12,20},{14,22},{16,24},... | collective-permute-start | bytes 196616 | tf_op jit(solution)/shard_map/ppermute | solution.py:616
  56.5 9.5 %collective-permute-start.19 = (bf16[256,128]{1,0:T(8,128)(2,1)S(1)}, bf16[256,128]{1,0:T(8,128)(2,1)S(1)}, u32[]{:S(2)}, u32[]{:S(2)}) collective-permute-start(bf16[256,128]{1,0:T(8,128)(2,1)S(1)} %get-tuple-element.76), channel_id=1, source_target_pairs={{0,24},{2,26},{4,28},{6,30},{8,0},{10,2},{12,4},{14,6},{16,8},{18,... | collective-permute-start | bytes 196616 | tf_op jit(solution)/shard_map/ppermute | solution.py:616
  59.0 7.0 %collective-permute-start.20 = (bf16[256,128]{1,0:T(8,128)(2,1)S(1)}, bf16[256,128]{1,0:T(8,128)(2,1)S(1)}, u32[]{:S(2)}, u32[]{:S(2)}) collective-permute-start(bf16[256,128]{1,0:T(8,128)(2,1)S(1)} %get-tuple-element.77), channel_id=1, source_target_pairs={{0,16},{2,18},{4,20},{6,22},{8,24},{10,26},{12,28},{14,30},{16,0},... | collective-permute-start | bytes 196616 | tf_op jit(solution)/shard_map/ppermute | solution.py:616
  66.2 9.9 %collective-permute-start.24 = (bf16[4,128,1536]{2,1,0:T(8,128)(2,1)S(1)}, bf16[4,128,1536]{2,1,0:T(8,128)(2,1)S(1)}, u32[]{:S(2)}, u32[]{:S(2)}) collective-permute-start(bf16[4,128,1536]{2,1,0:T(8,128)(2,1)S(1)} %shard_map.87.refs_1_), channel_id=1, source_target_pairs={{0,1},{1,0},{2,3},{3,2},{4,5},{5,4},{6,7},{7,6},{8,9},{9,8},{10,11... | collective-permute-start | bytes 4718600 | tf_op jit(solution)/shard_map/ppermute | solution.py:619
  66.2 14.3 %collective-permute-start.28 = (bf16[128,2048]{1,0:T(8,128)(2,1)S(1)}, bf16[128,2048]{1,0:T(8,128)(2,1)S(1)}, u32[]{:S(2)}, u32[]{:S(2)}) collective-permute-start(bf16[128,2048]{1,0:T(8,128)(2,1)S(1)} %shard_map.86.refs_1_.refs_0_), channel_id=1, source_target_pairs={{0,2},{2,0},{4,6},{6,4},{8,10},{10,8},{12,14},{14,12},{16,18},{18,... | collective-permute-start | bytes 1572872 | tf_op jit(solution)/shard_map/ppermute | solution.py:612
  67.0 8.2 %collective-permute-start.27 = (bf16[256,128]{1,0:T(8,128)(2,1)S(1)}, bf16[256,128]{1,0:T(8,128)(2,1)S(1)}, u32[]{:S(2)}, u32[]{:S(2)}) collective-permute-start(bf16[256,128]{1,0:T(8,128)(2,1)S(1)} %add_convert_fusion.2.refs_1_.refs_4_.refs_2_.refs_5_), channel_id=1, source_target_pairs={{0,24},{2,26},{4,28},{6,30},{8,0},{10,2},{12,4},{14,6},{16,8},{18,... | collective-permute-start | bytes 196616 | tf_op jit(solution)/shard_map/ppermute | solution.py:616
  68.5 7.5 %collective-permute-start.26 = (bf16[256,128]{1,0:T(8,128)(2,1)S(1)}, bf16[256,128]{1,0:T(8,128)(2,1)S(1)}, u32[]{:S(2)}, u32[]{:S(2)}) collective-permute-start(bf16[256,128]{1,0:T(8,128)(2,1)S(1)} %add_convert_fusion.2.refs_1_.refs_4_.refs_2_.refs_5_), channel_id=1, source_target_pairs={{0,16},{2,18},{4,20},{6,22},{8,24},{10,26},{12,28},{14,30},{16,0},... | collective-permute-start | bytes 196616 | tf_op jit(solution)/shard_map/ppermute | solution.py:616
  69.4 6.7 %collective-permute-start.25 = (bf16[256,128]{1,0:T(8,128)(2,1)S(1)}, bf16[256,128]{1,0:T(8,128)(2,1)S(1)}, u32[]{:S(2)}, u32[]{:S(2)}) collective-permute-start(bf16[256,128]{1,0:T(8,128)(2,1)S(1)} %add_convert_fusion.2.refs_1_.refs_4_.refs_2_.refs_5_), channel_id=1, source_target_pairs={{0,8},{2,10},{4,12},{6,14},{8,16},{10,18},{12,20},{14,22},{16,24},... | collective-permute-start | bytes 196616 | tf_op jit(solution)/shard_map/ppermute | solution.py:616
  77.4 5.9 %collective-permute-start.30 = (bf16[512,128]{1,0:T(8,128)(2,1)S(1)}, bf16[512,128]{1,0:T(8,128)(2,1)S(1)}, u32[]{:S(2)}, u32[]{:S(2)}) collective-permute-start(bf16[512,128]{1,0:T(8,128)(2,1)S(1)} %get-tuple-element.85), channel_id=1, source_target_pairs={{0,4},{2,6},{4,0},{6,2},{8,12},{10,14},{12,8},{14,10},{16,20},{18,... | collective-permute-start | bytes 393224 | tf_op jit(solution)/shard_map/ppermute | solution.py:612
  78.4 14.0 %collective-permute-start.29 = (bf16[128,2048]{1,0:T(8,128)(2,1)S(1)}, bf16[128,2048]{1,0:T(8,128)(2,1)S(1)}, u32[]{:S(2)}, u32[]{:S(2)}) collective-permute-start(bf16[128,2048]{1,0:T(8,128)(2,1)S(1)} %shard_map.90.refs_2_.refs_1_), channel_id=1, source_target_pairs={{0,2},{2,0},{4,6},{6,4},{8,10},{10,8},{12,14},{14,12},{16,18},{18,... | collective-permute-start | bytes 1572872 | tf_op jit(solution)/shard_map/ppermute | solution.py:612
  84.3 13.6 %collective-permute-start.36 = (bf16[1024,256]{1,0:T(8,128)(2,1)S(1)}, bf16[1024,256]{1,0:T(8,128)(2,1)S(1)}, u32[]{:S(2)}, u32[]{:S(2)}) collective-permute-start(bf16[1024,256]{1,0:T(8,128)(2,1)S(1)} %shard_map.93.refs_0_), channel_id=1, source_target_pairs={{0,4},{2,6},{4,0},{6,2},{8,12},{10,14},{12,8},{14,10},{16,20},{18,... | collective-permute-start | bytes 1572872 | tf_op jit(solution)/shard_map/ppermute | solution.py:612
  85.4 6.7 %collective-permute-start.35 = (bf16[256,128]{1,0:T(8,128)(2,1)S(1)}, bf16[256,128]{1,0:T(8,128)(2,1)S(1)}, u32[]{:S(2)}, u32[]{:S(2)}) collective-permute-start(bf16[256,128]{1,0:T(8,128)(2,1)S(1)} %get-tuple-element.91), channel_id=1, source_target_pairs={{0,8},{2,10},{4,12},{6,14},{8,16},{10,18},{12,20},{14,22},{16,24},... | collective-permute-start | bytes 196616 | tf_op jit(solution)/shard_map/ppermute | solution.py:616
  86.5 11.4 %collective-permute-start.33 = (bf16[256,128]{1,0:T(8,128)(2,1)S(1)}, bf16[256,128]{1,0:T(8,128)(2,1)S(1)}, u32[]{:S(2)}, u32[]{:S(2)}) collective-permute-start(bf16[256,128]{1,0:T(8,128)(2,1)S(1)} %get-tuple-element.89), channel_id=1, source_target_pairs={{0,24},{2,26},{4,28},{6,30},{8,0},{10,2},{12,4},{14,6},{16,8},{18,... | collective-permute-start | bytes 196616 | tf_op jit(solution)/shard_map/ppermute | solution.py:616
  89.2 8.7 %collective-permute-start.34 = (bf16[256,128]{1,0:T(8,128)(2,1)S(1)}, bf16[256,128]{1,0:T(8,128)(2,1)S(1)}, u32[]{:S(2)}, u32[]{:S(2)}) collective-permute-start(bf16[256,128]{1,0:T(8,128)(2,1)S(1)} %get-tuple-element.90), channel_id=1, source_target_pairs={{0,16},{2,18},{4,20},{6,22},{8,24},{10,26},{12,28},{14,30},{16,0},... | collective-permute-start | bytes 196616 | tf_op jit(solution)/shard_map/ppermute | solution.py:616
  98.1 10.1 %collective-permute-start.37 = (bf16[4,128,2048]{2,1,0:T(8,128)(2,1)S(1)}, bf16[4,128,2048]{2,1,0:T(8,128)(2,1)S(1)}, u32[]{:S(2)}, u32[]{:S(2)}) collective-permute-start(bf16[4,128,2048]{2,1,0:T(8,128)(2,1)S(1)} %shard_map.95.refs_1_), channel_id=1, source_target_pairs={{0,1},{1,0},{2,3},{3,2},{4,5},{5,4},{6,7},{7,6},{8,9},{9,8},{10,11... | collective-permute-start | bytes 6291464 | tf_op jit(solution)/shard_map/ppermute | solution.py:619
  98.2 15.0 %collective-permute-start.42 = (bf16[1024,256]{1,0:T(8,128)(2,1)S(1)}, bf16[1024,256]{1,0:T(8,128)(2,1)S(1)}, u32[]{:S(2)}, u32[]{:S(2)}) collective-permute-start(bf16[1024,256]{1,0:T(8,128)(2,1)S(1)} %shard_map.98.refs_1_), channel_id=1, source_target_pairs={{0,2},{2,0},{4,6},{6,4},{8,10},{10,8},{12,14},{14,12},{16,18},{18,... | collective-permute-start | bytes 1572872 | tf_op jit(solution)/shard_map/ppermute | solution.py:612
  99.2 8.3 %collective-permute-start.40 = (bf16[256,128]{1,0:T(8,128)(2,1)S(1)}, bf16[256,128]{1,0:T(8,128)(2,1)S(1)}, u32[]{:S(2)}, u32[]{:S(2)}) collective-permute-start(bf16[256,128]{1,0:T(8,128)(2,1)S(1)} %add_convert_fusion.1.refs_4_.refs_2_.refs_7_.refs_1_), channel_id=1, source_target_pairs={{0,24},{2,26},{4,28},{6,30},{8,0},{10,2},{12,4},{14,6},{16,8},{18,... | collective-permute-start | bytes 196616 | tf_op jit(solution)/shard_map/ppermute | solution.py:616
  101.1 7.1 %collective-permute-start.39 = (bf16[256,128]{1,0:T(8,128)(2,1)S(1)}, bf16[256,128]{1,0:T(8,128)(2,1)S(1)}, u32[]{:S(2)}, u32[]{:S(2)}) collective-permute-start(bf16[256,128]{1,0:T(8,128)(2,1)S(1)} %add_convert_fusion.1.refs_4_.refs_2_.refs_7_.refs_1_), channel_id=1, source_target_pairs={{0,16},{2,18},{4,20},{6,22},{8,24},{10,26},{12,28},{14,30},{16,0},... | collective-permute-start | bytes 196616 | tf_op jit(solution)/shard_map/ppermute | solution.py:616
  101.4 6.9 %collective-permute-start.38 = (bf16[256,128]{1,0:T(8,128)(2,1)S(1)}, bf16[256,128]{1,0:T(8,128)(2,1)S(1)}, u32[]{:S(2)}, u32[]{:S(2)}) collective-permute-start(bf16[256,128]{1,0:T(8,128)(2,1)S(1)} %add_convert_fusion.1.refs_4_.refs_2_.refs_7_.refs_1_), channel_id=1, source_target_pairs={{0,8},{2,10},{4,12},{6,14},{8,16},{10,18},{12,20},{14,22},{16,24},... | collective-permute-start | bytes 196616 | tf_op jit(solution)/shard_map/ppermute | solution.py:616
  109.8 16.4 %collective-permute-start.47 = (bf16[1024,256]{1,0:T(8,128)(2,1)S(1)}, bf16[1024,256]{1,0:T(8,128)(2,1)S(1)}, u32[]{:S(2)}, u32[]{:S(2)}) collective-permute-start(bf16[1024,256]{1,0:T(8,128)(2,1)S(1)} %shard_map.101.refs_2_), channel_id=1, source_target_pairs={{0,2},{2,0},{4,6},{6,4},{8,10},{10,8},{12,14},{14,12},{16,18},{18,... | collective-permute-start | bytes 1572872 | tf_op jit(solution)/shard_map/ppermute | solution.py:612
  111.2 5.9 %collective-permute-start.41 = (bf16[512,128]{1,0:T(8,128)(2,1)S(1)}, bf16[512,128]{1,0:T(8,128)(2,1)S(1)}, u32[]{:S(2)}, u32[]{:S(2)}) collective-permute-start(bf16[512,128]{1,0:T(8,128)(2,1)S(1)} %get-tuple-element.95), channel_id=1, source_target_pairs={{0,4},{2,6},{4,0},{6,2},{8,12},{10,14},{12,8},{14,10},{16,20},{18,... | collective-permute-start | bytes 393224 | tf_op jit(solution)/shard_map/ppermute | solution.py:612
  118.1 8.0 %collective-permute-start.48 = (bf16[512,256]{1,0:T(8,128)(2,1)S(1)}, bf16[512,256]{1,0:T(8,128)(2,1)S(1)}, u32[]{:S(2)}, u32[]{:S(2)}) collective-permute-start(bf16[512,256]{1,0:T(8,128)(2,1)S(1)} %shard_map.102.refs_0_), channel_id=1, source_target_pairs={{0,4},{2,6},{4,0},{6,2},{8,12},{10,14},{12,8},{14,10},{16,20},{18,... | collective-permute-start | bytes 786440 | tf_op jit(solution)/shard_map/ppermute | solution.py:612
  118.9 6.8 %collective-permute-start.46 = (bf16[256,128]{1,0:T(8,128)(2,1)S(1)}, bf16[256,128]{1,0:T(8,128)(2,1)S(1)}, u32[]{:S(2)}, u32[]{:S(2)}) collective-permute-start(bf16[256,128]{1,0:T(8,128)(2,1)S(1)} %get-tuple-element.101), channel_id=1, source_target_pairs={{0,8},{2,10},{4,12},{6,14},{8,16},{10,18},{12,20},{14,22},{16,24},... | collective-permute-start | bytes 196616 | tf_op jit(solution)/shard_map/ppermute | solution.py:616
  128.4 14.2 %collective-permute-start.54 = (bf16[2,512,256]{2,1,0:T(8,128)(2,1)S(1)}, bf16[2,512,256]{2,1,0:T(8,128)(2,1)S(1)}, u32[]{:S(2)}, u32[]{:S(2)}) collective-permute-start(bf16[2,512,256]{2,1,0:T(8,128)(2,1)S(1)} %shard_map.107.refs_4_.refs_1_), channel_id=1, source_target_pairs={{0,2},{2,0},{4,6},{6,4},{8,10},{10,8},{12,14},{14,12},{16,18},{18,... | collective-permute-start | bytes 1572872 | tf_op jit(solution)/shard_map/ppermute | solution.py:612
  131.7 6.4 %collective-permute-start.50 = (bf16[256,128]{1,0:T(8,128)(2,1)S(1)}, bf16[256,128]{1,0:T(8,128)(2,1)S(1)}, u32[]{:S(2)}, u32[]{:S(2)}) collective-permute-start(bf16[256,128]{1,0:T(8,128)(2,1)S(1)} %add_convert_fusion.refs_5_.refs_1_.refs_2_), channel_id=1, source_target_pairs={{0,16},{2,18},{4,20},{6,22},{8,24},{10,26},{12,28},{14,30},{16,0},... | collective-permute-start | bytes 196616 | tf_op jit(solution)/shard_map/ppermute | solution.py:616
  131.7 6.4 %collective-permute-start.49 = (bf16[256,128]{1,0:T(8,128)(2,1)S(1)}, bf16[256,128]{1,0:T(8,128)(2,1)S(1)}, u32[]{:S(2)}, u32[]{:S(2)}) collective-permute-start(bf16[256,128]{1,0:T(8,128)(2,1)S(1)} %add_convert_fusion.refs_5_.refs_1_.refs_2_), channel_id=1, source_target_pairs={{0,8},{2,10},{4,12},{6,14},{8,16},{10,18},{12,20},{14,22},{16,24},... | collective-permute-start | bytes 196616 | tf_op jit(solution)/shard_map/ppermute | solution.py:616
  140.8 16.3 %collective-permute-start.55 = (bf16[512,256]{1,0:T(8,128)(2,1)S(1)}, bf16[512,256]{1,0:T(8,128)(2,1)S(1)}, u32[]{:S(2)}, u32[]{:S(2)}) collective-permute-start(bf16[512,256]{1,0:T(8,128)(2,1)S(1)} %shard_map.106.refs_3_.refs_1_), channel_id=1, source_target_pairs={{0,2},{2,0},{4,6},{6,4},{8,10},{10,8},{12,14},{14,12},{16,18},{18,... | collective-permute-start | bytes 786440 | tf_op jit(solution)/shard_map/ppermute | solution.py:612
  141.2 8.1 %collective-permute-start.53 = (bf16[512,256]{1,0:T(8,128)(2,1)S(1)}, bf16[512,256]{1,0:T(8,128)(2,1)S(1)}, u32[]{:S(2)}, u32[]{:S(2)}) collective-permute-start(bf16[512,256]{1,0:T(8,128)(2,1)S(1)} %shard_map.106.refs_3_.refs_1_), channel_id=1, source_target_pairs={{0,4},{2,6},{4,0},{6,2},{8,12},{10,14},{12,8},{14,10},{16,20},{18,... | collective-permute-start | bytes 786440 | tf_op jit(solution)/shard_map/ppermute | solution.py:612
  149.3 7.7 %collective-permute-start.56 = (bf16[512,256]{1,0:T(8,128)(2,1)S(1)}, bf16[512,256]{1,0:T(8,128)(2,1)S(1)}, u32[]{:S(2)}, u32[]{:S(2)}) collective-permute-start(bf16[512,256]{1,0:T(8,128)(2,1)S(1)} %shard_map.109.refs_2_), channel_id=1, source_target_pairs={{0,2},{2,0},{4,6},{6,4},{8,10},{10,8},{12,14},{14,12},{16,18},{18,... | collective-permute-start | bytes 786440 | tf_op jit(solution)/shard_map/ppermute | solution.py:612
  (12 other events, 53.2 us)

commit v4 on v3

--- a/solution.py
+++ b/solution.py
@@ -209,23 +209,35 @@
     return outs[: form.py], outs[form.py : -1], outs[-1]
 
 
+def slots(s, steps):
+    own = [(s, t) for t in range(s) if s < 3 or t > 0]
+    return own + ([(s + 1, 0)] if 2 <= s < steps - 1 else [])
+
+
+def slot_of(s, t, steps):
+    for by in (s, s - 1):
+        if (s, t) in slots(by, steps):
+            return by, 1 + slots(by, steps).index((s, t))
+
+
 def prep_body(ss, form, meta, diag, lower, *refs):
-    py, width = form.py, form.width
+    py, width, steps = form.py, form.width, lower.shape[2]
     flat = refs[-1]
     for i, s in enumerate(ss):
-        outs = refs[i * py : (i + 1) * py]
         flat[...] = jnp.swapaxes(lower[i], 0, 1)
         for dy in range(py):
-            put_diag(form, meta, dy, diag.at[i], outs[dy])
+            put_diag(form, meta, dy, diag.at[i], refs[i * py + dy])
             at = lax.rem(meta[0] + dy, py) * width
             for t in range(s):
-                outs[dy][:, (1 + t) * width : (2 + t) * width] = flat[t, :, pl.ds(pl.multiple_of(at, width), width)]
+                by, slot = slot_of(s, t, steps)
+                out = refs[ss.index(by) * py + dy]
+                out[:, slot * width : (slot + 1) * width] = flat[t, :, pl.ds(pl.multiple_of(at, width), width)]
 
 
 def prep(ss, form, meta, diag_inverse, lower_pivot, after=()):
     width, eqs, share = form.width, form.eqs, form.py * form.width
     steps, count = lower_pivot.shape[0], len(ss)
-    dims = [(eqs, (s + 1) * width) for s in ss for _ in range(form.py)]
+    dims = [(eqs, (1 + len(slots(s, steps))) * width) for s in ss for _ in range(form.py)]
     outs = call(
         functools.partial(prep_body, ss, form),
         [shaped(d, BF16) for d in dims],
@@ -323,7 +335,9 @@
 def lower_body(s, form, meta, *refs):
     chips, n_cols, eqs = form.chips, form.n_cols, form.eqs
     refs = list(refs)
-    held = take(refs, n_cols * chips)
+    held = {s: take(refs, n_cols * chips)}
+    if s > 2:
+        held[s - 1] = take(refs, n_cols * chips)
     width = form.width
     known = [[refs.pop(0) for _ in range(n_cols)] for _ in range(s - 1)]
     pieces = [refs.pop(0) for _ in range(form.depth)]
@@ -334,8 +348,9 @@
     total = None
     for t, blocks in enumerate(known + [newest]):
         for c in range(n_cols):
-            lanes = slice((1 + t) * width, (2 + t) * width)
-            rows = jnp.concatenate([held[c * chips + k][:, lanes] for k in range(chips)], axis=0)
+            by, slot = slot_of(s, t, form.steps)
+            lanes = slice(slot * width, (slot + 1) * width)
+            rows = jnp.concatenate([held[by][c * chips + k][:, lanes] for k in range(chips)], axis=0)
             term = jnp.dot(rows, blocks[c][...], preferred_element_type=F32)
             total = term if total is None else total + term
     parts = [total[k * eqs : (k + 1) * eqs] for k in range(chips)]
@@ -350,10 +365,10 @@
             outs[e][k * eqs : (k + 1) * eqs] = parts[mine].astype(outs[e].dtype)
 
 
-def lower_product(s, form, meta, held, known, pieces, own, far, after=()):
+def lower_product(s, form, meta, held, older, known, pieces, own, far, after=()):
     rows, sides = form.chips * form.eqs, form.sides
     flat = [x for blocks in known for x in blocks]
-    ins = [meta, *held, *flat, *pieces, own, *far]
+    ins = [meta, *held, *(older if s > 2 else []), *flat, *pieces, own, *far]
     return call(
         functools.partial(lower_body, s, form),
         [shaped((rows, sides), F32)]
@@ -488,11 +503,11 @@
     )
 
 
-def rest_body(form, orders, counts, running, meta, *refs):
+def rest_body(form, counts, running, meta, *refs):
     turned, lower, refs = refs[: len(counts)], refs[len(counts)], refs[len(counts) + 1 :]
     before, outs = refs[:running], refs[running:]
     sides = form.px * form.sides
-    for order, out in zip(orders, outs):
+    for order, out in enumerate(outs):
         at = pl.multiple_of(lax.rem(meta[3] + order, form.n_cols) * sides, sides)
         total, t = None, 0
         for x, count in zip(turned, counts):
@@ -511,10 +526,10 @@
     counts = [x.shape[0] for x in turned]
     count = sum(counts)
     sides = form.px * form.sides
-    block = max(n for n in (512, 384, 256, 128) if rest % n == 0)
+    block = max(n for n in (768, 512, 384, 256, 128) if rest % n == 0)
     side_block = pl.BlockSpec((sides, block), lambda i: (0, i))
     return call(
-        functools.partial(rest_body, form, orders, counts, len(before)),
+        functools.partial(rest_body, form, counts, len(before)),
         [shaped((sides, rest), F32 if order == 0 else BF16) for order in orders],
         [meta, *turned, pltpu.with_memory_space_constraint(lower, pltpu.HBM), *before],
         [SMALL]
@@ -546,7 +561,7 @@
 def last_step(form, meta, parts, lower, buffer):
     steps, rest, share = lower.shape
     total, sides = form.px * form.n_cols * form.sides, form.px * form.sides
-    block = max(n for n in (512, 384, 256, 128) if rest % n == 0)
+    block = max(n for n in (768, 512, 384, 256, 128) if rest % n == 0)
     lower = pltpu.with_memory_space_constraint(lower, pltpu.HBM)
     side_block = pl.BlockSpec((sides, block), lambda i: (0, i))
     return call(
@@ -575,6 +590,7 @@
     eqs: int
     width: int
     sides: int
+    steps: int
 
     def __post_init__(self):
         self.shifts = [(dy, dx) for dx in range(self.px) for dy in range(self.py)]
@@ -588,7 +604,7 @@
     py = plane // px
     return Form(
         py, px, n_rows // plane, lax.axis_size("cols"), lower_pivot.shape[1], lower_pivot.shape[3] // py,
-        rhs_pivot.shape[2] // px,
+        rhs_pivot.shape[2] // px, lower_pivot.shape[0],
     )
 
 
@@ -650,21 +666,22 @@
     near, far, own = start(form, meta, diag_inverse, rhs_pivot)
     got = up(near)
     here = [along_plane(x, 0, dx + 1) for dx, x in enumerate(far)]
-    held = held_of(onward(got, here), ())
     packed = prep(tuple(range(1, steps)), form, meta, diag_inverse, lower_pivot)
-    first = up([gate(x, here + got[1:]) for x in packed[1]])
+    first = up([gate(x, got[1:]) for x in packed[1]])
+    got = onward(got, here, [packed[1][0]])
+    later = [gate(x, [*got[py + 1 :], *first[1:]]) for x in got[py :: py]]
+    held = held_of([later[k // py - 1] if k >= py and k % py == 0 else x for k, x in enumerate(got)], ())
     moved = pack(first)
     moved = [moved, *across(moved)]
     known, sums, turned, flat, buffer = [], [], [], None, None
     by_lower, by_diag, by_sum = ({s: [] for s in range(steps + 1)} for _ in range(3))
     by_diag[0] += [packed[last][0], *first[1:]]
+    by_sum[0] += moved
     for s in range(steps):
         if s > 0:
-            outs = lower_product(s, form, meta, held, known, pieces, own, here, by_lower[s])
+            outs = lower_product(s, form, meta, held, older, known, pieces, own, here, by_lower[s])
             known.append(outs[py:])
             sums = [outs[0]] + [along_plane(outs[e], e, 0) for e in range(1, py)]
-            if s > 0:
-                moved = onward(first, direct, [outs[0]])
             if s >= last - 1:
                 whole = joined(range(s) if s < last else [s - 1], [outs[0]])
                 by_diag[s].append(whole)
@@ -673,7 +690,7 @@
             first = up([gate(x, [products[0]]) for x in packed[s + 2]])
         else:
             first = up([gate(whole, [products[0]])] * py)
-        by_sum[s] += moved + first[1:]
+        by_sum[s] += first[1:]
         arrivals = [along_depth(products[k], -k) for k in range(1, depth)]
         arrivals[-1] = gate(arrivals[-1], by_sum[s])
         total = products[0]
@@ -681,28 +698,25 @@
             total = total + x.astype(F32)
         mine = total.astype(BF16)
         if s < last:
-            held = held_of(moved, [mine])
-            first = [gate(first[0], [mine]), *first[1:]]
-            direct = across(first[0])
-            by_diag[s + 1] += direct
-        else:
-            newest = pack(first, [mine])
-            newest = [newest, *across(newest)]
+            held, older = held_of(moved, [mine]), held
+        ready, moved = moved, pack(first, [mine])
+        moved = [moved, *across(moved)]
+        by_sum[s + 1] += moved if s < last else []
         pieces = [mine] + [along_depth(mine, k) for k in range(1, depth)]
         if s < turns:
             flat, mark = flat_rest(lower_rest, flat, s, turns, block, [mine])
             by_lower[s + 1].append(mark)
         if s == last:
-            buffer, new = write(0, steps, form, meta, moved, buffer, [mine])
+            buffer, new = write(0, steps, form, meta, ready, buffer, [mine])
             turned.append(new)
             by_lower[s + 1].append(new)
     known.append(place(form, meta, pieces, by_lower[steps]))
     whole = joined([last])
     got = up([whole] * py)
     direct = across(got[0])
-    early = rest_product(0, form, meta, turned, flat, (), [whole, *newest])
+    early = rest_product(0, form, meta, turned, flat, (), [whole, *moved])
     got = onward(got, direct, [early[0]])
-    buffer, new = write(last - 1, steps, form, meta, newest, buffer, [early[0]])
+    buffer, new = write(last - 1, steps, form, meta, moved, buffer, [early[0]])
     early = rest_product(last - 1, form, meta, [new], flat, early)
     buffer, *late = last_step(form, meta, got, flat, buffer)
     total = rhs_rest.astype(F32) - early[0] - late[0]

time: 167 us -> 165 us (0.988)
    ppermute x24, waiting for transfers between devices: 19.1 us -> 15.7 us  [along_depth(): return lax.ppermute(x, 'rows', pairs)]
    ppermute x22 -> x19, waiting for transfers between devices: 32.8 us -> 35.7 us  [along_plane(): return lax.ppermute(x, 'rows', pairs)]
    ppermute x22 -> x19, starting transfers between devices: 27.1 us -> 24.8 us  [along_plane(): return lax.ppermute(x, 'rows', pairs)]
    ppermute x24, starting transfers between devices: 28.1 us -> 29.9 us  [along_depth(): return lax.ppermute(x, 'rows', pairs)]
    pallas_call x45 -> x44, Pallas kernels: 50.6 us -> 49.7 us  [call(): pl.pallas_call(run, out_shape=tuple(outs), in_specs=list(specs) + [pl.Blo...]
  transfers between devices with their start and end apart: 59 -> 56, of which waited for: 26 -> 28; matrix products, arithmetic and copies ran while one was open for 0% -> 0% of each run, Pallas kernels for 29% -> 29%
where the time goes in v4:
time: 165 us; the launch traced here: 164 us
  starting transfers between devices  56.3 us (34%)
  waiting for transfers between devices  55.4 us (34%)
  Pallas kernels  49.7 us (30%)
    pallas_call x44, Pallas kernels, call(): pl.pallas_call(run, out_shape=tuple(outs), in_specs=list(specs) + [pl.Blo...  49.7 us
    ppermute x19, waiting for transfers between devices, along_plane(): return lax.ppermute(x, 'rows', pairs)  35.7 us
    ppermute x24, starting transfers between devices, along_depth(): return lax.ppermute(x, 'rows', pairs)  29.9 us
    ppermute x19, starting transfers between devices, along_plane(): return lax.ppermute(x, 'rows', pairs)  24.8 us
    ppermute x24, waiting for transfers between devices, along_depth(): return lax.ppermute(x, 'rows', pairs)  15.7 us
    ppermute x13, waiting for transfers between devices, along_cols(): lax.ppermute(x, 'cols', [(i, (i + k) % n_cols) for i in range(n_cols)])  4.07 us
  transfers between devices with their start and end apart: 56, of which 28 were waited for; matrix products, arithmetic and copies ran while one was open for 0% of the time, Pallas kernels for 29%

profile of v4, /device:TPU:0, one launch (start us, length us, event | category | flops | bytes accessed | tf_op | source)
XLA Modules:
  0.0 164.1 jit_solution(1112525119331305417)
XLA Ops:
  1.9 3.0 %collective-permute-start = (bf16[128,768]{1,0:T(8,128)(2,1)S(1)}, bf16[128,768]{1,0:T(8,128)(2,1)S(1)}, u32[]{:S(2)}, u32[]{:S(2)}) collective-permute-start(bf16[128,768]{1,0:T(8,128)(2,1)S(1)} %get-tuple-element.61), channel_id=1, source_target_pairs={{0,4},{2,6},{4,0},{6,2},{8,12},{10,14},{12,8},{14,10},{16,20},{18,... | collective-permute-start | bytes 589832 | tf_op jit(solution)/shard_map/ppermute | solution.py:628
  5.0 1.5 collective-permute-start.3
  6.4 3.4 %shard_map.68 = (bf16[128,1024]{1,0:T(8,128)(2,1)S(1)}, bf16[128,1024]{1,0:T(8,128)(2,1)S(1)}, bf16[128,2048]{1,0:T(8,128)(2,1)S(1)}, bf16[128,2048]{1,0:T(8,128...) custom-call(s32[4]{0:T(128)S(1)} %pad_add_fusion.refs_0_, bf16[4,1024,128]{2,1,0:T(8,128)(2,1)} %refs_1_.3, ...), custom_call_target="tpu_custom_call" | custom-call | bytes 60817536 | tf_op jit(solution)/shard_map/pallas_call | solution.py:149
  9.9 1.7 %collective-permute-start.1 = (bf16[128,1024]{1,0:T(8,128)(2,1)S(1)}, bf16[128,1024]{1,0:T(8,128)(2,1)S(1)}, u32[]{:S(2)}, u32[]{:S(2)}) collective-permute-start(bf16[128,1024]{1,0:T(8,128)(2,1)S(1)} %shard_map.71), channel_id=1, source_target_pairs={{0,4},{2,6},{4,0},{6,2},{8,12},{10,14},{12,8},{14,10},{16,20},{18,... | collective-permute-start | bytes 786440 | tf_op jit(solution)/shard_map/ppermute | solution.py:628
  11.6 1.6 collective-permute-start.4
  13.8 3.8 %collective-permute-done.4.refs_1_.refs_4_ = bf16[128,768]{1,0:T(8,128)(2,1)S(1)} collective-permute-done((bf16[128,768]{1,0:T(8,128)(2,1)S(1)}, bf16[128,768]{1,0:T(8,128)(2,1)S(1)}, u32[]{:S(2)}, u32[]{:S(2)}) %collective-permute-start.4) | collective-permute-done | bytes 196640 | tf_op jit(solution)/shard_map/ppermute | solution.py:628
  18.7 1.6 collective-permute-start.2
  22.5 1.6 collective-permute-start.11
  24.1 2.2 %collective-permute-start.9 = (bf16[256,128]{1,0:T(8,128)(2,1)S(1)}, bf16[256,128]{1,0:T(8,128)(2,1)S(1)}, u32[]{:S(2)}, u32[]{:S(2)}) collective-permute-start(bf16[256,128]{1,0:T(8,128)(2,1)S(1)} %get-tuple-element.66), channel_id=1, source_target_pairs={{0,24},{2,26},{4,28},{6,30},{8,0},{10,2},{12,4},{14,6},{16,8},{18,... | collective-permute-start | bytes 196616 | tf_op jit(solution)/shard_map/ppermute | solution.py:632
  27.1 2.0 %collective-permute-done.11.refs_0_ = bf16[256,128]{1,0:T(8,128)(2,1)S(1)} collective-permute-done((bf16[256,128]{1,0:T(8,128)(2,1)S(1)}, bf16[256,128]{1,0:T(8,128)(2,1)S(1)}, u32[]{:S(2)}, u32[]{:S(2)}) %collective-permute-start.11) | collective-permute-done | bytes 65568 | tf_op jit(solution)/shard_map/ppermute | solution.py:632
  29.1 3.6 %collective-permute-done.2.refs_2_.refs_1_ = bf16[2,128,1024]{2,1,0:T(8,128)(2,1)S(1)} collective-permute-done((bf16[2,128,1024]{2,1,0:T(8,128)(2,1)S(1)}, bf16[2,128,1024]{2,1,0:T(8,128)(2,1)S(1)}, u32[]{:S(2)}, u32[]{:S(2)}) %collective-permute-start.2) | collective-permute-done | bytes 524320 | tf_op jit(solution)/shard_map/ppermute | solution.py:628
  32.7 2.5 %collective-permute-done.12.refs_3_.refs_1_ = bf16[128,2048]{1,0:T(8,128)(2,1)S(1)} collective-permute-done((bf16[128,2048]{1,0:T(8,128)(2,1)S(1)}, bf16[128,2048]{1,0:T(8,128)(2,1)S(1)}, u32[]{:S(2)}, u32[]{:S(2)}) %collective-permute-start.12) | collective-permute-done | bytes 524320 | tf_op jit(solution)/shard_map/ppermute | solution.py:628
  35.4 1.6 collective-permute-start.22
  37.0 3.6 %collective-permute-start.16 = (bf16[256,128]{1,0:T(8,128)(2,1)S(1)}, bf16[256,128]{1,0:T(8,128)(2,1)S(1)}, u32[]{:S(2)}, u32[]{:S(2)}) collective-permute-start(bf16[256,128]{1,0:T(8,128)(2,1)S(1)} %add_convert_fusion.3.refs_2_.refs_1_.refs_3_), channel_id=1, source_target_pairs={{0,24},{2,26},{4,28},{6,30},{8,0},{10,2},{12,4},{14,6},{16,8},{18,... | collective-permute-start | bytes 196616 | tf_op jit(solution)/shard_map/ppermute | solution.py:632
  41.6 5.1 %shard_map.79 = (bf16[4,1536,1024]{2,1,0:T(8,128)(2,1)}, f32[8,128]{1,0:T(8,128)S(1)}) custom-call(bf16[1536,4,1024]{2,1,0:T(4,128)(2,1)} %refs_0_.5, bf16[256,128]{1,0:T(8,128)(2,1)S(1)} %add_convert_fusion.3.refs_2_.refs_1_.refs_3_), custom_call_target="tpu_custom_call" | custom-call | bytes 25169920 | tf_op jit(solution)/shard_map/pallas_call | solution.py:149
  49.6 4.1 %collective-permute-done.17.refs_4_ = bf16[512,128]{1,0:T(8,128)(2,1)S(1)} collective-permute-done((bf16[512,128]{1,0:T(8,128)(2,1)S(1)}, bf16[512,128]{1,0:T(8,128)(2,1)S(1)}, u32[]{:S(2)}, u32[]{:S(2)}) %collective-permute-start.17) | collective-permute-done | bytes 131104 | tf_op jit(solution)/shard_map/ppermute | solution.py:628
  56.0 1.5 collective-permute-start.21
  57.5 2.3 %collective-permute-start.19 = (bf16[256,128]{1,0:T(8,128)(2,1)S(1)}, bf16[256,128]{1,0:T(8,128)(2,1)S(1)}, u32[]{:S(2)}, u32[]{:S(2)}) collective-permute-start(bf16[256,128]{1,0:T(8,128)(2,1)S(1)} %get-tuple-element.76), channel_id=1, source_target_pairs={{0,24},{2,26},{4,28},{6,30},{8,0},{10,2},{12,4},{14,6},{16,8},{18,... | collective-permute-start | bytes 196616 | tf_op jit(solution)/shard_map/ppermute | solution.py:632
  62.1 2.7 %collective-permute-done.18.refs_3_.refs_1_ = bf16[128,1536]{1,0:T(8,128)(2,1)S(1)} collective-permute-done((bf16[128,1536]{1,0:T(8,128)(2,1)S(1)}, bf16[128,1536]{1,0:T(8,128)(2,1)S(1)}, u32[]{:S(2)}, u32[]{:S(2)}) %collective-permute-start.18) | collective-permute-done | bytes 393248 | tf_op jit(solution)/shard_map/ppermute | solution.py:628
  65.9 1.8 %collective-permute-start.27 = (bf16[256,128]{1,0:T(8,128)(2,1)S(1)}, bf16[256,128]{1,0:T(8,128)(2,1)S(1)}, u32[]{:S(2)}, u32[]{:S(2)}) collective-permute-start(bf16[256,128]{1,0:T(8,128)(2,1)S(1)} %add_convert_fusion.2.refs_2_.refs_5_), channel_id=1, source_target_pairs={{0,24},{2,26},{4,28},{6,30},{8,0},{10,2},{12,4},{14,6},{16,8},{18,... | collective-permute-start | bytes 196616 | tf_op jit(solution)/shard_map/ppermute | solution.py:632
  69.0 5.1 %shard_map.89 = (bf16[4,1536,1024]{2,1,0:T(8,128)(2,1)}, f32[8,128]{1,0:T(8,128)S(1)}) custom-call(bf16[1536,4,1024]{2,1,0:T(4,128)(2,1)} %refs_0_.5, bf16[4,1536,1024]{2,1,0:T(8,128)(2,1)} %get-tuple-element.82.refs_1_, bf16[256,128]{1,0:T(8,128)(2,1)S(1)} %add_convert_fusion.2.refs_2_.refs_5_), custom_call_target="tpu_custom_call", output_to_operand_aliasing={{0}: (1, {})} | custom-call | bytes 37752832 | tf_op jit(solution)/shard_map/pallas_call | solution.py:149
  75.0 1.3 shard_map.90
  78.4 3.9 %collective-permute-done.28.refs_4_ = bf16[512,128]{1,0:T(8,128)(2,1)S(1)} collective-permute-done((bf16[512,128]{1,0:T(8,128)(2,1)S(1)}, bf16[512,128]{1,0:T(8,128)(2,1)S(1)}, u32[]{:S(2)}, u32[]{:S(2)}) %collective-permute-start.28) | collective-permute-done | bytes 131104 | tf_op jit(solution)/shard_map/ppermute | solution.py:628
  84.4 1.3 collective-permute-start.33
  85.7 2.5 %collective-permute-start.31 = (bf16[256,128]{1,0:T(8,128)(2,1)S(1)}, bf16[256,128]{1,0:T(8,128)(2,1)S(1)}, u32[]{:S(2)}, u32[]{:S(2)}) collective-permute-start(bf16[256,128]{1,0:T(8,128)(2,1)S(1)} %get-tuple-element.89), channel_id=1, source_target_pairs={{0,24},{2,26},{4,28},{6,30},{8,0},{10,2},{12,4},{14,6},{16,8},{18,... | collective-permute-start | bytes 196616 | tf_op jit(solution)/shard_map/ppermute | solution.py:632
  88.2 2.9 %collective-permute-done.33.refs_0_ = bf16[256,128]{1,0:T(8,128)(2,1)S(1)} collective-permute-done((bf16[256,128]{1,0:T(8,128)(2,1)S(1)}, bf16[256,128]{1,0:T(8,128)(2,1)S(1)}, u32[]{:S(2)}, u32[]{:S(2)}) %collective-permute-start.33) | collective-permute-done | bytes 65568 | tf_op jit(solution)/shard_map/ppermute | solution.py:632
  91.1 5.8 %collective-permute-done.34.refs_3_.refs_1_ = bf16[1024,256]{1,0:T(8,128)(2,1)S(1)} collective-permute-done((bf16[1024,256]{1,0:T(8,128)(2,1)S(1)}, bf16[1024,256]{1,0:T(8,128)(2,1)S(1)}, u32[]{:S(2)}, u32[]{:S(2)}) %collective-permute-start.34) | collective-permute-done | bytes 524320 | tf_op jit(solution)/shard_map/ppermute | solution.py:628
  97.2 1.6 collective-permute-start.44
  98.8 2.0 %collective-permute-start.38 = (bf16[256,128]{1,0:T(8,128)(2,1)S(1)}, bf16[256,128]{1,0:T(8,128)(2,1)S(1)}, u32[]{:S(2)}, u32[]{:S(2)}) collective-permute-start(bf16[256,128]{1,0:T(8,128)(2,1)S(1)} %add_convert_fusion.1.refs_2_.refs_9_), channel_id=1, source_target_pairs={{0,24},{2,26},{4,28},{6,30},{8,0},{10,2},{12,4},{14,6},{16,8},{18,... | collective-permute-start | bytes 196616 | tf_op jit(solution)/shard_map/ppermute | solution.py:632
  102.3 5.1 %shard_map.96 = (bf16[4,1536,1024]{2,1,0:T(8,128)(2,1)}, f32[8,128]{1,0:T(8,128)S(1)}) custom-call(bf16[1536,4,1024]{2,1,0:T(4,128)(2,1)} %refs_0_.5, bf16[4,1536,1024]{2,1,0:T(8,128)(2,1)} %get-tuple-element.92.refs_1_, bf16[256,128]{1,0:T(8,128)(2,1)S(1)} %add_convert_fusion.1.refs_2_.refs_9_), custom_call_target="tpu_custom_call", output_to_operand_aliasing={{0}: (1, {})} | custom-call | bytes 37752832 | tf_op jit(solution)/shard_map/pallas_call | solution.py:149
  108.1 1.5 shard_map.97
  111.7 4.0 %collective-permute-done.39.refs_4_ = bf16[512,128]{1,0:T(8,128)(2,1)S(1)} collective-permute-done((bf16[512,128]{1,0:T(8,128)(2,1)S(1)}, bf16[512,128]{1,0:T(8,128)(2,1)S(1)}, u32[]{:S(2)}, u32[]{:S(2)}) %collective-permute-start.39) | collective-permute-done | bytes 131104 | tf_op jit(solution)/shard_map/ppermute | solution.py:628
  117.8 1.3 collective-permute-start.43
  119.1 2.5 %collective-permute-start.41 = (bf16[256,128]{1,0:T(8,128)(2,1)S(1)}, bf16[256,128]{1,0:T(8,128)(2,1)S(1)}, u32[]{:S(2)}, u32[]{:S(2)}) collective-permute-start(bf16[256,128]{1,0:T(8,128)(2,1)S(1)} %get-tuple-element.99), channel_id=1, source_target_pairs={{0,24},{2,26},{4,28},{6,30},{8,0},{10,2},{12,4},{14,6},{16,8},{18,... | collective-permute-start | bytes 196616 | tf_op jit(solution)/shard_map/ppermute | solution.py:632
  122.8 1.7 %collective-permute-done.43.refs_0_ = bf16[256,128]{1,0:T(8,128)(2,1)S(1)} collective-permute-done((bf16[256,128]{1,0:T(8,128)(2,1)S(1)}, bf16[256,128]{1,0:T(8,128)(2,1)S(1)}, u32[]{:S(2)}, u32[]{:S(2)}) %collective-permute-start.43) | collective-permute-done | bytes 65568 | tf_op jit(solution)/shard_map/ppermute | solution.py:632
  124.6 2.6 %collective-permute-done.42 = bf16[256,128]{1,0:T(8,128)(2,1)S(1)} collective-permute-done((bf16[256,128]{1,0:T(8,128)(2,1)S(1)}, bf16[256,128]{1,0:T(8,128)(2,1)S(1)}, u32[]{:S(2)}, u32[]{:S(2)}) %collective-permute-start.42) | collective-permute-done | bytes 65568 | tf_op jit(solution)/shard_map/ppermute | solution.py:632
  127.9 1.9 %collective-permute-start.48 = (bf16[256,128]{1,0:T(8,128)(2,1)S(1)}, bf16[256,128]{1,0:T(8,128)(2,1)S(1)}, u32[]{:S(2)}, u32[]{:S(2)}) collective-permute-start(bf16[256,128]{1,0:T(8,128)(2,1)S(1)} %add_convert_fusion.refs_3_.refs_1_.refs_2_), channel_id=1, source_target_pairs={{0,24},{2,26},{4,28},{6,30},{8,0},{10,2},{12,4},{14,6},{16,8},{18,... | collective-permute-start | bytes 196616 | tf_op jit(solution)/shard_map/ppermute | solution.py:632
  130.3 2.6 %shard_map.103 = (bf16[4,1024,512]{2,1,0:T(8,128)(2,1)}, bf16[2,512,1024]{2,1,0:T(8,128)(2,1)S(1)}) custom-call(s32[4]{0:T(128)S(1)} %pad_add_fusion.refs_0_, bf16[2,1024,256]{2,1,0:T(8,128)(2,1)S(1)} %shard_map.100.refs_1_, bf16[2,1024,256]{2,1,0:T(8,128)(2,1)S(1)} %collective-permute-done.44.refs_2_, ...), custom_call_target="tpu_custom_call" | custom-call | bytes 8388624 | tf_op jit(solution)/shard_map/pallas_call | solution.py:149
  132.9 3.2 %collective-permute-done.47.refs_3_ = bf16[256,128]{1,0:T(8,128)(2,1)S(1)} collective-permute-done((bf16[256,128]{1,0:T(8,128)(2,1)S(1)}, bf16[256,128]{1,0:T(8,128)(2,1)S(1)}, u32[]{:S(2)}, u32[]{:S(2)}) %collective-permute-start.47) | collective-permute-done | bytes 65568 | tf_op jit(solution)/shard_map/ppermute | solution.py:632
  136.8 1.3 collective-permute-done.49.refs_2_
  138.8 1.6 collective-permute-start.52
  141.3 5.8 %shard_map.107 = (f32[256,1536]{1,0:T(8,128)S(1)}, bf16[256,1536]{1,0:T(8,128)(2,1)S(1)}) custom-call(s32[4]{0:T(128)S(1)} %pad_add_fusion.refs_0_, bf16[2,512,1024]{2,1,0:T(8,128)(2,1)S(1)} %get-tuple-element.102.refs_5_.refs_1_, bf16[4,1536,1024]{2,1,0:T(8,128)(2,1)} %get-tuple-element.105.refs_2_.refs_5_, ...), custom_call_target="tpu_custom_call" | custom-call | flops 3221225472 | bytes 17039376 | tf_op jit(solution)/shard_map/pallas_call | solution.py:149
  147.1 1.3 collective-permute-done.50.refs_0_
  148.9 1.9 %shard_map.109 = (bf16[4,1024,512]{2,1,0:T(8,128)(2,1)}, bf16[1,512,1024]{2,1,0:T(8,128)(2,1)S(1)}) custom-call(s32[4]{0:T(128)S(1)} %pad_add_fusion.refs_0_, bf16[2,512,256]{2,1,0:T(8,128)(2,1)S(1)} %shard_map.106.refs_4_.refs_1_, bf16[2,512,256]{2,1,0:T(8,128)(2,1)S(1)} %collective-permute-done.51.refs_5_.refs_2_, ...), custom_call_target="tpu_custom_call", output_to_operand_aliasing={{0}: (3, {})} | custom-call | bytes 10485776 | tf_op jit(solution)/shard_map/pallas_call | solution.py:149
  150.8 3.7 %shard_map.111 = (f32[256,1536]{1,0:T(8,128)S(1)}, bf16[256,1536]{1,0:T(8,128)(2,1)S(1)}) custom-call(s32[4]{0:T(128)S(1)} %pad_add_fusion.refs_0_, bf16[1,512,1024]{2,1,0:T(8,128)(2,1)S(1)} %get-tuple-element.110.refs_1_, bf16[4,1536,1024]{2,1,0:T(8,128)(2,1)} %get-tuple-element.105.refs_2_.refs_5_, ...), custom_call_target="tpu_custom_call" | custom-call | flops 1610612736 | bytes 18350096 | tf_op jit(solution)/shard_map/pallas_call | solution.py:149
  155.6 4.8 %shard_map.110 = (bf16[4,1024,512]{2,1,0:T(8,128)(2,1)}, f32[256,1536]{1,0:T(8,128)S(1)}, bf16[256,1536]{1,0:T(8,128)(2,1)S(1)}) custom-call(s32[4]{0:T(128)S(1)} %pad_add_fusion.refs_0_, bf16[512,256]{1,0:T(8,128)(2,1)S(1)} %shard_map.105.refs_3_.refs_1_, bf16[512,256]{1,0:T(8,128)(2,1)S(1)} %shard_map.108.refs_2_, ...), custom_call_target="tpu_custom_call", output_to_operand_aliasing={{0}: (6, {})} | custom-call | flops 1610612736 | bytes 24379408 | tf_op jit(solution)/shard_map/pallas_call | solution.py:149
  160.4 2.3 %collective-permute-done.55 = bf16[256,1536]{1,0:T(8,128)(2,1)S(1)} collective-permute-done((bf16[256,1536]{1,0:T(8,128)(2,1)S(1)}, bf16[256,1536]{1,0:T(8,128)(2,1)S(1)}, u32[]{:S(2)}, u32[]{:S(2)}) %collective-permute-start.55) | collective-permute-done | bytes 786464 | tf_op jit(solution)/shard_map/ppermute | solution.py:635
  162.7 1.4 subtract_convert_fusion
  (118 shorter events, 35.3 us)
Async XLA Ops:
  1.9 7.9 %collective-permute-start = (bf16[128,768]{1,0:T(8,128)(2,1)S(1)}, bf16[128,768]{1,0:T(8,128)(2,1)S(1)}, u32[]{:S(2)}, u32[]{:S(2)}) collective-permute-start(bf16[128,768]{1,0:T(8,128)(2,1)S(1)} %get-tuple-element.61), channel_id=1, source_target_pairs={{0,4},{2,6},{4,0},{6,2},{8,12},{10,14},{12,8},{14,10},{16,20},{18,... | collective-permute-start | bytes 589832 | tf_op jit(solution)/shard_map/ppermute | solution.py:628
  5.0 8.9 %collective-permute-start.3 = (bf16[128,1152]{1,0:T(8,128)(2,1)S(1)}, bf16[128,1152]{1,0:T(8,128)(2,1)S(1)}, u32[]{:S(2)}, u32[]{:S(2)}) collective-permute-start(bf16[128,1152]{1,0:T(8,128)(2,1)S(1)} %get-tuple-element.64), channel_id=1, source_target_pairs={{0,2},{2,0},{4,6},{6,4},{8,10},{10,8},{12,14},{14,12},{16,18},{18,... | collective-permute-start | bytes 884744 | tf_op jit(solution)/shard_map/ppermute | solution.py:628
  9.9 7.8 %collective-permute-start.1 = (bf16[128,1024]{1,0:T(8,128)(2,1)S(1)}, bf16[128,1024]{1,0:T(8,128)(2,1)S(1)}, u32[]{:S(2)}, u32[]{:S(2)}) collective-permute-start(bf16[128,1024]{1,0:T(8,128)(2,1)S(1)} %shard_map.71), channel_id=1, source_target_pairs={{0,4},{2,6},{4,0},{6,2},{8,12},{10,14},{12,8},{14,10},{16,20},{18,... | collective-permute-start | bytes 786440 | tf_op jit(solution)/shard_map/ppermute | solution.py:628
  11.6 6.0 %collective-permute-start.4 = (bf16[128,768]{1,0:T(8,128)(2,1)S(1)}, bf16[128,768]{1,0:T(8,128)(2,1)S(1)}, u32[]{:S(2)}, u32[]{:S(2)}) collective-permute-start(bf16[128,768]{1,0:T(8,128)(2,1)S(1)} %shard_map.73.refs_2_), channel_id=1, source_target_pairs={{0,2},{2,0},{4,6},{6,4},{8,10},{10,8},{12,14},{14,12},{16,18},{18,... | collective-permute-start | bytes 589832 | tf_op jit(solution)/shard_map/ppermute | solution.py:628
  18.7 14.0 %collective-permute-start.2 = (bf16[2,128,1024]{2,1,0:T(8,128)(2,1)S(1)}, bf16[2,128,1024]{2,1,0:T(8,128)(2,1)S(1)}, u32[]{:S(2)}, u32[]{:S(2)}) collective-permute-start(bf16[2,128,1024]{2,1,0:T(8,128)(2,1)S(1)} %shard_map.72.refs_1_.refs_0_), channel_id=1, source_target_pairs={{0,2},{2,0},{4,6},{6,4},{8,10},{10,8},{12,14},{14,12},{16,18},{18,... | collective-permute-start | bytes 1572872 | tf_op jit(solution)/shard_map/ppermute | solution.py:628
  21.3 13.8 %collective-permute-start.12 = (bf16[128,2048]{1,0:T(8,128)(2,1)S(1)}, bf16[128,2048]{1,0:T(8,128)(2,1)S(1)}, u32[]{:S(2)}, u32[]{:S(2)}) collective-permute-start(bf16[128,2048]{1,0:T(8,128)(2,1)S(1)} %shard_map.76), channel_id=1, source_target_pairs={{0,4},{2,6},{4,0},{6,2},{8,12},{10,14},{12,8},{14,10},{16,20},{18,... | collective-permute-start | bytes 1572872 | tf_op jit(solution)/shard_map/ppermute | solution.py:628
  22.5 6.6 %collective-permute-start.11 = (bf16[256,128]{1,0:T(8,128)(2,1)S(1)}, bf16[256,128]{1,0:T(8,128)(2,1)S(1)}, u32[]{:S(2)}, u32[]{:S(2)}) collective-permute-start(bf16[256,128]{1,0:T(8,128)(2,1)S(1)} %get-tuple-element.68), channel_id=1, source_target_pairs={{0,8},{2,10},{4,12},{6,14},{8,16},{10,18},{12,20},{14,22},{16,24},... | collective-permute-start | bytes 196616 | tf_op jit(solution)/shard_map/ppermute | solution.py:632
  24.1 11.0 %collective-permute-start.9 = (bf16[256,128]{1,0:T(8,128)(2,1)S(1)}, bf16[256,128]{1,0:T(8,128)(2,1)S(1)}, u32[]{:S(2)}, u32[]{:S(2)}) collective-permute-start(bf16[256,128]{1,0:T(8,128)(2,1)S(1)} %get-tuple-element.66), channel_id=1, source_target_pairs={{0,24},{2,26},{4,28},{6,30},{8,0},{10,2},{12,4},{14,6},{16,8},{18,... | collective-permute-start | bytes 196616 | tf_op jit(solution)/shard_map/ppermute | solution.py:632
  26.3 8.8 %collective-permute-start.10 = (bf16[256,128]{1,0:T(8,128)(2,1)S(1)}, bf16[256,128]{1,0:T(8,128)(2,1)S(1)}, u32[]{:S(2)}, u32[]{:S(2)}) collective-permute-start(bf16[256,128]{1,0:T(8,128)(2,1)S(1)} %get-tuple-element.67), channel_id=1, source_target_pairs={{0,16},{2,18},{4,20},{6,22},{8,24},{10,26},{12,28},{14,30},{16,0},... | collective-permute-start | bytes 196616 | tf_op jit(solution)/shard_map/ppermute | solution.py:632
  35.3 12.2 %collective-permute-start.13 = (bf16[4,128,1024]{2,1,0:T(8,128)(2,1)S(1)}, bf16[4,128,1024]{2,1,0:T(8,128)(2,1)S(1)}, u32[]{:S(2)}, u32[]{:S(2)}) collective-permute-start(bf16[4,128,1024]{2,1,0:T(8,128)(2,1)S(1)} %shard_map.78.refs_1_), channel_id=1, source_target_pairs={{0,1},{1,0},{2,3},{3,2},{4,5},{5,4},{6,7},{7,6},{8,9},{9,8},{10,11... | collective-permute-start | bytes 3145736 | tf_op jit(solution)/shard_map/ppermute | solution.py:635
  35.4 25.6 %collective-permute-start.22 = (bf16[2,128,2048]{2,1,0:T(8,128)(2,1)S(1)}, bf16[2,128,2048]{2,1,0:T(8,128)(2,1)S(1)}, u32[]{:S(2)}, u32[]{:S(2)}) collective-permute-start(bf16[2,128,2048]{2,1,0:T(8,128)(2,1)S(1)} %shard_map.85.refs_1_.refs_0_), channel_id=1, source_target_pairs={{0,2},{2,0},{4,6},{6,4},{8,10},{10,8},{12,14},{14,12},{16,18},{18,... | collective-permute-start | bytes 3145736 | tf_op jit(solution)/shard_map/ppermute | solution.py:628
  37.0 9.7 %collective-permute-start.16 = (bf16[256,128]{1,0:T(8,128)(2,1)S(1)}, bf16[256,128]{1,0:T(8,128)(2,1)S(1)}, u32[]{:S(2)}, u32[]{:S(2)}) collective-permute-start(bf16[256,128]{1,0:T(8,128)(2,1)S(1)} %add_convert_fusion.3.refs_2_.refs_1_.refs_3_), channel_id=1, source_target_pairs={{0,24},{2,26},{4,28},{6,30},{8,0},{10,2},{12,4},{14,6},{16,8},{18,... | collective-permute-start | bytes 196616 | tf_op jit(solution)/shard_map/ppermute | solution.py:632
  40.6 6.8 %collective-permute-start.15 = (bf16[256,128]{1,0:T(8,128)(2,1)S(1)}, bf16[256,128]{1,0:T(8,128)(2,1)S(1)}, u32[]{:S(2)}, u32[]{:S(2)}) collective-permute-start(bf16[256,128]{1,0:T(8,128)(2,1)S(1)} %add_convert_fusion.3.refs_2_.refs_1_.refs_3_), channel_id=1, source_target_pairs={{0,16},{2,18},{4,20},{6,22},{8,24},{10,26},{12,28},{14,30},{16,0},... | collective-permute-start | bytes 196616 | tf_op jit(solution)/shard_map/ppermute | solution.py:632
  40.6 6.8 %collective-permute-start.14 = (bf16[256,128]{1,0:T(8,128)(2,1)S(1)}, bf16[256,128]{1,0:T(8,128)(2,1)S(1)}, u32[]{:S(2)}, u32[]{:S(2)}) collective-permute-start(bf16[256,128]{1,0:T(8,128)(2,1)S(1)} %add_convert_fusion.3.refs_2_.refs_1_.refs_3_), channel_id=1, source_target_pairs={{0,8},{2,10},{4,12},{6,14},{8,16},{10,18},{12,20},{14,22},{16,24},... | collective-permute-start | bytes 196616 | tf_op jit(solution)/shard_map/ppermute | solution.py:632
  48.4 5.3 %collective-permute-start.17 = (bf16[512,128]{1,0:T(8,128)(2,1)S(1)}, bf16[512,128]{1,0:T(8,128)(2,1)S(1)}, u32[]{:S(2)}, u32[]{:S(2)}) collective-permute-start(bf16[512,128]{1,0:T(8,128)(2,1)S(1)} %get-tuple-element.73), channel_id=1, source_target_pairs={{0,4},{2,6},{4,0},{6,2},{8,12},{10,14},{12,8},{14,10},{16,20},{18,... | collective-permute-start | bytes 393224 | tf_op jit(solution)/shard_map/ppermute | solution.py:628
  54.8 10.0 %collective-permute-start.18 = (bf16[128,1536]{1,0:T(8,128)(2,1)S(1)}, bf16[128,1536]{1,0:T(8,128)(2,1)S(1)}, u32[]{:S(2)}, u32[]{:S(2)}) collective-permute-start(bf16[128,1536]{1,0:T(8,128)(2,1)S(1)} %shard_map.83), channel_id=1, source_target_pairs={{0,4},{2,6},{4,0},{6,2},{8,12},{10,14},{12,8},{14,10},{16,20},{18,... | collective-permute-start | bytes 1179656 | tf_op jit(solution)/shard_map/ppermute | solution.py:628
  56.0 6.2 %collective-permute-start.21 = (bf16[256,128]{1,0:T(8,128)(2,1)S(1)}, bf16[256,128]{1,0:T(8,128)(2,1)S(1)}, u32[]{:S(2)}, u32[]{:S(2)}) collective-permute-start(bf16[256,128]{1,0:T(8,128)(2,1)S(1)} %get-tuple-element.78), channel_id=1, source_target_pairs={{0,8},{2,10},{4,12},{6,14},{8,16},{10,18},{12,20},{14,22},{16,24},... | collective-permute-start | bytes 196616 | tf_op jit(solution)/shard_map/ppermute | solution.py:632
  57.5 7.3 %collective-permute-start.19 = (bf16[256,128]{1,0:T(8,128)(2,1)S(1)}, bf16[256,128]{1,0:T(8,128)(2,1)S(1)}, u32[]{:S(2)}, u32[]{:S(2)}) collective-permute-start(bf16[256,128]{1,0:T(8,128)(2,1)S(1)} %get-tuple-element.76), channel_id=1, source_target_pairs={{0,24},{2,26},{4,28},{6,30},{8,0},{10,2},{12,4},{14,6},{16,8},{18,... | collective-permute-start | bytes 196616 | tf_op jit(solution)/shard_map/ppermute | solution.py:632
  59.8 5.2 %collective-permute-start.20 = (bf16[256,128]{1,0:T(8,128)(2,1)S(1)}, bf16[256,128]{1,0:T(8,128)(2,1)S(1)}, u32[]{:S(2)}, u32[]{:S(2)}) collective-permute-start(bf16[256,128]{1,0:T(8,128)(2,1)S(1)} %get-tuple-element.77), channel_id=1, source_target_pairs={{0,16},{2,18},{4,20},{6,22},{8,24},{10,26},{12,28},{14,30},{16,0},... | collective-permute-start | bytes 196616 | tf_op jit(solution)/shard_map/ppermute | solution.py:632
  65.2 9.8 %collective-permute-start.24 = (bf16[4,128,2048]{2,1,0:T(8,128)(2,1)S(1)}, bf16[4,128,2048]{2,1,0:T(8,128)(2,1)S(1)}, u32[]{:S(2)}, u32[]{:S(2)}) collective-permute-start(bf16[4,128,2048]{2,1,0:T(8,128)(2,1)S(1)} %shard_map.88.refs_1_.refs_3_), channel_id=1, source_target_pairs={{0,1},{1,0},{2,3},{3,2},{4,5},{5,4},{6,7},{7,6},{8,9},{9,8},{10,11... | collective-permute-start | bytes 6291464 | tf_op jit(solution)/shard_map/ppermute | solution.py:635
  65.3 22.9 %collective-permute-start.23 = (bf16[2,128,1536]{2,1,0:T(8,128)(2,1)S(1)}, bf16[2,128,1536]{2,1,0:T(8,128)(2,1)S(1)}, u32[]{:S(2)}, u32[]{:S(2)}) collective-permute-start(bf16[2,128,1536]{2,1,0:T(8,128)(2,1)S(1)} %shard_map.87.refs_1_.refs_0_), channel_id=1, source_target_pairs={{0,2},{2,0},{4,6},{6,4},{8,10},{10,8},{12,14},{14,12},{16,18},{18,... | collective-permute-start | bytes 2359304 | tf_op jit(solution)/shard_map/ppermute | solution.py:628
  65.9 8.3 %collective-permute-start.27 = (bf16[256,128]{1,0:T(8,128)(2,1)S(1)}, bf16[256,128]{1,0:T(8,128)(2,1)S(1)}, u32[]{:S(2)}, u32[]{:S(2)}) collective-permute-start(bf16[256,128]{1,0:T(8,128)(2,1)S(1)} %add_convert_fusion.2.refs_2_.refs_5_), channel_id=1, source_target_pairs={{0,24},{2,26},{4,28},{6,30},{8,0},{10,2},{12,4},{14,6},{16,8},{18,... | collective-permute-start | bytes 196616 | tf_op jit(solution)/shard_map/ppermute | solution.py:632
  67.7 7.3 %collective-permute-start.26 = (bf16[256,128]{1,0:T(8,128)(2,1)S(1)}, bf16[256,128]{1,0:T(8,128)(2,1)S(1)}, u32[]{:S(2)}, u32[]{:S(2)}) collective-permute-start(bf16[256,128]{1,0:T(8,128)(2,1)S(1)} %add_convert_fusion.2.refs_2_.refs_5_), channel_id=1, source_target_pairs={{0,16},{2,18},{4,20},{6,22},{8,24},{10,26},{12,28},{14,30},{16,0},... | collective-permute-start | bytes 196616 | tf_op jit(solution)/shard_map/ppermute | solution.py:632
  68.3 6.7 %collective-permute-start.25 = (bf16[256,128]{1,0:T(8,128)(2,1)S(1)}, bf16[256,128]{1,0:T(8,128)(2,1)S(1)}, u32[]{:S(2)}, u32[]{:S(2)}) collective-permute-start(bf16[256,128]{1,0:T(8,128)(2,1)S(1)} %add_convert_fusion.2.refs_2_.refs_5_), channel_id=1, source_target_pairs={{0,8},{2,10},{4,12},{6,14},{8,16},{10,18},{12,20},{14,22},{16,24},... | collective-permute-start | bytes 196616 | tf_op jit(solution)/shard_map/ppermute | solution.py:632
  74.2 3.3 %collective-permute-start.29 = (bf16[512,128]{1,0:T(8,128)(2,1)S(1)}, bf16[512,128]{1,0:T(8,128)(2,1)S(1)}, u32[]{:S(2)}, u32[]{:S(2)}) collective-permute-start(bf16[512,128]{1,0:T(8,128)(2,1)S(1)} %get-tuple-element.81.refs_4_.refs_6_), channel_id=1, source_target_pairs={{0,1},{1,0},{2,3},{3,2},{4,5},{5,4},{6,7},{7,6},{8,9},{9,8},{10,11... | collective-permute-start | bytes 393224 | tf_op jit(solution)/shard_map/ppermute | solution.py:635
  76.3 5.9 %collective-permute-start.28 = (bf16[512,128]{1,0:T(8,128)(2,1)S(1)}, bf16[512,128]{1,0:T(8,128)(2,1)S(1)}, u32[]{:S(2)}, u32[]{:S(2)}) collective-permute-start(bf16[512,128]{1,0:T(8,128)(2,1)S(1)} %get-tuple-element.85), channel_id=1, source_target_pairs={{0,4},{2,6},{4,0},{6,2},{8,12},{10,14},{12,8},{14,10},{16,20},{18,... | collective-permute-start | bytes 393224 | tf_op jit(solution)/shard_map/ppermute | solution.py:628
  83.3 13.6 %collective-permute-start.34 = (bf16[1024,256]{1,0:T(8,128)(2,1)S(1)}, bf16[1024,256]{1,0:T(8,128)(2,1)S(1)}, u32[]{:S(2)}, u32[]{:S(2)}) collective-permute-start(bf16[1024,256]{1,0:T(8,128)(2,1)S(1)} %shard_map.93.refs_0_), channel_id=1, source_target_pairs={{0,4},{2,6},{4,0},{6,2},{8,12},{10,14},{12,8},{14,10},{16,20},{18,... | collective-permute-start | bytes 1572872 | tf_op jit(solution)/shard_map/ppermute | solution.py:628
  84.4 6.7 %collective-permute-start.33 = (bf16[256,128]{1,0:T(8,128)(2,1)S(1)}, bf16[256,128]{1,0:T(8,128)(2,1)S(1)}, u32[]{:S(2)}, u32[]{:S(2)}) collective-permute-start(bf16[256,128]{1,0:T(8,128)(2,1)S(1)} %get-tuple-element.91), channel_id=1, source_target_pairs={{0,8},{2,10},{4,12},{6,14},{8,16},{10,18},{12,20},{14,22},{16,24},... | collective-permute-start | bytes 196616 | tf_op jit(solution)/shard_map/ppermute | solution.py:632
  85.7 11.1 %collective-permute-start.31 = (bf16[256,128]{1,0:T(8,128)(2,1)S(1)}, bf16[256,128]{1,0:T(8,128)(2,1)S(1)}, u32[]{:S(2)}, u32[]{:S(2)}) collective-permute-start(bf16[256,128]{1,0:T(8,128)(2,1)S(1)} %get-tuple-element.89), channel_id=1, source_target_pairs={{0,24},{2,26},{4,28},{6,30},{8,0},{10,2},{12,4},{14,6},{16,8},{18,... | collective-permute-start | bytes 196616 | tf_op jit(solution)/shard_map/ppermute | solution.py:632
  88.2 8.6 %collective-permute-start.32 = (bf16[256,128]{1,0:T(8,128)(2,1)S(1)}, bf16[256,128]{1,0:T(8,128)(2,1)S(1)}, u32[]{:S(2)}, u32[]{:S(2)}) collective-permute-start(bf16[256,128]{1,0:T(8,128)(2,1)S(1)} %get-tuple-element.90), channel_id=1, source_target_pairs={{0,16},{2,18},{4,20},{6,22},{8,24},{10,26},{12,28},{14,30},{16,0},... | collective-permute-start | bytes 196616 | tf_op jit(solution)/shard_map/ppermute | solution.py:632
  97.0 11.1 %collective-permute-start.35 = (bf16[4,128,1536]{2,1,0:T(8,128)(2,1)S(1)}, bf16[4,128,1536]{2,1,0:T(8,128)(2,1)S(1)}, u32[]{:S(2)}, u32[]{:S(2)}) collective-permute-start(bf16[4,128,1536]{2,1,0:T(8,128)(2,1)S(1)} %shard_map.95.refs_1_), channel_id=1, source_target_pairs={{0,1},{1,0},{2,3},{3,2},{4,5},{5,4},{6,7},{7,6},{8,9},{9,8},{10,11... | collective-permute-start | bytes 4718600 | tf_op jit(solution)/shard_map/ppermute | solution.py:635
  97.2 25.6 %collective-permute-start.44 = (bf16[2,1024,256]{2,1,0:T(8,128)(2,1)S(1)}, bf16[2,1024,256]{2,1,0:T(8,128)(2,1)S(1)}, u32[]{:S(2)}, u32[]{:S(2)}) collective-permute-start(bf16[2,1024,256]{2,1,0:T(8,128)(2,1)S(1)} %shard_map.100.refs_1_), channel_id=1, source_target_pairs={{0,2},{2,0},{4,6},{6,4},{8,10},{10,8},{12,14},{14,12},{16,18},{18,... | collective-permute-start | bytes 3145736 | tf_op jit(solution)/shard_map/ppermute | solution.py:628
  98.8 8.7 %collective-permute-start.38 = (bf16[256,128]{1,0:T(8,128)(2,1)S(1)}, bf16[256,128]{1,0:T(8,128)(2,1)S(1)}, u32[]{:S(2)}, u32[]{:S(2)}) collective-permute-start(bf16[256,128]{1,0:T(8,128)(2,1)S(1)} %add_convert_fusion.1.refs_2_.refs_9_), channel_id=1, source_target_pairs={{0,24},{2,26},{4,28},{6,30},{8,0},{10,2},{12,4},{14,6},{16,8},{18,... | collective-permute-start | bytes 196616 | tf_op jit(solution)/shard_map/ppermute | solution.py:632
  100.7 7.4 %collective-permute-start.37 = (bf16[256,128]{1,0:T(8,128)(2,1)S(1)}, bf16[256,128]{1,0:T(8,128)(2,1)S(1)}, u32[]{:S(2)}, u32[]{:S(2)}) collective-permute-start(bf16[256,128]{1,0:T(8,128)(2,1)S(1)} %add_convert_fusion.1.refs_2_.refs_9_), channel_id=1, source_target_pairs={{0,16},{2,18},{4,20},{6,22},{8,24},{10,26},{12,28},{14,30},{16,0},... | collective-permute-start | bytes 196616 | tf_op jit(solution)/shard_map/ppermute | solution.py:632
  101.2 6.9 %collective-permute-start.36 = (bf16[256,128]{1,0:T(8,128)(2,1)S(1)}, bf16[256,128]{1,0:T(8,128)(2,1)S(1)}, u32[]{:S(2)}, u32[]{:S(2)}) collective-permute-start(bf16[256,128]{1,0:T(8,128)(2,1)S(1)} %add_convert_fusion.1.refs_2_.refs_9_), channel_id=1, source_target_pairs={{0,8},{2,10},{4,12},{6,14},{8,16},{10,18},{12,20},{14,22},{16,24},... | collective-permute-start | bytes 196616 | tf_op jit(solution)/shard_map/ppermute | solution.py:632
  109.7 5.9 %collective-permute-start.39 = (bf16[512,128]{1,0:T(8,128)(2,1)S(1)}, bf16[512,128]{1,0:T(8,128)(2,1)S(1)}, u32[]{:S(2)}, u32[]{:S(2)}) collective-permute-start(bf16[512,128]{1,0:T(8,128)(2,1)S(1)} %get-tuple-element.95), channel_id=1, source_target_pairs={{0,4},{2,6},{4,0},{6,2},{8,12},{10,14},{12,8},{14,10},{16,20},{18,... | collective-permute-start | bytes 393224 | tf_op jit(solution)/shard_map/ppermute | solution.py:628
  116.7 7.9 %collective-permute-start.45 = (bf16[512,256]{1,0:T(8,128)(2,1)S(1)}, bf16[512,256]{1,0:T(8,128)(2,1)S(1)}, u32[]{:S(2)}, u32[]{:S(2)}) collective-permute-start(bf16[512,256]{1,0:T(8,128)(2,1)S(1)} %shard_map.101.refs_0_), channel_id=1, source_target_pairs={{0,4},{2,6},{4,0},{6,2},{8,12},{10,14},{12,8},{14,10},{16,20},{18,... | collective-permute-start | bytes 786440 | tf_op jit(solution)/shard_map/ppermute | solution.py:628
  117.8 6.7 %collective-permute-start.43 = (bf16[256,128]{1,0:T(8,128)(2,1)S(1)}, bf16[256,128]{1,0:T(8,128)(2,1)S(1)}, u32[]{:S(2)}, u32[]{:S(2)}) collective-permute-start(bf16[256,128]{1,0:T(8,128)(2,1)S(1)} %get-tuple-element.101), channel_id=1, source_target_pairs={{0,8},{2,10},{4,12},{6,14},{8,16},{10,18},{12,20},{14,22},{16,24},... | collective-permute-start | bytes 196616 | tf_op jit(solution)/shard_map/ppermute | solution.py:632
  119.1 5.5 %collective-permute-start.41 = (bf16[256,128]{1,0:T(8,128)(2,1)S(1)}, bf16[256,128]{1,0:T(8,128)(2,1)S(1)}, u32[]{:S(2)}, u32[]{:S(2)}) collective-permute-start(bf16[256,128]{1,0:T(8,128)(2,1)S(1)} %get-tuple-element.99), channel_id=1, source_target_pairs={{0,24},{2,26},{4,28},{6,30},{8,0},{10,2},{12,4},{14,6},{16,8},{18,... | collective-permute-start | bytes 196616 | tf_op jit(solution)/shard_map/ppermute | solution.py:632
  121.6 5.6 %collective-permute-start.42 = (bf16[256,128]{1,0:T(8,128)(2,1)S(1)}, bf16[256,128]{1,0:T(8,128)(2,1)S(1)}, u32[]{:S(2)}, u32[]{:S(2)}) collective-permute-start(bf16[256,128]{1,0:T(8,128)(2,1)S(1)} %get-tuple-element.100), channel_id=1, source_target_pairs={{0,16},{2,18},{4,20},{6,22},{8,24},{10,26},{12,28},{14,30},{16,0},... | collective-permute-start | bytes 196616 | tf_op jit(solution)/shard_map/ppermute | solution.py:632
  127.3 14.0 %collective-permute-start.51 = (bf16[2,512,256]{2,1,0:T(8,128)(2,1)S(1)}, bf16[2,512,256]{2,1,0:T(8,128)(2,1)S(1)}, u32[]{:S(2)}, u32[]{:S(2)}) collective-permute-start(bf16[2,512,256]{2,1,0:T(8,128)(2,1)S(1)} %shard_map.106.refs_4_.refs_1_), channel_id=1, source_target_pairs={{0,2},{2,0},{4,6},{6,4},{8,10},{10,8},{12,14},{14,12},{16,18},{18,... | collective-permute-start | bytes 1572872 | tf_op jit(solution)/shard_map/ppermute | solution.py:628
  127.9 5.1 %collective-permute-start.48 = (bf16[256,128]{1,0:T(8,128)(2,1)S(1)}, bf16[256,128]{1,0:T(8,128)(2,1)S(1)}, u32[]{:S(2)}, u32[]{:S(2)}) collective-permute-start(bf16[256,128]{1,0:T(8,128)(2,1)S(1)} %add_convert_fusion.refs_3_.refs_1_.refs_2_), channel_id=1, source_target_pairs={{0,24},{2,26},{4,28},{6,30},{8,0},{10,2},{12,4},{14,6},{16,8},{18,... | collective-permute-start | bytes 196616 | tf_op jit(solution)/shard_map/ppermute | solution.py:632
  129.8 6.4 %collective-permute-start.47 = (bf16[256,128]{1,0:T(8,128)(2,1)S(1)}, bf16[256,128]{1,0:T(8,128)(2,1)S(1)}, u32[]{:S(2)}, u32[]{:S(2)}) collective-permute-start(bf16[256,128]{1,0:T(8,128)(2,1)S(1)} %add_convert_fusion.refs_3_.refs_1_.refs_2_), channel_id=1, source_target_pairs={{0,16},{2,18},{4,20},{6,22},{8,24},{10,26},{12,28},{14,30},{16,0},... | collective-permute-start | bytes 196616 | tf_op jit(solution)/shard_map/ppermute | solution.py:632
  129.8 6.4 %collective-permute-start.46 = (bf16[256,128]{1,0:T(8,128)(2,1)S(1)}, bf16[256,128]{1,0:T(8,128)(2,1)S(1)}, u32[]{:S(2)}, u32[]{:S(2)}) collective-permute-start(bf16[256,128]{1,0:T(8,128)(2,1)S(1)} %add_convert_fusion.refs_3_.refs_1_.refs_2_), channel_id=1, source_target_pairs={{0,8},{2,10},{4,12},{6,14},{8,16},{10,18},{12,20},{14,22},{16,24},... | collective-permute-start | bytes 196616 | tf_op jit(solution)/shard_map/ppermute | solution.py:632
  138.8 15.8 %collective-permute-start.52 = (bf16[512,256]{1,0:T(8,128)(2,1)S(1)}, bf16[512,256]{1,0:T(8,128)(2,1)S(1)}, u32[]{:S(2)}, u32[]{:S(2)}) collective-permute-start(bf16[512,256]{1,0:T(8,128)(2,1)S(1)} %shard_map.105.refs_3_.refs_1_), channel_id=1, source_target_pairs={{0,2},{2,0},{4,6},{6,4},{8,10},{10,8},{12,14},{14,12},{16,18},{18,... | collective-permute-start | bytes 786440 | tf_op jit(solution)/shard_map/ppermute | solution.py:628
  140.3 8.1 %collective-permute-start.50 = (bf16[512,256]{1,0:T(8,128)(2,1)S(1)}, bf16[512,256]{1,0:T(8,128)(2,1)S(1)}, u32[]{:S(2)}, u32[]{:S(2)}) collective-permute-start(bf16[512,256]{1,0:T(8,128)(2,1)S(1)} %shard_map.105.refs_3_.refs_1_), channel_id=1, source_target_pairs={{0,4},{2,6},{4,0},{6,2},{8,12},{10,14},{12,8},{14,10},{16,20},{18,... | collective-permute-start | bytes 786440 | tf_op jit(solution)/shard_map/ppermute | solution.py:628
  148.4 7.2 %collective-permute-start.53 = (bf16[512,256]{1,0:T(8,128)(2,1)S(1)}, bf16[512,256]{1,0:T(8,128)(2,1)S(1)}, u32[]{:S(2)}, u32[]{:S(2)}) collective-permute-start(bf16[512,256]{1,0:T(8,128)(2,1)S(1)} %shard_map.108.refs_2_), channel_id=1, source_target_pairs={{0,2},{2,0},{4,6},{6,4},{8,10},{10,8},{12,14},{14,12},{16,18},{18,... | collective-permute-start | bytes 786440 | tf_op jit(solution)/shard_map/ppermute | solution.py:628
  154.5 5.9 %collective-permute-start.54 = (bf16[256,1536]{1,0:T(8,128)(2,1)S(1)}, bf16[256,1536]{1,0:T(8,128)(2,1)S(1)}, u32[]{:S(2)}, u32[]{:S(2)}) collective-permute-start(bf16[256,1536]{1,0:T(8,128)(2,1)S(1)} %get-tuple-element.114), channel_id=1, source_target_pairs={{0,1},{1,0},{2,3},{3,2},{4,5},{5,4},{6,7},{7,6},{8,9},{9,8},{10,11... | collective-permute-start | bytes 2359304 | tf_op jit(solution)/shard_map/ppermute | solution.py:635
  (9 other events, 23.0 us)

commit v5 on v3

--- a/solution.py
+++ b/solution.py
@@ -209,23 +209,39 @@
     return outs[: form.py], outs[form.py : -1], outs[-1]
 
 
+def slots(s):
+    return [t for t in range(s) if s < 3 or t > 0], [0] if s > 2 else []
+
+
+def slot_of(s, t):
+    later, ahead = slots(s)
+    return 1 + (later + ahead).index(t)
+
+
 def prep_body(ss, form, meta, diag, lower, *refs):
     py, width = form.py, form.width
-    flat = refs[-1]
+    refs, flat = list(refs[:-1]), refs[-1]
     for i, s in enumerate(ss):
-        outs = refs[i * py : (i + 1) * py]
         flat[...] = jnp.swapaxes(lower[i], 0, 1)
+        later, ahead = slots(s)
+        outs = [refs.pop(0) for _ in range(py)]
+        early = [refs.pop(0) for _ in range(py)] if ahead else []
         for dy in range(py):
             put_diag(form, meta, dy, diag.at[i], outs[dy])
-            at = lax.rem(meta[0] + dy, py) * width
-            for t in range(s):
-                outs[dy][:, (1 + t) * width : (2 + t) * width] = flat[t, :, pl.ds(pl.multiple_of(at, width), width)]
+            at = pl.ds(pl.multiple_of(lax.rem(meta[0] + dy, py) * width, width), width)
+            for j, t in enumerate(later):
+                outs[dy][:, (1 + j) * width : (2 + j) * width] = flat[t, :, at]
+            for j, t in enumerate(ahead):
+                early[dy][:, j * width : (j + 1) * width] = flat[t, :, at]
 
 
 def prep(ss, form, meta, diag_inverse, lower_pivot, after=()):
     width, eqs, share = form.width, form.eqs, form.py * form.width
     steps, count = lower_pivot.shape[0], len(ss)
-    dims = [(eqs, (s + 1) * width) for s in ss for _ in range(form.py)]
+    dims = []
+    for s in ss:
+        later, ahead = slots(s)
+        dims += [(eqs, (1 + len(later)) * width)] * form.py + [(eqs, len(ahead) * width)] * (form.py if ahead else 0)
     outs = call(
         functools.partial(prep_body, ss, form),
         [shaped(d, BF16) for d in dims],
@@ -243,21 +259,32 @@
         grid=(1,),
         out_specs=tuple(pl.BlockSpec(d, lambda i: (0, 0)) for d in dims),
     )
-    return {s: outs[i * form.py : (i + 1) * form.py] for i, s in enumerate(ss)}
-
-
-def pack_body(count, *refs):
-    for k, part in enumerate(take(list(refs), count)):
-        refs[-1][k] = part[...]
-
-
-def pack(parts, after=()):
+    packed, ahead, outs = {}, {}, list(outs)
+    for s in ss:
+        packed[s] = [outs.pop(0) for _ in range(form.py)]
+        if slots(s)[1]:
+            ahead[s] = [outs.pop(0) for _ in range(form.py)]
+    return packed, ahead
+
+
+def pack_body(count, first, *refs):
+    refs = list(refs)
+    for k, part in enumerate(take(refs, count)):
+        refs[-1][k, :, :first] = part[...]
+    for k in range(len(refs) - 1):
+        refs[-1][k, :, first:] = refs[k][...]
+
+
+def pack(parts, after=(), beside=()):
     count = sum(1 if x.ndim == 2 else x.shape[0] for x in parts)
-    return call(
-        functools.partial(pack_body, count),
-        [shaped((count, *parts[0].shape[-2:]), BF16)],
-        parts,
-        [WHOLE] * len(parts),
+    rows, first = parts[0].shape[-2:]
+    lanes = first + (beside[0].shape[-1] if beside else 0)
+    ins = [*parts, *beside]
+    return call(
+        functools.partial(pack_body, count, first),
+        [shaped((count, rows, lanes), BF16)],
+        ins,
+        [WHOLE] * len(ins),
         after=after,
         weight=WEIGHT,
     )[0]
@@ -334,7 +361,7 @@
     total = None
     for t, blocks in enumerate(known + [newest]):
         for c in range(n_cols):
-            lanes = slice((1 + t) * width, (2 + t) * width)
+            lanes = slice(slot_of(s, t) * width, (slot_of(s, t) + 1) * width)
             rows = jnp.concatenate([held[c * chips + k][:, lanes] for k in range(chips)], axis=0)
             term = jnp.dot(rows, blocks[c][...], preferred_element_type=F32)
             total = term if total is None else total + term
@@ -488,11 +515,11 @@
     )
 
 
-def rest_body(form, orders, counts, running, meta, *refs):
+def rest_body(form, counts, running, meta, *refs):
     turned, lower, refs = refs[: len(counts)], refs[len(counts)], refs[len(counts) + 1 :]
     before, outs = refs[:running], refs[running:]
     sides = form.px * form.sides
-    for order, out in zip(orders, outs):
+    for order, out in enumerate(outs):
         at = pl.multiple_of(lax.rem(meta[3] + order, form.n_cols) * sides, sides)
         total, t = None, 0
         for x, count in zip(turned, counts):
@@ -511,10 +538,10 @@
     counts = [x.shape[0] for x in turned]
     count = sum(counts)
     sides = form.px * form.sides
-    block = max(n for n in (512, 384, 256, 128) if rest % n == 0)
+    block = max(n for n in (768, 512, 384, 256, 128) if rest % n == 0)
     side_block = pl.BlockSpec((sides, block), lambda i: (0, i))
     return call(
-        functools.partial(rest_body, form, orders, counts, len(before)),
+        functools.partial(rest_body, form, counts, len(before)),
         [shaped((sides, rest), F32 if order == 0 else BF16) for order in orders],
         [meta, *turned, pltpu.with_memory_space_constraint(lower, pltpu.HBM), *before],
         [SMALL]
@@ -528,10 +555,10 @@
     )
 
 
-def last_body(form, meta, *refs):
+def last_body(form, running, meta, *refs):
     refs = list(refs)
     parts = take(refs, form.chips)
-    lower, _, out, *sums, turned = refs
+    lower, before, (out, *sums, turned) = refs[0], refs[1 : 1 + running], refs[2 + running :]
 
     @pl.when(pl.program_id(0) == 0)
     def _():
@@ -540,29 +567,34 @@
     sides = form.px * form.sides
     for order, to in enumerate(sums):
         at = pl.multiple_of(lax.rem(meta[3] + order, form.n_cols) * sides, sides)
-        to[...] = nt_dot(turned[0, pl.ds(at, sides), :], lower[0]).astype(to.dtype)
-
-
-def last_step(form, meta, parts, lower, buffer):
+        total = nt_dot(turned[0, pl.ds(at, sides), :], lower[0])
+        if running:
+            total = total + before[order][...].astype(F32)
+        to[...] = total.astype(to.dtype)
+
+
+def late_step(s, form, meta, parts, lower, buffer, before=(), after=()):
     steps, rest, share = lower.shape
     total, sides = form.px * form.n_cols * form.sides, form.px * form.sides
-    block = max(n for n in (512, 384, 256, 128) if rest % n == 0)
+    block = max(n for n in (768, 512, 384, 256, 128) if rest % n == 0)
     lower = pltpu.with_memory_space_constraint(lower, pltpu.HBM)
     side_block = pl.BlockSpec((sides, block), lambda i: (0, i))
     return call(
-        functools.partial(last_body, form),
+        functools.partial(last_body, form, len(before)),
         [pltpu.HBM((steps, share, total), BF16)]
         + [shaped((sides, rest), F32 if order == 0 else BF16) for order in range(form.n_cols)],
-        [meta, *parts, lower, buffer],
+        [meta, *parts, lower, *before, buffer],
         [SMALL]
         + [pl.BlockSpec(x.shape, lambda i, n=x.ndim: (0,) * n) for x in parts]
-        + [pl.BlockSpec((1, block, share), lambda i: (steps - 1, i, 0))]
+        + [pl.BlockSpec((1, block, share), lambda i: (s, i, 0))]
+        + [side_block] * len(before)
         + [pl.BlockSpec(memory_space=pltpu.HBM)],
         flops=2 * share * total * rest,
         scratch=[pltpu.VMEM((1, total, share), BF16)],
+        after=after,
         grid=(rest // block,),
-        out_specs=(pl.BlockSpec((1, share, total), lambda i: (steps - 1, 0, 0)), *[side_block] * form.n_cols),
-        input_output_aliases={len(parts) + 2: 0},
+        out_specs=(pl.BlockSpec((1, share, total), lambda i: (s, 0, 0)), *[side_block] * form.n_cols),
+        input_output_aliases={len(parts) + 2 + len(before): 0},
     )
 
 
@@ -650,21 +682,22 @@
     near, far, own = start(form, meta, diag_inverse, rhs_pivot)
     got = up(near)
     here = [along_plane(x, 0, dx + 1) for dx, x in enumerate(far)]
-    held = held_of(onward(got, here), ())
-    packed = prep(tuple(range(1, steps)), form, meta, diag_inverse, lower_pivot)
-    first = up([gate(x, here + got[1:]) for x in packed[1]])
+    packed, ahead = prep(tuple(range(1, steps)), form, meta, diag_inverse, lower_pivot)
+    first = up([gate(x, got[1:]) for x in packed[1]])
+    got = onward(got, here, [packed[1][0]])
+    later = [gate(x, [*got[py + 1 :], *first[1:]]) for x in got[py :: py]]
+    held = held_of([later[k // py - 1] if k >= py and k % py == 0 else x for k, x in enumerate(got)], ())
     moved = pack(first)
     moved = [moved, *across(moved)]
     known, sums, turned, flat, buffer = [], [], [], None, None
     by_lower, by_diag, by_sum = ({s: [] for s in range(steps + 1)} for _ in range(3))
     by_diag[0] += [packed[last][0], *first[1:]]
+    by_sum[0] += moved
     for s in range(steps):
         if s > 0:
             outs = lower_product(s, form, meta, held, known, pieces, own, here, by_lower[s])
             known.append(outs[py:])
             sums = [outs[0]] + [along_plane(outs[e], e, 0) for e in range(1, py)]
-            if s > 0:
-                moved = onward(first, direct, [outs[0]])
             if s >= last - 1:
                 whole = joined(range(s) if s < last else [s - 1], [outs[0]])
                 by_diag[s].append(whole)
@@ -673,7 +706,10 @@
             first = up([gate(x, [products[0]]) for x in packed[s + 2]])
         else:
             first = up([gate(whole, [products[0]])] * py)
-        by_sum[s] += moved + first[1:]
+        by_sum[s] += first[1:]
+        if s < turns and s % 2 == 0:
+            flat, mark = flat_rest(lower_rest, flat, s, turns, block, [products[0]])
+            by_sum[s].append(mark)
         arrivals = [along_depth(products[k], -k) for k in range(1, depth)]
         arrivals[-1] = gate(arrivals[-1], by_sum[s])
         total = products[0]
@@ -682,29 +718,28 @@
         mine = total.astype(BF16)
         if s < last:
             held = held_of(moved, [mine])
-            first = [gate(first[0], [mine]), *first[1:]]
-            direct = across(first[0])
-            by_diag[s + 1] += direct
-        else:
-            newest = pack(first, [mine])
-            newest = [newest, *across(newest)]
         pieces = [mine] + [along_depth(mine, k) for k in range(1, depth)]
-        if s < turns:
+        ready, moved = moved, pack(first, [mine], ahead.get(s + 2, ()))
+        moved = [moved, *across(moved)]
+        by_sum[s + 1] += moved if s < last - 1 else []
+        if s + 3 in ahead:
+            ahead[s + 3] = up([gate(x, pieces[1:2]) for x in ahead[s + 3]])
+            by_diag[s + 1] += ahead[s + 3][1:]
+        if s < turns and s % 2:
             flat, mark = flat_rest(lower_rest, flat, s, turns, block, [mine])
             by_lower[s + 1].append(mark)
         if s == last:
-            buffer, new = write(0, steps, form, meta, moved, buffer, [mine])
+            buffer, new = write(0, steps, form, meta, ready, buffer, [mine])
             turned.append(new)
             by_lower[s + 1].append(new)
     known.append(place(form, meta, pieces, by_lower[steps]))
     whole = joined([last])
     got = up([whole] * py)
     direct = across(got[0])
-    early = rest_product(0, form, meta, turned, flat, (), [whole, *newest])
-    got = onward(got, direct, [early[0]])
-    buffer, new = write(last - 1, steps, form, meta, newest, buffer, [early[0]])
-    early = rest_product(last - 1, form, meta, [new], flat, early)
-    buffer, *late = last_step(form, meta, got, flat, buffer)
+    early = rest_product(0, form, meta, turned, flat, (), [whole])
+    got = onward(got, direct, [early[0], *moved])
+    buffer, *early = late_step(last - 1, form, meta, moved, flat, buffer, early)
+    buffer, *late = late_step(last, form, meta, got, flat, buffer)
     total = rhs_rest.astype(F32) - early[0] - late[0]
     for c in range(1, n_cols):
         total = total - along_cols(early[c], c).astype(F32) - along_cols(late[c], c).astype(F32)

time: 167 us -> 159 us (0.952)
  waiting for transfers between devices: 55.8 us -> 43.9 us
  starting transfers between devices: 57.1 us -> 62.7 us
  Pallas kernels: 50.6 us -> 48.8 us
    ppermute x22 -> x20, waiting for transfers between devices: 32.8 us -> 23.2 us  [along_plane(): return lax.ppermute(x, 'rows', pairs)]
    ppermute x24, starting transfers between devices: 28.1 us -> 34.4 us  [along_depth(): return lax.ppermute(x, 'rows', pairs)]
    ppermute x24, waiting for transfers between devices: 19.1 us -> 16.6 us  [along_depth(): return lax.ppermute(x, 'rows', pairs)]
    pallas_call x45, Pallas kernels: 50.6 us -> 48.8 us  [call(): pl.pallas_call(run, out_shape=tuple(outs), in_specs=list(specs) + [pl.Blo...]
    ppermute x22 -> x20, starting transfers between devices: 27.1 us -> 26.3 us  [along_plane(): return lax.ppermute(x, 'rows', pairs)]
  transfers between devices with their start and end apart: 59 -> 57, of which waited for: 26 -> 24; matrix products, arithmetic and copies ran while one was open for 0% -> 0% of each run, Pallas kernels for 29% -> 30%
where the time goes in v5:
time: 159 us; the launch traced here: 158 us
  starting transfers between devices  62.7 us (39%)
  Pallas kernels  48.8 us (31%)
  waiting for transfers between devices  43.9 us (28%)
  other arithmetic  1.62 us (1%)
    pallas_call x45, Pallas kernels, call(): pl.pallas_call(run, out_shape=tuple(outs), in_specs=list(specs) + [pl.Blo...  48.8 us
    ppermute x24, starting transfers between devices, along_depth(): return lax.ppermute(x, 'rows', pairs)  34.4 us
    ppermute x20, starting transfers between devices, along_plane(): return lax.ppermute(x, 'rows', pairs)  26.3 us
    ppermute x20, waiting for transfers between devices, along_plane(): return lax.ppermute(x, 'rows', pairs)  23.2 us
    ppermute x24, waiting for transfers between devices, along_depth(): return lax.ppermute(x, 'rows', pairs)  16.6 us
    ppermute x13, waiting for transfers between devices, along_cols(): lax.ppermute(x, 'cols', [(i, (i + k) % n_cols) for i in range(n_cols)])  4.01 us
  transfers between devices with their start and end apart: 57, of which 24 were waited for; matrix products, arithmetic and copies ran while one was open for 0% of the time, Pallas kernels for 30%

profile of v5, /device:TPU:0, one launch (start us, length us, event | category | flops | bytes accessed | tf_op | source)
XLA Modules:
  0.0 158.1 jit_solution(15686307444880987266)
XLA Ops:
  1.9 3.0 %collective-permute-start = (bf16[128,768]{1,0:T(8,128)(2,1)S(1)}, bf16[128,768]{1,0:T(8,128)(2,1)S(1)}, u32[]{:S(2)}, u32[]{:S(2)}) collective-permute-start(bf16[128,768]{1,0:T(8,128)(2,1)S(1)} %get-tuple-element.62), channel_id=1, source_target_pairs={{0,4},{2,6},{4,0},{6,2},{8,12},{10,14},{12,8},{14,10},{16,20},{18,... | collective-permute-start | bytes 589832 | tf_op jit(solution)/shard_map/ppermute | solution.py:644
  5.0 1.5 collective-permute-start.3
  6.4 3.4 %shard_map.68 = (bf16[128,1024]{1,0:T(8,128)(2,1)S(1)}, bf16[128,1024]{1,0:T(8,128)(2,1)S(1)}, bf16[128,1536]{1,0:T(8,128)(2,1)S(1)}, bf16[128,1536]{1,0:T(8,128...) custom-call(s32[4]{0:T(128)S(1)} %pad_add_fusion.refs_0_, ...), custom_call_target="tpu_custom_call" | custom-call | bytes 60817536 | tf_op jit(solution)/shard_map/pallas_call | solution.py:149
  9.9 1.7 %collective-permute-start.1 = (bf16[128,1024]{1,0:T(8,128)(2,1)S(1)}, bf16[128,1024]{1,0:T(8,128)(2,1)S(1)}, u32[]{:S(2)}, u32[]{:S(2)}) collective-permute-start(bf16[128,1024]{1,0:T(8,128)(2,1)S(1)} %shard_map.71), channel_id=1, source_target_pairs={{0,4},{2,6},{4,0},{6,2},{8,12},{10,14},{12,8},{14,10},{16,20},{18,... | collective-permute-start | bytes 786440 | tf_op jit(solution)/shard_map/ppermute | solution.py:644
  11.6 1.6 collective-permute-start.4
  13.8 3.8 %collective-permute-done.4.refs_1_.refs_4_ = bf16[128,768]{1,0:T(8,128)(2,1)S(1)} collective-permute-done((bf16[128,768]{1,0:T(8,128)(2,1)S(1)}, bf16[128,768]{1,0:T(8,128)(2,1)S(1)}, u32[]{:S(2)}, u32[]{:S(2)}) %collective-permute-start.4) | collective-permute-done | bytes 196640 | tf_op jit(solution)/shard_map/ppermute | solution.py:644
  18.7 1.6 collective-permute-start.2
  22.5 1.6 collective-permute-start.11
  24.1 2.6 %collective-permute-start.10 = (bf16[256,128]{1,0:T(8,128)(2,1)S(1)}, bf16[256,128]{1,0:T(8,128)(2,1)S(1)}, u32[]{:S(2)}, u32[]{:S(2)}) collective-permute-start(bf16[256,128]{1,0:T(8,128)(2,1)S(1)} %get-tuple-element.68), channel_id=1, source_target_pairs={{0,16},{2,18},{4,20},{6,22},{8,24},{10,26},{12,28},{14,30},{16,0},... | collective-permute-start | bytes 196616 | tf_op jit(solution)/shard_map/ppermute | solution.py:648
  26.7 1.3 collective-permute-start.9
  28.0 5.1 %shard_map.77 = (bf16[4,1536,1024]{2,1,0:T(8,128)(2,1)}, f32[8,128]{1,0:T(8,128)S(1)}) custom-call(bf16[1536,4,1024]{2,1,0:T(4,128)(2,1)} %refs_0_.5, f32[256,128]{1,0:T(8,128)S(1)} %get-tuple-element.66.refs_1_), custom_call_target="tpu_custom_call" | custom-call | bytes 25169920 | tf_op jit(solution)/shard_map/pallas_call | solution.py:149
  33.5 1.3 collective-permute-start.23
  36.1 2.6 %collective-permute-start.15 = (bf16[256,128]{1,0:T(8,128)(2,1)S(1)}, bf16[256,128]{1,0:T(8,128)(2,1)S(1)}, u32[]{:S(2)}, u32[]{:S(2)}) collective-permute-start(bf16[256,128]{1,0:T(8,128)(2,1)S(1)} %add_convert_fusion.3.refs_2_.refs_3_), channel_id=1, source_target_pairs={{0,16},{2,18},{4,20},{6,22},{8,24},{10,26},{12,28},{14,30},{16,0},... | collective-permute-start | bytes 196616 | tf_op jit(solution)/shard_map/ppermute | solution.py:648
  38.7 1.3 collective-permute-start.16
  42.1 1.7 %collective-permute-done.15.refs_5_ = bf16[256,128]{1,0:T(8,128)(2,1)S(1)} collective-permute-done((bf16[256,128]{1,0:T(8,128)(2,1)S(1)}, bf16[256,128]{1,0:T(8,128)(2,1)S(1)}, u32[]{:S(2)}, u32[]{:S(2)}) %collective-permute-start.15) | collective-permute-done | bytes 65568 | tf_op jit(solution)/shard_map/ppermute | solution.py:648
  46.2 3.9 %collective-permute-done.17.refs_4_ = bf16[512,128]{1,0:T(8,128)(2,1)S(1)} collective-permute-done((bf16[512,128]{1,0:T(8,128)(2,1)S(1)}, bf16[512,128]{1,0:T(8,128)(2,1)S(1)}, u32[]{:S(2)}, u32[]{:S(2)}) %collective-permute-start.17) | collective-permute-done | bytes 131104 | tf_op jit(solution)/shard_map/ppermute | solution.py:644
  52.1 2.0 %collective-permute-start.22 = (bf16[256,128]{1,0:T(8,128)(2,1)S(1)}, bf16[256,128]{1,0:T(8,128)(2,1)S(1)}, u32[]{:S(2)}, u32[]{:S(2)}) collective-permute-start(bf16[256,128]{1,0:T(8,128)(2,1)S(1)} %get-tuple-element.81), channel_id=1, source_target_pairs={{0,8},{2,10},{4,12},{6,14},{8,16},{10,18},{12,20},{14,22},{16,24},... | collective-permute-start | bytes 196616 | tf_op jit(solution)/shard_map/ppermute | solution.py:648
  54.1 1.9 %collective-permute-start.20 = (bf16[256,128]{1,0:T(8,128)(2,1)S(1)}, bf16[256,128]{1,0:T(8,128)(2,1)S(1)}, u32[]{:S(2)}, u32[]{:S(2)}) collective-permute-start(bf16[256,128]{1,0:T(8,128)(2,1)S(1)} %get-tuple-element.79), channel_id=1, source_target_pairs={{0,24},{2,26},{4,28},{6,30},{8,0},{10,2},{12,4},{14,6},{16,8},{18,... | collective-permute-start | bytes 196616 | tf_op jit(solution)/shard_map/ppermute | solution.py:648
  56.0 3.0 %collective-permute-done.22.refs_0_ = bf16[256,128]{1,0:T(8,128)(2,1)S(1)} collective-permute-done((bf16[256,128]{1,0:T(8,128)(2,1)S(1)}, bf16[256,128]{1,0:T(8,128)(2,1)S(1)}, u32[]{:S(2)}, u32[]{:S(2)}) %collective-permute-start.22) | collective-permute-done | bytes 65568 | tf_op jit(solution)/shard_map/ppermute | solution.py:648
  59.0 2.1 %collective-permute-done.19.refs_3_.refs_1_ = bf16[128,1536]{1,0:T(8,128)(2,1)S(1)} collective-permute-done((bf16[128,1536]{1,0:T(8,128)(2,1)S(1)}, bf16[128,1536]{1,0:T(8,128)(2,1)S(1)}, u32[]{:S(2)}, u32[]{:S(2)}) %collective-permute-start.19) | collective-permute-done | bytes 393248 | tf_op jit(solution)/shard_map/ppermute | solution.py:644
  62.6 1.6 %collective-permute-start.26 = (bf16[256,128]{1,0:T(8,128)(2,1)S(1)}, bf16[256,128]{1,0:T(8,128)(2,1)S(1)}, u32[]{:S(2)}, u32[]{:S(2)}) collective-permute-start(bf16[256,128]{1,0:T(8,128)(2,1)S(1)} %add_convert_fusion.2.refs_4_.refs_2_.refs_5_), channel_id=1, source_target_pairs={{0,8},{2,10},{4,12},{6,14},{8,16},{10,18},{12,20},{14,22},{16,24},... | collective-permute-start | bytes 196616 | tf_op jit(solution)/shard_map/ppermute | solution.py:648
  64.8 1.7 %collective-permute-start.28 = (bf16[256,128]{1,0:T(8,128)(2,1)S(1)}, bf16[256,128]{1,0:T(8,128)(2,1)S(1)}, u32[]{:S(2)}, u32[]{:S(2)}) collective-permute-start(bf16[256,128]{1,0:T(8,128)(2,1)S(1)} %add_convert_fusion.2.refs_4_.refs_2_.refs_5_), channel_id=1, source_target_pairs={{0,24},{2,26},{4,28},{6,30},{8,0},{10,2},{12,4},{14,6},{16,8},{18,... | collective-permute-start | bytes 196616 | tf_op jit(solution)/shard_map/ppermute | solution.py:648
  66.5 5.1 %shard_map.91 = (bf16[4,1536,1024]{2,1,0:T(8,128)(2,1)}, f32[8,128]{1,0:T(8,128)S(1)}) custom-call(bf16[1536,4,1024]{2,1,0:T(4,128)(2,1)} %refs_0_.5, bf16[4,1536,1024]{2,1,0:T(8,128)(2,1)} %get-tuple-element.85.refs_1_, bf16[256,128]{1,0:T(8,128)(2,1)S(1)} %add_convert_fusion.2.refs_4_.refs_2_.refs_5_), custom_call_target="tpu_custom_call", output_to_operand_aliasing={{0}: (1, {})} | custom-call | bytes 37752832 | tf_op jit(solution)/shard_map/pallas_call | solution.py:149
  75.5 3.5 %collective-permute-done.29.refs_4_ = bf16[512,128]{1,0:T(8,128)(2,1)S(1)} collective-permute-done((bf16[512,128]{1,0:T(8,128)(2,1)S(1)}, bf16[512,128]{1,0:T(8,128)(2,1)S(1)}, u32[]{:S(2)}, u32[]{:S(2)}) %collective-permute-start.29) | collective-permute-done | bytes 131104 | tf_op jit(solution)/shard_map/ppermute | solution.py:644
  80.0 1.4 collective-permute-start.35
  82.6 2.6 %collective-permute-start.32 = (bf16[256,128]{1,0:T(8,128)(2,1)S(1)}, bf16[256,128]{1,0:T(8,128)(2,1)S(1)}, u32[]{:S(2)}, u32[]{:S(2)}) collective-permute-start(bf16[256,128]{1,0:T(8,128)(2,1)S(1)} %get-tuple-element.92), channel_id=1, source_target_pairs={{0,24},{2,26},{4,28},{6,30},{8,0},{10,2},{12,4},{14,6},{16,8},{18,... | collective-permute-start | bytes 196616 | tf_op jit(solution)/shard_map/ppermute | solution.py:648
  85.2 5.1 %shard_map.96 = (bf16[4,1536,1024]{2,1,0:T(8,128)(2,1)}, f32[8,128]{1,0:T(8,128)S(1)}) custom-call(bf16[1536,4,1024]{2,1,0:T(4,128)(2,1)} %refs_0_.5, bf16[4,1536,1024]{2,1,0:T(8,128)(2,1)} %get-tuple-element.95.refs_1_, f32[256,128]{1,0:T(8,128)S(1)} %get-tuple-element.91.refs_1_.refs_2_), custom_call_target="tpu_custom_call", output_to_operand_aliasing={{0}: (1, {})} | custom-call | bytes 37752832 | tf_op jit(solution)/shard_map/pallas_call | solution.py:149
  90.4 2.8 %collective-permute-done.35.refs_3_.refs_1_ = bf16[1024,256]{1,0:T(8,128)(2,1)S(1)} collective-permute-done((bf16[1024,256]{1,0:T(8,128)(2,1)S(1)}, bf16[1024,256]{1,0:T(8,128)(2,1)S(1)}, u32[]{:S(2)}, u32[]{:S(2)}) %collective-permute-start.35) | collective-permute-done | bytes 524320 | tf_op jit(solution)/shard_map/ppermute | solution.py:644
  93.5 1.7 %collective-permute-start.49 = (bf16[2,1024,256]{2,1,0:T(8,128)(2,1)S(1)}, bf16[2,1024,256]{2,1,0:T(8,128)(2,1)S(1)}, u32[]{:S(2)}, u32[]{:S(2)}) collective-permute-start(bf16[2,1024,256]{2,1,0:T(8,128)(2,1)S(1)} %shard_map.104.refs_1_), channel_id=1, source_target_pairs={{0,2},{2,0},{4,6},{6,4},{8,10},{10,8},{12,14},{14,12},{16,18},{18,... | collective-permute-start | bytes 3145736 | tf_op jit(solution)/shard_map/ppermute | solution.py:644
  95.3 1.6 %collective-permute-start.37 = (bf16[256,128]{1,0:T(8,128)(2,1)S(1)}, bf16[256,128]{1,0:T(8,128)(2,1)S(1)}, u32[]{:S(2)}, u32[]{:S(2)}) collective-permute-start(bf16[256,128]{1,0:T(8,128)(2,1)S(1)} %add_convert_fusion.1.refs_2_.refs_7_), channel_id=1, source_target_pairs={{0,8},{2,10},{4,12},{6,14},{8,16},{10,18},{12,20},{14,22},{16,24},... | collective-permute-start | bytes 196616 | tf_op jit(solution)/shard_map/ppermute | solution.py:648
  97.8 1.8 %collective-permute-start.39 = (bf16[256,128]{1,0:T(8,128)(2,1)S(1)}, bf16[256,128]{1,0:T(8,128)(2,1)S(1)}, u32[]{:S(2)}, u32[]{:S(2)}) collective-permute-start(bf16[256,128]{1,0:T(8,128)(2,1)S(1)} %add_convert_fusion.1.refs_2_.refs_7_), channel_id=1, source_target_pairs={{0,24},{2,26},{4,28},{6,30},{8,0},{10,2},{12,4},{14,6},{16,8},{18,... | collective-permute-start | bytes 196616 | tf_op jit(solution)/shard_map/ppermute | solution.py:648
  99.7 2.4 %collective-permute-done.37.refs_8_ = bf16[256,128]{1,0:T(8,128)(2,1)S(1)} collective-permute-done((bf16[256,128]{1,0:T(8,128)(2,1)S(1)}, bf16[256,128]{1,0:T(8,128)(2,1)S(1)}, u32[]{:S(2)}, u32[]{:S(2)}) %collective-permute-start.37) | collective-permute-done | bytes 65568 | tf_op jit(solution)/shard_map/ppermute | solution.py:648
  102.1 2.1 %collective-permute-done.38.refs_9_ = bf16[256,128]{1,0:T(8,128)(2,1)S(1)} collective-permute-done((bf16[256,128]{1,0:T(8,128)(2,1)S(1)}, bf16[256,128]{1,0:T(8,128)(2,1)S(1)}, u32[]{:S(2)}, u32[]{:S(2)}) %collective-permute-start.38) | collective-permute-done | bytes 65568 | tf_op jit(solution)/shard_map/ppermute | solution.py:648
  104.2 1.5 shard_map.99
  107.7 4.0 %collective-permute-done.40.refs_4_ = bf16[512,128]{1,0:T(8,128)(2,1)S(1)} collective-permute-done((bf16[512,128]{1,0:T(8,128)(2,1)S(1)}, bf16[512,128]{1,0:T(8,128)(2,1)S(1)}, u32[]{:S(2)}, u32[]{:S(2)}) %collective-permute-start.40) | collective-permute-done | bytes 131104 | tf_op jit(solution)/shard_map/ppermute | solution.py:644
  113.7 1.9 %collective-permute-start.44 = (bf16[256,128]{1,0:T(8,128)(2,1)S(1)}, bf16[256,128]{1,0:T(8,128)(2,1)S(1)}, u32[]{:S(2)}, u32[]{:S(2)}) collective-permute-start(bf16[256,128]{1,0:T(8,128)(2,1)S(1)} %get-tuple-element.104), channel_id=1, source_target_pairs={{0,8},{2,10},{4,12},{6,14},{8,16},{10,18},{12,20},{14,22},{16,24},... | collective-permute-start | bytes 196616 | tf_op jit(solution)/shard_map/ppermute | solution.py:648
  115.6 2.0 %collective-permute-start.42 = (bf16[256,128]{1,0:T(8,128)(2,1)S(1)}, bf16[256,128]{1,0:T(8,128)(2,1)S(1)}, u32[]{:S(2)}, u32[]{:S(2)}) collective-permute-start(bf16[256,128]{1,0:T(8,128)(2,1)S(1)} %get-tuple-element.102), channel_id=1, source_target_pairs={{0,24},{2,26},{4,28},{6,30},{8,0},{10,2},{12,4},{14,6},{16,8},{18,... | collective-permute-start | bytes 196616 | tf_op jit(solution)/shard_map/ppermute | solution.py:648
  117.5 2.8 %collective-permute-done.44.refs_0_ = bf16[256,128]{1,0:T(8,128)(2,1)S(1)} collective-permute-done((bf16[256,128]{1,0:T(8,128)(2,1)S(1)}, bf16[256,128]{1,0:T(8,128)(2,1)S(1)}, u32[]{:S(2)}, u32[]{:S(2)}) %collective-permute-start.44) | collective-permute-done | bytes 65568 | tf_op jit(solution)/shard_map/ppermute | solution.py:648
  120.7 2.2 %collective-permute-done.43 = bf16[256,128]{1,0:T(8,128)(2,1)S(1)} collective-permute-done((bf16[256,128]{1,0:T(8,128)(2,1)S(1)}, bf16[256,128]{1,0:T(8,128)(2,1)S(1)}, u32[]{:S(2)}, u32[]{:S(2)}) %collective-permute-start.43) | collective-permute-done | bytes 65568 | tf_op jit(solution)/shard_map/ppermute | solution.py:648
  123.8 2.8 %collective-permute-start.47 = (bf16[256,128]{1,0:T(8,128)(2,1)S(1)}, bf16[256,128]{1,0:T(8,128)(2,1)S(1)}, u32[]{:S(2)}, u32[]{:S(2)}) collective-permute-start(bf16[256,128]{1,0:T(8,128)(2,1)S(1)} %add_convert_fusion.refs_3_.refs_1_.refs_2_), channel_id=1, source_target_pairs={{0,16},{2,18},{4,20},{6,22},{8,24},{10,26},{12,28},{14,30},{16,0},... | collective-permute-start | bytes 196616 | tf_op jit(solution)/shard_map/ppermute | solution.py:648
  127.6 2.6 %shard_map.105 = (bf16[4,1024,512]{2,1,0:T(8,128)(2,1)}, bf16[2,512,1024]{2,1,0:T(8,128)(2,1)S(1)}) custom-call(s32[4]{0:T(128)S(1)} %pad_add_fusion.refs_0_, bf16[2,1024,256]{2,1,0:T(8,128)(2,1)S(1)} %shard_map.104.refs_1_, bf16[2,1024,256]{2,1,0:T(8,128)(2,1)S(1)} %collective-permute-done.49.refs_2_, ...), custom_call_target="tpu_custom_call" | custom-call | bytes 8388624 | tf_op jit(solution)/shard_map/pallas_call | solution.py:149
  134.3 1.7 %collective-permute-start.53 = (bf16[512,256]{1,0:T(8,128)(2,1)S(1)}, bf16[512,256]{1,0:T(8,128)(2,1)S(1)}, u32[]{:S(2)}, u32[]{:S(2)}) collective-permute-start(bf16[512,256]{1,0:T(8,128)(2,1)S(1)} %shard_map.107.refs_3_.refs_1_), channel_id=1, source_target_pairs={{0,2},{2,0},{4,6},{6,4},{8,10},{10,8},{12,14},{14,12},{16,18},{18,... | collective-permute-start | bytes 786440 | tf_op jit(solution)/shard_map/ppermute | solution.py:644
  136.0 5.8 %shard_map.108 = (f32[256,1536]{1,0:T(8,128)S(1)}, bf16[256,1536]{1,0:T(8,128)(2,1)S(1)}) custom-call(s32[4]{0:T(128)S(1)} %pad_add_fusion.refs_0_, bf16[2,512,1024]{2,1,0:T(8,128)(2,1)S(1)} %get-tuple-element.105.refs_5_.refs_1_, bf16[4,1536,1024]{2,1,0:T(8,128)(2,1)} %get-tuple-element.108.refs_2_.refs_3_.refs_5_, ...), custom_call_target="tpu_custom_call" | custom-call | flops 3221225472 | bytes 17039376 | tf_op jit(solution)/shard_map/pallas_call | solution.py:149
  143.2 4.7 %shard_map.111 = (bf16[4,1024,512]{2,1,0:T(8,128)(2,1)}, f32[256,1536]{1,0:T(8,128)S(1)}, bf16[256,1536]{1,0:T(8,128)(2,1)S(1)}) custom-call(s32[4]{0:T(128)S(1)} %pad_add_fusion.refs_0_, bf16[2,512,256]{2,1,0:T(8,128)(2,1)S(1)} %shard_map.109.refs_2_.refs_1_, ...), custom_call_target="tpu_custom_call", output_to_operand_aliasing={{0}: (6, {})} | custom-call | flops 1610612736 | bytes 26738704 | tf_op jit(solution)/shard_map/pallas_call | solution.py:149
  147.9 1.7 %collective-permute-done.54.refs_4_ = bf16[512,256]{1,0:T(8,128)(2,1)S(1)} collective-permute-done((bf16[512,256]{1,0:T(8,128)(2,1)S(1)}, bf16[512,256]{1,0:T(8,128)(2,1)S(1)}, u32[]{:S(2)}, u32[]{:S(2)}) %collective-permute-start.54) | collective-permute-done | bytes 262176 | tf_op jit(solution)/shard_map/ppermute | solution.py:644
  149.6 4.8 %shard_map.112 = (bf16[4,1024,512]{2,1,0:T(8,128)(2,1)}, f32[256,1536]{1,0:T(8,128)S(1)}, bf16[256,1536]{1,0:T(8,128)(2,1)S(1)}) custom-call(s32[4]{0:T(128)S(1)} %pad_add_fusion.refs_0_, bf16[512,256]{1,0:T(8,128)(2,1)S(1)} %shard_map.107.refs_3_.refs_1_, bf16[512,256]{1,0:T(8,128)(2,1)S(1)} %shard_map.110.refs_2_, ...), custom_call_target="tpu_custom_call", output_to_operand_aliasing={{0}: (6, {})} | custom-call | flops 1610612736 | bytes 24379408 | tf_op jit(solution)/shard_map/pallas_call | solution.py:149
  154.4 2.3 %collective-permute-done.56 = bf16[256,1536]{1,0:T(8,128)(2,1)S(1)} collective-permute-done((bf16[256,1536]{1,0:T(8,128)(2,1)S(1)}, bf16[256,1536]{1,0:T(8,128)(2,1)S(1)}, u32[]{:S(2)}, u32[]{:S(2)}) %collective-permute-start.56) | collective-permute-done | bytes 786464 | tf_op jit(solution)/shard_map/ppermute | solution.py:651
  156.7 1.4 subtract_convert_fusion
  (121 shorter events, 34.6 us)
Async XLA Ops:
  1.9 7.9 %collective-permute-start = (bf16[128,768]{1,0:T(8,128)(2,1)S(1)}, bf16[128,768]{1,0:T(8,128)(2,1)S(1)}, u32[]{:S(2)}, u32[]{:S(2)}) collective-permute-start(bf16[128,768]{1,0:T(8,128)(2,1)S(1)} %get-tuple-element.62), channel_id=1, source_target_pairs={{0,4},{2,6},{4,0},{6,2},{8,12},{10,14},{12,8},{14,10},{16,20},{18,... | collective-permute-start | bytes 589832 | tf_op jit(solution)/shard_map/ppermute | solution.py:644
  5.0 8.9 %collective-permute-start.3 = (bf16[128,1152]{1,0:T(8,128)(2,1)S(1)}, bf16[128,1152]{1,0:T(8,128)(2,1)S(1)}, u32[]{:S(2)}, u32[]{:S(2)}) collective-permute-start(bf16[128,1152]{1,0:T(8,128)(2,1)S(1)} %get-tuple-element.65), channel_id=1, source_target_pairs={{0,2},{2,0},{4,6},{6,4},{8,10},{10,8},{12,14},{14,12},{16,18},{18,... | collective-permute-start | bytes 884744 | tf_op jit(solution)/shard_map/ppermute | solution.py:644
  9.9 7.8 %collective-permute-start.1 = (bf16[128,1024]{1,0:T(8,128)(2,1)S(1)}, bf16[128,1024]{1,0:T(8,128)(2,1)S(1)}, u32[]{:S(2)}, u32[]{:S(2)}) collective-permute-start(bf16[128,1024]{1,0:T(8,128)(2,1)S(1)} %shard_map.71), channel_id=1, source_target_pairs={{0,4},{2,6},{4,0},{6,2},{8,12},{10,14},{12,8},{14,10},{16,20},{18,... | collective-permute-start | bytes 786440 | tf_op jit(solution)/shard_map/ppermute | solution.py:644
  11.6 6.0 %collective-permute-start.4 = (bf16[128,768]{1,0:T(8,128)(2,1)S(1)}, bf16[128,768]{1,0:T(8,128)(2,1)S(1)}, u32[]{:S(2)}, u32[]{:S(2)}) collective-permute-start(bf16[128,768]{1,0:T(8,128)(2,1)S(1)} %shard_map.73.refs_2_), channel_id=1, source_target_pairs={{0,2},{2,0},{4,6},{6,4},{8,10},{10,8},{12,14},{14,12},{16,18},{18,... | collective-permute-start | bytes 589832 | tf_op jit(solution)/shard_map/ppermute | solution.py:644
  18.7 14.5 %collective-permute-start.2 = (bf16[2,128,1024]{2,1,0:T(8,128)(2,1)S(1)}, bf16[2,128,1024]{2,1,0:T(8,128)(2,1)S(1)}, u32[]{:S(2)}, u32[]{:S(2)}) collective-permute-start(bf16[2,128,1024]{2,1,0:T(8,128)(2,1)S(1)} %shard_map.72.refs_1_.refs_0_), channel_id=1, source_target_pairs={{0,2},{2,0},{4,6},{6,4},{8,10},{10,8},{12,14},{14,12},{16,18},{18,... | collective-permute-start | bytes 1572872 | tf_op jit(solution)/shard_map/ppermute | solution.py:644
  21.3 11.8 %collective-permute-start.12 = (bf16[128,1536]{1,0:T(8,128)(2,1)S(1)}, bf16[128,1536]{1,0:T(8,128)(2,1)S(1)}, u32[]{:S(2)}, u32[]{:S(2)}) collective-permute-start(bf16[128,1536]{1,0:T(8,128)(2,1)S(1)} %shard_map.76), channel_id=1, source_target_pairs={{0,4},{2,6},{4,0},{6,2},{8,12},{10,14},{12,8},{14,10},{16,20},{18,... | collective-permute-start | bytes 1179656 | tf_op jit(solution)/shard_map/ppermute | solution.py:644
  22.5 10.6 %collective-permute-start.11 = (bf16[256,128]{1,0:T(8,128)(2,1)S(1)}, bf16[256,128]{1,0:T(8,128)(2,1)S(1)}, u32[]{:S(2)}, u32[]{:S(2)}) collective-permute-start(bf16[256,128]{1,0:T(8,128)(2,1)S(1)} %get-tuple-element.69), channel_id=1, source_target_pairs={{0,8},{2,10},{4,12},{6,14},{8,16},{10,18},{12,20},{14,22},{16,24},... | collective-permute-start | bytes 196616 | tf_op jit(solution)/shard_map/ppermute | solution.py:648
  24.1 9.1 %collective-permute-start.10 = (bf16[256,128]{1,0:T(8,128)(2,1)S(1)}, bf16[256,128]{1,0:T(8,128)(2,1)S(1)}, u32[]{:S(2)}, u32[]{:S(2)}) collective-permute-start(bf16[256,128]{1,0:T(8,128)(2,1)S(1)} %get-tuple-element.68), channel_id=1, source_target_pairs={{0,16},{2,18},{4,20},{6,22},{8,24},{10,26},{12,28},{14,30},{16,0},... | collective-permute-start | bytes 196616 | tf_op jit(solution)/shard_map/ppermute | solution.py:648
  26.7 6.5 %collective-permute-start.9 = (bf16[256,128]{1,0:T(8,128)(2,1)S(1)}, bf16[256,128]{1,0:T(8,128)(2,1)S(1)}, u32[]{:S(2)}, u32[]{:S(2)}) collective-permute-start(bf16[256,128]{1,0:T(8,128)(2,1)S(1)} %get-tuple-element.67), channel_id=1, source_target_pairs={{0,24},{2,26},{4,28},{6,30},{8,0},{10,2},{12,4},{14,6},{16,8},{18,... | collective-permute-start | bytes 196616 | tf_op jit(solution)/shard_map/ppermute | solution.py:648
  33.3 10.6 %collective-permute-start.13 = (bf16[4,128,1024]{2,1,0:T(8,128)(2,1)S(1)}, bf16[4,128,1024]{2,1,0:T(8,128)(2,1)S(1)}, u32[]{:S(2)}, u32[]{:S(2)}) collective-permute-start(bf16[4,128,1024]{2,1,0:T(8,128)(2,1)S(1)} %shard_map.79.refs_1_), channel_id=1, source_target_pairs={{0,1},{1,0},{2,3},{3,2},{4,5},{5,4},{6,7},{7,6},{8,9},{9,8},{10,11... | collective-permute-start | bytes 3145736 | tf_op jit(solution)/shard_map/ppermute | solution.py:651
  33.5 22.5 %collective-permute-start.23 = (bf16[2,128,1536]{2,1,0:T(8,128)(2,1)S(1)}, bf16[2,128,1536]{2,1,0:T(8,128)(2,1)S(1)}, u32[]{:S(2)}, u32[]{:S(2)}) collective-permute-start(bf16[2,128,1536]{2,1,0:T(8,128)(2,1)S(1)} %shard_map.87.refs_1_.refs_0_), channel_id=1, source_target_pairs={{0,2},{2,0},{4,6},{6,4},{8,10},{10,8},{12,14},{14,12},{16,18},{18,... | collective-permute-start | bytes 2359304 | tf_op jit(solution)/shard_map/ppermute | solution.py:644
  34.8 6.5 %collective-permute-start.14 = (bf16[256,128]{1,0:T(8,128)(2,1)S(1)}, bf16[256,128]{1,0:T(8,128)(2,1)S(1)}, u32[]{:S(2)}, u32[]{:S(2)}) collective-permute-start(bf16[256,128]{1,0:T(8,128)(2,1)S(1)} %add_convert_fusion.3.refs_2_.refs_3_), channel_id=1, source_target_pairs={{0,8},{2,10},{4,12},{6,14},{8,16},{10,18},{12,20},{14,22},{16,24},... | collective-permute-start | bytes 196616 | tf_op jit(solution)/shard_map/ppermute | solution.py:648
  36.1 7.6 %collective-permute-start.15 = (bf16[256,128]{1,0:T(8,128)(2,1)S(1)}, bf16[256,128]{1,0:T(8,128)(2,1)S(1)}, u32[]{:S(2)}, u32[]{:S(2)}) collective-permute-start(bf16[256,128]{1,0:T(8,128)(2,1)S(1)} %add_convert_fusion.3.refs_2_.refs_3_), channel_id=1, source_target_pairs={{0,16},{2,18},{4,20},{6,22},{8,24},{10,26},{12,28},{14,30},{16,0},... | collective-permute-start | bytes 196616 | tf_op jit(solution)/shard_map/ppermute | solution.py:648
  38.7 5.3 %collective-permute-start.16 = (bf16[256,128]{1,0:T(8,128)(2,1)S(1)}, bf16[256,128]{1,0:T(8,128)(2,1)S(1)}, u32[]{:S(2)}, u32[]{:S(2)}) collective-permute-start(bf16[256,128]{1,0:T(8,128)(2,1)S(1)} %add_convert_fusion.3.refs_2_.refs_3_), channel_id=1, source_target_pairs={{0,24},{2,26},{4,28},{6,30},{8,0},{10,2},{12,4},{14,6},{16,8},{18,... | collective-permute-start | bytes 196616 | tf_op jit(solution)/shard_map/ppermute | solution.py:648
  41.3 5.0 %collective-permute-start.18 = (bf16[128,512]{1,0:T(8,128)(2,1)S(1)}, bf16[128,512]{1,0:T(8,128)(2,1)S(1)}, u32[]{:S(2)}, u32[]{:S(2)}) collective-permute-start(bf16[128,512]{1,0:T(8,128)(2,1)S(1)} %shard_map.81), channel_id=1, source_target_pairs={{0,4},{2,6},{4,0},{6,2},{8,12},{10,14},{12,8},{14,10},{16,20},{18,... | collective-permute-start | bytes 393224 | tf_op jit(solution)/shard_map/ppermute | solution.py:644
  45.0 5.2 %collective-permute-start.17 = (bf16[512,128]{1,0:T(8,128)(2,1)S(1)}, bf16[512,128]{1,0:T(8,128)(2,1)S(1)}, u32[]{:S(2)}, u32[]{:S(2)}) collective-permute-start(bf16[512,128]{1,0:T(8,128)(2,1)S(1)} %get-tuple-element.74), channel_id=1, source_target_pairs={{0,4},{2,6},{4,0},{6,2},{8,12},{10,14},{12,8},{14,10},{16,20},{18,... | collective-permute-start | bytes 393224 | tf_op jit(solution)/shard_map/ppermute | solution.py:644
  51.2 9.9 %collective-permute-start.19 = (bf16[128,1536]{1,0:T(8,128)(2,1)S(1)}, bf16[128,1536]{1,0:T(8,128)(2,1)S(1)}, u32[]{:S(2)}, u32[]{:S(2)}) collective-permute-start(bf16[128,1536]{1,0:T(8,128)(2,1)S(1)} %shard_map.84), channel_id=1, source_target_pairs={{0,4},{2,6},{4,0},{6,2},{8,12},{10,14},{12,8},{14,10},{16,20},{18,... | collective-permute-start | bytes 1179656 | tf_op jit(solution)/shard_map/ppermute | solution.py:644
  52.1 6.9 %collective-permute-start.22 = (bf16[256,128]{1,0:T(8,128)(2,1)S(1)}, bf16[256,128]{1,0:T(8,128)(2,1)S(1)}, u32[]{:S(2)}, u32[]{:S(2)}) collective-permute-start(bf16[256,128]{1,0:T(8,128)(2,1)S(1)} %get-tuple-element.81), channel_id=1, source_target_pairs={{0,8},{2,10},{4,12},{6,14},{8,16},{10,18},{12,20},{14,22},{16,24},... | collective-permute-start | bytes 196616 | tf_op jit(solution)/shard_map/ppermute | solution.py:648
  54.1 7.0 %collective-permute-start.20 = (bf16[256,128]{1,0:T(8,128)(2,1)S(1)}, bf16[256,128]{1,0:T(8,128)(2,1)S(1)}, u32[]{:S(2)}, u32[]{:S(2)}) collective-permute-start(bf16[256,128]{1,0:T(8,128)(2,1)S(1)} %get-tuple-element.79), channel_id=1, source_target_pairs={{0,24},{2,26},{4,28},{6,30},{8,0},{10,2},{12,4},{14,6},{16,8},{18,... | collective-permute-start | bytes 196616 | tf_op jit(solution)/shard_map/ppermute | solution.py:648
  56.0 5.5 %collective-permute-start.21 = (bf16[256,128]{1,0:T(8,128)(2,1)S(1)}, bf16[256,128]{1,0:T(8,128)(2,1)S(1)}, u32[]{:S(2)}, u32[]{:S(2)}) collective-permute-start(bf16[256,128]{1,0:T(8,128)(2,1)S(1)} %get-tuple-element.80), channel_id=1, source_target_pairs={{0,16},{2,18},{4,20},{6,22},{8,24},{10,26},{12,28},{14,30},{16,0},... | collective-permute-start | bytes 196616 | tf_op jit(solution)/shard_map/ppermute | solution.py:648
  61.6 10.1 %collective-permute-start.25 = (bf16[4,128,1536]{2,1,0:T(8,128)(2,1)S(1)}, bf16[4,128,1536]{2,1,0:T(8,128)(2,1)S(1)}, u32[]{:S(2)}, u32[]{:S(2)}) collective-permute-start(bf16[4,128,1536]{2,1,0:T(8,128)(2,1)S(1)} %shard_map.90.refs_1_), channel_id=1, source_target_pairs={{0,1},{1,0},{2,3},{3,2},{4,5},{5,4},{6,7},{7,6},{8,9},{9,8},{10,11... | collective-permute-start | bytes 4718600 | tf_op jit(solution)/shard_map/ppermute | solution.py:651
  61.7 28.6 %collective-permute-start.24 = (bf16[2,128,2048]{2,1,0:T(8,128)(2,1)S(1)}, bf16[2,128,2048]{2,1,0:T(8,128)(2,1)S(1)}, u32[]{:S(2)}, u32[]{:S(2)}) collective-permute-start(bf16[2,128,2048]{2,1,0:T(8,128)(2,1)S(1)} %shard_map.89.refs_1_.refs_0_), channel_id=1, source_target_pairs={{0,2},{2,0},{4,6},{6,4},{8,10},{10,8},{12,14},{14,12},{16,18},{18,... | collective-permute-start | bytes 3145736 | tf_op jit(solution)/shard_map/ppermute | solution.py:644
  62.6 9.1 %collective-permute-start.26 = (bf16[256,128]{1,0:T(8,128)(2,1)S(1)}, bf16[256,128]{1,0:T(8,128)(2,1)S(1)}, u32[]{:S(2)}, u32[]{:S(2)}) collective-permute-start(bf16[256,128]{1,0:T(8,128)(2,1)S(1)} %add_convert_fusion.2.refs_4_.refs_2_.refs_5_), channel_id=1, source_target_pairs={{0,8},{2,10},{4,12},{6,14},{8,16},{10,18},{12,20},{14,22},{16,24},... | collective-permute-start | bytes 196616 | tf_op jit(solution)/shard_map/ppermute | solution.py:648
  64.1 7.5 %collective-permute-start.27 = (bf16[256,128]{1,0:T(8,128)(2,1)S(1)}, bf16[256,128]{1,0:T(8,128)(2,1)S(1)}, u32[]{:S(2)}, u32[]{:S(2)}) collective-permute-start(bf16[256,128]{1,0:T(8,128)(2,1)S(1)} %add_convert_fusion.2.refs_4_.refs_2_.refs_5_), channel_id=1, source_target_pairs={{0,16},{2,18},{4,20},{6,22},{8,24},{10,26},{12,28},{14,30},{16,0},... | collective-permute-start | bytes 196616 | tf_op jit(solution)/shard_map/ppermute | solution.py:648
  64.8 6.8 %collective-permute-start.28 = (bf16[256,128]{1,0:T(8,128)(2,1)S(1)}, bf16[256,128]{1,0:T(8,128)(2,1)S(1)}, u32[]{:S(2)}, u32[]{:S(2)}) collective-permute-start(bf16[256,128]{1,0:T(8,128)(2,1)S(1)} %add_convert_fusion.2.refs_4_.refs_2_.refs_5_), channel_id=1, source_target_pairs={{0,24},{2,26},{4,28},{6,30},{8,0},{10,2},{12,4},{14,6},{16,8},{18,... | collective-permute-start | bytes 196616 | tf_op jit(solution)/shard_map/ppermute | solution.py:648
  73.5 5.5 %collective-permute-start.29 = (bf16[512,128]{1,0:T(8,128)(2,1)S(1)}, bf16[512,128]{1,0:T(8,128)(2,1)S(1)}, u32[]{:S(2)}, u32[]{:S(2)}) collective-permute-start(bf16[512,128]{1,0:T(8,128)(2,1)S(1)} %get-tuple-element.88), channel_id=1, source_target_pairs={{0,4},{2,6},{4,0},{6,2},{8,12},{10,14},{12,8},{14,10},{16,20},{18,... | collective-permute-start | bytes 393224 | tf_op jit(solution)/shard_map/ppermute | solution.py:644
  80.0 13.1 %collective-permute-start.35 = (bf16[1024,256]{1,0:T(8,128)(2,1)S(1)}, bf16[1024,256]{1,0:T(8,128)(2,1)S(1)}, u32[]{:S(2)}, u32[]{:S(2)}) collective-permute-start(bf16[1024,256]{1,0:T(8,128)(2,1)S(1)} %shard_map.95.refs_0_), channel_id=1, source_target_pairs={{0,4},{2,6},{4,0},{6,2},{8,12},{10,14},{12,8},{14,10},{16,20},{18,... | collective-permute-start | bytes 1572872 | tf_op jit(solution)/shard_map/ppermute | solution.py:644
  81.4 9.0 %collective-permute-start.34 = (bf16[256,128]{1,0:T(8,128)(2,1)S(1)}, bf16[256,128]{1,0:T(8,128)(2,1)S(1)}, u32[]{:S(2)}, u32[]{:S(2)}) collective-permute-start(bf16[256,128]{1,0:T(8,128)(2,1)S(1)} %get-tuple-element.94), channel_id=1, source_target_pairs={{0,8},{2,10},{4,12},{6,14},{8,16},{10,18},{12,20},{14,22},{16,24},... | collective-permute-start | bytes 196616 | tf_op jit(solution)/shard_map/ppermute | solution.py:648
  82.6 10.6 %collective-permute-start.32 = (bf16[256,128]{1,0:T(8,128)(2,1)S(1)}, bf16[256,128]{1,0:T(8,128)(2,1)S(1)}, u32[]{:S(2)}, u32[]{:S(2)}) collective-permute-start(bf16[256,128]{1,0:T(8,128)(2,1)S(1)} %get-tuple-element.92), channel_id=1, source_target_pairs={{0,24},{2,26},{4,28},{6,30},{8,0},{10,2},{12,4},{14,6},{16,8},{18,... | collective-permute-start | bytes 196616 | tf_op jit(solution)/shard_map/ppermute | solution.py:648
  85.2 8.0 %collective-permute-start.33 = (bf16[256,128]{1,0:T(8,128)(2,1)S(1)}, bf16[256,128]{1,0:T(8,128)(2,1)S(1)}, u32[]{:S(2)}, u32[]{:S(2)}) collective-permute-start(bf16[256,128]{1,0:T(8,128)(2,1)S(1)} %get-tuple-element.93), channel_id=1, source_target_pairs={{0,16},{2,18},{4,20},{6,22},{8,24},{10,26},{12,28},{14,30},{16,0},... | collective-permute-start | bytes 196616 | tf_op jit(solution)/shard_map/ppermute | solution.py:648
  93.4 10.8 %collective-permute-start.36 = (bf16[4,128,2048]{2,1,0:T(8,128)(2,1)S(1)}, bf16[4,128,2048]{2,1,0:T(8,128)(2,1)S(1)}, u32[]{:S(2)}, u32[]{:S(2)}) collective-permute-start(bf16[4,128,2048]{2,1,0:T(8,128)(2,1)S(1)} %shard_map.98.refs_1_), channel_id=1, source_target_pairs={{0,1},{1,0},{2,3},{3,2},{4,5},{5,4},{6,7},{7,6},{8,9},{9,8},{10,11... | collective-permute-start | bytes 6291464 | tf_op jit(solution)/shard_map/ppermute | solution.py:651
  93.5 34.1 %collective-permute-start.49 = (bf16[2,1024,256]{2,1,0:T(8,128)(2,1)S(1)}, bf16[2,1024,256]{2,1,0:T(8,128)(2,1)S(1)}, u32[]{:S(2)}, u32[]{:S(2)}) collective-permute-start(bf16[2,1024,256]{2,1,0:T(8,128)(2,1)S(1)} %shard_map.104.refs_1_), channel_id=1, source_target_pairs={{0,2},{2,0},{4,6},{6,4},{8,10},{10,8},{12,14},{14,12},{16,18},{18,... | collective-permute-start | bytes 3145736 | tf_op jit(solution)/shard_map/ppermute | solution.py:644
  95.3 6.8 %collective-permute-start.37 = (bf16[256,128]{1,0:T(8,128)(2,1)S(1)}, bf16[256,128]{1,0:T(8,128)(2,1)S(1)}, u32[]{:S(2)}, u32[]{:S(2)}) collective-permute-start(bf16[256,128]{1,0:T(8,128)(2,1)S(1)} %add_convert_fusion.1.refs_2_.refs_7_), channel_id=1, source_target_pairs={{0,8},{2,10},{4,12},{6,14},{8,16},{10,18},{12,20},{14,22},{16,24},... | collective-permute-start | bytes 196616 | tf_op jit(solution)/shard_map/ppermute | solution.py:648
  96.9 7.3 %collective-permute-start.38 = (bf16[256,128]{1,0:T(8,128)(2,1)S(1)}, bf16[256,128]{1,0:T(8,128)(2,1)S(1)}, u32[]{:S(2)}, u32[]{:S(2)}) collective-permute-start(bf16[256,128]{1,0:T(8,128)(2,1)S(1)} %add_convert_fusion.1.refs_2_.refs_7_), channel_id=1, source_target_pairs={{0,16},{2,18},{4,20},{6,22},{8,24},{10,26},{12,28},{14,30},{16,0},... | collective-permute-start | bytes 196616 | tf_op jit(solution)/shard_map/ppermute | solution.py:648
  97.8 6.3 %collective-permute-start.39 = (bf16[256,128]{1,0:T(8,128)(2,1)S(1)}, bf16[256,128]{1,0:T(8,128)(2,1)S(1)}, u32[]{:S(2)}, u32[]{:S(2)}) collective-permute-start(bf16[256,128]{1,0:T(8,128)(2,1)S(1)} %add_convert_fusion.1.refs_2_.refs_7_), channel_id=1, source_target_pairs={{0,24},{2,26},{4,28},{6,30},{8,0},{10,2},{12,4},{14,6},{16,8},{18,... | collective-permute-start | bytes 196616 | tf_op jit(solution)/shard_map/ppermute | solution.py:648
  105.8 5.9 %collective-permute-start.40 = (bf16[512,128]{1,0:T(8,128)(2,1)S(1)}, bf16[512,128]{1,0:T(8,128)(2,1)S(1)}, u32[]{:S(2)}, u32[]{:S(2)}) collective-permute-start(bf16[512,128]{1,0:T(8,128)(2,1)S(1)} %get-tuple-element.98), channel_id=1, source_target_pairs={{0,4},{2,6},{4,0},{6,2},{8,12},{10,14},{12,8},{14,10},{16,20},{18,... | collective-permute-start | bytes 393224 | tf_op jit(solution)/shard_map/ppermute | solution.py:644
  112.7 7.9 %collective-permute-start.45 = (bf16[512,256]{1,0:T(8,128)(2,1)S(1)}, bf16[512,256]{1,0:T(8,128)(2,1)S(1)}, u32[]{:S(2)}, u32[]{:S(2)}) collective-permute-start(bf16[512,256]{1,0:T(8,128)(2,1)S(1)} %shard_map.102.refs_0_), channel_id=1, source_target_pairs={{0,4},{2,6},{4,0},{6,2},{8,12},{10,14},{12,8},{14,10},{16,20},{18,... | collective-permute-start | bytes 786440 | tf_op jit(solution)/shard_map/ppermute | solution.py:644
  113.7 6.6 %collective-permute-start.44 = (bf16[256,128]{1,0:T(8,128)(2,1)S(1)}, bf16[256,128]{1,0:T(8,128)(2,1)S(1)}, u32[]{:S(2)}, u32[]{:S(2)}) collective-permute-start(bf16[256,128]{1,0:T(8,128)(2,1)S(1)} %get-tuple-element.104), channel_id=1, source_target_pairs={{0,8},{2,10},{4,12},{6,14},{8,16},{10,18},{12,20},{14,22},{16,24},... | collective-permute-start | bytes 196616 | tf_op jit(solution)/shard_map/ppermute | solution.py:648
  115.6 5.1 %collective-permute-start.42 = (bf16[256,128]{1,0:T(8,128)(2,1)S(1)}, bf16[256,128]{1,0:T(8,128)(2,1)S(1)}, u32[]{:S(2)}, u32[]{:S(2)}) collective-permute-start(bf16[256,128]{1,0:T(8,128)(2,1)S(1)} %get-tuple-element.102), channel_id=1, source_target_pairs={{0,24},{2,26},{4,28},{6,30},{8,0},{10,2},{12,4},{14,6},{16,8},{18,... | collective-permute-start | bytes 196616 | tf_op jit(solution)/shard_map/ppermute | solution.py:648
  117.5 5.4 %collective-permute-start.43 = (bf16[256,128]{1,0:T(8,128)(2,1)S(1)}, bf16[256,128]{1,0:T(8,128)(2,1)S(1)}, u32[]{:S(2)}, u32[]{:S(2)}) collective-permute-start(bf16[256,128]{1,0:T(8,128)(2,1)S(1)} %get-tuple-element.103), channel_id=1, source_target_pairs={{0,16},{2,18},{4,20},{6,22},{8,24},{10,26},{12,28},{14,30},{16,0},... | collective-permute-start | bytes 196616 | tf_op jit(solution)/shard_map/ppermute | solution.py:648
  123.0 18.9 %collective-permute-start.52 = (bf16[2,512,256]{2,1,0:T(8,128)(2,1)S(1)}, bf16[2,512,256]{2,1,0:T(8,128)(2,1)S(1)}, u32[]{:S(2)}, u32[]{:S(2)}) collective-permute-start(bf16[2,512,256]{2,1,0:T(8,128)(2,1)S(1)} %shard_map.109.refs_2_.refs_1_), channel_id=1, source_target_pairs={{0,2},{2,0},{4,6},{6,4},{8,10},{10,8},{12,14},{14,12},{16,18},{18,... | collective-permute-start | bytes 1572872 | tf_op jit(solution)/shard_map/ppermute | solution.py:644
  123.8 6.5 %collective-permute-start.46 = (bf16[256,128]{1,0:T(8,128)(2,1)S(1)}, bf16[256,128]{1,0:T(8,128)(2,1)S(1)}, u32[]{:S(2)}, u32[]{:S(2)}) collective-permute-start(bf16[256,128]{1,0:T(8,128)(2,1)S(1)} %add_convert_fusion.refs_3_.refs_1_.refs_2_), channel_id=1, source_target_pairs={{0,8},{2,10},{4,12},{6,14},{8,16},{10,18},{12,20},{14,22},{16,24},... | collective-permute-start | bytes 196616 | tf_op jit(solution)/shard_map/ppermute | solution.py:648
  123.8 6.5 %collective-permute-start.47 = (bf16[256,128]{1,0:T(8,128)(2,1)S(1)}, bf16[256,128]{1,0:T(8,128)(2,1)S(1)}, u32[]{:S(2)}, u32[]{:S(2)}) collective-permute-start(bf16[256,128]{1,0:T(8,128)(2,1)S(1)} %add_convert_fusion.refs_3_.refs_1_.refs_2_), channel_id=1, source_target_pairs={{0,16},{2,18},{4,20},{6,22},{8,24},{10,26},{12,28},{14,30},{16,0},... | collective-permute-start | bytes 196616 | tf_op jit(solution)/shard_map/ppermute | solution.py:648
  126.6 4.3 %collective-permute-start.48 = (bf16[256,128]{1,0:T(8,128)(2,1)S(1)}, bf16[256,128]{1,0:T(8,128)(2,1)S(1)}, u32[]{:S(2)}, u32[]{:S(2)}) collective-permute-start(bf16[256,128]{1,0:T(8,128)(2,1)S(1)} %add_convert_fusion.refs_3_.refs_1_.refs_2_), channel_id=1, source_target_pairs={{0,24},{2,26},{4,28},{6,30},{8,0},{10,2},{12,4},{14,6},{16,8},{18,... | collective-permute-start | bytes 196616 | tf_op jit(solution)/shard_map/ppermute | solution.py:648
  133.5 8.4 %collective-permute-start.51 = (bf16[512,256]{1,0:T(8,128)(2,1)S(1)}, bf16[512,256]{1,0:T(8,128)(2,1)S(1)}, u32[]{:S(2)}, u32[]{:S(2)}) collective-permute-start(bf16[512,256]{1,0:T(8,128)(2,1)S(1)} %shard_map.107.refs_3_.refs_1_), channel_id=1, source_target_pairs={{0,4},{2,6},{4,0},{6,2},{8,12},{10,14},{12,8},{14,10},{16,20},{18,... | collective-permute-start | bytes 786440 | tf_op jit(solution)/shard_map/ppermute | solution.py:644
  134.3 13.6 %collective-permute-start.53 = (bf16[512,256]{1,0:T(8,128)(2,1)S(1)}, bf16[512,256]{1,0:T(8,128)(2,1)S(1)}, u32[]{:S(2)}, u32[]{:S(2)}) collective-permute-start(bf16[512,256]{1,0:T(8,128)(2,1)S(1)} %shard_map.107.refs_3_.refs_1_), channel_id=1, source_target_pairs={{0,2},{2,0},{4,6},{6,4},{8,10},{10,8},{12,14},{14,12},{16,18},{18,... | collective-permute-start | bytes 786440 | tf_op jit(solution)/shard_map/ppermute | solution.py:644
  141.9 7.7 %collective-permute-start.54 = (bf16[512,256]{1,0:T(8,128)(2,1)S(1)}, bf16[512,256]{1,0:T(8,128)(2,1)S(1)}, u32[]{:S(2)}, u32[]{:S(2)}) collective-permute-start(bf16[512,256]{1,0:T(8,128)(2,1)S(1)} %shard_map.110.refs_2_), channel_id=1, source_target_pairs={{0,2},{2,0},{4,6},{6,4},{8,10},{10,8},{12,14},{14,12},{16,18},{18,... | collective-permute-start | bytes 786440 | tf_op jit(solution)/shard_map/ppermute | solution.py:644
  147.9 6.5 %collective-permute-start.55 = (bf16[256,1536]{1,0:T(8,128)(2,1)S(1)}, bf16[256,1536]{1,0:T(8,128)(2,1)S(1)}, u32[]{:S(2)}, u32[]{:S(2)}) collective-permute-start(bf16[256,1536]{1,0:T(8,128)(2,1)S(1)} %get-tuple-element.116), channel_id=1, source_target_pairs={{0,1},{1,0},{2,3},{3,2},{4,5},{5,4},{6,7},{7,6},{8,9},{9,8},{10,11... | collective-permute-start | bytes 2359304 | tf_op jit(solution)/shard_map/ppermute | solution.py:651
  (10 other events, 26.6 us)

commit v6 on v5

--- a/solution.py
+++ b/solution.py
@@ -314,11 +314,11 @@
         right = pl.ds(pl.multiple_of(width + meta[1] * sides, sides), sides)
         residual = jnp.concatenate([held[k][:, right] for k in range(chips)], axis=0)
     for c in range(n_cols):
-        for h in range(width // eqs):
-            rows = jnp.concatenate(
-                [held[c * chips + k][:, h * eqs : (h + 1) * eqs] for k in range(chips)], axis=1
-            )
-            product[c, h * eqs : (h + 1) * eqs] = jnp.dot(rows, residual, preferred_element_type=F32)
+        rows = [
+            jnp.concatenate([held[c * chips + k][:, h * eqs : (h + 1) * eqs] for k in range(chips)], axis=1)
+            for h in range(width // eqs)
+        ]
+        product[c] = jnp.dot(jnp.concatenate(rows, axis=0), residual, preferred_element_type=F32)
     for k in range(depth):
         at = pl.multiple_of(lax.rem(meta[2] + depth - k, depth) * sub, sub)
         for c in range(n_cols):
@@ -719,7 +719,8 @@
         if s < last:
             held = held_of(moved, [mine])
         pieces = [mine] + [along_depth(mine, k) for k in range(1, depth)]
-        ready, moved = moved, pack(first, [mine], ahead.get(s + 2, ()))
+        soon = pieces[1:2] if s == last - 1 else [mine]
+        ready, moved = moved, pack(first, soon, ahead.get(s + 2, ()))
         moved = [moved, *across(moved)]
         by_sum[s + 1] += moved if s < last - 1 else []
         if s + 3 in ahead:
@@ -736,13 +737,13 @@
     whole = joined([last])
     got = up([whole] * py)
     direct = across(got[0])
-    early = rest_product(0, form, meta, turned, flat, (), [whole])
+    early = rest_product(0, form, meta, turned, flat, (), [whole, *moved])
     got = onward(got, direct, [early[0], *moved])
     buffer, *early = late_step(last - 1, form, meta, moved, flat, buffer, early)
-    buffer, *late = late_step(last, form, meta, got, flat, buffer)
-    total = rhs_rest.astype(F32) - early[0] - late[0]
+    buffer, *late = late_step(last, form, meta, got, flat, buffer, early)
+    total = rhs_rest.astype(F32) - late[0]
     for c in range(1, n_cols):
-        total = total - along_cols(early[c], c).astype(F32) - along_cols(late[c], c).astype(F32)
+        total = total - along_cols(late[c], c).astype(F32)
     return buffer, total.astype(BF16)
 
 

time: 159 us -> 158 us (level)
  waiting for transfers between devices: 43.9 us -> 41.9 us
    ppermute x13 -> x12, waiting for transfers between devices: 4.01 us -> 3.72 us  [along_cols(): lax.ppermute(x, 'cols', [(i, (i + k) % n_cols) for i in range(n_cols)])]
  transfers between devices with their start and end apart: 57 -> 56, of which waited for: 24 -> 25; matrix products, arithmetic and copies ran while one was open for 0% -> 0% of each run, Pallas kernels for 30% -> 27%
where the time goes in v6:
time: 158 us; the launch traced here: 157 us
  starting transfers between devices  63.8 us (40%)
  Pallas kernels  48.8 us (31%)
  waiting for transfers between devices  41.9 us (27%)
    pallas_call x45, Pallas kernels, call(): pl.pallas_call(run, out_shape=tuple(outs), in_specs=list(specs) + [pl.Blo...  48.8 us
    ppermute x24, starting transfers between devices, along_depth(): return lax.ppermute(x, 'rows', pairs)  34.9 us
    ppermute x20, starting transfers between devices, along_plane(): return lax.ppermute(x, 'rows', pairs)  27 us
    ppermute x20, waiting for transfers between devices, along_plane(): return lax.ppermute(x, 'rows', pairs)  23 us
    ppermute x24, waiting for transfers between devices, along_depth(): return lax.ppermute(x, 'rows', pairs)  15.2 us
    ppermute x12, waiting for transfers between devices, along_cols(): lax.ppermute(x, 'cols', [(i, (i + k) % n_cols) for i in range(n_cols)])  3.72 us
  transfers between devices with their start and end apart: 56, of which 25 were waited for; matrix products, arithmetic and copies ran while one was open for 0% of the time, Pallas kernels for 27%

profile of v6, /device:TPU:0, one launch (start us, length us, event | category | flops | bytes accessed | tf_op | source)
XLA Modules:
  0.0 157.1 jit_solution(8901389133730539300)
XLA Ops:
  1.9 3.0 %collective-permute-start = (bf16[128,768]{1,0:T(8,128)(2,1)S(1)}, bf16[128,768]{1,0:T(8,128)(2,1)S(1)}, u32[]{:S(2)}, u32[]{:S(2)}) collective-permute-start(bf16[128,768]{1,0:T(8,128)(2,1)S(1)} %get-tuple-element.62), channel_id=1, source_target_pairs={{0,4},{2,6},{4,0},{6,2},{8,12},{10,14},{12,8},{14,10},{16,20},{18,... | collective-permute-start | bytes 589832 | tf_op jit(solution)/shard_map/ppermute | solution.py:644
  5.0 1.5 collective-permute-start.3
  6.4 3.4 %shard_map.68 = (bf16[128,1024]{1,0:T(8,128)(2,1)S(1)}, bf16[128,1024]{1,0:T(8,128)(2,1)S(1)}, bf16[128,1536]{1,0:T(8,128)(2,1)S(1)}, bf16[128,1536]{1,0:T(8,128...) custom-call(s32[4]{0:T(128)S(1)} %pad_add_fusion.refs_0_, ...), custom_call_target="tpu_custom_call" | custom-call | bytes 60817536 | tf_op jit(solution)/shard_map/pallas_call | solution.py:149
  9.9 1.7 %collective-permute-start.1 = (bf16[128,1024]{1,0:T(8,128)(2,1)S(1)}, bf16[128,1024]{1,0:T(8,128)(2,1)S(1)}, u32[]{:S(2)}, u32[]{:S(2)}) collective-permute-start(bf16[128,1024]{1,0:T(8,128)(2,1)S(1)} %shard_map.71), channel_id=1, source_target_pairs={{0,4},{2,6},{4,0},{6,2},{8,12},{10,14},{12,8},{14,10},{16,20},{18,... | collective-permute-start | bytes 786440 | tf_op jit(solution)/shard_map/ppermute | solution.py:644
  11.6 1.6 collective-permute-start.4
  13.8 3.8 %collective-permute-done.4.refs_1_.refs_4_ = bf16[128,768]{1,0:T(8,128)(2,1)S(1)} collective-permute-done((bf16[128,768]{1,0:T(8,128)(2,1)S(1)}, bf16[128,768]{1,0:T(8,128)(2,1)S(1)}, u32[]{:S(2)}, u32[]{:S(2)}) %collective-permute-start.4) | collective-permute-done | bytes 196640 | tf_op jit(solution)/shard_map/ppermute | solution.py:644
  18.7 1.6 collective-permute-start.2
  22.5 1.6 %collective-permute-start.11 = (bf16[256,128]{1,0:T(8,128)(2,1)S(1)}, bf16[256,128]{1,0:T(8,128)(2,1)S(1)}, u32[]{:S(2)}, u32[]{:S(2)}) collective-permute-start(bf16[256,128]{1,0:T(8,128)(2,1)S(1)} %get-tuple-element.69), channel_id=1, source_target_pairs={{0,8},{2,10},{4,12},{6,14},{8,16},{10,18},{12,20},{14,22},{16,24},... | collective-permute-start | bytes 196616 | tf_op jit(solution)/shard_map/ppermute | solution.py:648
  24.1 2.6 %collective-permute-start.10 = (bf16[256,128]{1,0:T(8,128)(2,1)S(1)}, bf16[256,128]{1,0:T(8,128)(2,1)S(1)}, u32[]{:S(2)}, u32[]{:S(2)}) collective-permute-start(bf16[256,128]{1,0:T(8,128)(2,1)S(1)} %get-tuple-element.68), channel_id=1, source_target_pairs={{0,16},{2,18},{4,20},{6,22},{8,24},{10,26},{12,28},{14,30},{16,0},... | collective-permute-start | bytes 196616 | tf_op jit(solution)/shard_map/ppermute | solution.py:648
  26.7 1.3 collective-permute-start.9
  28.0 5.1 %shard_map.77 = (bf16[4,1536,1024]{2,1,0:T(8,128)(2,1)}, f32[8,128]{1,0:T(8,128)S(1)}) custom-call(bf16[1536,4,1024]{2,1,0:T(4,128)(2,1)} %refs_0_.5, f32[256,128]{1,0:T(8,128)S(1)} %get-tuple-element.66.refs_1_), custom_call_target="tpu_custom_call" | custom-call | bytes 25169920 | tf_op jit(solution)/shard_map/pallas_call | solution.py:149
  33.4 1.3 collective-permute-start.23
  34.8 1.3 collective-permute-start.14
  36.1 2.6 %collective-permute-start.15 = (bf16[256,128]{1,0:T(8,128)(2,1)S(1)}, bf16[256,128]{1,0:T(8,128)(2,1)S(1)}, u32[]{:S(2)}, u32[]{:S(2)}) collective-permute-start(bf16[256,128]{1,0:T(8,128)(2,1)S(1)} %add_convert_fusion.3.refs_2_.refs_3_), channel_id=1, source_target_pairs={{0,16},{2,18},{4,20},{6,22},{8,24},{10,26},{12,28},{14,30},{16,0},... | collective-permute-start | bytes 196616 | tf_op jit(solution)/shard_map/ppermute | solution.py:648
  38.7 1.3 collective-permute-start.16
  42.0 1.7 %collective-permute-done.15.refs_5_ = bf16[256,128]{1,0:T(8,128)(2,1)S(1)} collective-permute-done((bf16[256,128]{1,0:T(8,128)(2,1)S(1)}, bf16[256,128]{1,0:T(8,128)(2,1)S(1)}, u32[]{:S(2)}, u32[]{:S(2)}) %collective-permute-start.15) | collective-permute-done | bytes 65568 | tf_op jit(solution)/shard_map/ppermute | solution.py:648
  46.3 3.8 %collective-permute-done.17.refs_4_ = bf16[512,128]{1,0:T(8,128)(2,1)S(1)} collective-permute-done((bf16[512,128]{1,0:T(8,128)(2,1)S(1)}, bf16[512,128]{1,0:T(8,128)(2,1)S(1)}, u32[]{:S(2)}, u32[]{:S(2)}) %collective-permute-start.17) | collective-permute-done | bytes 131104 | tf_op jit(solution)/shard_map/ppermute | solution.py:644
  52.1 2.0 %collective-permute-start.22 = (bf16[256,128]{1,0:T(8,128)(2,1)S(1)}, bf16[256,128]{1,0:T(8,128)(2,1)S(1)}, u32[]{:S(2)}, u32[]{:S(2)}) collective-permute-start(bf16[256,128]{1,0:T(8,128)(2,1)S(1)} %get-tuple-element.81), channel_id=1, source_target_pairs={{0,8},{2,10},{4,12},{6,14},{8,16},{10,18},{12,20},{14,22},{16,24},... | collective-permute-start | bytes 196616 | tf_op jit(solution)/shard_map/ppermute | solution.py:648
  54.1 1.9 %collective-permute-start.20 = (bf16[256,128]{1,0:T(8,128)(2,1)S(1)}, bf16[256,128]{1,0:T(8,128)(2,1)S(1)}, u32[]{:S(2)}, u32[]{:S(2)}) collective-permute-start(bf16[256,128]{1,0:T(8,128)(2,1)S(1)} %get-tuple-element.79), channel_id=1, source_target_pairs={{0,24},{2,26},{4,28},{6,30},{8,0},{10,2},{12,4},{14,6},{16,8},{18,... | collective-permute-start | bytes 196616 | tf_op jit(solution)/shard_map/ppermute | solution.py:648
  55.9 3.0 %collective-permute-done.22.refs_0_ = bf16[256,128]{1,0:T(8,128)(2,1)S(1)} collective-permute-done((bf16[256,128]{1,0:T(8,128)(2,1)S(1)}, bf16[256,128]{1,0:T(8,128)(2,1)S(1)}, u32[]{:S(2)}, u32[]{:S(2)}) %collective-permute-start.22) | collective-permute-done | bytes 65568 | tf_op jit(solution)/shard_map/ppermute | solution.py:648
  59.0 2.1 %collective-permute-done.19.refs_3_.refs_1_ = bf16[128,1536]{1,0:T(8,128)(2,1)S(1)} collective-permute-done((bf16[128,1536]{1,0:T(8,128)(2,1)S(1)}, bf16[128,1536]{1,0:T(8,128)(2,1)S(1)}, u32[]{:S(2)}, u32[]{:S(2)}) %collective-permute-start.19) | collective-permute-done | bytes 393248 | tf_op jit(solution)/shard_map/ppermute | solution.py:644
  62.5 1.7 %collective-permute-start.26 = (bf16[256,128]{1,0:T(8,128)(2,1)S(1)}, bf16[256,128]{1,0:T(8,128)(2,1)S(1)}, u32[]{:S(2)}, u32[]{:S(2)}) collective-permute-start(bf16[256,128]{1,0:T(8,128)(2,1)S(1)} %add_convert_fusion.2.refs_4_.refs_2_.refs_5_), channel_id=1, source_target_pairs={{0,8},{2,10},{4,12},{6,14},{8,16},{10,18},{12,20},{14,22},{16,24},... | collective-permute-start | bytes 196616 | tf_op jit(solution)/shard_map/ppermute | solution.py:648
  64.8 1.7 %collective-permute-start.28 = (bf16[256,128]{1,0:T(8,128)(2,1)S(1)}, bf16[256,128]{1,0:T(8,128)(2,1)S(1)}, u32[]{:S(2)}, u32[]{:S(2)}) collective-permute-start(bf16[256,128]{1,0:T(8,128)(2,1)S(1)} %add_convert_fusion.2.refs_4_.refs_2_.refs_5_), channel_id=1, source_target_pairs={{0,24},{2,26},{4,28},{6,30},{8,0},{10,2},{12,4},{14,6},{16,8},{18,... | collective-permute-start | bytes 196616 | tf_op jit(solution)/shard_map/ppermute | solution.py:648
  66.6 5.1 %shard_map.91 = (bf16[4,1536,1024]{2,1,0:T(8,128)(2,1)}, f32[8,128]{1,0:T(8,128)S(1)}) custom-call(bf16[1536,4,1024]{2,1,0:T(4,128)(2,1)} %refs_0_.5, bf16[4,1536,1024]{2,1,0:T(8,128)(2,1)} %get-tuple-element.85.refs_1_, bf16[256,128]{1,0:T(8,128)(2,1)S(1)} %add_convert_fusion.2.refs_4_.refs_2_.refs_5_), custom_call_target="tpu_custom_call", output_to_operand_aliasing={{0}: (1, {})} | custom-call | bytes 37752832 | tf_op jit(solution)/shard_map/pallas_call | solution.py:149
  75.5 3.6 %collective-permute-done.29.refs_4_ = bf16[512,128]{1,0:T(8,128)(2,1)S(1)} collective-permute-done((bf16[512,128]{1,0:T(8,128)(2,1)S(1)}, bf16[512,128]{1,0:T(8,128)(2,1)S(1)}, u32[]{:S(2)}, u32[]{:S(2)}) %collective-permute-start.29) | collective-permute-done | bytes 131104 | tf_op jit(solution)/shard_map/ppermute | solution.py:644
  82.6 2.6 %collective-permute-start.32 = (bf16[256,128]{1,0:T(8,128)(2,1)S(1)}, bf16[256,128]{1,0:T(8,128)(2,1)S(1)}, u32[]{:S(2)}, u32[]{:S(2)}) collective-permute-start(bf16[256,128]{1,0:T(8,128)(2,1)S(1)} %get-tuple-element.92), channel_id=1, source_target_pairs={{0,24},{2,26},{4,28},{6,30},{8,0},{10,2},{12,4},{14,6},{16,8},{18,... | collective-permute-start | bytes 196616 | tf_op jit(solution)/shard_map/ppermute | solution.py:648
  85.2 5.1 %shard_map.96 = (bf16[4,1536,1024]{2,1,0:T(8,128)(2,1)}, f32[8,128]{1,0:T(8,128)S(1)}) custom-call(bf16[1536,4,1024]{2,1,0:T(4,128)(2,1)} %refs_0_.5, bf16[4,1536,1024]{2,1,0:T(8,128)(2,1)} %get-tuple-element.95.refs_1_, f32[256,128]{1,0:T(8,128)S(1)} %get-tuple-element.91.refs_1_.refs_2_), custom_call_target="tpu_custom_call", output_to_operand_aliasing={{0}: (1, {})} | custom-call | bytes 37752832 | tf_op jit(solution)/shard_map/pallas_call | solution.py:149
  90.3 2.9 %collective-permute-done.35.refs_3_.refs_1_ = bf16[1024,256]{1,0:T(8,128)(2,1)S(1)} collective-permute-done((bf16[1024,256]{1,0:T(8,128)(2,1)S(1)}, bf16[1024,256]{1,0:T(8,128)(2,1)S(1)}, u32[]{:S(2)}, u32[]{:S(2)}) %collective-permute-start.35) | collective-permute-done | bytes 524320 | tf_op jit(solution)/shard_map/ppermute | solution.py:644
  93.5 2.0 %collective-permute-start.37 = (bf16[256,128]{1,0:T(8,128)(2,1)S(1)}, bf16[256,128]{1,0:T(8,128)(2,1)S(1)}, u32[]{:S(2)}, u32[]{:S(2)}) collective-permute-start(bf16[256,128]{1,0:T(8,128)(2,1)S(1)} %add_convert_fusion.1.refs_2_.refs_7_), channel_id=1, source_target_pairs={{0,8},{2,10},{4,12},{6,14},{8,16},{10,18},{12,20},{14,22},{16,24},... | collective-permute-start | bytes 196616 | tf_op jit(solution)/shard_map/ppermute | solution.py:648
  96.1 2.1 %collective-permute-start.39 = (bf16[256,128]{1,0:T(8,128)(2,1)S(1)}, bf16[256,128]{1,0:T(8,128)(2,1)S(1)}, u32[]{:S(2)}, u32[]{:S(2)}) collective-permute-start(bf16[256,128]{1,0:T(8,128)(2,1)S(1)} %add_convert_fusion.1.refs_2_.refs_7_), channel_id=1, source_target_pairs={{0,24},{2,26},{4,28},{6,30},{8,0},{10,2},{12,4},{14,6},{16,8},{18,... | collective-permute-start | bytes 196616 | tf_op jit(solution)/shard_map/ppermute | solution.py:648
  98.3 2.1 %collective-permute-done.37.refs_8_.refs_2_ = bf16[256,128]{1,0:T(8,128)(2,1)S(1)} collective-permute-done((bf16[256,128]{1,0:T(8,128)(2,1)S(1)}, bf16[256,128]{1,0:T(8,128)(2,1)S(1)}, u32[]{:S(2)}, u32[]{:S(2)}) %collective-permute-start.37) | collective-permute-done | bytes 65568 | tf_op jit(solution)/shard_map/ppermute | solution.py:648
  100.4 1.6 %collective-permute-start.49 = (bf16[2,1024,256]{2,1,0:T(8,128)(2,1)S(1)}, bf16[2,1024,256]{2,1,0:T(8,128)(2,1)S(1)}, u32[]{:S(2)}, u32[]{:S(2)}) collective-permute-start(bf16[2,1024,256]{2,1,0:T(8,128)(2,1)S(1)} %shard_map.104.refs_1_), channel_id=1, source_target_pairs={{0,2},{2,0},{4,6},{6,4},{8,10},{10,8},{12,14},{14,12},{16,18},{18,... | collective-permute-start | bytes 3145736 | tf_op jit(solution)/shard_map/ppermute | solution.py:644
  102.7 1.5 shard_map.99
  106.2 4.0 %collective-permute-done.40.refs_4_ = bf16[512,128]{1,0:T(8,128)(2,1)S(1)} collective-permute-done((bf16[512,128]{1,0:T(8,128)(2,1)S(1)}, bf16[512,128]{1,0:T(8,128)(2,1)S(1)}, u32[]{:S(2)}, u32[]{:S(2)}) %collective-permute-start.40) | collective-permute-done | bytes 131104 | tf_op jit(solution)/shard_map/ppermute | solution.py:644
  112.5 1.9 %collective-permute-start.44 = (bf16[256,128]{1,0:T(8,128)(2,1)S(1)}, bf16[256,128]{1,0:T(8,128)(2,1)S(1)}, u32[]{:S(2)}, u32[]{:S(2)}) collective-permute-start(bf16[256,128]{1,0:T(8,128)(2,1)S(1)} %get-tuple-element.104), channel_id=1, source_target_pairs={{0,8},{2,10},{4,12},{6,14},{8,16},{10,18},{12,20},{14,22},{16,24},... | collective-permute-start | bytes 196616 | tf_op jit(solution)/shard_map/ppermute | solution.py:648
  114.4 1.9 %collective-permute-start.42 = (bf16[256,128]{1,0:T(8,128)(2,1)S(1)}, bf16[256,128]{1,0:T(8,128)(2,1)S(1)}, u32[]{:S(2)}, u32[]{:S(2)}) collective-permute-start(bf16[256,128]{1,0:T(8,128)(2,1)S(1)} %get-tuple-element.102), channel_id=1, source_target_pairs={{0,24},{2,26},{4,28},{6,30},{8,0},{10,2},{12,4},{14,6},{16,8},{18,... | collective-permute-start | bytes 196616 | tf_op jit(solution)/shard_map/ppermute | solution.py:648
  116.3 2.7 %collective-permute-done.44.refs_0_ = bf16[256,128]{1,0:T(8,128)(2,1)S(1)} collective-permute-done((bf16[256,128]{1,0:T(8,128)(2,1)S(1)}, bf16[256,128]{1,0:T(8,128)(2,1)S(1)}, u32[]{:S(2)}, u32[]{:S(2)}) %collective-permute-start.44) | collective-permute-done | bytes 65568 | tf_op jit(solution)/shard_map/ppermute | solution.py:648
  119.4 2.3 %collective-permute-done.43 = bf16[256,128]{1,0:T(8,128)(2,1)S(1)} collective-permute-done((bf16[256,128]{1,0:T(8,128)(2,1)S(1)}, bf16[256,128]{1,0:T(8,128)(2,1)S(1)}, u32[]{:S(2)}, u32[]{:S(2)}) %collective-permute-start.43) | collective-permute-done | bytes 65568 | tf_op jit(solution)/shard_map/ppermute | solution.py:648
  121.8 1.3 collective-permute-start.52
  123.2 2.8 %collective-permute-start.47 = (bf16[256,128]{1,0:T(8,128)(2,1)S(1)}, bf16[256,128]{1,0:T(8,128)(2,1)S(1)}, u32[]{:S(2)}, u32[]{:S(2)}) collective-permute-start(bf16[256,128]{1,0:T(8,128)(2,1)S(1)} %add_convert_fusion.refs_3_.refs_1_.refs_2_), channel_id=1, source_target_pairs={{0,16},{2,18},{4,20},{6,22},{8,24},{10,26},{12,28},{14,30},{16,0},... | collective-permute-start | bytes 196616 | tf_op jit(solution)/shard_map/ppermute | solution.py:648
  127.0 2.6 %shard_map.105 = (bf16[4,1024,512]{2,1,0:T(8,128)(2,1)}, bf16[2,512,1024]{2,1,0:T(8,128)(2,1)S(1)}) custom-call(s32[4]{0:T(128)S(1)} %pad_add_fusion.refs_0_, bf16[2,1024,256]{2,1,0:T(8,128)(2,1)S(1)} %shard_map.104.refs_1_, bf16[2,1024,256]{2,1,0:T(8,128)(2,1)S(1)} %collective-permute-done.49.refs_2_, ...), custom_call_target="tpu_custom_call" | custom-call | bytes 8388624 | tf_op jit(solution)/shard_map/pallas_call | solution.py:149
  130.9 1.3 collective-permute-done.50.refs_2_
  134.5 1.4 collective-permute-done.52.refs_5_.refs_3_.refs_2_
  135.9 5.8 %shard_map.109 = (f32[256,1536]{1,0:T(8,128)S(1)}, bf16[256,1536]{1,0:T(8,128)(2,1)S(1)}) custom-call(s32[4]{0:T(128)S(1)} %pad_add_fusion.refs_0_, bf16[2,512,1024]{2,1,0:T(8,128)(2,1)S(1)} %get-tuple-element.105.refs_5_.refs_1_, bf16[4,1536,1024]{2,1,0:T(8,128)(2,1)} %get-tuple-element.108.refs_2_.refs_3_.refs_5_, ...), custom_call_target="tpu_custom_call" | custom-call | flops 3221225472 | bytes 17039376 | tf_op jit(solution)/shard_map/pallas_call | solution.py:149
  141.7 2.1 %collective-permute-start.54 = (bf16[512,256]{1,0:T(8,128)(2,1)S(1)}, bf16[512,256]{1,0:T(8,128)(2,1)S(1)}, u32[]{:S(2)}, u32[]{:S(2)}) collective-permute-start(bf16[512,256]{1,0:T(8,128)(2,1)S(1)} %shard_map.110.refs_2_), channel_id=1, source_target_pairs={{0,2},{2,0},{4,6},{6,4},{8,10},{10,8},{12,14},{14,12},{16,18},{18,... | collective-permute-start | bytes 786440 | tf_op jit(solution)/shard_map/ppermute | solution.py:644
  143.8 4.7 %shard_map.111 = (bf16[4,1024,512]{2,1,0:T(8,128)(2,1)}, f32[256,1536]{1,0:T(8,128)S(1)}, bf16[256,1536]{1,0:T(8,128)(2,1)S(1)}) custom-call(s32[4]{0:T(128)S(1)} %pad_add_fusion.refs_0_, bf16[2,512,256]{2,1,0:T(8,128)(2,1)S(1)} %shard_map.108.refs_4_.refs_2_.refs_1_, ...), custom_call_target="tpu_custom_call", output_to_operand_aliasing={{0}: (6, {})} | custom-call | flops 1610612736 | bytes 26738704 | tf_op jit(solution)/shard_map/pallas_call | solution.py:149
  148.8 4.8 %shard_map.112 = (bf16[4,1024,512]{2,1,0:T(8,128)(2,1)}, f32[256,1536]{1,0:T(8,128)S(1)}, bf16[256,1536]{1,0:T(8,128)(2,1)S(1)}) custom-call(s32[4]{0:T(128)S(1)} %pad_add_fusion.refs_0_, bf16[512,256]{1,0:T(8,128)(2,1)S(1)} %shard_map.107.refs_3_.refs_1_, bf16[512,256]{1,0:T(8,128)(2,1)S(1)} %shard_map.110.refs_2_, ...), custom_call_target="tpu_custom_call", output_to_operand_aliasing={{0}: (8, {})} | custom-call | flops 1610612736 | bytes 26738704 | tf_op jit(solution)/shard_map/pallas_call | solution.py:149
  153.6 2.3 %collective-permute-done.55 = bf16[256,1536]{1,0:T(8,128)(2,1)S(1)} collective-permute-done((bf16[256,1536]{1,0:T(8,128)(2,1)S(1)}, bf16[256,1536]{1,0:T(8,128)(2,1)S(1)}, u32[]{:S(2)}, u32[]{:S(2)}) %collective-permute-start.55) | collective-permute-done | bytes 786464 | tf_op jit(solution)/shard_map/ppermute | solution.py:651
  (119 shorter events, 33.9 us)
Async XLA Ops:
  1.9 7.9 %collective-permute-start = (bf16[128,768]{1,0:T(8,128)(2,1)S(1)}, bf16[128,768]{1,0:T(8,128)(2,1)S(1)}, u32[]{:S(2)}, u32[]{:S(2)}) collective-permute-start(bf16[128,768]{1,0:T(8,128)(2,1)S(1)} %get-tuple-element.62), channel_id=1, source_target_pairs={{0,4},{2,6},{4,0},{6,2},{8,12},{10,14},{12,8},{14,10},{16,20},{18,... | collective-permute-start | bytes 589832 | tf_op jit(solution)/shard_map/ppermute | solution.py:644
  5.0 8.9 %collective-permute-start.3 = (bf16[128,1152]{1,0:T(8,128)(2,1)S(1)}, bf16[128,1152]{1,0:T(8,128)(2,1)S(1)}, u32[]{:S(2)}, u32[]{:S(2)}) collective-permute-start(bf16[128,1152]{1,0:T(8,128)(2,1)S(1)} %get-tuple-element.65), channel_id=1, source_target_pairs={{0,2},{2,0},{4,6},{6,4},{8,10},{10,8},{12,14},{14,12},{16,18},{18,... | collective-permute-start | bytes 884744 | tf_op jit(solution)/shard_map/ppermute | solution.py:644
  9.9 7.8 %collective-permute-start.1 = (bf16[128,1024]{1,0:T(8,128)(2,1)S(1)}, bf16[128,1024]{1,0:T(8,128)(2,1)S(1)}, u32[]{:S(2)}, u32[]{:S(2)}) collective-permute-start(bf16[128,1024]{1,0:T(8,128)(2,1)S(1)} %shard_map.71), channel_id=1, source_target_pairs={{0,4},{2,6},{4,0},{6,2},{8,12},{10,14},{12,8},{14,10},{16,20},{18,... | collective-permute-start | bytes 786440 | tf_op jit(solution)/shard_map/ppermute | solution.py:644
  11.6 6.0 %collective-permute-start.4 = (bf16[128,768]{1,0:T(8,128)(2,1)S(1)}, bf16[128,768]{1,0:T(8,128)(2,1)S(1)}, u32[]{:S(2)}, u32[]{:S(2)}) collective-permute-start(bf16[128,768]{1,0:T(8,128)(2,1)S(1)} %shard_map.73.refs_2_), channel_id=1, source_target_pairs={{0,2},{2,0},{4,6},{6,4},{8,10},{10,8},{12,14},{14,12},{16,18},{18,... | collective-permute-start | bytes 589832 | tf_op jit(solution)/shard_map/ppermute | solution.py:644
  18.7 14.4 %collective-permute-start.2 = (bf16[2,128,1024]{2,1,0:T(8,128)(2,1)S(1)}, bf16[2,128,1024]{2,1,0:T(8,128)(2,1)S(1)}, u32[]{:S(2)}, u32[]{:S(2)}) collective-permute-start(bf16[2,128,1024]{2,1,0:T(8,128)(2,1)S(1)} %shard_map.72.refs_1_.refs_0_), channel_id=1, source_target_pairs={{0,2},{2,0},{4,6},{6,4},{8,10},{10,8},{12,14},{14,12},{16,18},{18,... | collective-permute-start | bytes 1572872 | tf_op jit(solution)/shard_map/ppermute | solution.py:644
  21.3 11.8 %collective-permute-start.12 = (bf16[128,1536]{1,0:T(8,128)(2,1)S(1)}, bf16[128,1536]{1,0:T(8,128)(2,1)S(1)}, u32[]{:S(2)}, u32[]{:S(2)}) collective-permute-start(bf16[128,1536]{1,0:T(8,128)(2,1)S(1)} %shard_map.76), channel_id=1, source_target_pairs={{0,4},{2,6},{4,0},{6,2},{8,12},{10,14},{12,8},{14,10},{16,20},{18,... | collective-permute-start | bytes 1179656 | tf_op jit(solution)/shard_map/ppermute | solution.py:644
  22.5 10.6 %collective-permute-start.11 = (bf16[256,128]{1,0:T(8,128)(2,1)S(1)}, bf16[256,128]{1,0:T(8,128)(2,1)S(1)}, u32[]{:S(2)}, u32[]{:S(2)}) collective-permute-start(bf16[256,128]{1,0:T(8,128)(2,1)S(1)} %get-tuple-element.69), channel_id=1, source_target_pairs={{0,8},{2,10},{4,12},{6,14},{8,16},{10,18},{12,20},{14,22},{16,24},... | collective-permute-start | bytes 196616 | tf_op jit(solution)/shard_map/ppermute | solution.py:648
  24.1 9.1 %collective-permute-start.10 = (bf16[256,128]{1,0:T(8,128)(2,1)S(1)}, bf16[256,128]{1,0:T(8,128)(2,1)S(1)}, u32[]{:S(2)}, u32[]{:S(2)}) collective-permute-start(bf16[256,128]{1,0:T(8,128)(2,1)S(1)} %get-tuple-element.68), channel_id=1, source_target_pairs={{0,16},{2,18},{4,20},{6,22},{8,24},{10,26},{12,28},{14,30},{16,0},... | collective-permute-start | bytes 196616 | tf_op jit(solution)/shard_map/ppermute | solution.py:648
  26.7 6.5 %collective-permute-start.9 = (bf16[256,128]{1,0:T(8,128)(2,1)S(1)}, bf16[256,128]{1,0:T(8,128)(2,1)S(1)}, u32[]{:S(2)}, u32[]{:S(2)}) collective-permute-start(bf16[256,128]{1,0:T(8,128)(2,1)S(1)} %get-tuple-element.67), channel_id=1, source_target_pairs={{0,24},{2,26},{4,28},{6,30},{8,0},{10,2},{12,4},{14,6},{16,8},{18,... | collective-permute-start | bytes 196616 | tf_op jit(solution)/shard_map/ppermute | solution.py:648
  33.3 10.6 %collective-permute-start.13 = (bf16[4,128,1024]{2,1,0:T(8,128)(2,1)S(1)}, bf16[4,128,1024]{2,1,0:T(8,128)(2,1)S(1)}, u32[]{:S(2)}, u32[]{:S(2)}) collective-permute-start(bf16[4,128,1024]{2,1,0:T(8,128)(2,1)S(1)} %shard_map.79.refs_1_), channel_id=1, source_target_pairs={{0,1},{1,0},{2,3},{3,2},{4,5},{5,4},{6,7},{7,6},{8,9},{9,8},{10,11... | collective-permute-start | bytes 3145736 | tf_op jit(solution)/shard_map/ppermute | solution.py:651
  33.4 22.5 %collective-permute-start.23 = (bf16[2,128,1536]{2,1,0:T(8,128)(2,1)S(1)}, bf16[2,128,1536]{2,1,0:T(8,128)(2,1)S(1)}, u32[]{:S(2)}, u32[]{:S(2)}) collective-permute-start(bf16[2,128,1536]{2,1,0:T(8,128)(2,1)S(1)} %shard_map.87.refs_1_.refs_0_), channel_id=1, source_target_pairs={{0,2},{2,0},{4,6},{6,4},{8,10},{10,8},{12,14},{14,12},{16,18},{18,... | collective-permute-start | bytes 2359304 | tf_op jit(solution)/shard_map/ppermute | solution.py:644
  34.8 6.5 %collective-permute-start.14 = (bf16[256,128]{1,0:T(8,128)(2,1)S(1)}, bf16[256,128]{1,0:T(8,128)(2,1)S(1)}, u32[]{:S(2)}, u32[]{:S(2)}) collective-permute-start(bf16[256,128]{1,0:T(8,128)(2,1)S(1)} %add_convert_fusion.3.refs_2_.refs_3_), channel_id=1, source_target_pairs={{0,8},{2,10},{4,12},{6,14},{8,16},{10,18},{12,20},{14,22},{16,24},... | collective-permute-start | bytes 196616 | tf_op jit(solution)/shard_map/ppermute | solution.py:648
  36.1 7.6 %collective-permute-start.15 = (bf16[256,128]{1,0:T(8,128)(2,1)S(1)}, bf16[256,128]{1,0:T(8,128)(2,1)S(1)}, u32[]{:S(2)}, u32[]{:S(2)}) collective-permute-start(bf16[256,128]{1,0:T(8,128)(2,1)S(1)} %add_convert_fusion.3.refs_2_.refs_3_), channel_id=1, source_target_pairs={{0,16},{2,18},{4,20},{6,22},{8,24},{10,26},{12,28},{14,30},{16,0},... | collective-permute-start | bytes 196616 | tf_op jit(solution)/shard_map/ppermute | solution.py:648
  38.7 5.3 %collective-permute-start.16 = (bf16[256,128]{1,0:T(8,128)(2,1)S(1)}, bf16[256,128]{1,0:T(8,128)(2,1)S(1)}, u32[]{:S(2)}, u32[]{:S(2)}) collective-permute-start(bf16[256,128]{1,0:T(8,128)(2,1)S(1)} %add_convert_fusion.3.refs_2_.refs_3_), channel_id=1, source_target_pairs={{0,24},{2,26},{4,28},{6,30},{8,0},{10,2},{12,4},{14,6},{16,8},{18,... | collective-permute-start | bytes 196616 | tf_op jit(solution)/shard_map/ppermute | solution.py:648
  41.3 5.0 %collective-permute-start.18 = (bf16[128,512]{1,0:T(8,128)(2,1)S(1)}, bf16[128,512]{1,0:T(8,128)(2,1)S(1)}, u32[]{:S(2)}, u32[]{:S(2)}) collective-permute-start(bf16[128,512]{1,0:T(8,128)(2,1)S(1)} %shard_map.81), channel_id=1, source_target_pairs={{0,4},{2,6},{4,0},{6,2},{8,12},{10,14},{12,8},{14,10},{16,20},{18,... | collective-permute-start | bytes 393224 | tf_op jit(solution)/shard_map/ppermute | solution.py:644
  44.9 5.2 %collective-permute-start.17 = (bf16[512,128]{1,0:T(8,128)(2,1)S(1)}, bf16[512,128]{1,0:T(8,128)(2,1)S(1)}, u32[]{:S(2)}, u32[]{:S(2)}) collective-permute-start(bf16[512,128]{1,0:T(8,128)(2,1)S(1)} %get-tuple-element.74), channel_id=1, source_target_pairs={{0,4},{2,6},{4,0},{6,2},{8,12},{10,14},{12,8},{14,10},{16,20},{18,... | collective-permute-start | bytes 393224 | tf_op jit(solution)/shard_map/ppermute | solution.py:644
  51.1 9.9 %collective-permute-start.19 = (bf16[128,1536]{1,0:T(8,128)(2,1)S(1)}, bf16[128,1536]{1,0:T(8,128)(2,1)S(1)}, u32[]{:S(2)}, u32[]{:S(2)}) collective-permute-start(bf16[128,1536]{1,0:T(8,128)(2,1)S(1)} %shard_map.84), channel_id=1, source_target_pairs={{0,4},{2,6},{4,0},{6,2},{8,12},{10,14},{12,8},{14,10},{16,20},{18,... | collective-permute-start | bytes 1179656 | tf_op jit(solution)/shard_map/ppermute | solution.py:644
  52.1 6.9 %collective-permute-start.22 = (bf16[256,128]{1,0:T(8,128)(2,1)S(1)}, bf16[256,128]{1,0:T(8,128)(2,1)S(1)}, u32[]{:S(2)}, u32[]{:S(2)}) collective-permute-start(bf16[256,128]{1,0:T(8,128)(2,1)S(1)} %get-tuple-element.81), channel_id=1, source_target_pairs={{0,8},{2,10},{4,12},{6,14},{8,16},{10,18},{12,20},{14,22},{16,24},... | collective-permute-start | bytes 196616 | tf_op jit(solution)/shard_map/ppermute | solution.py:648
  54.1 7.0 %collective-permute-start.20 = (bf16[256,128]{1,0:T(8,128)(2,1)S(1)}, bf16[256,128]{1,0:T(8,128)(2,1)S(1)}, u32[]{:S(2)}, u32[]{:S(2)}) collective-permute-start(bf16[256,128]{1,0:T(8,128)(2,1)S(1)} %get-tuple-element.79), channel_id=1, source_target_pairs={{0,24},{2,26},{4,28},{6,30},{8,0},{10,2},{12,4},{14,6},{16,8},{18,... | collective-permute-start | bytes 196616 | tf_op jit(solution)/shard_map/ppermute | solution.py:648
  55.9 5.5 %collective-permute-start.21 = (bf16[256,128]{1,0:T(8,128)(2,1)S(1)}, bf16[256,128]{1,0:T(8,128)(2,1)S(1)}, u32[]{:S(2)}, u32[]{:S(2)}) collective-permute-start(bf16[256,128]{1,0:T(8,128)(2,1)S(1)} %get-tuple-element.80), channel_id=1, source_target_pairs={{0,16},{2,18},{4,20},{6,22},{8,24},{10,26},{12,28},{14,30},{16,0},... | collective-permute-start | bytes 196616 | tf_op jit(solution)/shard_map/ppermute | solution.py:648
  61.5 10.2 %collective-permute-start.25 = (bf16[4,128,1536]{2,1,0:T(8,128)(2,1)S(1)}, bf16[4,128,1536]{2,1,0:T(8,128)(2,1)S(1)}, u32[]{:S(2)}, u32[]{:S(2)}) collective-permute-start(bf16[4,128,1536]{2,1,0:T(8,128)(2,1)S(1)} %shard_map.90.refs_1_), channel_id=1, source_target_pairs={{0,1},{1,0},{2,3},{3,2},{4,5},{5,4},{6,7},{7,6},{8,9},{9,8},{10,11... | collective-permute-start | bytes 4718600 | tf_op jit(solution)/shard_map/ppermute | solution.py:651
  61.7 28.6 %collective-permute-start.24 = (bf16[2,128,2048]{2,1,0:T(8,128)(2,1)S(1)}, bf16[2,128,2048]{2,1,0:T(8,128)(2,1)S(1)}, u32[]{:S(2)}, u32[]{:S(2)}) collective-permute-start(bf16[2,128,2048]{2,1,0:T(8,128)(2,1)S(1)} %shard_map.89.refs_1_.refs_0_), channel_id=1, source_target_pairs={{0,2},{2,0},{4,6},{6,4},{8,10},{10,8},{12,14},{14,12},{16,18},{18,... | collective-permute-start | bytes 3145736 | tf_op jit(solution)/shard_map/ppermute | solution.py:644
  62.5 9.2 %collective-permute-start.26 = (bf16[256,128]{1,0:T(8,128)(2,1)S(1)}, bf16[256,128]{1,0:T(8,128)(2,1)S(1)}, u32[]{:S(2)}, u32[]{:S(2)}) collective-permute-start(bf16[256,128]{1,0:T(8,128)(2,1)S(1)} %add_convert_fusion.2.refs_4_.refs_2_.refs_5_), channel_id=1, source_target_pairs={{0,8},{2,10},{4,12},{6,14},{8,16},{10,18},{12,20},{14,22},{16,24},... | collective-permute-start | bytes 196616 | tf_op jit(solution)/shard_map/ppermute | solution.py:648
  64.2 7.5 %collective-permute-start.27 = (bf16[256,128]{1,0:T(8,128)(2,1)S(1)}, bf16[256,128]{1,0:T(8,128)(2,1)S(1)}, u32[]{:S(2)}, u32[]{:S(2)}) collective-permute-start(bf16[256,128]{1,0:T(8,128)(2,1)S(1)} %add_convert_fusion.2.refs_4_.refs_2_.refs_5_), channel_id=1, source_target_pairs={{0,16},{2,18},{4,20},{6,22},{8,24},{10,26},{12,28},{14,30},{16,0},... | collective-permute-start | bytes 196616 | tf_op jit(solution)/shard_map/ppermute | solution.py:648
  64.8 6.9 %collective-permute-start.28 = (bf16[256,128]{1,0:T(8,128)(2,1)S(1)}, bf16[256,128]{1,0:T(8,128)(2,1)S(1)}, u32[]{:S(2)}, u32[]{:S(2)}) collective-permute-start(bf16[256,128]{1,0:T(8,128)(2,1)S(1)} %add_convert_fusion.2.refs_4_.refs_2_.refs_5_), channel_id=1, source_target_pairs={{0,24},{2,26},{4,28},{6,30},{8,0},{10,2},{12,4},{14,6},{16,8},{18,... | collective-permute-start | bytes 196616 | tf_op jit(solution)/shard_map/ppermute | solution.py:648
  71.7 3.1 %collective-permute-start.30 = (bf16[512,128]{1,0:T(8,128)(2,1)S(1)}, bf16[512,128]{1,0:T(8,128)(2,1)S(1)}, u32[]{:S(2)}, u32[]{:S(2)}) collective-permute-start(bf16[512,128]{1,0:T(8,128)(2,1)S(1)} %get-tuple-element.84.refs_4_), channel_id=1, source_target_pairs={{0,1},{1,0},{2,3},{3,2},{4,5},{5,4},{6,7},{7,6},{8,9},{9,8},{10,11... | collective-permute-start | bytes 393224 | tf_op jit(solution)/shard_map/ppermute | solution.py:651
  73.6 5.5 %collective-permute-start.29 = (bf16[512,128]{1,0:T(8,128)(2,1)S(1)}, bf16[512,128]{1,0:T(8,128)(2,1)S(1)}, u32[]{:S(2)}, u32[]{:S(2)}) collective-permute-start(bf16[512,128]{1,0:T(8,128)(2,1)S(1)} %get-tuple-element.88), channel_id=1, source_target_pairs={{0,4},{2,6},{4,0},{6,2},{8,12},{10,14},{12,8},{14,10},{16,20},{18,... | collective-permute-start | bytes 393224 | tf_op jit(solution)/shard_map/ppermute | solution.py:644
  80.1 13.1 %collective-permute-start.35 = (bf16[1024,256]{1,0:T(8,128)(2,1)S(1)}, bf16[1024,256]{1,0:T(8,128)(2,1)S(1)}, u32[]{:S(2)}, u32[]{:S(2)}) collective-permute-start(bf16[1024,256]{1,0:T(8,128)(2,1)S(1)} %shard_map.95.refs_0_), channel_id=1, source_target_pairs={{0,4},{2,6},{4,0},{6,2},{8,12},{10,14},{12,8},{14,10},{16,20},{18,... | collective-permute-start | bytes 1572872 | tf_op jit(solution)/shard_map/ppermute | solution.py:644
  81.4 8.9 %collective-permute-start.34 = (bf16[256,128]{1,0:T(8,128)(2,1)S(1)}, bf16[256,128]{1,0:T(8,128)(2,1)S(1)}, u32[]{:S(2)}, u32[]{:S(2)}) collective-permute-start(bf16[256,128]{1,0:T(8,128)(2,1)S(1)} %get-tuple-element.94), channel_id=1, source_target_pairs={{0,8},{2,10},{4,12},{6,14},{8,16},{10,18},{12,20},{14,22},{16,24},... | collective-permute-start | bytes 196616 | tf_op jit(solution)/shard_map/ppermute | solution.py:648
  82.6 10.6 %collective-permute-start.32 = (bf16[256,128]{1,0:T(8,128)(2,1)S(1)}, bf16[256,128]{1,0:T(8,128)(2,1)S(1)}, u32[]{:S(2)}, u32[]{:S(2)}) collective-permute-start(bf16[256,128]{1,0:T(8,128)(2,1)S(1)} %get-tuple-element.92), channel_id=1, source_target_pairs={{0,24},{2,26},{4,28},{6,30},{8,0},{10,2},{12,4},{14,6},{16,8},{18,... | collective-permute-start | bytes 196616 | tf_op jit(solution)/shard_map/ppermute | solution.py:648
  85.2 8.1 %collective-permute-start.33 = (bf16[256,128]{1,0:T(8,128)(2,1)S(1)}, bf16[256,128]{1,0:T(8,128)(2,1)S(1)}, u32[]{:S(2)}, u32[]{:S(2)}) collective-permute-start(bf16[256,128]{1,0:T(8,128)(2,1)S(1)} %get-tuple-element.93), channel_id=1, source_target_pairs={{0,16},{2,18},{4,20},{6,22},{8,24},{10,26},{12,28},{14,30},{16,0},... | collective-permute-start | bytes 196616 | tf_op jit(solution)/shard_map/ppermute | solution.py:648
  93.4 9.3 %collective-permute-start.36 = (bf16[4,128,2048]{2,1,0:T(8,128)(2,1)S(1)}, bf16[4,128,2048]{2,1,0:T(8,128)(2,1)S(1)}, u32[]{:S(2)}, u32[]{:S(2)}) collective-permute-start(bf16[4,128,2048]{2,1,0:T(8,128)(2,1)S(1)} %shard_map.98.refs_1_), channel_id=1, source_target_pairs={{0,1},{1,0},{2,3},{3,2},{4,5},{5,4},{6,7},{7,6},{8,9},{9,8},{10,11... | collective-permute-start | bytes 6291464 | tf_op jit(solution)/shard_map/ppermute | solution.py:651
  93.5 6.8 %collective-permute-start.37 = (bf16[256,128]{1,0:T(8,128)(2,1)S(1)}, bf16[256,128]{1,0:T(8,128)(2,1)S(1)}, u32[]{:S(2)}, u32[]{:S(2)}) collective-permute-start(bf16[256,128]{1,0:T(8,128)(2,1)S(1)} %add_convert_fusion.1.refs_2_.refs_7_), channel_id=1, source_target_pairs={{0,8},{2,10},{4,12},{6,14},{8,16},{10,18},{12,20},{14,22},{16,24},... | collective-permute-start | bytes 196616 | tf_op jit(solution)/shard_map/ppermute | solution.py:648
  95.5 7.2 %collective-permute-start.38 = (bf16[256,128]{1,0:T(8,128)(2,1)S(1)}, bf16[256,128]{1,0:T(8,128)(2,1)S(1)}, u32[]{:S(2)}, u32[]{:S(2)}) collective-permute-start(bf16[256,128]{1,0:T(8,128)(2,1)S(1)} %add_convert_fusion.1.refs_2_.refs_7_), channel_id=1, source_target_pairs={{0,16},{2,18},{4,20},{6,22},{8,24},{10,26},{12,28},{14,30},{16,0},... | collective-permute-start | bytes 196616 | tf_op jit(solution)/shard_map/ppermute | solution.py:648
  96.1 6.5 %collective-permute-start.39 = (bf16[256,128]{1,0:T(8,128)(2,1)S(1)}, bf16[256,128]{1,0:T(8,128)(2,1)S(1)}, u32[]{:S(2)}, u32[]{:S(2)}) collective-permute-start(bf16[256,128]{1,0:T(8,128)(2,1)S(1)} %add_convert_fusion.1.refs_2_.refs_7_), channel_id=1, source_target_pairs={{0,24},{2,26},{4,28},{6,30},{8,0},{10,2},{12,4},{14,6},{16,8},{18,... | collective-permute-start | bytes 196616 | tf_op jit(solution)/shard_map/ppermute | solution.py:648
  100.4 26.6 %collective-permute-start.49 = (bf16[2,1024,256]{2,1,0:T(8,128)(2,1)S(1)}, bf16[2,1024,256]{2,1,0:T(8,128)(2,1)S(1)}, u32[]{:S(2)}, u32[]{:S(2)}) collective-permute-start(bf16[2,1024,256]{2,1,0:T(8,128)(2,1)S(1)} %shard_map.104.refs_1_), channel_id=1, source_target_pairs={{0,2},{2,0},{4,6},{6,4},{8,10},{10,8},{12,14},{14,12},{16,18},{18,... | collective-permute-start | bytes 3145736 | tf_op jit(solution)/shard_map/ppermute | solution.py:644
  104.3 5.9 %collective-permute-start.40 = (bf16[512,128]{1,0:T(8,128)(2,1)S(1)}, bf16[512,128]{1,0:T(8,128)(2,1)S(1)}, u32[]{:S(2)}, u32[]{:S(2)}) collective-permute-start(bf16[512,128]{1,0:T(8,128)(2,1)S(1)} %get-tuple-element.98), channel_id=1, source_target_pairs={{0,4},{2,6},{4,0},{6,2},{8,12},{10,14},{12,8},{14,10},{16,20},{18,... | collective-permute-start | bytes 393224 | tf_op jit(solution)/shard_map/ppermute | solution.py:644
  111.2 7.9 %collective-permute-start.45 = (bf16[512,256]{1,0:T(8,128)(2,1)S(1)}, bf16[512,256]{1,0:T(8,128)(2,1)S(1)}, u32[]{:S(2)}, u32[]{:S(2)}) collective-permute-start(bf16[512,256]{1,0:T(8,128)(2,1)S(1)} %shard_map.102.refs_0_), channel_id=1, source_target_pairs={{0,4},{2,6},{4,0},{6,2},{8,12},{10,14},{12,8},{14,10},{16,20},{18,... | collective-permute-start | bytes 786440 | tf_op jit(solution)/shard_map/ppermute | solution.py:644
  112.5 6.6 %collective-permute-start.44 = (bf16[256,128]{1,0:T(8,128)(2,1)S(1)}, bf16[256,128]{1,0:T(8,128)(2,1)S(1)}, u32[]{:S(2)}, u32[]{:S(2)}) collective-permute-start(bf16[256,128]{1,0:T(8,128)(2,1)S(1)} %get-tuple-element.104), channel_id=1, source_target_pairs={{0,8},{2,10},{4,12},{6,14},{8,16},{10,18},{12,20},{14,22},{16,24},... | collective-permute-start | bytes 196616 | tf_op jit(solution)/shard_map/ppermute | solution.py:648
  114.4 5.0 %collective-permute-start.42 = (bf16[256,128]{1,0:T(8,128)(2,1)S(1)}, bf16[256,128]{1,0:T(8,128)(2,1)S(1)}, u32[]{:S(2)}, u32[]{:S(2)}) collective-permute-start(bf16[256,128]{1,0:T(8,128)(2,1)S(1)} %get-tuple-element.102), channel_id=1, source_target_pairs={{0,24},{2,26},{4,28},{6,30},{8,0},{10,2},{12,4},{14,6},{16,8},{18,... | collective-permute-start | bytes 196616 | tf_op jit(solution)/shard_map/ppermute | solution.py:648
  116.3 5.4 %collective-permute-start.43 = (bf16[256,128]{1,0:T(8,128)(2,1)S(1)}, bf16[256,128]{1,0:T(8,128)(2,1)S(1)}, u32[]{:S(2)}, u32[]{:S(2)}) collective-permute-start(bf16[256,128]{1,0:T(8,128)(2,1)S(1)} %get-tuple-element.103), channel_id=1, source_target_pairs={{0,16},{2,18},{4,20},{6,22},{8,24},{10,26},{12,28},{14,30},{16,0},... | collective-permute-start | bytes 196616 | tf_op jit(solution)/shard_map/ppermute | solution.py:648
  121.8 14.1 %collective-permute-start.52 = (bf16[2,512,256]{2,1,0:T(8,128)(2,1)S(1)}, bf16[2,512,256]{2,1,0:T(8,128)(2,1)S(1)}, u32[]{:S(2)}, u32[]{:S(2)}) collective-permute-start(bf16[2,512,256]{2,1,0:T(8,128)(2,1)S(1)} %shard_map.108.refs_4_.refs_2_.refs_1_), channel_id=1, source_target_pairs={{0,2},{2,0},{4,6},{6,4},{8,10},{10,8},{12,14},{14,12},{16,18},{18,... | collective-permute-start | bytes 1572872 | tf_op jit(solution)/shard_map/ppermute | solution.py:644
  123.2 6.5 %collective-permute-start.46 = (bf16[256,128]{1,0:T(8,128)(2,1)S(1)}, bf16[256,128]{1,0:T(8,128)(2,1)S(1)}, u32[]{:S(2)}, u32[]{:S(2)}) collective-permute-start(bf16[256,128]{1,0:T(8,128)(2,1)S(1)} %add_convert_fusion.refs_3_.refs_1_.refs_2_), channel_id=1, source_target_pairs={{0,8},{2,10},{4,12},{6,14},{8,16},{10,18},{12,20},{14,22},{16,24},... | collective-permute-start | bytes 196616 | tf_op jit(solution)/shard_map/ppermute | solution.py:648
  123.2 6.5 %collective-permute-start.47 = (bf16[256,128]{1,0:T(8,128)(2,1)S(1)}, bf16[256,128]{1,0:T(8,128)(2,1)S(1)}, u32[]{:S(2)}, u32[]{:S(2)}) collective-permute-start(bf16[256,128]{1,0:T(8,128)(2,1)S(1)} %add_convert_fusion.refs_3_.refs_1_.refs_2_), channel_id=1, source_target_pairs={{0,16},{2,18},{4,20},{6,22},{8,24},{10,26},{12,28},{14,30},{16,0},... | collective-permute-start | bytes 196616 | tf_op jit(solution)/shard_map/ppermute | solution.py:648
  126.0 4.3 %collective-permute-start.48 = (bf16[256,128]{1,0:T(8,128)(2,1)S(1)}, bf16[256,128]{1,0:T(8,128)(2,1)S(1)}, u32[]{:S(2)}, u32[]{:S(2)}) collective-permute-start(bf16[256,128]{1,0:T(8,128)(2,1)S(1)} %add_convert_fusion.refs_3_.refs_1_.refs_2_), channel_id=1, source_target_pairs={{0,24},{2,26},{4,28},{6,30},{8,0},{10,2},{12,4},{14,6},{16,8},{18,... | collective-permute-start | bytes 196616 | tf_op jit(solution)/shard_map/ppermute | solution.py:648
  132.9 8.8 %collective-permute-start.51 = (bf16[512,256]{1,0:T(8,128)(2,1)S(1)}, bf16[512,256]{1,0:T(8,128)(2,1)S(1)}, u32[]{:S(2)}, u32[]{:S(2)}) collective-permute-start(bf16[512,256]{1,0:T(8,128)(2,1)S(1)} %shard_map.107.refs_3_.refs_1_), channel_id=1, source_target_pairs={{0,4},{2,6},{4,0},{6,2},{8,12},{10,14},{12,8},{14,10},{16,20},{18,... | collective-permute-start | bytes 786440 | tf_op jit(solution)/shard_map/ppermute | solution.py:644
  134.1 14.5 %collective-permute-start.53 = (bf16[512,256]{1,0:T(8,128)(2,1)S(1)}, bf16[512,256]{1,0:T(8,128)(2,1)S(1)}, u32[]{:S(2)}, u32[]{:S(2)}) collective-permute-start(bf16[512,256]{1,0:T(8,128)(2,1)S(1)} %shard_map.107.refs_3_.refs_1_), channel_id=1, source_target_pairs={{0,2},{2,0},{4,6},{6,4},{8,10},{10,8},{12,14},{14,12},{16,18},{18,... | collective-permute-start | bytes 786440 | tf_op jit(solution)/shard_map/ppermute | solution.py:644
  141.7 7.1 %collective-permute-start.54 = (bf16[512,256]{1,0:T(8,128)(2,1)S(1)}, bf16[512,256]{1,0:T(8,128)(2,1)S(1)}, u32[]{:S(2)}, u32[]{:S(2)}) collective-permute-start(bf16[512,256]{1,0:T(8,128)(2,1)S(1)} %shard_map.110.refs_2_), channel_id=1, source_target_pairs={{0,2},{2,0},{4,6},{6,4},{8,10},{10,8},{12,14},{14,12},{16,18},{18,... | collective-permute-start | bytes 786440 | tf_op jit(solution)/shard_map/ppermute | solution.py:644
  (9 other events, 23.4 us)

commit v7 on v6

--- a/solution.py
+++ b/solution.py
@@ -675,7 +675,7 @@
         return join(form, meta, parts, after)
 
     turns = 3
-    block = 128
+    block = 256
     while rest % (turns * block):
         turns -= 1
     last = steps - 1
@@ -707,7 +707,7 @@
         else:
             first = up([gate(whole, [products[0]])] * py)
         by_sum[s] += first[1:]
-        if s < turns and s % 2 == 0:
+        if s < turns:
             flat, mark = flat_rest(lower_rest, flat, s, turns, block, [products[0]])
             by_sum[s].append(mark)
         arrivals = [along_depth(products[k], -k) for k in range(1, depth)]
@@ -726,9 +726,6 @@
         if s + 3 in ahead:
             ahead[s + 3] = up([gate(x, pieces[1:2]) for x in ahead[s + 3]])
             by_diag[s + 1] += ahead[s + 3][1:]
-        if s < turns and s % 2:
-            flat, mark = flat_rest(lower_rest, flat, s, turns, block, [mine])
-            by_lower[s + 1].append(mark)
         if s == last:
             buffer, new = write(0, steps, form, meta, ready, buffer, [mine])
             turned.append(new)

time: 158 us -> 157 us (level)
  waiting for transfers between devices: 41.9 us -> 44.9 us
  Pallas kernels: 48.8 us -> 45.9 us
    pallas_call x45, Pallas kernels: 48.8 us -> 45.9 us  [call(): pl.pallas_call(run, out_shape=tuple(outs), in_specs=list(specs) + [pl.Blo...]
  transfers between devices with their start and end apart: 56 -> 56, of which waited for: 25 -> 26; matrix products, arithmetic and copies ran while one was open for 0% -> 0% of each run, Pallas kernels for 27% -> 25%
where the time goes in v7:
time: 157 us
  starting transfers between devices  63.6 us (41%)
  Pallas kernels  45.9 us (29%)
  waiting for transfers between devices  44.9 us (29%)
    pallas_call x45, Pallas kernels, call(): pl.pallas_call(run, out_shape=tuple(outs), in_specs=list(specs) + [pl.Blo...  45.9 us
    ppermute x24, starting transfers between devices, along_depth(): return lax.ppermute(x, 'rows', pairs)  35.3 us
    ppermute x20, starting transfers between devices, along_plane(): return lax.ppermute(x, 'rows', pairs)  26.8 us
    ppermute x20, waiting for transfers between devices, along_plane(): return lax.ppermute(x, 'rows', pairs)  24.3 us
    ppermute x24, waiting for transfers between devices, along_depth(): return lax.ppermute(x, 'rows', pairs)  16.3 us
    ppermute x12, waiting for transfers between devices, along_cols(): lax.ppermute(x, 'cols', [(i, (i + k) % n_cols) for i in range(n_cols)])  4.27 us
  transfers between devices with their start and end apart: 56, of which 26 were waited for; matrix products, arithmetic and copies ran while one was open for 0% of the time, Pallas kernels for 25%

profile of v7, /device:TPU:0, one launch (start us, length us, event | category | flops | bytes accessed | tf_op | source)
XLA Modules:
  0.0 156.9 jit_solution(7469034734534626265)
XLA Ops:
  1.9 3.0 %collective-permute-start = (bf16[128,768]{1,0:T(8,128)(2,1)S(1)}, bf16[128,768]{1,0:T(8,128)(2,1)S(1)}, u32[]{:S(2)}, u32[]{:S(2)}) collective-permute-start(bf16[128,768]{1,0:T(8,128)(2,1)S(1)} %get-tuple-element.62), channel_id=1, source_target_pairs={{0,4},{2,6},{4,0},{6,2},{8,12},{10,14},{12,8},{14,10},{16,20},{18,... | collective-permute-start | bytes 589832 | tf_op jit(solution)/shard_map/ppermute | solution.py:644
  5.0 1.5 collective-permute-start.3
  6.4 3.4 %shard_map.68 = (bf16[128,1024]{1,0:T(8,128)(2,1)S(1)}, bf16[128,1024]{1,0:T(8,128)(2,1)S(1)}, bf16[128,1536]{1,0:T(8,128)(2,1)S(1)}, bf16[128,1536]{1,0:T(8,128...) custom-call(s32[4]{0:T(128)S(1)} %pad_add_fusion.refs_0_, ...), custom_call_target="tpu_custom_call" | custom-call | bytes 60817536 | tf_op jit(solution)/shard_map/pallas_call | solution.py:149
  9.9 1.7 %collective-permute-start.1 = (bf16[128,1024]{1,0:T(8,128)(2,1)S(1)}, bf16[128,1024]{1,0:T(8,128)(2,1)S(1)}, u32[]{:S(2)}, u32[]{:S(2)}) collective-permute-start(bf16[128,1024]{1,0:T(8,128)(2,1)S(1)} %shard_map.71), channel_id=1, source_target_pairs={{0,4},{2,6},{4,0},{6,2},{8,12},{10,14},{12,8},{14,10},{16,20},{18,... | collective-permute-start | bytes 786440 | tf_op jit(solution)/shard_map/ppermute | solution.py:644
  11.6 1.6 collective-permute-start.4
  13.8 3.8 %collective-permute-done.4.refs_1_.refs_4_ = bf16[128,768]{1,0:T(8,128)(2,1)S(1)} collective-permute-done((bf16[128,768]{1,0:T(8,128)(2,1)S(1)}, bf16[128,768]{1,0:T(8,128)(2,1)S(1)}, u32[]{:S(2)}, u32[]{:S(2)}) %collective-permute-start.4) | collective-permute-done | bytes 196640 | tf_op jit(solution)/shard_map/ppermute | solution.py:644
  18.7 1.6 collective-permute-start.2
  22.5 1.6 %collective-permute-start.11 = (bf16[256,128]{1,0:T(8,128)(2,1)S(1)}, bf16[256,128]{1,0:T(8,128)(2,1)S(1)}, u32[]{:S(2)}, u32[]{:S(2)}) collective-permute-start(bf16[256,128]{1,0:T(8,128)(2,1)S(1)} %get-tuple-element.69), channel_id=1, source_target_pairs={{0,8},{2,10},{4,12},{6,14},{8,16},{10,18},{12,20},{14,22},{16,24},... | collective-permute-start | bytes 196616 | tf_op jit(solution)/shard_map/ppermute | solution.py:648
  24.1 2.6 %collective-permute-start.10 = (bf16[256,128]{1,0:T(8,128)(2,1)S(1)}, bf16[256,128]{1,0:T(8,128)(2,1)S(1)}, u32[]{:S(2)}, u32[]{:S(2)}) collective-permute-start(bf16[256,128]{1,0:T(8,128)(2,1)S(1)} %get-tuple-element.68), channel_id=1, source_target_pairs={{0,16},{2,18},{4,20},{6,22},{8,24},{10,26},{12,28},{14,30},{16,0},... | collective-permute-start | bytes 196616 | tf_op jit(solution)/shard_map/ppermute | solution.py:648
  26.7 1.3 collective-permute-start.9
  28.0 4.2 %shard_map.77 = (bf16[4,1536,1024]{2,1,0:T(8,128)(2,1)}, f32[8,128]{1,0:T(8,128)S(1)}) custom-call(bf16[1536,4,1024]{2,1,0:T(4,128)(2,1)} %refs_0_.5, f32[256,128]{1,0:T(8,128)S(1)} %get-tuple-element.66.refs_1_), custom_call_target="tpu_custom_call" | custom-call | bytes 25169920 | tf_op jit(solution)/shard_map/pallas_call | solution.py:149
  32.9 1.6 collective-permute-start.23
  34.5 1.6 %collective-permute-start.14 = (bf16[256,128]{1,0:T(8,128)(2,1)S(1)}, bf16[256,128]{1,0:T(8,128)(2,1)S(1)}, u32[]{:S(2)}, u32[]{:S(2)}) collective-permute-start(bf16[256,128]{1,0:T(8,128)(2,1)S(1)} %add_convert_fusion.3.refs_2_.refs_3_), channel_id=1, source_target_pairs={{0,8},{2,10},{4,12},{6,14},{8,16},{10,18},{12,20},{14,22},{16,24},... | collective-permute-start | bytes 196616 | tf_op jit(solution)/shard_map/ppermute | solution.py:648
  36.1 2.6 %collective-permute-start.15 = (bf16[256,128]{1,0:T(8,128)(2,1)S(1)}, bf16[256,128]{1,0:T(8,128)(2,1)S(1)}, u32[]{:S(2)}, u32[]{:S(2)}) collective-permute-start(bf16[256,128]{1,0:T(8,128)(2,1)S(1)} %add_convert_fusion.3.refs_2_.refs_3_), channel_id=1, source_target_pairs={{0,16},{2,18},{4,20},{6,22},{8,24},{10,26},{12,28},{14,30},{16,0},... | collective-permute-start | bytes 196616 | tf_op jit(solution)/shard_map/ppermute | solution.py:648
  38.7 1.3 collective-permute-start.16
  41.8 1.6 %collective-permute-done.15.refs_5_ = bf16[256,128]{1,0:T(8,128)(2,1)S(1)} collective-permute-done((bf16[256,128]{1,0:T(8,128)(2,1)S(1)}, bf16[256,128]{1,0:T(8,128)(2,1)S(1)}, u32[]{:S(2)}, u32[]{:S(2)}) %collective-permute-start.15) | collective-permute-done | bytes 65568 | tf_op jit(solution)/shard_map/ppermute | solution.py:648
  45.9 4.0 %collective-permute-done.17.refs_4_ = bf16[512,128]{1,0:T(8,128)(2,1)S(1)} collective-permute-done((bf16[512,128]{1,0:T(8,128)(2,1)S(1)}, bf16[512,128]{1,0:T(8,128)(2,1)S(1)}, u32[]{:S(2)}, u32[]{:S(2)}) %collective-permute-start.17) | collective-permute-done | bytes 131104 | tf_op jit(solution)/shard_map/ppermute | solution.py:644
  52.1 2.0 %collective-permute-start.22 = (bf16[256,128]{1,0:T(8,128)(2,1)S(1)}, bf16[256,128]{1,0:T(8,128)(2,1)S(1)}, u32[]{:S(2)}, u32[]{:S(2)}) collective-permute-start(bf16[256,128]{1,0:T(8,128)(2,1)S(1)} %get-tuple-element.81), channel_id=1, source_target_pairs={{0,8},{2,10},{4,12},{6,14},{8,16},{10,18},{12,20},{14,22},{16,24},... | collective-permute-start | bytes 196616 | tf_op jit(solution)/shard_map/ppermute | solution.py:648
  54.0 1.9 %collective-permute-start.20 = (bf16[256,128]{1,0:T(8,128)(2,1)S(1)}, bf16[256,128]{1,0:T(8,128)(2,1)S(1)}, u32[]{:S(2)}, u32[]{:S(2)}) collective-permute-start(bf16[256,128]{1,0:T(8,128)(2,1)S(1)} %get-tuple-element.79), channel_id=1, source_target_pairs={{0,24},{2,26},{4,28},{6,30},{8,0},{10,2},{12,4},{14,6},{16,8},{18,... | collective-permute-start | bytes 196616 | tf_op jit(solution)/shard_map/ppermute | solution.py:648
  55.9 4.1 %shard_map.88 = (bf16[4,1536,1024]{2,1,0:T(8,128)(2,1)}, f32[8,128]{1,0:T(8,128)S(1)}) custom-call(bf16[1536,4,1024]{2,1,0:T(4,128)(2,1)} %refs_0_.5, bf16[4,1536,1024]{2,1,0:T(8,128)(2,1)} %get-tuple-element.83.refs_1_, f32[256,128]{1,0:T(8,128)S(1)} %get-tuple-element.76.refs_1_.refs_2_), custom_call_target="tpu_custom_call", output_to_operand_aliasing={{0}: (1, {})} | custom-call | bytes 37752832 | tf_op jit(solution)/shard_map/pallas_call | solution.py:149
  62.3 1.8 %collective-permute-start.26 = (bf16[256,128]{1,0:T(8,128)(2,1)S(1)}, bf16[256,128]{1,0:T(8,128)(2,1)S(1)}, u32[]{:S(2)}, u32[]{:S(2)}) collective-permute-start(bf16[256,128]{1,0:T(8,128)(2,1)S(1)} %add_convert_fusion.2.refs_4_.refs_2_.refs_5_), channel_id=1, source_target_pairs={{0,8},{2,10},{4,12},{6,14},{8,16},{10,18},{12,20},{14,22},{16,24},... | collective-permute-start | bytes 196616 | tf_op jit(solution)/shard_map/ppermute | solution.py:648
  64.8 2.1 %collective-permute-start.28 = (bf16[256,128]{1,0:T(8,128)(2,1)S(1)}, bf16[256,128]{1,0:T(8,128)(2,1)S(1)}, u32[]{:S(2)}, u32[]{:S(2)}) collective-permute-start(bf16[256,128]{1,0:T(8,128)(2,1)S(1)} %add_convert_fusion.2.refs_4_.refs_2_.refs_5_), channel_id=1, source_target_pairs={{0,24},{2,26},{4,28},{6,30},{8,0},{10,2},{12,4},{14,6},{16,8},{18,... | collective-permute-start | bytes 196616 | tf_op jit(solution)/shard_map/ppermute | solution.py:648
  66.9 2.2 %collective-permute-done.26.refs_6_ = bf16[256,128]{1,0:T(8,128)(2,1)S(1)} collective-permute-done((bf16[256,128]{1,0:T(8,128)(2,1)S(1)}, bf16[256,128]{1,0:T(8,128)(2,1)S(1)}, u32[]{:S(2)}, u32[]{:S(2)}) %collective-permute-start.26) | collective-permute-done | bytes 65568 | tf_op jit(solution)/shard_map/ppermute | solution.py:648
  69.1 2.1 %collective-permute-done.27.refs_7_ = bf16[256,128]{1,0:T(8,128)(2,1)S(1)} collective-permute-done((bf16[256,128]{1,0:T(8,128)(2,1)S(1)}, bf16[256,128]{1,0:T(8,128)(2,1)S(1)}, u32[]{:S(2)}, u32[]{:S(2)}) %collective-permute-start.27) | collective-permute-done | bytes 65568 | tf_op jit(solution)/shard_map/ppermute | solution.py:648
  74.5 3.9 %collective-permute-done.29.refs_4_ = bf16[512,128]{1,0:T(8,128)(2,1)S(1)} collective-permute-done((bf16[512,128]{1,0:T(8,128)(2,1)S(1)}, bf16[512,128]{1,0:T(8,128)(2,1)S(1)}, u32[]{:S(2)}, u32[]{:S(2)}) %collective-permute-start.29) | collective-permute-done | bytes 131104 | tf_op jit(solution)/shard_map/ppermute | solution.py:644
  80.5 1.9 %collective-permute-start.34 = (bf16[256,128]{1,0:T(8,128)(2,1)S(1)}, bf16[256,128]{1,0:T(8,128)(2,1)S(1)}, u32[]{:S(2)}, u32[]{:S(2)}) collective-permute-start(bf16[256,128]{1,0:T(8,128)(2,1)S(1)} %get-tuple-element.94), channel_id=1, source_target_pairs={{0,8},{2,10},{4,12},{6,14},{8,16},{10,18},{12,20},{14,22},{16,24},... | collective-permute-start | bytes 196616 | tf_op jit(solution)/shard_map/ppermute | solution.py:648
  82.4 2.0 %collective-permute-start.32 = (bf16[256,128]{1,0:T(8,128)(2,1)S(1)}, bf16[256,128]{1,0:T(8,128)(2,1)S(1)}, u32[]{:S(2)}, u32[]{:S(2)}) collective-permute-start(bf16[256,128]{1,0:T(8,128)(2,1)S(1)} %get-tuple-element.92), channel_id=1, source_target_pairs={{0,24},{2,26},{4,28},{6,30},{8,0},{10,2},{12,4},{14,6},{16,8},{18,... | collective-permute-start | bytes 196616 | tf_op jit(solution)/shard_map/ppermute | solution.py:648
  84.3 4.1 %shard_map.96 = (bf16[4,1536,1024]{2,1,0:T(8,128)(2,1)}, f32[8,128]{1,0:T(8,128)S(1)}) custom-call(bf16[1536,4,1024]{2,1,0:T(4,128)(2,1)} %refs_0_.5, bf16[4,1536,1024]{2,1,0:T(8,128)(2,1)} %get-tuple-element.95.refs_1_, f32[256,128]{1,0:T(8,128)S(1)} %get-tuple-element.91.refs_1_.refs_2_), custom_call_target="tpu_custom_call", output_to_operand_aliasing={{0}: (1, {})} | custom-call | bytes 37752832 | tf_op jit(solution)/shard_map/pallas_call | solution.py:149
  88.5 4.6 %collective-permute-done.35.refs_3_.refs_1_ = bf16[1024,256]{1,0:T(8,128)(2,1)S(1)} collective-permute-done((bf16[1024,256]{1,0:T(8,128)(2,1)S(1)}, bf16[1024,256]{1,0:T(8,128)(2,1)S(1)}, u32[]{:S(2)}, u32[]{:S(2)}) %collective-permute-start.35) | collective-permute-done | bytes 524320 | tf_op jit(solution)/shard_map/ppermute | solution.py:644
  93.3 1.9 %collective-permute-start.37 = (bf16[256,128]{1,0:T(8,128)(2,1)S(1)}, bf16[256,128]{1,0:T(8,128)(2,1)S(1)}, u32[]{:S(2)}, u32[]{:S(2)}) collective-permute-start(bf16[256,128]{1,0:T(8,128)(2,1)S(1)} %add_convert_fusion.1.refs_2_.refs_7_), channel_id=1, source_target_pairs={{0,8},{2,10},{4,12},{6,14},{8,16},{10,18},{12,20},{14,22},{16,24},... | collective-permute-start | bytes 196616 | tf_op jit(solution)/shard_map/ppermute | solution.py:648
  97.7 2.5 %collective-permute-done.37.refs_8_.refs_2_ = bf16[256,128]{1,0:T(8,128)(2,1)S(1)} collective-permute-done((bf16[256,128]{1,0:T(8,128)(2,1)S(1)}, bf16[256,128]{1,0:T(8,128)(2,1)S(1)}, u32[]{:S(2)}, u32[]{:S(2)}) %collective-permute-start.37) | collective-permute-done | bytes 65568 | tf_op jit(solution)/shard_map/ppermute | solution.py:648
  100.2 1.6 collective-permute-start.49
  102.5 1.5 shard_map.99
  106.0 4.0 %collective-permute-done.40.refs_4_ = bf16[512,128]{1,0:T(8,128)(2,1)S(1)} collective-permute-done((bf16[512,128]{1,0:T(8,128)(2,1)S(1)}, bf16[512,128]{1,0:T(8,128)(2,1)S(1)}, u32[]{:S(2)}, u32[]{:S(2)}) %collective-permute-start.40) | collective-permute-done | bytes 131104 | tf_op jit(solution)/shard_map/ppermute | solution.py:644
  112.1 1.9 %collective-permute-start.44 = (bf16[256,128]{1,0:T(8,128)(2,1)S(1)}, bf16[256,128]{1,0:T(8,128)(2,1)S(1)}, u32[]{:S(2)}, u32[]{:S(2)}) collective-permute-start(bf16[256,128]{1,0:T(8,128)(2,1)S(1)} %get-tuple-element.104), channel_id=1, source_target_pairs={{0,8},{2,10},{4,12},{6,14},{8,16},{10,18},{12,20},{14,22},{16,24},... | collective-permute-start | bytes 196616 | tf_op jit(solution)/shard_map/ppermute | solution.py:648
  114.0 1.9 %collective-permute-start.42 = (bf16[256,128]{1,0:T(8,128)(2,1)S(1)}, bf16[256,128]{1,0:T(8,128)(2,1)S(1)}, u32[]{:S(2)}, u32[]{:S(2)}) collective-permute-start(bf16[256,128]{1,0:T(8,128)(2,1)S(1)} %get-tuple-element.102), channel_id=1, source_target_pairs={{0,24},{2,26},{4,28},{6,30},{8,0},{10,2},{12,4},{14,6},{16,8},{18,... | collective-permute-start | bytes 196616 | tf_op jit(solution)/shard_map/ppermute | solution.py:648
  115.9 2.7 %collective-permute-done.44.refs_0_ = bf16[256,128]{1,0:T(8,128)(2,1)S(1)} collective-permute-done((bf16[256,128]{1,0:T(8,128)(2,1)S(1)}, bf16[256,128]{1,0:T(8,128)(2,1)S(1)}, u32[]{:S(2)}, u32[]{:S(2)}) %collective-permute-start.44) | collective-permute-done | bytes 65568 | tf_op jit(solution)/shard_map/ppermute | solution.py:648
  119.0 2.3 %collective-permute-done.43 = bf16[256,128]{1,0:T(8,128)(2,1)S(1)} collective-permute-done((bf16[256,128]{1,0:T(8,128)(2,1)S(1)}, bf16[256,128]{1,0:T(8,128)(2,1)S(1)}, u32[]{:S(2)}, u32[]{:S(2)}) %collective-permute-start.43) | collective-permute-done | bytes 65568 | tf_op jit(solution)/shard_map/ppermute | solution.py:648
  121.4 1.6 collective-permute-start.52
  122.9 2.8 %collective-permute-start.47 = (bf16[256,128]{1,0:T(8,128)(2,1)S(1)}, bf16[256,128]{1,0:T(8,128)(2,1)S(1)}, u32[]{:S(2)}, u32[]{:S(2)}) collective-permute-start(bf16[256,128]{1,0:T(8,128)(2,1)S(1)} %add_convert_fusion.refs_3_.refs_1_.refs_2_), channel_id=1, source_target_pairs={{0,16},{2,18},{4,20},{6,22},{8,24},{10,26},{12,28},{14,30},{16,0},... | collective-permute-start | bytes 196616 | tf_op jit(solution)/shard_map/ppermute | solution.py:648
  126.8 2.6 %shard_map.105 = (bf16[4,1024,512]{2,1,0:T(8,128)(2,1)}, bf16[2,512,1024]{2,1,0:T(8,128)(2,1)S(1)}) custom-call(s32[4]{0:T(128)S(1)} %pad_add_fusion.refs_0_, bf16[2,1024,256]{2,1,0:T(8,128)(2,1)S(1)} %shard_map.104.refs_1_, bf16[2,1024,256]{2,1,0:T(8,128)(2,1)S(1)} %collective-permute-done.49.refs_2_, ...), custom_call_target="tpu_custom_call" | custom-call | bytes 8388624 | tf_op jit(solution)/shard_map/pallas_call | solution.py:149
  130.7 1.3 collective-permute-done.50.refs_2_
  134.3 1.4 collective-permute-done.52.refs_5_.refs_3_.refs_2_
  135.7 5.8 %shard_map.109 = (f32[256,1536]{1,0:T(8,128)S(1)}, bf16[256,1536]{1,0:T(8,128)(2,1)S(1)}) custom-call(s32[4]{0:T(128)S(1)} %pad_add_fusion.refs_0_, bf16[2,512,1024]{2,1,0:T(8,128)(2,1)S(1)} %get-tuple-element.105.refs_5_.refs_1_, bf16[4,1536,1024]{2,1,0:T(8,128)(2,1)} %get-tuple-element.108.refs_2_.refs_3_.refs_5_, ...), custom_call_target="tpu_custom_call" | custom-call | flops 3221225472 | bytes 17039376 | tf_op jit(solution)/shard_map/pallas_call | solution.py:149
  141.5 1.9 %collective-permute-start.54 = (bf16[512,256]{1,0:T(8,128)(2,1)S(1)}, bf16[512,256]{1,0:T(8,128)(2,1)S(1)}, u32[]{:S(2)}, u32[]{:S(2)}) collective-permute-start(bf16[512,256]{1,0:T(8,128)(2,1)S(1)} %shard_map.110.refs_2_), channel_id=1, source_target_pairs={{0,2},{2,0},{4,6},{6,4},{8,10},{10,8},{12,14},{14,12},{16,18},{18,... | collective-permute-start | bytes 786440 | tf_op jit(solution)/shard_map/ppermute | solution.py:644
  143.4 4.7 %shard_map.111 = (bf16[4,1024,512]{2,1,0:T(8,128)(2,1)}, f32[256,1536]{1,0:T(8,128)S(1)}, bf16[256,1536]{1,0:T(8,128)(2,1)S(1)}) custom-call(s32[4]{0:T(128)S(1)} %pad_add_fusion.refs_0_, bf16[2,512,256]{2,1,0:T(8,128)(2,1)S(1)} %shard_map.108.refs_4_.refs_2_.refs_1_, ...), custom_call_target="tpu_custom_call", output_to_operand_aliasing={{0}: (6, {})} | custom-call | flops 1610612736 | bytes 26738704 | tf_op jit(solution)/shard_map/pallas_call | solution.py:149
  148.6 4.8 %shard_map.112 = (bf16[4,1024,512]{2,1,0:T(8,128)(2,1)}, f32[256,1536]{1,0:T(8,128)S(1)}, bf16[256,1536]{1,0:T(8,128)(2,1)S(1)}) custom-call(s32[4]{0:T(128)S(1)} %pad_add_fusion.refs_0_, bf16[512,256]{1,0:T(8,128)(2,1)S(1)} %shard_map.107.refs_3_.refs_1_, bf16[512,256]{1,0:T(8,128)(2,1)S(1)} %shard_map.110.refs_2_, ...), custom_call_target="tpu_custom_call", output_to_operand_aliasing={{0}: (8, {})} | custom-call | flops 1610612736 | bytes 26738704 | tf_op jit(solution)/shard_map/pallas_call | solution.py:149
  153.4 2.3 %collective-permute-done.55 = bf16[256,1536]{1,0:T(8,128)(2,1)S(1)} collective-permute-done((bf16[256,1536]{1,0:T(8,128)(2,1)S(1)}, bf16[256,1536]{1,0:T(8,128)(2,1)S(1)}, u32[]{:S(2)}, u32[]{:S(2)}) %collective-permute-start.55) | collective-permute-done | bytes 786464 | tf_op jit(solution)/shard_map/ppermute | solution.py:651
  (119 shorter events, 34.9 us)
Async XLA Ops:
  1.9 7.9 %collective-permute-start = (bf16[128,768]{1,0:T(8,128)(2,1)S(1)}, bf16[128,768]{1,0:T(8,128)(2,1)S(1)}, u32[]{:S(2)}, u32[]{:S(2)}) collective-permute-start(bf16[128,768]{1,0:T(8,128)(2,1)S(1)} %get-tuple-element.62), channel_id=1, source_target_pairs={{0,4},{2,6},{4,0},{6,2},{8,12},{10,14},{12,8},{14,10},{16,20},{18,... | collective-permute-start | bytes 589832 | tf_op jit(solution)/shard_map/ppermute | solution.py:644
  5.0 8.9 %collective-permute-start.3 = (bf16[128,1152]{1,0:T(8,128)(2,1)S(1)}, bf16[128,1152]{1,0:T(8,128)(2,1)S(1)}, u32[]{:S(2)}, u32[]{:S(2)}) collective-permute-start(bf16[128,1152]{1,0:T(8,128)(2,1)S(1)} %get-tuple-element.65), channel_id=1, source_target_pairs={{0,2},{2,0},{4,6},{6,4},{8,10},{10,8},{12,14},{14,12},{16,18},{18,... | collective-permute-start | bytes 884744 | tf_op jit(solution)/shard_map/ppermute | solution.py:644
  9.9 7.8 %collective-permute-start.1 = (bf16[128,1024]{1,0:T(8,128)(2,1)S(1)}, bf16[128,1024]{1,0:T(8,128)(2,1)S(1)}, u32[]{:S(2)}, u32[]{:S(2)}) collective-permute-start(bf16[128,1024]{1,0:T(8,128)(2,1)S(1)} %shard_map.71), channel_id=1, source_target_pairs={{0,4},{2,6},{4,0},{6,2},{8,12},{10,14},{12,8},{14,10},{16,20},{18,... | collective-permute-start | bytes 786440 | tf_op jit(solution)/shard_map/ppermute | solution.py:644
  11.6 6.0 %collective-permute-start.4 = (bf16[128,768]{1,0:T(8,128)(2,1)S(1)}, bf16[128,768]{1,0:T(8,128)(2,1)S(1)}, u32[]{:S(2)}, u32[]{:S(2)}) collective-permute-start(bf16[128,768]{1,0:T(8,128)(2,1)S(1)} %shard_map.73.refs_2_), channel_id=1, source_target_pairs={{0,2},{2,0},{4,6},{6,4},{8,10},{10,8},{12,14},{14,12},{16,18},{18,... | collective-permute-start | bytes 589832 | tf_op jit(solution)/shard_map/ppermute | solution.py:644
  18.7 14.0 %collective-permute-start.2 = (bf16[2,128,1024]{2,1,0:T(8,128)(2,1)S(1)}, bf16[2,128,1024]{2,1,0:T(8,128)(2,1)S(1)}, u32[]{:S(2)}, u32[]{:S(2)}) collective-permute-start(bf16[2,128,1024]{2,1,0:T(8,128)(2,1)S(1)} %shard_map.72.refs_1_.refs_0_), channel_id=1, source_target_pairs={{0,2},{2,0},{4,6},{6,4},{8,10},{10,8},{12,14},{14,12},{16,18},{18,... | collective-permute-start | bytes 1572872 | tf_op jit(solution)/shard_map/ppermute | solution.py:644
  21.3 11.3 %collective-permute-start.12 = (bf16[128,1536]{1,0:T(8,128)(2,1)S(1)}, bf16[128,1536]{1,0:T(8,128)(2,1)S(1)}, u32[]{:S(2)}, u32[]{:S(2)}) collective-permute-start(bf16[128,1536]{1,0:T(8,128)(2,1)S(1)} %shard_map.76), channel_id=1, source_target_pairs={{0,4},{2,6},{4,0},{6,2},{8,12},{10,14},{12,8},{14,10},{16,20},{18,... | collective-permute-start | bytes 1179656 | tf_op jit(solution)/shard_map/ppermute | solution.py:644
  22.5 9.7 %collective-permute-start.11 = (bf16[256,128]{1,0:T(8,128)(2,1)S(1)}, bf16[256,128]{1,0:T(8,128)(2,1)S(1)}, u32[]{:S(2)}, u32[]{:S(2)}) collective-permute-start(bf16[256,128]{1,0:T(8,128)(2,1)S(1)} %get-tuple-element.69), channel_id=1, source_target_pairs={{0,8},{2,10},{4,12},{6,14},{8,16},{10,18},{12,20},{14,22},{16,24},... | collective-permute-start | bytes 196616 | tf_op jit(solution)/shard_map/ppermute | solution.py:648
  24.1 8.6 %collective-permute-start.10 = (bf16[256,128]{1,0:T(8,128)(2,1)S(1)}, bf16[256,128]{1,0:T(8,128)(2,1)S(1)}, u32[]{:S(2)}, u32[]{:S(2)}) collective-permute-start(bf16[256,128]{1,0:T(8,128)(2,1)S(1)} %get-tuple-element.68), channel_id=1, source_target_pairs={{0,16},{2,18},{4,20},{6,22},{8,24},{10,26},{12,28},{14,30},{16,0},... | collective-permute-start | bytes 196616 | tf_op jit(solution)/shard_map/ppermute | solution.py:648
  26.7 6.0 %collective-permute-start.9 = (bf16[256,128]{1,0:T(8,128)(2,1)S(1)}, bf16[256,128]{1,0:T(8,128)(2,1)S(1)}, u32[]{:S(2)}, u32[]{:S(2)}) collective-permute-start(bf16[256,128]{1,0:T(8,128)(2,1)S(1)} %get-tuple-element.67), channel_id=1, source_target_pairs={{0,24},{2,26},{4,28},{6,30},{8,0},{10,2},{12,4},{14,6},{16,8},{18,... | collective-permute-start | bytes 196616 | tf_op jit(solution)/shard_map/ppermute | solution.py:648
  32.8 10.9 %collective-permute-start.13 = (bf16[4,128,1024]{2,1,0:T(8,128)(2,1)S(1)}, bf16[4,128,1024]{2,1,0:T(8,128)(2,1)S(1)}, u32[]{:S(2)}, u32[]{:S(2)}) collective-permute-start(bf16[4,128,1024]{2,1,0:T(8,128)(2,1)S(1)} %shard_map.79.refs_1_), channel_id=1, source_target_pairs={{0,1},{1,0},{2,3},{3,2},{4,5},{5,4},{6,7},{7,6},{8,9},{9,8},{10,11... | collective-permute-start | bytes 3145736 | tf_op jit(solution)/shard_map/ppermute | solution.py:651
  32.9 27.1 %collective-permute-start.23 = (bf16[2,128,1536]{2,1,0:T(8,128)(2,1)S(1)}, bf16[2,128,1536]{2,1,0:T(8,128)(2,1)S(1)}, u32[]{:S(2)}, u32[]{:S(2)}) collective-permute-start(bf16[2,128,1536]{2,1,0:T(8,128)(2,1)S(1)} %shard_map.87.refs_1_.refs_0_), channel_id=1, source_target_pairs={{0,2},{2,0},{4,6},{6,4},{8,10},{10,8},{12,14},{14,12},{16,18},{18,... | collective-permute-start | bytes 2359304 | tf_op jit(solution)/shard_map/ppermute | solution.py:644
  34.5 6.3 %collective-permute-start.14 = (bf16[256,128]{1,0:T(8,128)(2,1)S(1)}, bf16[256,128]{1,0:T(8,128)(2,1)S(1)}, u32[]{:S(2)}, u32[]{:S(2)}) collective-permute-start(bf16[256,128]{1,0:T(8,128)(2,1)S(1)} %add_convert_fusion.3.refs_2_.refs_3_), channel_id=1, source_target_pairs={{0,8},{2,10},{4,12},{6,14},{8,16},{10,18},{12,20},{14,22},{16,24},... | collective-permute-start | bytes 196616 | tf_op jit(solution)/shard_map/ppermute | solution.py:648
  36.1 7.4 %collective-permute-start.15 = (bf16[256,128]{1,0:T(8,128)(2,1)S(1)}, bf16[256,128]{1,0:T(8,128)(2,1)S(1)}, u32[]{:S(2)}, u32[]{:S(2)}) collective-permute-start(bf16[256,128]{1,0:T(8,128)(2,1)S(1)} %add_convert_fusion.3.refs_2_.refs_3_), channel_id=1, source_target_pairs={{0,16},{2,18},{4,20},{6,22},{8,24},{10,26},{12,28},{14,30},{16,0},... | collective-permute-start | bytes 196616 | tf_op jit(solution)/shard_map/ppermute | solution.py:648
  38.7 5.0 %collective-permute-start.16 = (bf16[256,128]{1,0:T(8,128)(2,1)S(1)}, bf16[256,128]{1,0:T(8,128)(2,1)S(1)}, u32[]{:S(2)}, u32[]{:S(2)}) collective-permute-start(bf16[256,128]{1,0:T(8,128)(2,1)S(1)} %add_convert_fusion.3.refs_2_.refs_3_), channel_id=1, source_target_pairs={{0,24},{2,26},{4,28},{6,30},{8,0},{10,2},{12,4},{14,6},{16,8},{18,... | collective-permute-start | bytes 196616 | tf_op jit(solution)/shard_map/ppermute | solution.py:648
  40.8 5.1 %collective-permute-start.18 = (bf16[128,512]{1,0:T(8,128)(2,1)S(1)}, bf16[128,512]{1,0:T(8,128)(2,1)S(1)}, u32[]{:S(2)}, u32[]{:S(2)}) collective-permute-start(bf16[128,512]{1,0:T(8,128)(2,1)S(1)} %shard_map.81), channel_id=1, source_target_pairs={{0,4},{2,6},{4,0},{6,2},{8,12},{10,14},{12,8},{14,10},{16,20},{18,... | collective-permute-start | bytes 393224 | tf_op jit(solution)/shard_map/ppermute | solution.py:644
  44.7 5.2 %collective-permute-start.17 = (bf16[512,128]{1,0:T(8,128)(2,1)S(1)}, bf16[512,128]{1,0:T(8,128)(2,1)S(1)}, u32[]{:S(2)}, u32[]{:S(2)}) collective-permute-start(bf16[512,128]{1,0:T(8,128)(2,1)S(1)} %get-tuple-element.74), channel_id=1, source_target_pairs={{0,4},{2,6},{4,0},{6,2},{8,12},{10,14},{12,8},{14,10},{16,20},{18,... | collective-permute-start | bytes 393224 | tf_op jit(solution)/shard_map/ppermute | solution.py:644
  50.9 9.9 %collective-permute-start.19 = (bf16[128,1536]{1,0:T(8,128)(2,1)S(1)}, bf16[128,1536]{1,0:T(8,128)(2,1)S(1)}, u32[]{:S(2)}, u32[]{:S(2)}) collective-permute-start(bf16[128,1536]{1,0:T(8,128)(2,1)S(1)} %shard_map.84), channel_id=1, source_target_pairs={{0,4},{2,6},{4,0},{6,2},{8,12},{10,14},{12,8},{14,10},{16,20},{18,... | collective-permute-start | bytes 1179656 | tf_op jit(solution)/shard_map/ppermute | solution.py:644
  52.1 8.0 %collective-permute-start.22 = (bf16[256,128]{1,0:T(8,128)(2,1)S(1)}, bf16[256,128]{1,0:T(8,128)(2,1)S(1)}, u32[]{:S(2)}, u32[]{:S(2)}) collective-permute-start(bf16[256,128]{1,0:T(8,128)(2,1)S(1)} %get-tuple-element.81), channel_id=1, source_target_pairs={{0,8},{2,10},{4,12},{6,14},{8,16},{10,18},{12,20},{14,22},{16,24},... | collective-permute-start | bytes 196616 | tf_op jit(solution)/shard_map/ppermute | solution.py:648
  54.0 6.8 %collective-permute-start.20 = (bf16[256,128]{1,0:T(8,128)(2,1)S(1)}, bf16[256,128]{1,0:T(8,128)(2,1)S(1)}, u32[]{:S(2)}, u32[]{:S(2)}) collective-permute-start(bf16[256,128]{1,0:T(8,128)(2,1)S(1)} %get-tuple-element.79), channel_id=1, source_target_pairs={{0,24},{2,26},{4,28},{6,30},{8,0},{10,2},{12,4},{14,6},{16,8},{18,... | collective-permute-start | bytes 196616 | tf_op jit(solution)/shard_map/ppermute | solution.py:648
  55.9 5.5 %collective-permute-start.21 = (bf16[256,128]{1,0:T(8,128)(2,1)S(1)}, bf16[256,128]{1,0:T(8,128)(2,1)S(1)}, u32[]{:S(2)}, u32[]{:S(2)}) collective-permute-start(bf16[256,128]{1,0:T(8,128)(2,1)S(1)} %get-tuple-element.80), channel_id=1, source_target_pairs={{0,16},{2,18},{4,20},{6,22},{8,24},{10,26},{12,28},{14,30},{16,0},... | collective-permute-start | bytes 196616 | tf_op jit(solution)/shard_map/ppermute | solution.py:648
  61.5 9.7 %collective-permute-start.25 = (bf16[4,128,1536]{2,1,0:T(8,128)(2,1)S(1)}, bf16[4,128,1536]{2,1,0:T(8,128)(2,1)S(1)}, u32[]{:S(2)}, u32[]{:S(2)}) collective-permute-start(bf16[4,128,1536]{2,1,0:T(8,128)(2,1)S(1)} %shard_map.91.refs_1_), channel_id=1, source_target_pairs={{0,1},{1,0},{2,3},{3,2},{4,5},{5,4},{6,7},{7,6},{8,9},{9,8},{10,11... | collective-permute-start | bytes 4718600 | tf_op jit(solution)/shard_map/ppermute | solution.py:651
  61.7 26.8 %collective-permute-start.24 = (bf16[2,128,2048]{2,1,0:T(8,128)(2,1)S(1)}, bf16[2,128,2048]{2,1,0:T(8,128)(2,1)S(1)}, u32[]{:S(2)}, u32[]{:S(2)}) collective-permute-start(bf16[2,128,2048]{2,1,0:T(8,128)(2,1)S(1)} %shard_map.90.refs_1_.refs_0_), channel_id=1, source_target_pairs={{0,2},{2,0},{4,6},{6,4},{8,10},{10,8},{12,14},{14,12},{16,18},{18,... | collective-permute-start | bytes 3145736 | tf_op jit(solution)/shard_map/ppermute | solution.py:644
  62.3 6.8 %collective-permute-start.26 = (bf16[256,128]{1,0:T(8,128)(2,1)S(1)}, bf16[256,128]{1,0:T(8,128)(2,1)S(1)}, u32[]{:S(2)}, u32[]{:S(2)}) collective-permute-start(bf16[256,128]{1,0:T(8,128)(2,1)S(1)} %add_convert_fusion.2.refs_4_.refs_2_.refs_5_), channel_id=1, source_target_pairs={{0,8},{2,10},{4,12},{6,14},{8,16},{10,18},{12,20},{14,22},{16,24},... | collective-permute-start | bytes 196616 | tf_op jit(solution)/shard_map/ppermute | solution.py:648
  64.1 7.1 %collective-permute-start.27 = (bf16[256,128]{1,0:T(8,128)(2,1)S(1)}, bf16[256,128]{1,0:T(8,128)(2,1)S(1)}, u32[]{:S(2)}, u32[]{:S(2)}) collective-permute-start(bf16[256,128]{1,0:T(8,128)(2,1)S(1)} %add_convert_fusion.2.refs_4_.refs_2_.refs_5_), channel_id=1, source_target_pairs={{0,16},{2,18},{4,20},{6,22},{8,24},{10,26},{12,28},{14,30},{16,0},... | collective-permute-start | bytes 196616 | tf_op jit(solution)/shard_map/ppermute | solution.py:648
  64.8 6.4 %collective-permute-start.28 = (bf16[256,128]{1,0:T(8,128)(2,1)S(1)}, bf16[256,128]{1,0:T(8,128)(2,1)S(1)}, u32[]{:S(2)}, u32[]{:S(2)}) collective-permute-start(bf16[256,128]{1,0:T(8,128)(2,1)S(1)} %add_convert_fusion.2.refs_4_.refs_2_.refs_5_), channel_id=1, source_target_pairs={{0,24},{2,26},{4,28},{6,30},{8,0},{10,2},{12,4},{14,6},{16,8},{18,... | collective-permute-start | bytes 196616 | tf_op jit(solution)/shard_map/ppermute | solution.py:648
  69.1 4.5 %collective-permute-start.30 = (bf16[512,128]{1,0:T(8,128)(2,1)S(1)}, bf16[512,128]{1,0:T(8,128)(2,1)S(1)}, u32[]{:S(2)}, u32[]{:S(2)}) collective-permute-start(bf16[512,128]{1,0:T(8,128)(2,1)S(1)} %get-tuple-element.86.refs_4_), channel_id=1, source_target_pairs={{0,1},{1,0},{2,3},{3,2},{4,5},{5,4},{6,7},{7,6},{8,9},{9,8},{10,11... | collective-permute-start | bytes 393224 | tf_op jit(solution)/shard_map/ppermute | solution.py:651
  72.5 5.9 %collective-permute-start.29 = (bf16[512,128]{1,0:T(8,128)(2,1)S(1)}, bf16[512,128]{1,0:T(8,128)(2,1)S(1)}, u32[]{:S(2)}, u32[]{:S(2)}) collective-permute-start(bf16[512,128]{1,0:T(8,128)(2,1)S(1)} %get-tuple-element.88), channel_id=1, source_target_pairs={{0,4},{2,6},{4,0},{6,2},{8,12},{10,14},{12,8},{14,10},{16,20},{18,... | collective-permute-start | bytes 393224 | tf_op jit(solution)/shard_map/ppermute | solution.py:644
  79.5 13.6 %collective-permute-start.35 = (bf16[1024,256]{1,0:T(8,128)(2,1)S(1)}, bf16[1024,256]{1,0:T(8,128)(2,1)S(1)}, u32[]{:S(2)}, u32[]{:S(2)}) collective-permute-start(bf16[1024,256]{1,0:T(8,128)(2,1)S(1)} %shard_map.95.refs_0_), channel_id=1, source_target_pairs={{0,4},{2,6},{4,0},{6,2},{8,12},{10,14},{12,8},{14,10},{16,20},{18,... | collective-permute-start | bytes 1572872 | tf_op jit(solution)/shard_map/ppermute | solution.py:644
  80.5 8.0 %collective-permute-start.34 = (bf16[256,128]{1,0:T(8,128)(2,1)S(1)}, bf16[256,128]{1,0:T(8,128)(2,1)S(1)}, u32[]{:S(2)}, u32[]{:S(2)}) collective-permute-start(bf16[256,128]{1,0:T(8,128)(2,1)S(1)} %get-tuple-element.94), channel_id=1, source_target_pairs={{0,8},{2,10},{4,12},{6,14},{8,16},{10,18},{12,20},{14,22},{16,24},... | collective-permute-start | bytes 196616 | tf_op jit(solution)/shard_map/ppermute | solution.py:648
  82.4 10.7 %collective-permute-start.32 = (bf16[256,128]{1,0:T(8,128)(2,1)S(1)}, bf16[256,128]{1,0:T(8,128)(2,1)S(1)}, u32[]{:S(2)}, u32[]{:S(2)}) collective-permute-start(bf16[256,128]{1,0:T(8,128)(2,1)S(1)} %get-tuple-element.92), channel_id=1, source_target_pairs={{0,24},{2,26},{4,28},{6,30},{8,0},{10,2},{12,4},{14,6},{16,8},{18,... | collective-permute-start | bytes 196616 | tf_op jit(solution)/shard_map/ppermute | solution.py:648
  84.3 8.7 %collective-permute-start.33 = (bf16[256,128]{1,0:T(8,128)(2,1)S(1)}, bf16[256,128]{1,0:T(8,128)(2,1)S(1)}, u32[]{:S(2)}, u32[]{:S(2)}) collective-permute-start(bf16[256,128]{1,0:T(8,128)(2,1)S(1)} %get-tuple-element.93), channel_id=1, source_target_pairs={{0,16},{2,18},{4,20},{6,22},{8,24},{10,26},{12,28},{14,30},{16,0},... | collective-permute-start | bytes 196616 | tf_op jit(solution)/shard_map/ppermute | solution.py:648
  93.2 9.3 %collective-permute-start.36 = (bf16[4,128,2048]{2,1,0:T(8,128)(2,1)S(1)}, bf16[4,128,2048]{2,1,0:T(8,128)(2,1)S(1)}, u32[]{:S(2)}, u32[]{:S(2)}) collective-permute-start(bf16[4,128,2048]{2,1,0:T(8,128)(2,1)S(1)} %shard_map.98.refs_1_), channel_id=1, source_target_pairs={{0,1},{1,0},{2,3},{3,2},{4,5},{5,4},{6,7},{7,6},{8,9},{9,8},{10,11... | collective-permute-start | bytes 6291464 | tf_op jit(solution)/shard_map/ppermute | solution.py:651
  93.3 6.8 %collective-permute-start.37 = (bf16[256,128]{1,0:T(8,128)(2,1)S(1)}, bf16[256,128]{1,0:T(8,128)(2,1)S(1)}, u32[]{:S(2)}, u32[]{:S(2)}) collective-permute-start(bf16[256,128]{1,0:T(8,128)(2,1)S(1)} %add_convert_fusion.1.refs_2_.refs_7_), channel_id=1, source_target_pairs={{0,8},{2,10},{4,12},{6,14},{8,16},{10,18},{12,20},{14,22},{16,24},... | collective-permute-start | bytes 196616 | tf_op jit(solution)/shard_map/ppermute | solution.py:648
  95.2 7.2 %collective-permute-start.38 = (bf16[256,128]{1,0:T(8,128)(2,1)S(1)}, bf16[256,128]{1,0:T(8,128)(2,1)S(1)}, u32[]{:S(2)}, u32[]{:S(2)}) collective-permute-start(bf16[256,128]{1,0:T(8,128)(2,1)S(1)} %add_convert_fusion.1.refs_2_.refs_7_), channel_id=1, source_target_pairs={{0,16},{2,18},{4,20},{6,22},{8,24},{10,26},{12,28},{14,30},{16,0},... | collective-permute-start | bytes 196616 | tf_op jit(solution)/shard_map/ppermute | solution.py:648
  96.4 6.1 %collective-permute-start.39 = (bf16[256,128]{1,0:T(8,128)(2,1)S(1)}, bf16[256,128]{1,0:T(8,128)(2,1)S(1)}, u32[]{:S(2)}, u32[]{:S(2)}) collective-permute-start(bf16[256,128]{1,0:T(8,128)(2,1)S(1)} %add_convert_fusion.1.refs_2_.refs_7_), channel_id=1, source_target_pairs={{0,24},{2,26},{4,28},{6,30},{8,0},{10,2},{12,4},{14,6},{16,8},{18,... | collective-permute-start | bytes 196616 | tf_op jit(solution)/shard_map/ppermute | solution.py:648
  100.2 26.5 %collective-permute-start.49 = (bf16[2,1024,256]{2,1,0:T(8,128)(2,1)S(1)}, bf16[2,1024,256]{2,1,0:T(8,128)(2,1)S(1)}, u32[]{:S(2)}, u32[]{:S(2)}) collective-permute-start(bf16[2,1024,256]{2,1,0:T(8,128)(2,1)S(1)} %shard_map.104.refs_1_), channel_id=1, source_target_pairs={{0,2},{2,0},{4,6},{6,4},{8,10},{10,8},{12,14},{14,12},{16,18},{18,... | collective-permute-start | bytes 3145736 | tf_op jit(solution)/shard_map/ppermute | solution.py:644
  104.1 5.9 %collective-permute-start.40 = (bf16[512,128]{1,0:T(8,128)(2,1)S(1)}, bf16[512,128]{1,0:T(8,128)(2,1)S(1)}, u32[]{:S(2)}, u32[]{:S(2)}) collective-permute-start(bf16[512,128]{1,0:T(8,128)(2,1)S(1)} %get-tuple-element.98), channel_id=1, source_target_pairs={{0,4},{2,6},{4,0},{6,2},{8,12},{10,14},{12,8},{14,10},{16,20},{18,... | collective-permute-start | bytes 393224 | tf_op jit(solution)/shard_map/ppermute | solution.py:644
  111.1 7.9 %collective-permute-start.45 = (bf16[512,256]{1,0:T(8,128)(2,1)S(1)}, bf16[512,256]{1,0:T(8,128)(2,1)S(1)}, u32[]{:S(2)}, u32[]{:S(2)}) collective-permute-start(bf16[512,256]{1,0:T(8,128)(2,1)S(1)} %shard_map.102.refs_0_), channel_id=1, source_target_pairs={{0,4},{2,6},{4,0},{6,2},{8,12},{10,14},{12,8},{14,10},{16,20},{18,... | collective-permute-start | bytes 786440 | tf_op jit(solution)/shard_map/ppermute | solution.py:644
  112.1 6.6 %collective-permute-start.44 = (bf16[256,128]{1,0:T(8,128)(2,1)S(1)}, bf16[256,128]{1,0:T(8,128)(2,1)S(1)}, u32[]{:S(2)}, u32[]{:S(2)}) collective-permute-start(bf16[256,128]{1,0:T(8,128)(2,1)S(1)} %get-tuple-element.104), channel_id=1, source_target_pairs={{0,8},{2,10},{4,12},{6,14},{8,16},{10,18},{12,20},{14,22},{16,24},... | collective-permute-start | bytes 196616 | tf_op jit(solution)/shard_map/ppermute | solution.py:648
  114.0 5.0 %collective-permute-start.42 = (bf16[256,128]{1,0:T(8,128)(2,1)S(1)}, bf16[256,128]{1,0:T(8,128)(2,1)S(1)}, u32[]{:S(2)}, u32[]{:S(2)}) collective-permute-start(bf16[256,128]{1,0:T(8,128)(2,1)S(1)} %get-tuple-element.102), channel_id=1, source_target_pairs={{0,24},{2,26},{4,28},{6,30},{8,0},{10,2},{12,4},{14,6},{16,8},{18,... | collective-permute-start | bytes 196616 | tf_op jit(solution)/shard_map/ppermute | solution.py:648
  115.9 5.4 %collective-permute-start.43 = (bf16[256,128]{1,0:T(8,128)(2,1)S(1)}, bf16[256,128]{1,0:T(8,128)(2,1)S(1)}, u32[]{:S(2)}, u32[]{:S(2)}) collective-permute-start(bf16[256,128]{1,0:T(8,128)(2,1)S(1)} %get-tuple-element.103), channel_id=1, source_target_pairs={{0,16},{2,18},{4,20},{6,22},{8,24},{10,26},{12,28},{14,30},{16,0},... | collective-permute-start | bytes 196616 | tf_op jit(solution)/shard_map/ppermute | solution.py:648
  121.4 14.3 %collective-permute-start.52 = (bf16[2,512,256]{2,1,0:T(8,128)(2,1)S(1)}, bf16[2,512,256]{2,1,0:T(8,128)(2,1)S(1)}, u32[]{:S(2)}, u32[]{:S(2)}) collective-permute-start(bf16[2,512,256]{2,1,0:T(8,128)(2,1)S(1)} %shard_map.108.refs_4_.refs_2_.refs_1_), channel_id=1, source_target_pairs={{0,2},{2,0},{4,6},{6,4},{8,10},{10,8},{12,14},{14,12},{16,18},{18,... | collective-permute-start | bytes 1572872 | tf_op jit(solution)/shard_map/ppermute | solution.py:644
  122.9 6.5 %collective-permute-start.46 = (bf16[256,128]{1,0:T(8,128)(2,1)S(1)}, bf16[256,128]{1,0:T(8,128)(2,1)S(1)}, u32[]{:S(2)}, u32[]{:S(2)}) collective-permute-start(bf16[256,128]{1,0:T(8,128)(2,1)S(1)} %add_convert_fusion.refs_3_.refs_1_.refs_2_), channel_id=1, source_target_pairs={{0,8},{2,10},{4,12},{6,14},{8,16},{10,18},{12,20},{14,22},{16,24},... | collective-permute-start | bytes 196616 | tf_op jit(solution)/shard_map/ppermute | solution.py:648
  122.9 6.5 %collective-permute-start.47 = (bf16[256,128]{1,0:T(8,128)(2,1)S(1)}, bf16[256,128]{1,0:T(8,128)(2,1)S(1)}, u32[]{:S(2)}, u32[]{:S(2)}) collective-permute-start(bf16[256,128]{1,0:T(8,128)(2,1)S(1)} %add_convert_fusion.refs_3_.refs_1_.refs_2_), channel_id=1, source_target_pairs={{0,16},{2,18},{4,20},{6,22},{8,24},{10,26},{12,28},{14,30},{16,0},... | collective-permute-start | bytes 196616 | tf_op jit(solution)/shard_map/ppermute | solution.py:648
  125.7 4.3 %collective-permute-start.48 = (bf16[256,128]{1,0:T(8,128)(2,1)S(1)}, bf16[256,128]{1,0:T(8,128)(2,1)S(1)}, u32[]{:S(2)}, u32[]{:S(2)}) collective-permute-start(bf16[256,128]{1,0:T(8,128)(2,1)S(1)} %add_convert_fusion.refs_3_.refs_1_.refs_2_), channel_id=1, source_target_pairs={{0,24},{2,26},{4,28},{6,30},{8,0},{10,2},{12,4},{14,6},{16,8},{18,... | collective-permute-start | bytes 196616 | tf_op jit(solution)/shard_map/ppermute | solution.py:648
  132.6 8.8 %collective-permute-start.51 = (bf16[512,256]{1,0:T(8,128)(2,1)S(1)}, bf16[512,256]{1,0:T(8,128)(2,1)S(1)}, u32[]{:S(2)}, u32[]{:S(2)}) collective-permute-start(bf16[512,256]{1,0:T(8,128)(2,1)S(1)} %shard_map.107.refs_3_.refs_1_), channel_id=1, source_target_pairs={{0,4},{2,6},{4,0},{6,2},{8,12},{10,14},{12,8},{14,10},{16,20},{18,... | collective-permute-start | bytes 786440 | tf_op jit(solution)/shard_map/ppermute | solution.py:644
  133.8 14.4 %collective-permute-start.53 = (bf16[512,256]{1,0:T(8,128)(2,1)S(1)}, bf16[512,256]{1,0:T(8,128)(2,1)S(1)}, u32[]{:S(2)}, u32[]{:S(2)}) collective-permute-start(bf16[512,256]{1,0:T(8,128)(2,1)S(1)} %shard_map.107.refs_3_.refs_1_), channel_id=1, source_target_pairs={{0,2},{2,0},{4,6},{6,4},{8,10},{10,8},{12,14},{14,12},{16,18},{18,... | collective-permute-start | bytes 786440 | tf_op jit(solution)/shard_map/ppermute | solution.py:644
  141.5 7.1 %collective-permute-start.54 = (bf16[512,256]{1,0:T(8,128)(2,1)S(1)}, bf16[512,256]{1,0:T(8,128)(2,1)S(1)}, u32[]{:S(2)}, u32[]{:S(2)}) collective-permute-start(bf16[512,256]{1,0:T(8,128)(2,1)S(1)} %shard_map.110.refs_2_), channel_id=1, source_target_pairs={{0,2},{2,0},{4,6},{6,4},{8,10},{10,8},{12,14},{14,12},{16,18},{18,... | collective-permute-start | bytes 786440 | tf_op jit(solution)/shard_map/ppermute | solution.py:644
  (9 other events, 23.0 us)

commit v8 on v7

--- a/solution.py
+++ b/solution.py
@@ -675,7 +675,7 @@
         return join(form, meta, parts, after)
 
     turns = 3
-    block = 256
+    block = 512
     while rest % (turns * block):
         turns -= 1
     last = steps - 1

time: 157 us -> 157 us (level)
  waiting for transfers between devices: 44.9 us -> 41.5 us
  Pallas kernels: 45.9 us -> 49.2 us
    pallas_call x45, Pallas kernels: 45.9 us -> 49.2 us  [call(): pl.pallas_call(run, out_shape=tuple(outs), in_specs=list(specs) + [pl.Blo...]
    ppermute x20, waiting for transfers between devices: 24.3 us -> 21.6 us  [along_plane(): return lax.ppermute(x, 'rows', pairs)]
  transfers between devices with their start and end apart: 56 -> 56, of which waited for: 26 -> 26; matrix products, arithmetic and copies ran while one was open for 0% -> 0% of each run, Pallas kernels for 25% -> 27%
where the time goes in v8:
time: 157 us
  starting transfers between devices  64 us (41%)
  Pallas kernels  49.2 us (31%)
  waiting for transfers between devices  41.5 us (26%)
    pallas_call x45, Pallas kernels, call(): pl.pallas_call(run, out_shape=tuple(outs), in_specs=list(specs) + [pl.Blo...  49.2 us
    ppermute x24, starting transfers between devices, along_depth(): return lax.ppermute(x, 'rows', pairs)  35.8 us
    ppermute x20, starting transfers between devices, along_plane(): return lax.ppermute(x, 'rows', pairs)  26.7 us
    ppermute x20, waiting for transfers between devices, along_plane(): return lax.ppermute(x, 'rows', pairs)  21.6 us
    ppermute x24, waiting for transfers between devices, along_depth(): return lax.ppermute(x, 'rows', pairs)  15.7 us
    ppermute x12, waiting for transfers between devices, along_cols(): lax.ppermute(x, 'cols', [(i, (i + k) % n_cols) for i in range(n_cols)])  4.1 us
  transfers between devices with their start and end apart: 56, of which 26 were waited for; matrix products, arithmetic and copies ran while one was open for 0% of the time, Pallas kernels for 27%

profile of v8, /device:TPU:0, one launch (start us, length us, event | category | flops | bytes accessed | tf_op | source)
XLA Modules:
  0.0 157.2 jit_solution(213346812078012646)
XLA Ops:
  1.9 3.0 %collective-permute-start = (bf16[128,768]{1,0:T(8,128)(2,1)S(1)}, bf16[128,768]{1,0:T(8,128)(2,1)S(1)}, u32[]{:S(2)}, u32[]{:S(2)}) collective-permute-start(bf16[128,768]{1,0:T(8,128)(2,1)S(1)} %get-tuple-element.62), channel_id=1, source_target_pairs={{0,4},{2,6},{4,0},{6,2},{8,12},{10,14},{12,8},{14,10},{16,20},{18,... | collective-permute-start | bytes 589832 | tf_op jit(solution)/shard_map/ppermute | solution.py:644
  5.0 1.5 collective-permute-start.3
  6.4 3.4 %shard_map.68 = (bf16[128,1024]{1,0:T(8,128)(2,1)S(1)}, bf16[128,1024]{1,0:T(8,128)(2,1)S(1)}, bf16[128,1536]{1,0:T(8,128)(2,1)S(1)}, bf16[128,1536]{1,0:T(8,128...) custom-call(s32[4]{0:T(128)S(1)} %pad_add_fusion.refs_0_, ...), custom_call_target="tpu_custom_call" | custom-call | bytes 60817536 | tf_op jit(solution)/shard_map/pallas_call | solution.py:149
  9.9 1.7 %collective-permute-start.1 = (bf16[128,1024]{1,0:T(8,128)(2,1)S(1)}, bf16[128,1024]{1,0:T(8,128)(2,1)S(1)}, u32[]{:S(2)}, u32[]{:S(2)}) collective-permute-start(bf16[128,1024]{1,0:T(8,128)(2,1)S(1)} %shard_map.71), channel_id=1, source_target_pairs={{0,4},{2,6},{4,0},{6,2},{8,12},{10,14},{12,8},{14,10},{16,20},{18,... | collective-permute-start | bytes 786440 | tf_op jit(solution)/shard_map/ppermute | solution.py:644
  11.6 1.6 collective-permute-start.4
  13.8 3.8 %collective-permute-done.4.refs_1_.refs_4_ = bf16[128,768]{1,0:T(8,128)(2,1)S(1)} collective-permute-done((bf16[128,768]{1,0:T(8,128)(2,1)S(1)}, bf16[128,768]{1,0:T(8,128)(2,1)S(1)}, u32[]{:S(2)}, u32[]{:S(2)}) %collective-permute-start.4) | collective-permute-done | bytes 196640 | tf_op jit(solution)/shard_map/ppermute | solution.py:644
  18.7 1.6 collective-permute-start.2
  22.5 1.6 %collective-permute-start.11 = (bf16[256,128]{1,0:T(8,128)(2,1)S(1)}, bf16[256,128]{1,0:T(8,128)(2,1)S(1)}, u32[]{:S(2)}, u32[]{:S(2)}) collective-permute-start(bf16[256,128]{1,0:T(8,128)(2,1)S(1)} %get-tuple-element.69), channel_id=1, source_target_pairs={{0,8},{2,10},{4,12},{6,14},{8,16},{10,18},{12,20},{14,22},{16,24},... | collective-permute-start | bytes 196616 | tf_op jit(solution)/shard_map/ppermute | solution.py:648
  24.1 2.6 %collective-permute-start.10 = (bf16[256,128]{1,0:T(8,128)(2,1)S(1)}, bf16[256,128]{1,0:T(8,128)(2,1)S(1)}, u32[]{:S(2)}, u32[]{:S(2)}) collective-permute-start(bf16[256,128]{1,0:T(8,128)(2,1)S(1)} %get-tuple-element.68), channel_id=1, source_target_pairs={{0,16},{2,18},{4,20},{6,22},{8,24},{10,26},{12,28},{14,30},{16,0},... | collective-permute-start | bytes 196616 | tf_op jit(solution)/shard_map/ppermute | solution.py:648
  26.7 1.3 collective-permute-start.9
  28.0 5.3 %shard_map.77 = (bf16[4,1536,1024]{2,1,0:T(8,128)(2,1)}, f32[8,128]{1,0:T(8,128)S(1)}) custom-call(bf16[1536,4,1024]{2,1,0:T(4,128)(2,1)} %refs_0_.5, f32[256,128]{1,0:T(8,128)S(1)} %get-tuple-element.66.refs_1_), custom_call_target="tpu_custom_call" | custom-call | bytes 25169920 | tf_op jit(solution)/shard_map/pallas_call | solution.py:149
  33.7 1.3 collective-permute-start.23
  36.1 2.6 %collective-permute-start.15 = (bf16[256,128]{1,0:T(8,128)(2,1)S(1)}, bf16[256,128]{1,0:T(8,128)(2,1)S(1)}, u32[]{:S(2)}, u32[]{:S(2)}) collective-permute-start(bf16[256,128]{1,0:T(8,128)(2,1)S(1)} %add_convert_fusion.3.refs_2_.refs_3_), channel_id=1, source_target_pairs={{0,16},{2,18},{4,20},{6,22},{8,24},{10,26},{12,28},{14,30},{16,0},... | collective-permute-start | bytes 196616 | tf_op jit(solution)/shard_map/ppermute | solution.py:648
  38.7 1.3 collective-permute-start.16
  40.0 1.6 %collective-permute-done.14.refs_4_.refs_1_ = bf16[256,128]{1,0:T(8,128)(2,1)S(1)} collective-permute-done((bf16[256,128]{1,0:T(8,128)(2,1)S(1)}, bf16[256,128]{1,0:T(8,128)(2,1)S(1)}, u32[]{:S(2)}, u32[]{:S(2)}) %collective-permute-start.14) | collective-permute-done | bytes 65568 | tf_op jit(solution)/shard_map/ppermute | solution.py:648
  42.4 1.5 collective-permute-done.15.refs_5_
  46.6 3.5 %collective-permute-done.17.refs_4_ = bf16[512,128]{1,0:T(8,128)(2,1)S(1)} collective-permute-done((bf16[512,128]{1,0:T(8,128)(2,1)S(1)}, bf16[512,128]{1,0:T(8,128)(2,1)S(1)}, u32[]{:S(2)}, u32[]{:S(2)}) %collective-permute-start.17) | collective-permute-done | bytes 131104 | tf_op jit(solution)/shard_map/ppermute | solution.py:644
  52.3 2.0 %collective-permute-start.22 = (bf16[256,128]{1,0:T(8,128)(2,1)S(1)}, bf16[256,128]{1,0:T(8,128)(2,1)S(1)}, u32[]{:S(2)}, u32[]{:S(2)}) collective-permute-start(bf16[256,128]{1,0:T(8,128)(2,1)S(1)} %get-tuple-element.81), channel_id=1, source_target_pairs={{0,8},{2,10},{4,12},{6,14},{8,16},{10,18},{12,20},{14,22},{16,24},... | collective-permute-start | bytes 196616 | tf_op jit(solution)/shard_map/ppermute | solution.py:648
  54.3 1.9 %collective-permute-start.20 = (bf16[256,128]{1,0:T(8,128)(2,1)S(1)}, bf16[256,128]{1,0:T(8,128)(2,1)S(1)}, u32[]{:S(2)}, u32[]{:S(2)}) collective-permute-start(bf16[256,128]{1,0:T(8,128)(2,1)S(1)} %get-tuple-element.79), channel_id=1, source_target_pairs={{0,24},{2,26},{4,28},{6,30},{8,0},{10,2},{12,4},{14,6},{16,8},{18,... | collective-permute-start | bytes 196616 | tf_op jit(solution)/shard_map/ppermute | solution.py:648
  56.2 5.2 %shard_map.88 = (bf16[4,1536,1024]{2,1,0:T(8,128)(2,1)}, f32[8,128]{1,0:T(8,128)S(1)}) custom-call(bf16[1536,4,1024]{2,1,0:T(4,128)(2,1)} %refs_0_.5, bf16[4,1536,1024]{2,1,0:T(8,128)(2,1)} %get-tuple-element.83.refs_1_, f32[256,128]{1,0:T(8,128)S(1)} %get-tuple-element.76.refs_1_.refs_2_), custom_call_target="tpu_custom_call", output_to_operand_aliasing={{0}: (1, {})} | custom-call | bytes 37752832 | tf_op jit(solution)/shard_map/pallas_call | solution.py:149
  63.7 1.6 %collective-permute-start.27 = (bf16[256,128]{1,0:T(8,128)(2,1)S(1)}, bf16[256,128]{1,0:T(8,128)(2,1)S(1)}, u32[]{:S(2)}, u32[]{:S(2)}) collective-permute-start(bf16[256,128]{1,0:T(8,128)(2,1)S(1)} %add_convert_fusion.2.refs_4_.refs_2_.refs_5_), channel_id=1, source_target_pairs={{0,16},{2,18},{4,20},{6,22},{8,24},{10,26},{12,28},{14,30},{16,0},... | collective-permute-start | bytes 196616 | tf_op jit(solution)/shard_map/ppermute | solution.py:648
  65.4 2.8 %collective-permute-start.28 = (bf16[256,128]{1,0:T(8,128)(2,1)S(1)}, bf16[256,128]{1,0:T(8,128)(2,1)S(1)}, u32[]{:S(2)}, u32[]{:S(2)}) collective-permute-start(bf16[256,128]{1,0:T(8,128)(2,1)S(1)} %add_convert_fusion.2.refs_4_.refs_2_.refs_5_), channel_id=1, source_target_pairs={{0,24},{2,26},{4,28},{6,30},{8,0},{10,2},{12,4},{14,6},{16,8},{18,... | collective-permute-start | bytes 196616 | tf_op jit(solution)/shard_map/ppermute | solution.py:648
  68.7 2.7 %collective-permute-done.27.refs_7_ = bf16[256,128]{1,0:T(8,128)(2,1)S(1)} collective-permute-done((bf16[256,128]{1,0:T(8,128)(2,1)S(1)}, bf16[256,128]{1,0:T(8,128)(2,1)S(1)}, u32[]{:S(2)}, u32[]{:S(2)}) %collective-permute-start.27) | collective-permute-done | bytes 65568 | tf_op jit(solution)/shard_map/ppermute | solution.py:648
  74.7 3.9 %collective-permute-done.29.refs_4_ = bf16[512,128]{1,0:T(8,128)(2,1)S(1)} collective-permute-done((bf16[512,128]{1,0:T(8,128)(2,1)S(1)}, bf16[512,128]{1,0:T(8,128)(2,1)S(1)}, u32[]{:S(2)}, u32[]{:S(2)}) %collective-permute-start.29) | collective-permute-done | bytes 131104 | tf_op jit(solution)/shard_map/ppermute | solution.py:644
  80.8 1.7 %collective-permute-start.34 = (bf16[256,128]{1,0:T(8,128)(2,1)S(1)}, bf16[256,128]{1,0:T(8,128)(2,1)S(1)}, u32[]{:S(2)}, u32[]{:S(2)}) collective-permute-start(bf16[256,128]{1,0:T(8,128)(2,1)S(1)} %get-tuple-element.94), channel_id=1, source_target_pairs={{0,8},{2,10},{4,12},{6,14},{8,16},{10,18},{12,20},{14,22},{16,24},... | collective-permute-start | bytes 196616 | tf_op jit(solution)/shard_map/ppermute | solution.py:648
  82.5 2.2 %collective-permute-start.32 = (bf16[256,128]{1,0:T(8,128)(2,1)S(1)}, bf16[256,128]{1,0:T(8,128)(2,1)S(1)}, u32[]{:S(2)}, u32[]{:S(2)}) collective-permute-start(bf16[256,128]{1,0:T(8,128)(2,1)S(1)} %get-tuple-element.92), channel_id=1, source_target_pairs={{0,24},{2,26},{4,28},{6,30},{8,0},{10,2},{12,4},{14,6},{16,8},{18,... | collective-permute-start | bytes 196616 | tf_op jit(solution)/shard_map/ppermute | solution.py:648
  84.6 5.3 %shard_map.96 = (bf16[4,1536,1024]{2,1,0:T(8,128)(2,1)}, f32[8,128]{1,0:T(8,128)S(1)}) custom-call(bf16[1536,4,1024]{2,1,0:T(4,128)(2,1)} %refs_0_.5, bf16[4,1536,1024]{2,1,0:T(8,128)(2,1)} %get-tuple-element.95.refs_1_, f32[256,128]{1,0:T(8,128)S(1)} %get-tuple-element.91.refs_1_.refs_2_), custom_call_target="tpu_custom_call", output_to_operand_aliasing={{0}: (1, {})} | custom-call | bytes 37752832 | tf_op jit(solution)/shard_map/pallas_call | solution.py:149
  89.9 3.3 %collective-permute-done.35.refs_3_.refs_1_ = bf16[1024,256]{1,0:T(8,128)(2,1)S(1)} collective-permute-done((bf16[1024,256]{1,0:T(8,128)(2,1)S(1)}, bf16[1024,256]{1,0:T(8,128)(2,1)S(1)}, u32[]{:S(2)}, u32[]{:S(2)}) %collective-permute-start.35) | collective-permute-done | bytes 524320 | tf_op jit(solution)/shard_map/ppermute | solution.py:644
  93.5 1.9 %collective-permute-start.37 = (bf16[256,128]{1,0:T(8,128)(2,1)S(1)}, bf16[256,128]{1,0:T(8,128)(2,1)S(1)}, u32[]{:S(2)}, u32[]{:S(2)}) collective-permute-start(bf16[256,128]{1,0:T(8,128)(2,1)S(1)} %add_convert_fusion.1.refs_2_.refs_7_), channel_id=1, source_target_pairs={{0,8},{2,10},{4,12},{6,14},{8,16},{10,18},{12,20},{14,22},{16,24},... | collective-permute-start | bytes 196616 | tf_op jit(solution)/shard_map/ppermute | solution.py:648
  95.4 1.9 %collective-permute-start.38 = (bf16[256,128]{1,0:T(8,128)(2,1)S(1)}, bf16[256,128]{1,0:T(8,128)(2,1)S(1)}, u32[]{:S(2)}, u32[]{:S(2)}) collective-permute-start(bf16[256,128]{1,0:T(8,128)(2,1)S(1)} %add_convert_fusion.1.refs_2_.refs_7_), channel_id=1, source_target_pairs={{0,16},{2,18},{4,20},{6,22},{8,24},{10,26},{12,28},{14,30},{16,0},... | collective-permute-start | bytes 196616 | tf_op jit(solution)/shard_map/ppermute | solution.py:648
  97.9 2.5 %collective-permute-done.37.refs_8_.refs_2_ = bf16[256,128]{1,0:T(8,128)(2,1)S(1)} collective-permute-done((bf16[256,128]{1,0:T(8,128)(2,1)S(1)}, bf16[256,128]{1,0:T(8,128)(2,1)S(1)}, u32[]{:S(2)}, u32[]{:S(2)}) %collective-permute-start.37) | collective-permute-done | bytes 65568 | tf_op jit(solution)/shard_map/ppermute | solution.py:648
  100.4 1.6 %collective-permute-start.49 = (bf16[2,1024,256]{2,1,0:T(8,128)(2,1)S(1)}, bf16[2,1024,256]{2,1,0:T(8,128)(2,1)S(1)}, u32[]{:S(2)}, u32[]{:S(2)}) collective-permute-start(bf16[2,1024,256]{2,1,0:T(8,128)(2,1)S(1)} %shard_map.104.refs_1_), channel_id=1, source_target_pairs={{0,2},{2,0},{4,6},{6,4},{8,10},{10,8},{12,14},{14,12},{16,18},{18,... | collective-permute-start | bytes 3145736 | tf_op jit(solution)/shard_map/ppermute | solution.py:644
  102.9 1.5 shard_map.99
  106.5 4.0 %collective-permute-done.40.refs_4_ = bf16[512,128]{1,0:T(8,128)(2,1)S(1)} collective-permute-done((bf16[512,128]{1,0:T(8,128)(2,1)S(1)}, bf16[512,128]{1,0:T(8,128)(2,1)S(1)}, u32[]{:S(2)}, u32[]{:S(2)}) %collective-permute-start.40) | collective-permute-done | bytes 131104 | tf_op jit(solution)/shard_map/ppermute | solution.py:644
  112.5 1.8 %collective-permute-start.44 = (bf16[256,128]{1,0:T(8,128)(2,1)S(1)}, bf16[256,128]{1,0:T(8,128)(2,1)S(1)}, u32[]{:S(2)}, u32[]{:S(2)}) collective-permute-start(bf16[256,128]{1,0:T(8,128)(2,1)S(1)} %get-tuple-element.104), channel_id=1, source_target_pairs={{0,8},{2,10},{4,12},{6,14},{8,16},{10,18},{12,20},{14,22},{16,24},... | collective-permute-start | bytes 196616 | tf_op jit(solution)/shard_map/ppermute | solution.py:648
  114.3 2.1 %collective-permute-start.42 = (bf16[256,128]{1,0:T(8,128)(2,1)S(1)}, bf16[256,128]{1,0:T(8,128)(2,1)S(1)}, u32[]{:S(2)}, u32[]{:S(2)}) collective-permute-start(bf16[256,128]{1,0:T(8,128)(2,1)S(1)} %get-tuple-element.102), channel_id=1, source_target_pairs={{0,24},{2,26},{4,28},{6,30},{8,0},{10,2},{12,4},{14,6},{16,8},{18,... | collective-permute-start | bytes 196616 | tf_op jit(solution)/shard_map/ppermute | solution.py:648
  116.3 2.9 %collective-permute-done.44.refs_0_ = bf16[256,128]{1,0:T(8,128)(2,1)S(1)} collective-permute-done((bf16[256,128]{1,0:T(8,128)(2,1)S(1)}, bf16[256,128]{1,0:T(8,128)(2,1)S(1)}, u32[]{:S(2)}, u32[]{:S(2)}) %collective-permute-start.44) | collective-permute-done | bytes 65568 | tf_op jit(solution)/shard_map/ppermute | solution.py:648
  119.4 2.2 %collective-permute-done.43 = bf16[256,128]{1,0:T(8,128)(2,1)S(1)} collective-permute-done((bf16[256,128]{1,0:T(8,128)(2,1)S(1)}, bf16[256,128]{1,0:T(8,128)(2,1)S(1)}, u32[]{:S(2)}, u32[]{:S(2)}) %collective-permute-start.43) | collective-permute-done | bytes 65568 | tf_op jit(solution)/shard_map/ppermute | solution.py:648
  121.7 1.5 collective-permute-start.52
  123.2 2.8 %collective-permute-start.47 = (bf16[256,128]{1,0:T(8,128)(2,1)S(1)}, bf16[256,128]{1,0:T(8,128)(2,1)S(1)}, u32[]{:S(2)}, u32[]{:S(2)}) collective-permute-start(bf16[256,128]{1,0:T(8,128)(2,1)S(1)} %add_convert_fusion.refs_3_.refs_1_.refs_2_), channel_id=1, source_target_pairs={{0,16},{2,18},{4,20},{6,22},{8,24},{10,26},{12,28},{14,30},{16,0},... | collective-permute-start | bytes 196616 | tf_op jit(solution)/shard_map/ppermute | solution.py:648
  127.1 2.6 %shard_map.105 = (bf16[4,1024,512]{2,1,0:T(8,128)(2,1)}, bf16[2,512,1024]{2,1,0:T(8,128)(2,1)S(1)}) custom-call(s32[4]{0:T(128)S(1)} %pad_add_fusion.refs_0_, bf16[2,1024,256]{2,1,0:T(8,128)(2,1)S(1)} %shard_map.104.refs_1_, bf16[2,1024,256]{2,1,0:T(8,128)(2,1)S(1)} %collective-permute-done.49.refs_2_, ...), custom_call_target="tpu_custom_call" | custom-call | bytes 8388624 | tf_op jit(solution)/shard_map/pallas_call | solution.py:149
  131.0 1.3 collective-permute-done.50.refs_2_
  134.5 1.4 collective-permute-done.52.refs_5_.refs_3_.refs_2_
  135.9 5.8 %shard_map.109 = (f32[256,1536]{1,0:T(8,128)S(1)}, bf16[256,1536]{1,0:T(8,128)(2,1)S(1)}) custom-call(s32[4]{0:T(128)S(1)} %pad_add_fusion.refs_0_, bf16[2,512,1024]{2,1,0:T(8,128)(2,1)S(1)} %get-tuple-element.105.refs_5_.refs_1_, bf16[4,1536,1024]{2,1,0:T(8,128)(2,1)} %get-tuple-element.108.refs_2_.refs_3_.refs_5_, ...), custom_call_target="tpu_custom_call" | custom-call | flops 3221225472 | bytes 17039376 | tf_op jit(solution)/shard_map/pallas_call | solution.py:149
  141.7 2.1 %collective-permute-start.54 = (bf16[512,256]{1,0:T(8,128)(2,1)S(1)}, bf16[512,256]{1,0:T(8,128)(2,1)S(1)}, u32[]{:S(2)}, u32[]{:S(2)}) collective-permute-start(bf16[512,256]{1,0:T(8,128)(2,1)S(1)} %shard_map.110.refs_2_), channel_id=1, source_target_pairs={{0,2},{2,0},{4,6},{6,4},{8,10},{10,8},{12,14},{14,12},{16,18},{18,... | collective-permute-start | bytes 786440 | tf_op jit(solution)/shard_map/ppermute | solution.py:644
  143.8 4.7 %shard_map.111 = (bf16[4,1024,512]{2,1,0:T(8,128)(2,1)}, f32[256,1536]{1,0:T(8,128)S(1)}, bf16[256,1536]{1,0:T(8,128)(2,1)S(1)}) custom-call(s32[4]{0:T(128)S(1)} %pad_add_fusion.refs_0_, bf16[2,512,256]{2,1,0:T(8,128)(2,1)S(1)} %shard_map.108.refs_4_.refs_2_.refs_1_, ...), custom_call_target="tpu_custom_call", output_to_operand_aliasing={{0}: (6, {})} | custom-call | flops 1610612736 | bytes 26738704 | tf_op jit(solution)/shard_map/pallas_call | solution.py:149
  148.9 4.8 %shard_map.112 = (bf16[4,1024,512]{2,1,0:T(8,128)(2,1)}, f32[256,1536]{1,0:T(8,128)S(1)}, bf16[256,1536]{1,0:T(8,128)(2,1)S(1)}) custom-call(s32[4]{0:T(128)S(1)} %pad_add_fusion.refs_0_, bf16[512,256]{1,0:T(8,128)(2,1)S(1)} %shard_map.107.refs_3_.refs_1_, bf16[512,256]{1,0:T(8,128)(2,1)S(1)} %shard_map.110.refs_2_, ...), custom_call_target="tpu_custom_call", output_to_operand_aliasing={{0}: (8, {})} | custom-call | flops 1610612736 | bytes 26738704 | tf_op jit(solution)/shard_map/pallas_call | solution.py:149
  153.7 2.3 %collective-permute-done.55 = bf16[256,1536]{1,0:T(8,128)(2,1)S(1)} collective-permute-done((bf16[256,1536]{1,0:T(8,128)(2,1)S(1)}, bf16[256,1536]{1,0:T(8,128)(2,1)S(1)}, u32[]{:S(2)}, u32[]{:S(2)}) %collective-permute-start.55) | collective-permute-done | bytes 786464 | tf_op jit(solution)/shard_map/ppermute | solution.py:651
  (119 shorter events, 32.8 us)
Async XLA Ops:
  1.9 7.9 %collective-permute-start = (bf16[128,768]{1,0:T(8,128)(2,1)S(1)}, bf16[128,768]{1,0:T(8,128)(2,1)S(1)}, u32[]{:S(2)}, u32[]{:S(2)}) collective-permute-start(bf16[128,768]{1,0:T(8,128)(2,1)S(1)} %get-tuple-element.62), channel_id=1, source_target_pairs={{0,4},{2,6},{4,0},{6,2},{8,12},{10,14},{12,8},{14,10},{16,20},{18,... | collective-permute-start | bytes 589832 | tf_op jit(solution)/shard_map/ppermute | solution.py:644
  5.0 8.9 %collective-permute-start.3 = (bf16[128,1152]{1,0:T(8,128)(2,1)S(1)}, bf16[128,1152]{1,0:T(8,128)(2,1)S(1)}, u32[]{:S(2)}, u32[]{:S(2)}) collective-permute-start(bf16[128,1152]{1,0:T(8,128)(2,1)S(1)} %get-tuple-element.65), channel_id=1, source_target_pairs={{0,2},{2,0},{4,6},{6,4},{8,10},{10,8},{12,14},{14,12},{16,18},{18,... | collective-permute-start | bytes 884744 | tf_op jit(solution)/shard_map/ppermute | solution.py:644
  9.9 7.8 %collective-permute-start.1 = (bf16[128,1024]{1,0:T(8,128)(2,1)S(1)}, bf16[128,1024]{1,0:T(8,128)(2,1)S(1)}, u32[]{:S(2)}, u32[]{:S(2)}) collective-permute-start(bf16[128,1024]{1,0:T(8,128)(2,1)S(1)} %shard_map.71), channel_id=1, source_target_pairs={{0,4},{2,6},{4,0},{6,2},{8,12},{10,14},{12,8},{14,10},{16,20},{18,... | collective-permute-start | bytes 786440 | tf_op jit(solution)/shard_map/ppermute | solution.py:644
  11.6 6.0 %collective-permute-start.4 = (bf16[128,768]{1,0:T(8,128)(2,1)S(1)}, bf16[128,768]{1,0:T(8,128)(2,1)S(1)}, u32[]{:S(2)}, u32[]{:S(2)}) collective-permute-start(bf16[128,768]{1,0:T(8,128)(2,1)S(1)} %shard_map.73.refs_2_), channel_id=1, source_target_pairs={{0,2},{2,0},{4,6},{6,4},{8,10},{10,8},{12,14},{14,12},{16,18},{18,... | collective-permute-start | bytes 589832 | tf_op jit(solution)/shard_map/ppermute | solution.py:644
  18.7 14.6 %collective-permute-start.2 = (bf16[2,128,1024]{2,1,0:T(8,128)(2,1)S(1)}, bf16[2,128,1024]{2,1,0:T(8,128)(2,1)S(1)}, u32[]{:S(2)}, u32[]{:S(2)}) collective-permute-start(bf16[2,128,1024]{2,1,0:T(8,128)(2,1)S(1)} %shard_map.72.refs_1_.refs_0_), channel_id=1, source_target_pairs={{0,2},{2,0},{4,6},{6,4},{8,10},{10,8},{12,14},{14,12},{16,18},{18,... | collective-permute-start | bytes 1572872 | tf_op jit(solution)/shard_map/ppermute | solution.py:644
  21.3 12.0 %collective-permute-start.12 = (bf16[128,1536]{1,0:T(8,128)(2,1)S(1)}, bf16[128,1536]{1,0:T(8,128)(2,1)S(1)}, u32[]{:S(2)}, u32[]{:S(2)}) collective-permute-start(bf16[128,1536]{1,0:T(8,128)(2,1)S(1)} %shard_map.76), channel_id=1, source_target_pairs={{0,4},{2,6},{4,0},{6,2},{8,12},{10,14},{12,8},{14,10},{16,20},{18,... | collective-permute-start | bytes 1179656 | tf_op jit(solution)/shard_map/ppermute | solution.py:644
  22.5 10.8 %collective-permute-start.11 = (bf16[256,128]{1,0:T(8,128)(2,1)S(1)}, bf16[256,128]{1,0:T(8,128)(2,1)S(1)}, u32[]{:S(2)}, u32[]{:S(2)}) collective-permute-start(bf16[256,128]{1,0:T(8,128)(2,1)S(1)} %get-tuple-element.69), channel_id=1, source_target_pairs={{0,8},{2,10},{4,12},{6,14},{8,16},{10,18},{12,20},{14,22},{16,24},... | collective-permute-start | bytes 196616 | tf_op jit(solution)/shard_map/ppermute | solution.py:648
  24.1 9.3 %collective-permute-start.10 = (bf16[256,128]{1,0:T(8,128)(2,1)S(1)}, bf16[256,128]{1,0:T(8,128)(2,1)S(1)}, u32[]{:S(2)}, u32[]{:S(2)}) collective-permute-start(bf16[256,128]{1,0:T(8,128)(2,1)S(1)} %get-tuple-element.68), channel_id=1, source_target_pairs={{0,16},{2,18},{4,20},{6,22},{8,24},{10,26},{12,28},{14,30},{16,0},... | collective-permute-start | bytes 196616 | tf_op jit(solution)/shard_map/ppermute | solution.py:648
  26.7 6.7 %collective-permute-start.9 = (bf16[256,128]{1,0:T(8,128)(2,1)S(1)}, bf16[256,128]{1,0:T(8,128)(2,1)S(1)}, u32[]{:S(2)}, u32[]{:S(2)}) collective-permute-start(bf16[256,128]{1,0:T(8,128)(2,1)S(1)} %get-tuple-element.67), channel_id=1, source_target_pairs={{0,24},{2,26},{4,28},{6,30},{8,0},{10,2},{12,4},{14,6},{16,8},{18,... | collective-permute-start | bytes 196616 | tf_op jit(solution)/shard_map/ppermute | solution.py:648
  33.5 10.5 %collective-permute-start.13 = (bf16[4,128,1024]{2,1,0:T(8,128)(2,1)S(1)}, bf16[4,128,1024]{2,1,0:T(8,128)(2,1)S(1)}, u32[]{:S(2)}, u32[]{:S(2)}) collective-permute-start(bf16[4,128,1024]{2,1,0:T(8,128)(2,1)S(1)} %shard_map.79.refs_1_), channel_id=1, source_target_pairs={{0,1},{1,0},{2,3},{3,2},{4,5},{5,4},{6,7},{7,6},{8,9},{9,8},{10,11... | collective-permute-start | bytes 3145736 | tf_op jit(solution)/shard_map/ppermute | solution.py:651
  33.7 27.7 %collective-permute-start.23 = (bf16[2,128,1536]{2,1,0:T(8,128)(2,1)S(1)}, bf16[2,128,1536]{2,1,0:T(8,128)(2,1)S(1)}, u32[]{:S(2)}, u32[]{:S(2)}) collective-permute-start(bf16[2,128,1536]{2,1,0:T(8,128)(2,1)S(1)} %shard_map.87.refs_1_.refs_0_), channel_id=1, source_target_pairs={{0,2},{2,0},{4,6},{6,4},{8,10},{10,8},{12,14},{14,12},{16,18},{18,... | collective-permute-start | bytes 2359304 | tf_op jit(solution)/shard_map/ppermute | solution.py:644
  35.0 6.7 %collective-permute-start.14 = (bf16[256,128]{1,0:T(8,128)(2,1)S(1)}, bf16[256,128]{1,0:T(8,128)(2,1)S(1)}, u32[]{:S(2)}, u32[]{:S(2)}) collective-permute-start(bf16[256,128]{1,0:T(8,128)(2,1)S(1)} %add_convert_fusion.3.refs_2_.refs_3_), channel_id=1, source_target_pairs={{0,8},{2,10},{4,12},{6,14},{8,16},{10,18},{12,20},{14,22},{16,24},... | collective-permute-start | bytes 196616 | tf_op jit(solution)/shard_map/ppermute | solution.py:648
  36.1 7.8 %collective-permute-start.15 = (bf16[256,128]{1,0:T(8,128)(2,1)S(1)}, bf16[256,128]{1,0:T(8,128)(2,1)S(1)}, u32[]{:S(2)}, u32[]{:S(2)}) collective-permute-start(bf16[256,128]{1,0:T(8,128)(2,1)S(1)} %add_convert_fusion.3.refs_2_.refs_3_), channel_id=1, source_target_pairs={{0,16},{2,18},{4,20},{6,22},{8,24},{10,26},{12,28},{14,30},{16,0},... | collective-permute-start | bytes 196616 | tf_op jit(solution)/shard_map/ppermute | solution.py:648
  38.7 5.3 %collective-permute-start.16 = (bf16[256,128]{1,0:T(8,128)(2,1)S(1)}, bf16[256,128]{1,0:T(8,128)(2,1)S(1)}, u32[]{:S(2)}, u32[]{:S(2)}) collective-permute-start(bf16[256,128]{1,0:T(8,128)(2,1)S(1)} %add_convert_fusion.3.refs_2_.refs_3_), channel_id=1, source_target_pairs={{0,24},{2,26},{4,28},{6,30},{8,0},{10,2},{12,4},{14,6},{16,8},{18,... | collective-permute-start | bytes 196616 | tf_op jit(solution)/shard_map/ppermute | solution.py:648
  41.7 5.0 %collective-permute-start.18 = (bf16[128,512]{1,0:T(8,128)(2,1)S(1)}, bf16[128,512]{1,0:T(8,128)(2,1)S(1)}, u32[]{:S(2)}, u32[]{:S(2)}) collective-permute-start(bf16[128,512]{1,0:T(8,128)(2,1)S(1)} %shard_map.81), channel_id=1, source_target_pairs={{0,4},{2,6},{4,0},{6,2},{8,12},{10,14},{12,8},{14,10},{16,20},{18,... | collective-permute-start | bytes 393224 | tf_op jit(solution)/shard_map/ppermute | solution.py:644
  45.0 5.1 %collective-permute-start.17 = (bf16[512,128]{1,0:T(8,128)(2,1)S(1)}, bf16[512,128]{1,0:T(8,128)(2,1)S(1)}, u32[]{:S(2)}, u32[]{:S(2)}) collective-permute-start(bf16[512,128]{1,0:T(8,128)(2,1)S(1)} %get-tuple-element.74), channel_id=1, source_target_pairs={{0,4},{2,6},{4,0},{6,2},{8,12},{10,14},{12,8},{14,10},{16,20},{18,... | collective-permute-start | bytes 393224 | tf_op jit(solution)/shard_map/ppermute | solution.py:644
  51.1 10.2 %collective-permute-start.19 = (bf16[128,1536]{1,0:T(8,128)(2,1)S(1)}, bf16[128,1536]{1,0:T(8,128)(2,1)S(1)}, u32[]{:S(2)}, u32[]{:S(2)}) collective-permute-start(bf16[128,1536]{1,0:T(8,128)(2,1)S(1)} %shard_map.84), channel_id=1, source_target_pairs={{0,4},{2,6},{4,0},{6,2},{8,12},{10,14},{12,8},{14,10},{16,20},{18,... | collective-permute-start | bytes 1179656 | tf_op jit(solution)/shard_map/ppermute | solution.py:644
  52.3 9.0 %collective-permute-start.22 = (bf16[256,128]{1,0:T(8,128)(2,1)S(1)}, bf16[256,128]{1,0:T(8,128)(2,1)S(1)}, u32[]{:S(2)}, u32[]{:S(2)}) collective-permute-start(bf16[256,128]{1,0:T(8,128)(2,1)S(1)} %get-tuple-element.81), channel_id=1, source_target_pairs={{0,8},{2,10},{4,12},{6,14},{8,16},{10,18},{12,20},{14,22},{16,24},... | collective-permute-start | bytes 196616 | tf_op jit(solution)/shard_map/ppermute | solution.py:648
  54.3 7.1 %collective-permute-start.20 = (bf16[256,128]{1,0:T(8,128)(2,1)S(1)}, bf16[256,128]{1,0:T(8,128)(2,1)S(1)}, u32[]{:S(2)}, u32[]{:S(2)}) collective-permute-start(bf16[256,128]{1,0:T(8,128)(2,1)S(1)} %get-tuple-element.79), channel_id=1, source_target_pairs={{0,24},{2,26},{4,28},{6,30},{8,0},{10,2},{12,4},{14,6},{16,8},{18,... | collective-permute-start | bytes 196616 | tf_op jit(solution)/shard_map/ppermute | solution.py:648
  56.1 5.5 %collective-permute-start.21 = (bf16[256,128]{1,0:T(8,128)(2,1)S(1)}, bf16[256,128]{1,0:T(8,128)(2,1)S(1)}, u32[]{:S(2)}, u32[]{:S(2)}) collective-permute-start(bf16[256,128]{1,0:T(8,128)(2,1)S(1)} %get-tuple-element.80), channel_id=1, source_target_pairs={{0,16},{2,18},{4,20},{6,22},{8,24},{10,26},{12,28},{14,30},{16,0},... | collective-permute-start | bytes 196616 | tf_op jit(solution)/shard_map/ppermute | solution.py:648
  61.8 9.6 %collective-permute-start.25 = (bf16[4,128,1536]{2,1,0:T(8,128)(2,1)S(1)}, bf16[4,128,1536]{2,1,0:T(8,128)(2,1)S(1)}, u32[]{:S(2)}, u32[]{:S(2)}) collective-permute-start(bf16[4,128,1536]{2,1,0:T(8,128)(2,1)S(1)} %shard_map.91.refs_1_), channel_id=1, source_target_pairs={{0,1},{1,0},{2,3},{3,2},{4,5},{5,4},{6,7},{7,6},{8,9},{9,8},{10,11... | collective-permute-start | bytes 4718600 | tf_op jit(solution)/shard_map/ppermute | solution.py:651
  61.9 28.0 %collective-permute-start.24 = (bf16[2,128,2048]{2,1,0:T(8,128)(2,1)S(1)}, bf16[2,128,2048]{2,1,0:T(8,128)(2,1)S(1)}, u32[]{:S(2)}, u32[]{:S(2)}) collective-permute-start(bf16[2,128,2048]{2,1,0:T(8,128)(2,1)S(1)} %shard_map.90.refs_1_.refs_0_), channel_id=1, source_target_pairs={{0,2},{2,0},{4,6},{6,4},{8,10},{10,8},{12,14},{14,12},{16,18},{18,... | collective-permute-start | bytes 3145736 | tf_op jit(solution)/shard_map/ppermute | solution.py:644
  62.5 6.2 %collective-permute-start.26 = (bf16[256,128]{1,0:T(8,128)(2,1)S(1)}, bf16[256,128]{1,0:T(8,128)(2,1)S(1)}, u32[]{:S(2)}, u32[]{:S(2)}) collective-permute-start(bf16[256,128]{1,0:T(8,128)(2,1)S(1)} %add_convert_fusion.2.refs_4_.refs_2_.refs_5_), channel_id=1, source_target_pairs={{0,8},{2,10},{4,12},{6,14},{8,16},{10,18},{12,20},{14,22},{16,24},... | collective-permute-start | bytes 196616 | tf_op jit(solution)/shard_map/ppermute | solution.py:648
  63.7 7.7 %collective-permute-start.27 = (bf16[256,128]{1,0:T(8,128)(2,1)S(1)}, bf16[256,128]{1,0:T(8,128)(2,1)S(1)}, u32[]{:S(2)}, u32[]{:S(2)}) collective-permute-start(bf16[256,128]{1,0:T(8,128)(2,1)S(1)} %add_convert_fusion.2.refs_4_.refs_2_.refs_5_), channel_id=1, source_target_pairs={{0,16},{2,18},{4,20},{6,22},{8,24},{10,26},{12,28},{14,30},{16,0},... | collective-permute-start | bytes 196616 | tf_op jit(solution)/shard_map/ppermute | solution.py:648
  65.4 6.0 %collective-permute-start.28 = (bf16[256,128]{1,0:T(8,128)(2,1)S(1)}, bf16[256,128]{1,0:T(8,128)(2,1)S(1)}, u32[]{:S(2)}, u32[]{:S(2)}) collective-permute-start(bf16[256,128]{1,0:T(8,128)(2,1)S(1)} %add_convert_fusion.2.refs_4_.refs_2_.refs_5_), channel_id=1, source_target_pairs={{0,24},{2,26},{4,28},{6,30},{8,0},{10,2},{12,4},{14,6},{16,8},{18,... | collective-permute-start | bytes 196616 | tf_op jit(solution)/shard_map/ppermute | solution.py:648
  68.7 5.2 %collective-permute-start.30 = (bf16[512,128]{1,0:T(8,128)(2,1)S(1)}, bf16[512,128]{1,0:T(8,128)(2,1)S(1)}, u32[]{:S(2)}, u32[]{:S(2)}) collective-permute-start(bf16[512,128]{1,0:T(8,128)(2,1)S(1)} %get-tuple-element.86.refs_4_), channel_id=1, source_target_pairs={{0,1},{1,0},{2,3},{3,2},{4,5},{5,4},{6,7},{7,6},{8,9},{9,8},{10,11... | collective-permute-start | bytes 393224 | tf_op jit(solution)/shard_map/ppermute | solution.py:651
  72.7 5.9 %collective-permute-start.29 = (bf16[512,128]{1,0:T(8,128)(2,1)S(1)}, bf16[512,128]{1,0:T(8,128)(2,1)S(1)}, u32[]{:S(2)}, u32[]{:S(2)}) collective-permute-start(bf16[512,128]{1,0:T(8,128)(2,1)S(1)} %get-tuple-element.88), channel_id=1, source_target_pairs={{0,4},{2,6},{4,0},{6,2},{8,12},{10,14},{12,8},{14,10},{16,20},{18,... | collective-permute-start | bytes 393224 | tf_op jit(solution)/shard_map/ppermute | solution.py:644
  79.7 13.6 %collective-permute-start.35 = (bf16[1024,256]{1,0:T(8,128)(2,1)S(1)}, bf16[1024,256]{1,0:T(8,128)(2,1)S(1)}, u32[]{:S(2)}, u32[]{:S(2)}) collective-permute-start(bf16[1024,256]{1,0:T(8,128)(2,1)S(1)} %shard_map.95.refs_0_), channel_id=1, source_target_pairs={{0,4},{2,6},{4,0},{6,2},{8,12},{10,14},{12,8},{14,10},{16,20},{18,... | collective-permute-start | bytes 1572872 | tf_op jit(solution)/shard_map/ppermute | solution.py:644
  80.8 9.1 %collective-permute-start.34 = (bf16[256,128]{1,0:T(8,128)(2,1)S(1)}, bf16[256,128]{1,0:T(8,128)(2,1)S(1)}, u32[]{:S(2)}, u32[]{:S(2)}) collective-permute-start(bf16[256,128]{1,0:T(8,128)(2,1)S(1)} %get-tuple-element.94), channel_id=1, source_target_pairs={{0,8},{2,10},{4,12},{6,14},{8,16},{10,18},{12,20},{14,22},{16,24},... | collective-permute-start | bytes 196616 | tf_op jit(solution)/shard_map/ppermute | solution.py:648
  82.5 10.7 %collective-permute-start.32 = (bf16[256,128]{1,0:T(8,128)(2,1)S(1)}, bf16[256,128]{1,0:T(8,128)(2,1)S(1)}, u32[]{:S(2)}, u32[]{:S(2)}) collective-permute-start(bf16[256,128]{1,0:T(8,128)(2,1)S(1)} %get-tuple-element.92), channel_id=1, source_target_pairs={{0,24},{2,26},{4,28},{6,30},{8,0},{10,2},{12,4},{14,6},{16,8},{18,... | collective-permute-start | bytes 196616 | tf_op jit(solution)/shard_map/ppermute | solution.py:648
  84.6 8.6 %collective-permute-start.33 = (bf16[256,128]{1,0:T(8,128)(2,1)S(1)}, bf16[256,128]{1,0:T(8,128)(2,1)S(1)}, u32[]{:S(2)}, u32[]{:S(2)}) collective-permute-start(bf16[256,128]{1,0:T(8,128)(2,1)S(1)} %get-tuple-element.93), channel_id=1, source_target_pairs={{0,16},{2,18},{4,20},{6,22},{8,24},{10,26},{12,28},{14,30},{16,0},... | collective-permute-start | bytes 196616 | tf_op jit(solution)/shard_map/ppermute | solution.py:648
  93.4 9.5 %collective-permute-start.36 = (bf16[4,128,2048]{2,1,0:T(8,128)(2,1)S(1)}, bf16[4,128,2048]{2,1,0:T(8,128)(2,1)S(1)}, u32[]{:S(2)}, u32[]{:S(2)}) collective-permute-start(bf16[4,128,2048]{2,1,0:T(8,128)(2,1)S(1)} %shard_map.98.refs_1_), channel_id=1, source_target_pairs={{0,1},{1,0},{2,3},{3,2},{4,5},{5,4},{6,7},{7,6},{8,9},{9,8},{10,11... | collective-permute-start | bytes 6291464 | tf_op jit(solution)/shard_map/ppermute | solution.py:651
  93.5 6.8 %collective-permute-start.37 = (bf16[256,128]{1,0:T(8,128)(2,1)S(1)}, bf16[256,128]{1,0:T(8,128)(2,1)S(1)}, u32[]{:S(2)}, u32[]{:S(2)}) collective-permute-start(bf16[256,128]{1,0:T(8,128)(2,1)S(1)} %add_convert_fusion.1.refs_2_.refs_7_), channel_id=1, source_target_pairs={{0,8},{2,10},{4,12},{6,14},{8,16},{10,18},{12,20},{14,22},{16,24},... | collective-permute-start | bytes 196616 | tf_op jit(solution)/shard_map/ppermute | solution.py:648
  95.4 7.3 %collective-permute-start.38 = (bf16[256,128]{1,0:T(8,128)(2,1)S(1)}, bf16[256,128]{1,0:T(8,128)(2,1)S(1)}, u32[]{:S(2)}, u32[]{:S(2)}) collective-permute-start(bf16[256,128]{1,0:T(8,128)(2,1)S(1)} %add_convert_fusion.1.refs_2_.refs_7_), channel_id=1, source_target_pairs={{0,16},{2,18},{4,20},{6,22},{8,24},{10,26},{12,28},{14,30},{16,0},... | collective-permute-start | bytes 196616 | tf_op jit(solution)/shard_map/ppermute | solution.py:648
  97.3 5.6 %collective-permute-start.39 = (bf16[256,128]{1,0:T(8,128)(2,1)S(1)}, bf16[256,128]{1,0:T(8,128)(2,1)S(1)}, u32[]{:S(2)}, u32[]{:S(2)}) collective-permute-start(bf16[256,128]{1,0:T(8,128)(2,1)S(1)} %add_convert_fusion.1.refs_2_.refs_7_), channel_id=1, source_target_pairs={{0,24},{2,26},{4,28},{6,30},{8,0},{10,2},{12,4},{14,6},{16,8},{18,... | collective-permute-start | bytes 196616 | tf_op jit(solution)/shard_map/ppermute | solution.py:648
  100.4 26.7 %collective-permute-start.49 = (bf16[2,1024,256]{2,1,0:T(8,128)(2,1)S(1)}, bf16[2,1024,256]{2,1,0:T(8,128)(2,1)S(1)}, u32[]{:S(2)}, u32[]{:S(2)}) collective-permute-start(bf16[2,1024,256]{2,1,0:T(8,128)(2,1)S(1)} %shard_map.104.refs_1_), channel_id=1, source_target_pairs={{0,2},{2,0},{4,6},{6,4},{8,10},{10,8},{12,14},{14,12},{16,18},{18,... | collective-permute-start | bytes 3145736 | tf_op jit(solution)/shard_map/ppermute | solution.py:644
  104.5 5.9 %collective-permute-start.40 = (bf16[512,128]{1,0:T(8,128)(2,1)S(1)}, bf16[512,128]{1,0:T(8,128)(2,1)S(1)}, u32[]{:S(2)}, u32[]{:S(2)}) collective-permute-start(bf16[512,128]{1,0:T(8,128)(2,1)S(1)} %get-tuple-element.98), channel_id=1, source_target_pairs={{0,4},{2,6},{4,0},{6,2},{8,12},{10,14},{12,8},{14,10},{16,20},{18,... | collective-permute-start | bytes 393224 | tf_op jit(solution)/shard_map/ppermute | solution.py:644
  111.5 7.9 %collective-permute-start.45 = (bf16[512,256]{1,0:T(8,128)(2,1)S(1)}, bf16[512,256]{1,0:T(8,128)(2,1)S(1)}, u32[]{:S(2)}, u32[]{:S(2)}) collective-permute-start(bf16[512,256]{1,0:T(8,128)(2,1)S(1)} %shard_map.102.refs_0_), channel_id=1, source_target_pairs={{0,4},{2,6},{4,0},{6,2},{8,12},{10,14},{12,8},{14,10},{16,20},{18,... | collective-permute-start | bytes 786440 | tf_op jit(solution)/shard_map/ppermute | solution.py:644
  112.5 6.7 %collective-permute-start.44 = (bf16[256,128]{1,0:T(8,128)(2,1)S(1)}, bf16[256,128]{1,0:T(8,128)(2,1)S(1)}, u32[]{:S(2)}, u32[]{:S(2)}) collective-permute-start(bf16[256,128]{1,0:T(8,128)(2,1)S(1)} %get-tuple-element.104), channel_id=1, source_target_pairs={{0,8},{2,10},{4,12},{6,14},{8,16},{10,18},{12,20},{14,22},{16,24},... | collective-permute-start | bytes 196616 | tf_op jit(solution)/shard_map/ppermute | solution.py:648
  114.3 5.1 %collective-permute-start.42 = (bf16[256,128]{1,0:T(8,128)(2,1)S(1)}, bf16[256,128]{1,0:T(8,128)(2,1)S(1)}, u32[]{:S(2)}, u32[]{:S(2)}) collective-permute-start(bf16[256,128]{1,0:T(8,128)(2,1)S(1)} %get-tuple-element.102), channel_id=1, source_target_pairs={{0,24},{2,26},{4,28},{6,30},{8,0},{10,2},{12,4},{14,6},{16,8},{18,... | collective-permute-start | bytes 196616 | tf_op jit(solution)/shard_map/ppermute | solution.py:648
  116.3 5.3 %collective-permute-start.43 = (bf16[256,128]{1,0:T(8,128)(2,1)S(1)}, bf16[256,128]{1,0:T(8,128)(2,1)S(1)}, u32[]{:S(2)}, u32[]{:S(2)}) collective-permute-start(bf16[256,128]{1,0:T(8,128)(2,1)S(1)} %get-tuple-element.103), channel_id=1, source_target_pairs={{0,16},{2,18},{4,20},{6,22},{8,24},{10,26},{12,28},{14,30},{16,0},... | collective-permute-start | bytes 196616 | tf_op jit(solution)/shard_map/ppermute | solution.py:648
  121.7 14.2 %collective-permute-start.52 = (bf16[2,512,256]{2,1,0:T(8,128)(2,1)S(1)}, bf16[2,512,256]{2,1,0:T(8,128)(2,1)S(1)}, u32[]{:S(2)}, u32[]{:S(2)}) collective-permute-start(bf16[2,512,256]{2,1,0:T(8,128)(2,1)S(1)} %shard_map.108.refs_4_.refs_2_.refs_1_), channel_id=1, source_target_pairs={{0,2},{2,0},{4,6},{6,4},{8,10},{10,8},{12,14},{14,12},{16,18},{18,... | collective-permute-start | bytes 1572872 | tf_op jit(solution)/shard_map/ppermute | solution.py:644
  123.2 6.5 %collective-permute-start.46 = (bf16[256,128]{1,0:T(8,128)(2,1)S(1)}, bf16[256,128]{1,0:T(8,128)(2,1)S(1)}, u32[]{:S(2)}, u32[]{:S(2)}) collective-permute-start(bf16[256,128]{1,0:T(8,128)(2,1)S(1)} %add_convert_fusion.refs_3_.refs_1_.refs_2_), channel_id=1, source_target_pairs={{0,8},{2,10},{4,12},{6,14},{8,16},{10,18},{12,20},{14,22},{16,24},... | collective-permute-start | bytes 196616 | tf_op jit(solution)/shard_map/ppermute | solution.py:648
  123.2 6.5 %collective-permute-start.47 = (bf16[256,128]{1,0:T(8,128)(2,1)S(1)}, bf16[256,128]{1,0:T(8,128)(2,1)S(1)}, u32[]{:S(2)}, u32[]{:S(2)}) collective-permute-start(bf16[256,128]{1,0:T(8,128)(2,1)S(1)} %add_convert_fusion.refs_3_.refs_1_.refs_2_), channel_id=1, source_target_pairs={{0,16},{2,18},{4,20},{6,22},{8,24},{10,26},{12,28},{14,30},{16,0},... | collective-permute-start | bytes 196616 | tf_op jit(solution)/shard_map/ppermute | solution.py:648
  126.0 4.3 %collective-permute-start.48 = (bf16[256,128]{1,0:T(8,128)(2,1)S(1)}, bf16[256,128]{1,0:T(8,128)(2,1)S(1)}, u32[]{:S(2)}, u32[]{:S(2)}) collective-permute-start(bf16[256,128]{1,0:T(8,128)(2,1)S(1)} %add_convert_fusion.refs_3_.refs_1_.refs_2_), channel_id=1, source_target_pairs={{0,24},{2,26},{4,28},{6,30},{8,0},{10,2},{12,4},{14,6},{16,8},{18,... | collective-permute-start | bytes 196616 | tf_op jit(solution)/shard_map/ppermute | solution.py:648
  132.9 8.7 %collective-permute-start.51 = (bf16[512,256]{1,0:T(8,128)(2,1)S(1)}, bf16[512,256]{1,0:T(8,128)(2,1)S(1)}, u32[]{:S(2)}, u32[]{:S(2)}) collective-permute-start(bf16[512,256]{1,0:T(8,128)(2,1)S(1)} %shard_map.107.refs_3_.refs_1_), channel_id=1, source_target_pairs={{0,4},{2,6},{4,0},{6,2},{8,12},{10,14},{12,8},{14,10},{16,20},{18,... | collective-permute-start | bytes 786440 | tf_op jit(solution)/shard_map/ppermute | solution.py:644
  134.1 14.4 %collective-permute-start.53 = (bf16[512,256]{1,0:T(8,128)(2,1)S(1)}, bf16[512,256]{1,0:T(8,128)(2,1)S(1)}, u32[]{:S(2)}, u32[]{:S(2)}) collective-permute-start(bf16[512,256]{1,0:T(8,128)(2,1)S(1)} %shard_map.107.refs_3_.refs_1_), channel_id=1, source_target_pairs={{0,2},{2,0},{4,6},{6,4},{8,10},{10,8},{12,14},{14,12},{16,18},{18,... | collective-permute-start | bytes 786440 | tf_op jit(solution)/shard_map/ppermute | solution.py:644
  141.7 7.2 %collective-permute-start.54 = (bf16[512,256]{1,0:T(8,128)(2,1)S(1)}, bf16[512,256]{1,0:T(8,128)(2,1)S(1)}, u32[]{:S(2)}, u32[]{:S(2)}) collective-permute-start(bf16[512,256]{1,0:T(8,128)(2,1)S(1)} %shard_map.110.refs_2_), channel_id=1, source_target_pairs={{0,2},{2,0},{4,6},{6,4},{8,10},{10,8},{12,14},{14,12},{16,18},{18,... | collective-permute-start | bytes 786440 | tf_op jit(solution)/shard_map/ppermute | solution.py:644
  (9 other events, 23.0 us)
